TPU v7x, 32 devices: a whole 2x2x4 slice. The times are simulated.
32 devices in a mesh: seq: 8 (over y, x, core), tp: 4 (over z).
Axes of the slice: x: 2, y: 2, z: 4, core: 2. Of those that a mesh axis runs over, the one named last changes fastest.
Arguments:
- tokens: bfloat16 [16384, 1024], P(('seq', 'tp')), may hold values from -6 to 6
- w_qkv: bfloat16 [1024, 3, 1024], P(None, None, 'tp'), may hold values from -0.1875 to 0.1875
- w_out: bfloat16 [1024, 1024], P('tp'), may hold values from -3 to 3
- w_up: bfloat16 [1024, 4096], P(None, 'tp'), may hold values from -0.1875 to 0.1875
- w_down: bfloat16 [4096, 1024], P('tp'), may hold values from -0.09375 to 0.09375
- gain_one: float32 [1024], replicated, may hold values from 0.1 to 1.9
- gain_two: float32 [1024], replicated, may hold values from 0.1 to 1.9
- cotangent: bfloat16 [16384, 1024], P(('seq', 'tp')), may hold values from -6 to 6
- bucket: int32 [8], P('seq'), may hold values from 0 to 1, as said below
- lengths: int32 [8, 4], P('seq'), may hold values from 0 to 2048, as said below
Outputs:
- mixed: bfloat16 [16384, 1024], P(('seq', 'tp'))
- tokens_grad: bfloat16 [16384, 1024], P(('seq', 'tp'))
- grad_qkv: float32 [1024, 3, 1024], P(None, None, 'tp')
- grad_out: float32 [1024, 1024], P('tp')
- grad_up: float32 [1024, 4096], P(None, 'tp')
- grad_down: float32 [4096, 1024], P('tp')
- grad_gain_one: float32 [1024], replicated
- grad_gain_two: float32 [1024], replicated
Inputs may be any that keep to these rules, and one draw needn't show every extreme that they name: Every draw has groups of both buckets; bucket 1 means one sequence of 2048 positions, bucket 0 means 4 sequences of 512 positions. `lengths`: for a group of bucket 1 the first entry is its sequence's length, from 1024 to 2048, and the others are 0; for bucket 0 each entry is from 256 to 512; padding stands at the end of a sequence, and some group holds a sequence of full length 2048.
All inputs are finite; a program needn't handle non-finite values.
Results may differ from a plain program's by a relative error of at most 0.014.
Values may be sent and summed in bfloat16 or wider, within the bound.
No kernel may reach another device: no remote copies, remote signals or barrier semaphores. Data moves between devices by JAX's collectives and lax.ppermute only.
A program may use at most 192 MiB of HBM per device.

v0:
```python
import jax
import jax.numpy as jnp
from jax import lax
from jax.sharding import PartitionSpec as P

HEAD = 64
SLOTS = 4


ln_eps = 1e-05


def layer_norm(values, gain):
    centre = values - jnp.mean(values, axis=-1, keepdims=True)
    spread = jnp.mean(centre * centre, axis=-1, keepdims=True)
    return centre * lax.rsqrt(spread + ln_eps) * gain


def exact_gelu(values):
    return jax.nn.gelu(values, approximate=False)


def group_mask(bucket_id, slot_lengths, row_count):
    slot_rows = row_count // SLOTS
    position = jnp.arange(row_count, dtype=jnp.int32)
    whole_group = bucket_id == 1
    segment = jnp.where(whole_group, 0, position // slot_rows)
    inside = jnp.where(whole_group, position, position % slot_rows)
    chosen = segment[:, None] == jnp.arange(SLOTS, dtype=jnp.int32)[None, :]
    limit = jnp.sum(jnp.where(chosen, slot_lengths[None, :], 0), axis=1)
    return (segment, inside < limit)


def split_rows(array, batch):
    return array.reshape((batch, array.shape[0] // batch) + array.shape[1:])


def masked_scores(block_queries, keys_all, block_segment, segment, valid, score_scale):
    scores = (
        jnp.einsum("bqhe,bkhe->bhqk", block_queries, keys_all, preferred_element_type=jnp.float32)
        * score_scale
    )
    allowed = (block_segment[:, :, None] == segment[:, None, :]) & valid[:, None, :]
    return jnp.where(allowed[:, None], scores, -1000000000.0)


def batched_forward(members):
    queries, keys_all, values_all, segment, valid = members
    batch, length, heads, width = queries.shape
    block_rows = min(512, length)
    block_count = length // block_rows
    score_scale = width ** (-0.5)
    query_blocks = jnp.moveaxis(queries.reshape(batch, block_count, block_rows, heads, width), 1, 0)
    segment_blocks = jnp.moveaxis(segment.reshape(batch, block_count, block_rows), 1, 0)

    def one_block(member):
        block_queries, block_segment = member
        scores = masked_scores(block_queries, keys_all, block_segment, segment, valid, score_scale)
        log_total = jax.nn.logsumexp(scores, axis=-1)
        weights = jnp.exp(scores - log_total[..., None]).astype(jnp.bfloat16)
        outputs = jnp.einsum(
            "bhqk,bkhe->bqhe", weights, values_all, preferred_element_type=jnp.float32
        )
        return (outputs, log_total)

    outputs, log_totals = lax.map(one_block, (query_blocks, segment_blocks))
    outputs = jnp.moveaxis(outputs, 0, 1).reshape(batch * length, heads, width)
    log_totals = jnp.moveaxis(jnp.moveaxis(log_totals, 3, 2), 0, 1).reshape(batch * length, heads)
    return (outputs, log_totals)


def batched_backward(members):
    queries, keys_all, values_all, log_totals, grad_attended, segment, valid = members
    batch, length, heads, width = queries.shape
    block_rows = min(512, length)
    block_count = length // block_rows
    score_scale = width ** (-0.5)

    def blocks_of(array):
        return jnp.moveaxis(array.reshape((batch, block_count, block_rows) + array.shape[2:]), 1, 0)

    def one_block(carry, member):
        grad_keys, grad_values = carry
        block_queries, block_segment, block_totals, block_grad = member
        scores = masked_scores(block_queries, keys_all, block_segment, segment, valid, score_scale)
        weights = jnp.exp(scores - jnp.moveaxis(block_totals, 2, 1)[..., None])
        grad_weights = jnp.einsum(
            "bqhe,bkhe->bhqk", block_grad, values_all, preferred_element_type=jnp.float32
        )
        inner = jnp.sum(weights * grad_weights, axis=-1, keepdims=True)
        grad_scores = (weights * (grad_weights - inner)).astype(jnp.bfloat16)
        grad_queries = (
            jnp.einsum("bhqk,bkhe->bqhe", grad_scores, keys_all, preferred_element_type=jnp.float32)
            * score_scale
        )
        grad_keys = (
            grad_keys
            + jnp.einsum(
                "bhqk,bqhe->bkhe", grad_scores, block_queries, preferred_element_type=jnp.float32
            )
            * score_scale
        )
        grad_values = grad_values + jnp.einsum(
            "bhqk,bqhe->bkhe",
            weights.astype(jnp.bfloat16),
            block_grad,
            preferred_element_type=jnp.float32,
        )
        return ((grad_keys, grad_values), grad_queries)

    zero_grads = jnp.zeros(keys_all.shape, jnp.float32)
    (grad_keys, grad_values), grad_queries = lax.scan(
        one_block,
        (zero_grads, zero_grads),
        (blocks_of(queries), blocks_of(segment), blocks_of(log_totals), blocks_of(grad_attended)),
    )
    grad_queries = jnp.moveaxis(grad_queries, 0, 1).reshape(batch * length, heads, width)
    return (
        grad_queries,
        grad_keys.reshape(batch * length, heads, width),
        grad_values.reshape(batch * length, heads, width),
    )


def attention_forward(queries, keys_all, values_all, segment, valid):
    operands = (queries, keys_all, values_all, segment, valid)

    def whole_group(members):
        return batched_forward(tuple((split_rows(member, 1) for member in members)))

    return whole_group(operands)


def attention_backward(queries, keys_all, values_all, log_totals, grad_attended, segment, valid):
    operands = (queries, keys_all, values_all, log_totals, grad_attended, segment, valid)

    def whole_group(members):
        return batched_backward(tuple((split_rows(member, 1) for member in members)))

    return whole_group(operands)


def per_device(tokens, w_qkv, w_out, w_up, w_down, gain_one, gain_two, cotangent, bucket, lengths):
    gathered = lax.all_gather(tokens, "tp", axis=0, tiled=True)
    row_count = gathered.shape[0]
    local_heads = w_qkv.shape[2] // HEAD
    segment, valid = group_mask(bucket[0], lengths[0], row_count)
    projected = jnp.einsum(
        "rd,dcn->rcn", gathered, w_qkv, preferred_element_type=jnp.float32
    ).astype(jnp.bfloat16)
    queries = projected[:, 0].reshape(row_count, local_heads, HEAD)
    keys_all = projected[:, 1].reshape(row_count, local_heads, HEAD)
    values_all = projected[:, 2].reshape(row_count, local_heads, HEAD)
    attended, log_totals = attention_forward(queries, keys_all, values_all, segment, valid)
    attended = attended.reshape(row_count, -1).astype(jnp.bfloat16)
    branch = lax.psum_scatter(
        jnp.dot(attended, w_out, preferred_element_type=jnp.float32),
        "tp",
        scatter_dimension=0,
        tiled=True,
    )
    first_sum = tokens.astype(jnp.float32) + branch
    normed, first_pull = jax.vjp(layer_norm, first_sum, gain_one)
    normed_all = lax.all_gather(normed.astype(jnp.bfloat16), "tp", axis=0, tiled=True)
    expanded = jnp.dot(normed_all, w_up, preferred_element_type=jnp.float32)
    activated_full, gelu_pull = jax.vjp(exact_gelu, expanded)
    activated = activated_full.astype(jnp.bfloat16)
    shrunk = lax.psum_scatter(
        jnp.dot(activated, w_down, preferred_element_type=jnp.float32),
        "tp",
        scatter_dimension=0,
        tiled=True,
    )
    mixed, second_pull = jax.vjp(layer_norm, normed + shrunk, gain_two)
    grad_second, grad_gain_two = second_pull(cotangent.astype(jnp.float32))
    grad_second_all = lax.all_gather(grad_second.astype(jnp.bfloat16), "tp", axis=0, tiled=True)
    grad_down = jnp.einsum(
        "rf,rd->fd", activated, grad_second_all, preferred_element_type=jnp.float32
    )
    grad_activated = jnp.einsum(
        "rd,fd->rf", grad_second_all, w_down, preferred_element_type=jnp.float32
    )
    grad_expanded = gelu_pull(grad_activated)[0].astype(jnp.bfloat16)
    grad_up = jnp.einsum("rd,rf->df", normed_all, grad_expanded, preferred_element_type=jnp.float32)
    grad_normed_part = jnp.einsum(
        "rf,df->rd", grad_expanded, w_up, preferred_element_type=jnp.float32
    )
    grad_normed = grad_second + lax.psum_scatter(
        grad_normed_part, "tp", scatter_dimension=0, tiled=True
    )
    grad_first, grad_gain_one = first_pull(grad_normed)
    grad_first_all = lax.all_gather(grad_first.astype(jnp.bfloat16), "tp", axis=0, tiled=True)
    grad_out = jnp.einsum("rn,rd->nd", attended, grad_first_all, preferred_element_type=jnp.float32)
    grad_attended = jnp.einsum(
        "rd,nd->rn", grad_first_all, w_out, preferred_element_type=jnp.float32
    )
    grad_attended = grad_attended.astype(jnp.bfloat16).reshape(row_count, local_heads, HEAD)
    grad_queries, grad_keys, grad_values = attention_backward(
        queries, keys_all, values_all, log_totals, grad_attended, segment, valid
    )
    grad_projected = jnp.stack((grad_queries, grad_keys, grad_values), axis=1).reshape(
        row_count, 3, -1
    )
    grad_projected = grad_projected.astype(jnp.bfloat16)
    grad_qkv = jnp.einsum(
        "rd,rcn->dcn", gathered, grad_projected, preferred_element_type=jnp.float32
    )
    input_part = jnp.einsum(
        "rcn,dcn->rd", grad_projected, w_qkv, preferred_element_type=jnp.float32
    )
    tokens_grad = grad_first + lax.psum_scatter(input_part, "tp", scatter_dimension=0, tiled=True)
    grad_qkv, grad_out, grad_up, grad_down = lax.psum(
        (grad_qkv, grad_out, grad_up, grad_down), "seq"
    )
    gain_sums = lax.psum((grad_gain_one, grad_gain_two), ("seq", "tp"))
    return (
        mixed.astype(jnp.bfloat16),
        tokens_grad.astype(jnp.bfloat16),
        grad_qkv,
        grad_out,
        grad_up,
        grad_down,
        gain_sums[0],
        gain_sums[1],
    )


def solution(mesh):
    return jax.shard_map(
        per_device,
        mesh=mesh,
        in_specs=(
            P(("seq", "tp"), None),
            P(None, None, "tp"),
            P("tp", None),
            P(None, "tp"),
            P("tp", None),
            P(),
            P(),
            P(("seq", "tp"), None),
            P("seq"),
            P("seq", None),
        ),
        out_specs=(
            P(("seq", "tp"), None),
            P(("seq", "tp"), None),
            P(None, None, "tp"),
            P("tp", None),
            P(None, "tp"),
            P("tp", None),
            P(),
            P(),
        ),
        check_vma=False,
    )
```

profile of v0, /device:TPU:0, one launch (start us, length us, event | category | flops | bytes accessed | tf_op | source)
XLA Modules:
  0.0 1485.7 jit_solution(17806406919977911814)
XLA Ops:
  9.4 83.7 %all-gather.5.cloned.1.call-done = bf16[2048,1024]{1,0:T(8,128)(2,1)} async-done(((bf16[512,1024]{1,0:T(8,128)(2,1)}), bf16[2048,1024]{1,0:T(8,128)(2,1)}) %all-gather.5.cloned.1.call-update) | async-done | bytes 4194320 | tf_op jit(solution)/shard_map/all_gather | solution.py:144
  93.1 6.1 fusion.71
  107.3 59.6 %while.28 = (s32[]{:T(128)}, bf16[4,1,512,4,64]{2,4,3,1,0:T(8,128)(2,1)}, f32[4,1,4,512]{3,2,1,0:T(4,128)}, s32[4,1,512]{2,1,0:T(1,128)S(1)}, pred[2048]{0:T(102...) while((s32[]{:T(128)}, ...), condition=%wide.region_4.5_spmd.clone, body=%wide.region_1.4_spmd.clone.sunk | while | flops 1122011136 | bytes 70115544 | solution.py:66
  108.0 4.4 fusion.150
  122.9 4.4 fusion.150
  137.8 4.4 fusion.150
  152.7 4.4 fusion.150
  170.5 4.6 fusion.101
  175.3 143.1 %reduce-scatter.5.cloned.1.call-done = f32[512,1024]{1,0:T(8,128)} async-done(((f32[2048,1024]{1,0:T(8,128)}), f32[512,1024]{1,0:T(8,128)}) %reduce-scatter.5.cloned.1.call-update) | async-done | bytes 2097168 | tf_op jit(solution)/shard_map/reduce_scatter | solution.py:156
  322.9 81.6 %all-gather.7.cloned.1.call-done = bf16[2048,1024]{1,0:T(8,128)(2,1)} async-done(((bf16[512,1024]{1,0:T(8,128)(2,1)}), bf16[2048,1024]{1,0:T(8,128)(2,1)}) %all-gather.7.cloned.1.call-update) | async-done | bytes 4194320 | tf_op jit(solution)/shard_map/all_gather | solution.py:164
  404.5 25.5 %multiply_convert_fusion.1 = (bf16[2048,1024]{1,0:T(8,128)(2,1)S(1)}, f32[2048,1024]{1,0:T(8,128)}, f32[2048,1024]{1,0:T(8,128)}) fusion(bf16[2048,1024]{1,0:T(8,128)(2,1)} %all-gather.7.cloned.1.call-done, bf16[1024,1024]{1,0:T(8,128)(2,1)S(1)} %copy-done), kind=kOutput, calls=%fused_computation.81 | convolution fusion | flops 4431282176 | bytes 27262976 | tf_op jit(solution)/shard_map/dot_general | solution.py:165
  432.1 6.6 fusion.102
  438.8 143.1 %reduce-scatter.7.cloned.1.call-done = f32[512,1024]{1,0:T(8,128)} async-done(((f32[2048,1024]{1,0:T(8,128)}), f32[512,1024]{1,0:T(8,128)}) %reduce-scatter.7.cloned.1.call-update) | async-done | bytes 2097168 | tf_op jit(solution)/shard_map/reduce_scatter | solution.py:168
  590.7 81.6 %all-gather.9.cloned.1.call-done = bf16[2048,1024]{1,0:T(8,128)(2,1)} async-done(((bf16[512,1024]{1,0:T(8,128)(2,1)}), bf16[2048,1024]{1,0:T(8,128)(2,1)}) %all-gather.9.cloned.1.call-update) | async-done | bytes 4194320 | tf_op jit(solution)/shard_map/all_gather | solution.py:176
  672.3 12.9 add_convert_fusion
  687.3 6.9 fusion.103
  694.2 143.1 %reduce-scatter.9.cloned.1.call-done = f32[512,1024]{1,0:T(8,128)} async-done(((f32[2048,1024]{1,0:T(8,128)}), f32[512,1024]{1,0:T(8,128)}) %reduce-scatter.9.cloned.1.call-update) | async-done | bytes 2097168 | tf_op jit(solution)/shard_map/reduce_scatter | solution.py:188
  844.3 10.2 fusion.106
  854.5 6.1 fusion.105
  860.6 65.3 %all-gather.11.cloned.1.call-done = bf16[2048,1024]{1,0:T(8,128)(2,1)} async-done(((bf16[512,1024]{1,0:T(8,128)(2,1)}), bf16[2048,1024]{1,0:T(8,128)(2,1)}) %all-gather.11.cloned.1.call-update) | async-done | bytes 4194320 | tf_op jit(solution)/shard_map/all_gather | solution.py:192
  925.9 4.5 convolution_convert_fusion
  937.1 188.6 %while.29 = (s32[]{:T(128)}, f32[1,2048,4,64]{1,3,2,0:T(8,128)}, f32[1,2048,4,64]{1,3,2,0:T(8,128)}, bf16[4,1,512,4,64]{2,4,3,1,0:T(8,128)(2,1)}, bf16[4,1,512,4...) while((s32[]{:T(128)}, f32[1,2048,4,64]{1,3,2,0:T(8,128)}, ...), condition=%wide.region_18.19_spmd.clone, body=%wide.region_16.18_spmd.clone.sunk | while | flops 2752135168 | bytes 180961520 | solution.py:112
  943.2 7.2 fusion.165
  950.4 11.5 multiply_reduce_fusion.6
  961.9 11.0 multiply_convert_fusion.5
  972.8 6.9 fusion.166
  989.4 7.6 fusion.165
  997.0 11.5 multiply_reduce_fusion.6
  1008.5 11.0 multiply_convert_fusion.5
  1019.4 6.9 fusion.166
  1026.4 4.6 fusion.164
  1036.7 7.6 fusion.165
  1044.3 11.5 multiply_reduce_fusion.6
  1055.8 11.0 multiply_convert_fusion.5
  1066.7 6.9 fusion.166
  1073.7 4.6 fusion.164
  1084.0 7.6 fusion.165
  1091.6 11.5 multiply_reduce_fusion.6
  1103.1 11.0 multiply_convert_fusion.5
  1114.0 6.9 fusion.166
  1121.0 4.6 fusion.164
  1130.0 4.3 reshape.435
  1138.9 4.6 fusion.104
  1143.5 5.2 fusion.78
  1149.9 7.1 convolution_bitcast_fusion
  1157.8 40.3 %all-reduce = (f32[1024]{0:T(1024)}, f32[1024]{0:T(1024)}) all-reduce(f32[1024]{0:T(1024)S(1)} %copy-done.35, f32[1024]{0:T(1024)S(1)} %copy-done.34), channel_id=1, replica_groups=mesh['seq'=8,'tp'=4] {'seq','tp'}, use_global_device_ids=true, to_apply=%region_25.26 | all-reduce | flops 2048 | bytes 16384 | tf_op jit(solution)/shard_map/psum | solution.py:215
  1198.0 124.2 %all-reduce.4.cloned.1.call-done = (f32[1024,3,256]{0,2,1:T(8,128)}, f32[256,1024]{1,0:T(8,128)}, f32[1024,1024]{1,0:T(8,128)}, f32[1024,1024]{1,0:T(8,128)}) async-done(((f32[1024,3,256]{0,2,1:T(8,128)}, f32[256,1024]{1,0:T(8,128)}, f32[1024,1024]{1,0:T(8,128)}, f32[1024,1024]{1,0:T(8,128)}), (f32[1024,3,256]{0,2,1:T(8,128)}, f32[256,1024]{1,0:T(8,128)}, f32[1024,1024]{1,0:T(8,128)}, ...) | async-done | bytes 12582928 | tf_op jit(solution)/shard_map/psum | solution.py:212
  1325.7 143.5 %reduce-scatter.11.cloned.1.call-done = f32[512,1024]{1,0:T(8,128)} async-done(((f32[2048,1024]{1,0:T(8,128)}), f32[512,1024]{1,0:T(8,128)}) %reduce-scatter.11.cloned.1.call-update) | async-done | bytes 2097168 | tf_op jit(solution)/shard_map/reduce_scatter | solution.py:211
  (232 shorter events, 136.4 us)
Async XLA Ops:
  7.2 397.4 %copy-start = (bf16[1024,1024]{1,0:T(8,128)(2,1)S(1)}, bf16[1024,1024]{1,0:T(8,128)(2,1)}, u32[]{:S(2)}) copy-start(bf16[1024,1024]{1,0:T(8,128)(2,1)} %param.17) | copy-start | bytes 6291460
  7.2 85.9 %all-gather.5.cloned.1.call-start = ((), (), s32[]{:S(2)}) async-start(), calls=%async_computation.4 | async-start | bytes 5242880 | tf_op jit(solution)/shard_map/all_gather | solution.py:144
  7.9 310.4 %reduce-scatter.5.cloned.1.call-start = ((), (), s32[]{:S(2)}) async-start(), calls=%async_computation.5 | async-start | bytes 10485760 | tf_op jit(solution)/shard_map/reduce_scatter | solution.py:156
  112.5 4.4 copy-start.9
  112.5 4.4 copy-start.18
  127.4 4.4 copy-start.9
  127.4 4.4 copy-start.18
  142.3 4.4 copy-start.9
  142.3 4.4 copy-start.18
  157.2 4.4 copy-start.9
  157.2 4.4 copy-start.18
  166.8 8.3 copy-start.3
  166.8 8.3 copy-start.28
  166.8 8.3 copy-start.30
  166.8 3.7 copy-start.26
  175.2 143.2 %copy-start.15 = (bf16[512,1024]{1,0:T(8,128)(2,1)S(1)}, bf16[512,1024]{1,0:T(8,128)(2,1)}, u32[]{:S(2)}) copy-start(bf16[512,1024]{1,0:T(8,128)(2,1)} %param.14) | copy-start | bytes 3145732
  175.2 146.3 %copy-start.31 = (f32[1024]{0:T(1024)S(1)}, f32[1024]{0:T(1024)}, u32[]{:S(2)}) copy-start(f32[1024]{0:T(1024)} %param.19) | copy-start | bytes 12292
  175.2 229.3 %all-gather.7.cloned.1.call-start = ((), (), s32[]{:S(2)}) async-start(), calls=%async_computation.6 | async-start | bytes 5242880 | tf_op jit(solution)/shard_map/all_gather | solution.py:164
  322.9 259.0 %reduce-scatter.7.cloned.1.call-start = ((), (), s32[]{:S(2)}) async-start(), calls=%async_computation.7 | async-start | bytes 10485760 | tf_op jit(solution)/shard_map/reduce_scatter | solution.py:168
  404.5 27.5 %copy-start.39 = (bf16[1024,1024]{1,0:T(8,128)(2,1)S(1)}, bf16[1024,1024]{1,0:T(8,128)(2,1)}, u32[]{:S(2)}) copy-start(bf16[1024,1024]{1,0:T(8,128)(2,1)} %param.18) | copy-start | bytes 6291460
  438.7 146.3 %copy-start.20 = (bf16[512,1024]{1,0:T(8,128)(2,1)S(1)}, bf16[512,1024]{1,0:T(8,128)(2,1)}, u32[]{:S(2)}) copy-start(bf16[512,1024]{1,0:T(8,128)(2,1)} %param.21) | copy-start | bytes 3145732
  438.7 146.3 %copy-start.36 = (f32[1024]{0:T(1024)S(1)}, f32[1024]{0:T(1024)}, u32[]{:S(2)}) copy-start(f32[1024]{0:T(1024)} %param.20) | copy-start | bytes 12292
  438.7 233.6 %all-gather.9.cloned.1.call-start = ((), (), s32[]{:S(2)}) async-start(), calls=%async_computation.8 | async-start | bytes 5242880 | tf_op jit(solution)/shard_map/all_gather | solution.py:176
  590.7 246.6 %reduce-scatter.9.cloned.1.call-start = ((), (), s32[]{:S(2)}) async-start(), calls=%async_computation.9 | async-start | bytes 10485760 | tf_op jit(solution)/shard_map/reduce_scatter | solution.py:188
  694.1 143.2 %copy-start.8 = (f32[512,1024]{1,0:T(8,128)S(1)}, f32[512,1024]{1,0:T(8,128)}, u32[]{:S(2)}) copy-start(f32[512,1024]{1,0:T(8,128)} %copy-done.7) | copy-start | bytes 6291460
  694.1 231.7 %all-gather.11.cloned.1.call-start = ((), (), s32[]{:S(2)}) async-start(), calls=%async_computation.10 | async-start | bytes 5242880 | tf_op jit(solution)/shard_map/all_gather | solution.py:192
  844.2 478.0 %all-reduce.4.cloned.1.call-start = ((), (), s32[]{:S(2)}) async-start(), calls=%async_computation.12 | async-start | bytes 25165824 | tf_op jit(solution)/shard_map/psum | solution.py:212
  844.3 10.2 copy-start.38
  844.3 10.2 copy-start.42
  854.5 71.4 %copy-start.27 = (bf16[256,1024]{1,0:T(8,128)(2,1)S(1)}, bf16[256,1024]{1,0:T(8,128)(2,1)}, u32[]{:S(2)}) copy-start(bf16[256,1024]{1,0:T(8,128)(2,1)} %param.16) | copy-start | bytes 1572868
  930.3 6.8 copy-start.4
  930.3 6.8 copy-start.29
  972.8 7.0 copy-start.2
  1019.4 7.0 copy-start.2
  1066.7 7.0 copy-start.2
  1114.0 7.0 copy-start.2
  1125.8 8.6 copy-start.6
  1134.5 4.4 copy-start.14
  1138.9 4.6 copy-start.21
  1138.9 4.6 copy-start.23
  1138.9 4.6 copy-start.24
  1138.9 4.6 copy-start.37
  1148.7 320.6 %reduce-scatter.11.cloned.1.call-start = ((), (), s32[]{:S(2)}) async-start(), calls=%async_computation.11 | async-start | bytes 10485760 | tf_op jit(solution)/shard_map/reduce_scatter | solution.py:211
  1157.1 312.2 %copy-start.11 = (f32[512,1024]{1,0:T(8,128)S(1)}, f32[512,1024]{1,0:T(8,128)}, u32[]{:S(2)}) copy-start(f32[512,1024]{1,0:T(8,128)} %copy-done.10) | copy-start | bytes 6291460
  1157.1 312.2 %copy-start.33 = (f32[512]{0:T(512)S(1)}, f32[512]{0:T(512)}, u32[]{:S(2)}) copy-start(f32[512]{0:T(512)} %copy-done.32) | copy-start | bytes 6148
  1325.7 146.5 %copy-start.22 = (f32[256,1024]{1,0:T(8,128)S(1)}, f32[256,1024]{1,0:T(8,128)}, u32[]{:S(2)}) copy-start(f32[256,1024]{1,0:T(8,128)} %get-tuple-element.558) | copy-start | bytes 3145732
  1469.3 3.9 copy-start.17
  1473.2 5.7 copy-start.1
  (19 other events, 34.8 us)
Sparse Core Ops, SparseCore 0:
  9.6 83.4 all-gather.4
  175.3 142.9 reduce-scatter.4
  323.0 81.4 all-gather.6
  438.8 142.9 reduce-scatter.6
  590.8 81.4 all-gather.8
  694.3 142.9 reduce-scatter.8
  844.3 81.4 all-gather.10
  1148.8 173.3 all-reduce.3
  1324.7 144.5 reduce-scatter.10
where the time goes:
time: 1490 us
  waiting for transfers between devices  1010 us (68%)
  matrix products  271 us (18%)
  other arithmetic  92 us (6%)
  local copies, waits for them, and re-layouts  56.3 us (4%)
  blocking collectives  40.3 us (3%)
  between operations  15 us (1%)
    reduce_scatter x1, waiting for transfers between devices, per_device(): lax.psum_scatter(input_part, 'tp', scatter_dimension=0, tiled=True)  144 us
    reduce_scatter x1, waiting for transfers between devices, per_device(): lax.psum_scatter(grad_normed_part, 'tp', scatter_dimension=0, tiled=True)  143 us
    reduce_scatter x1, waiting for transfers between devices, per_device(): lax.psum_scatter(jnp.dot(attended, w_out, preferred_element_type=jnp.floa...  143 us
    reduce_scatter x1, waiting for transfers between devices, per_device(): lax.psum_scatter(jnp.dot(activated, w_down, preferred_element_type=jnp.fl...  143 us
    psum x1, waiting for transfers between devices, per_device(): lax.psum((grad_qkv, grad_out, grad_up, grad_down), 'seq')  124 us
    all_gather x1, waiting for transfers between devices, per_device(): gathered = lax.all_gather(tokens, 'tp', axis=0, tiled=True)  83.7 us
    all_gather x1, waiting for transfers between devices, per_device(): lax.all_gather(normed.astype(jnp.bfloat16), 'tp', axis=0, tiled=True)  81.6 us
    all_gather x1, waiting for transfers between devices, per_device(): lax.all_gather(grad_second.astype(jnp.bfloat16), 'tp', axis=0, tiled=True)  81.6 us
  transfers between devices with their start and end apart: 9, of which 9 were waited for; matrix products, arithmetic and copies ran while one was open for 2% of the time, Pallas kernels for 0%

commit v1 on v0

v1 whole, which is shorter than its diff:
```python
import functools

import jax
import jax.numpy as jnp
from jax import lax
from jax.experimental import pallas as pl
from jax.experimental.pallas import tpu as pltpu
from jax.sharding import PartitionSpec as P

HEAD = 64
SLOTS = 4
BF = jnp.bfloat16
F32 = jnp.float32
LOG2E = 1.4426950408889634
LN_EPS = 1e-5
NT = (((1,), (1,)), ((), ()))
NN = (((1,), (0,)), ((), ()))
TN = (((0,), (0,)), ((), ()))

PAIR = [(0, 1), (1, 0), (2, 3), (3, 2)]
MIDDLE = [(1, 2), (2, 1)]
OUTWARD = [(1, 0), (2, 3)]
INWARD = [(0, 1), (3, 2)]


def mm(a, b, dims, out=F32):
    return lax.dot_general(a, b, dims, preferred_element_type=F32).astype(out)


def along(array, pairs):
    return lax.ppermute(array, "tp", pairs)


def line_gather(own, middle):
    near = along(own, PAIR)
    far = along(own, MIDDLE)
    second = along(near, MIDDLE)
    second_end = along(far, OUTWARD)
    third_end = along(second, OUTWARD)
    return [
        own,
        near,
        jnp.where(middle, second, second_end),
        jnp.where(middle, far, third_end),
    ]


def line_scatter(parts):
    first, near, second, third = parts
    up = lambda a: a.astype(F32)
    from_third = along(third, INWARD)
    from_second = along(second, INWARD)
    second_sum = (up(second) + up(from_third)).astype(BF)
    near_in = along(second_sum, MIDDLE)
    third_sum = (up(third) + up(from_second)).astype(BF)
    near_sum = (up(near) + up(near_in)).astype(BF)
    far_in = along(third_sum, MIDDLE)
    last = along(near_sum, PAIR)
    return up(first) + up(last) + up(far_in)


class Plane:
    def __init__(self, size):
        self.size = size

    def swap(self, array, bit):
        return lax.ppermute(array, "seq", [(i, i ^ bit) for i in range(self.size)])

    def gather(self, own):
        half = own.shape[0] // 2
        by_x = self.swap(own, 2)
        by_y = self.swap(own, 4)
        diag = (self.swap(by_y[:half], 2), self.swap(by_x[half:], 4))
        other = [self.swap(a, 1) for a in (own, by_x, by_y) + diag]
        diag, other_diag = jnp.concatenate(diag), jnp.concatenate(other[3:])
        return [own, other[0], by_x, other[1], by_y, other[2], diag, other_diag]

    def reduce(self, pieces):
        up = lambda a: a.astype(F32)
        came = [self.swap(pieces[i], 1) for i in (7, 5, 3, 1)][::-1]
        own, by_x, by_y, diag = [
            (up(pieces[2 * i]) + up(came[i])).astype(BF) for i in range(4)
        ]
        axis = diag.ndim - 2
        half = diag.shape[axis] // 2
        cut = lambda a, at: lax.slice_in_dim(a, at * half, (at + 1) * half, axis=axis)
        diag_x = self.swap(cut(diag, 0), 2)
        diag_y = self.swap(cut(diag, 1), 4)
        y_first = (up(cut(by_y, 0)) + up(diag_x)).astype(BF)
        x_second = (up(cut(by_x, 1)) + up(diag_y)).astype(BF)
        by_y = jnp.concatenate([y_first, cut(by_y, 1)], axis=axis)
        by_x = jnp.concatenate([cut(by_x, 0), x_second], axis=axis)
        total = up(own) + up(self.swap(by_x, 2)) + up(self.swap(by_y, 4))
        total = total.astype(BF)
        bit = 8
        while bit < self.size:
            total = (up(total) + up(self.swap(total, bit))).astype(BF)
            bit *= 2
        return total


def forward_kernel(q_ref, k_ref, v_ref, bias_ref, out_ref, lse_ref):
    scale = HEAD**-0.5
    rows = q_ref.shape[0]
    lane = lax.broadcasted_iota(jnp.int32, (1, 2 * HEAD), 1)
    bias = bias_ref[...]
    sub = 256
    for at in range(rows // sub):
        span = pl.ds(at * sub, sub)
        q = q_ref[span, :]
        outs, lses = [], []
        for head in range(2):
            mine = (lane < HEAD) == (head == 0)
            k = jnp.where(mine, k_ref[...], jnp.zeros((), BF))
            v = jnp.where(mine, v_ref[...], jnp.zeros((), BF))
            s = lax.dot_general(q, k, NT, preferred_element_type=F32)
            s = s * scale + bias
            top = jnp.max(s, axis=1, keepdims=True)
            p = jnp.exp(s - top)
            total = jnp.sum(p, axis=1, keepdims=True)
            o = lax.dot_general(p.astype(BF), v, NN, preferred_element_type=F32)
            outs.append(o / total)
            lses.append(top + jnp.log(total))
        out_ref[span, :] = (outs[0] + outs[1]).astype(BF)
        wide = jnp.where(lane < HEAD, lses[0], lses[1])
        flat = jnp.transpose(wide)
        lse_ref[0, :, span] = jnp.concatenate(
            [flat[0:1], flat[HEAD : HEAD + 1]], axis=0
        )


def attention_forward(q, kv, bias):
    rows, width = q.shape
    keys = kv.shape[0]
    pairs = width // (2 * HEAD)
    wide = 2 * HEAD
    return pl.pallas_call(
        forward_kernel,
        grid=(pairs,),
        in_specs=[
            pl.BlockSpec((rows, wide), lambda h: (0, h)),
            pl.BlockSpec((keys, wide), lambda h: (0, h)),
            pl.BlockSpec((keys, wide), lambda h: (0, h + pairs)),
            pl.BlockSpec((1, keys), lambda h: (0, 0)),
        ],
        out_specs=[
            pl.BlockSpec((rows, wide), lambda h: (0, h)),
            pl.BlockSpec((1, 2, rows), lambda h: (h, 0, 0)),
        ],
        out_shape=[
            jax.ShapeDtypeStruct((rows, width), BF),
            jax.ShapeDtypeStruct((pairs, 2, rows), F32),
        ],
        compiler_params=pltpu.CompilerParams(vmem_limit_bytes=48 * 2**20),
        cost_estimate=pl.CostEstimate(
            flops=16 * rows * keys * width, bytes_accessed=10 * keys * width, transcendentals=0
        ),
        name="attention_forward",
    )(q, kv, kv, bias)


def backward_kernel(
    q_ref, k_ref, v_ref, go_ref, lse_ref, inner_ref, bias_ref, gq_ref, gk_ref, gv_ref
):
    scale = HEAD**-0.5
    rows = q_ref.shape[0]
    keys = k_ref.shape[0]
    lane = lax.broadcasted_iota(jnp.int32, (1, 2 * HEAD), 1)
    q, go = q_ref[...], go_ref[...]
    sub = 512
    zero = jnp.zeros((), BF)
    total_q = jnp.zeros((rows, 2 * HEAD), F32)
    for at in range(keys // sub):
        span = pl.ds(at * sub, sub)
        bias = bias_ref[span, 0:1]
        total_k = jnp.zeros((sub, 2 * HEAD), F32)
        total_v = jnp.zeros((sub, 2 * HEAD), F32)
        for head in range(2):
            mine = (lane < HEAD) == (head == 0)
            k = jnp.where(mine, k_ref[span, :], zero)
            v = jnp.where(mine, v_ref[span, :], zero)
            s = lax.dot_general(k, q, NT, preferred_element_type=F32)
            p = jnp.exp(s * scale + (bias - lse_ref[0, head : head + 1, :]))
            gp = lax.dot_general(v, go, NT, preferred_element_type=F32)
            gs = (p * (gp - inner_ref[0, head : head + 1, :])).astype(BF)
            total_v += lax.dot_general(
                p.astype(BF), jnp.where(mine, go, zero), NN, preferred_element_type=F32
            )
            total_k += lax.dot_general(
                gs, jnp.where(mine, q, zero), NN, preferred_element_type=F32
            )
            total_q += lax.dot_general(gs, k, TN, preferred_element_type=F32)
        gk_ref[span, :] = (total_k * scale).astype(BF)
        gv_ref[span, :] = total_v.astype(BF)
    gq_ref[...] = (total_q * scale).astype(BF)


def attention_backward(q, kv, go, lse, inner, bias):
    rows, width = q.shape
    keys = kv.shape[0]
    pairs = width // (2 * HEAD)
    wide = 2 * HEAD
    return pl.pallas_call(
        backward_kernel,
        grid=(pairs,),
        in_specs=[
            pl.BlockSpec((rows, wide), lambda h: (0, h)),
            pl.BlockSpec((keys, wide), lambda h: (0, h)),
            pl.BlockSpec((keys, wide), lambda h: (0, h + pairs)),
            pl.BlockSpec((rows, wide), lambda h: (0, h)),
            pl.BlockSpec((1, 2, rows), lambda h: (h, 0, 0)),
            pl.BlockSpec((1, 2, rows), lambda h: (h, 0, 0)),
            pl.BlockSpec((keys, 128), lambda h: (0, 0)),
        ],
        out_specs=[
            pl.BlockSpec((rows, wide), lambda h: (0, h)),
            pl.BlockSpec((keys, wide), lambda h: (0, h)),
            pl.BlockSpec((keys, wide), lambda h: (0, h)),
        ],
        out_shape=[
            jax.ShapeDtypeStruct((rows, width), BF),
            jax.ShapeDtypeStruct((keys, width), BF),
            jax.ShapeDtypeStruct((keys, width), BF),
        ],
        compiler_params=pltpu.CompilerParams(vmem_limit_bytes=48 * 2**20),
        cost_estimate=pl.CostEstimate(
            flops=40 * rows * keys * width, bytes_accessed=14 * keys * width, transcendentals=0
        ),
        name="attention_backward",
    )(q, kv, kv, go, lse, inner, bias)


def centred(values):
    centre = values - jnp.mean(values, axis=-1, keepdims=True)
    root = lax.rsqrt(jnp.mean(centre * centre, axis=-1, keepdims=True) + LN_EPS)
    return centre * root, root


def norm_pull(grad, gain, unit, root):
    scaled = grad * gain
    mean = jnp.mean(scaled, axis=-1, keepdims=True)
    slope = jnp.mean(scaled * unit, axis=-1, keepdims=True)
    return root * (scaled - mean - unit * slope), jnp.sum(grad * unit, axis=0)


def gelu_pair(values):
    cdf = 0.5 * lax.erfc(values * -(0.5**0.5))
    pdf = jnp.exp(-0.5 * values * values) * 0.3989422804014327
    return (values * cdf).astype(BF), (cdf + values * pdf).astype(BF)


def per_device(
    seq_size, tokens, w_qkv, w_out, w_up, w_down, gain_one, gain_two, cotangent, bucket, lengths
):
    rows, width = tokens.shape
    t = lax.axis_index("tp")
    s8 = lax.axis_index("seq") % 8
    middle = (t == 1) | (t == 2)
    plane = Plane(seq_size)
    hid = w_out.shape[0]
    ff = w_down.shape[0]
    qp, fp = hid // 8, ff // 8

    attn_own = jnp.stack([w_qkv[:, 0].T, w_qkv[:, 1].T, w_qkv[:, 2].T, w_out])
    ff_own = jnp.stack([w_up.T, w_down])

    def piece(stacked, size):
        kinds = stacked.shape[0]
        part = lax.dynamic_slice_in_dim(stacked, s8 * size, size, axis=1)
        return part.reshape(kinds * size, width)

    attn_blocks = line_gather(piece(attn_own, qp), middle)
    token_blocks = line_gather(tokens, middle)
    ff_blocks = line_gather(piece(ff_own, fp), middle)

    attn_far = plane.gather(jnp.concatenate(attn_blocks[1:]))
    ff_far = plane.gather(jnp.concatenate(ff_blocks[1:]))
    attn_far = jnp.stack([a.reshape(3, 4, qp, width) for a in attn_far])
    attn_far = attn_far.reshape(4, 2, 3, 4, qp, width).transpose(3, 0, 2, 1, 4, 5)
    w_attn = jnp.concatenate([attn_own, attn_far.reshape(4, 3 * hid, width)], axis=1)
    ff_far = jnp.stack([a.reshape(3, 2, fp, width) for a in ff_far])
    ff_far = ff_far.transpose(2, 0, 1, 3, 4).reshape(2, 3 * ff, width)
    w_ff = jnp.concatenate([ff_own, ff_far], axis=1)
    wq, wkv, wo = w_attn[0], w_attn[1:3].reshape(2 * width, width), w_attn[3]
    wu, wd = w_ff[0], w_ff[1]

    whole = bucket[0] == 1
    place = jnp.arange(rows, dtype=jnp.int32)
    limits = []
    for j in range(4):
        block = t ^ j
        alone = lengths[0, block] if j == 0 else 0
        limits.append(jnp.where(whole, lengths[0, 0] - block * rows, alone))
    seen = jnp.concatenate([place < limit for limit in limits])
    bias = jnp.where(seen, 0.0, -1e9).astype(F32)
    bias_cols = jnp.broadcast_to(bias[:, None], (4 * rows, 128))

    gathered = jnp.concatenate(token_blocks)
    q = mm(tokens, wq, NT, BF)
    kv = mm(gathered, wkv, NT, BF)
    attended, lse = attention_forward(q, kv, bias[None])
    first_sum = tokens.astype(F32) + mm(attended, wo, NN)
    unit_one, root_one = centred(first_sum)
    normed = unit_one * gain_one
    normed_low = normed.astype(BF)
    activated, slope = gelu_pair(mm(normed_low, wu, NT))
    unit_two, root_two = centred(normed + mm(activated, wd, NN))
    mixed = (unit_two * gain_two).astype(BF)

    grad_second, gain_grad_two = norm_pull(cotangent.astype(F32), gain_two, unit_two, root_two)
    grad_second_low = grad_second.astype(BF)
    grad_down = mm(activated, grad_second_low, TN, BF)
    grad_expanded = (mm(grad_second_low, wd, NT) * slope.astype(F32)).astype(BF)
    grad_up = mm(grad_expanded, normed_low, TN, BF)

    def reduced(grads, kinds, size, split):
        own = grads[:, : 8 * size].reshape(kinds, 8, size, width)
        own = jnp.stack(
            [lax.dynamic_index_in_dim(own, s8 ^ i, axis=1, keepdims=False) for i in range(8)]
        )
        if split:
            far = grads[:, 8 * size :].reshape(kinds, 4, 3, 2, size, width)
            far = far.transpose(1, 3, 2, 0, 4, 5).reshape(8, 3, kinds, size, width)
        else:
            far = grads[:, 8 * size :].reshape(kinds, 8, 3, size, width)
            far = far.transpose(1, 2, 0, 3, 4)
        pieces = jnp.concatenate([own[:, None], far], axis=1)
        pieces = pieces.reshape(8, 4, kinds * size, width)
        mine = plane.reduce([pieces[i] for i in range(8)])
        total = line_scatter([mine[j] for j in range(4)]).astype(BF)
        all_eight = jnp.stack(plane.gather(total))
        ordered = jnp.stack(
            [lax.dynamic_index_in_dim(all_eight, s8 ^ i, keepdims=False) for i in range(8)]
        )
        ordered = ordered.reshape(8, kinds, size, width).transpose(1, 0, 2, 3)
        return ordered.reshape(kinds, 8 * size, width)

    ff_sum = reduced(jnp.stack([grad_up, grad_down]), 2, fp, False)

    grad_normed = grad_second + mm(grad_expanded, wu, NN)
    grad_first, gain_grad_one = norm_pull(grad_normed, gain_one, unit_one, root_one)
    grad_first_low = grad_first.astype(BF)
    grad_out = mm(attended, grad_first_low, TN, BF)
    go = mm(grad_first_low, wo, NT, BF)
    inner = (go.astype(F32) * attended.astype(F32)).reshape(rows, width // HEAD, HEAD).sum(-1)
    inner = inner.T.reshape(width // (2 * HEAD), 2, rows)
    gq, gk, gv = attention_backward(q, kv, go, lse, inner, bias_cols)
    wk, wv = w_attn[1], w_attn[2]
    parts = []
    for j in range(4):
        span = slice(j * rows, (j + 1) * rows)
        part = mm(gk[span], wk, NN) + mm(gv[span], wv, NN)
        if j == 0:
            part = part + mm(gq, wq, NN) + grad_first
        parts.append(part if j == 0 else part.astype(BF))
    tokens_grad = line_scatter(parts).astype(BF)
    grad_q = mm(gq, tokens, TN, BF)
    grad_k = mm(gk, gathered, TN, BF)
    grad_v = mm(gv, gathered, TN, BF)
    attn_sum = reduced(jnp.stack([grad_q, grad_k, grad_v, grad_out]), 4, qp, True)

    gains = jnp.stack([gain_grad_one, gain_grad_two])
    bit = 1
    while bit < seq_size:
        gains = gains + plane.swap(gains, bit)
        bit *= 2
    gains = gains + along(gains, [(i, i ^ 1) for i in range(4)])
    gains = gains + along(gains, [(i, i ^ 2) for i in range(4)])

    attn_sum, ff_sum = attn_sum.astype(F32), ff_sum.astype(F32)
    return (
        mixed,
        tokens_grad,
        attn_sum[:3].transpose(2, 0, 1),
        attn_sum[3],
        ff_sum[0].T,
        ff_sum[1],
        gains[0],
        gains[1],
    )


def solution(mesh):
    rows = P(("seq", "tp"), None)
    weights = (P(None, None, "tp"), P("tp", None), P(None, "tp"), P("tp", None), P(), P())
    return jax.shard_map(
        functools.partial(per_device, mesh.shape["seq"]),
        mesh=mesh,
        in_specs=(rows,) + weights + (rows, P("seq"), P("seq", None)),
        out_specs=(rows, rows) + weights,
        check_vma=False,
    )
```

time: 1490 us -> 746 us (0.50)
  waiting for transfers between devices: 1010 us -> 232 us
  matrix products: 271 us -> 137 us
  starting transfers between devices: 0.37 us -> 120 us
  Pallas kernels: 0 us -> 85.6 us
  blocking collectives: 40.3 us -> 0 us
  local copies, waits for them, and re-layouts: 56.3 us -> 82.1 us
  other arithmetic: 92 us -> 75.3 us
    reduce_scatter x4 -> x0, waiting for transfers between devices: 573 us -> none  [the longest x1 144 us: per_device(): lax.psum_scatter(input_part, 'tp', scatter_dimension=0, tiled=True)]
    all_gather x4 -> x0, waiting for transfers between devices: 312 us -> none  [the longest x1 83.7 us: per_device(): gathered = lax.all_gather(tokens, 'tp', axis=0, tiled=True)]
    ppermute x0 -> x87, waiting for transfers between devices: none -> 232 us  [the longest x32 149 us: along(): return lax.ppermute(array, 'tp', pairs)]
    dot_general x40 -> x23, matrix products: 271 us -> 137 us  [mm(): return lax.dot_general(a, b, dims, preferred_element_type=F32).astype(out)]
    psum x1 -> x0, waiting for transfers between devices: 124 us -> none  [per_device(): lax.psum((grad_qkv, grad_out, grad_up, grad_down), 'seq')]
    ppermute x0 -> x87, starting transfers between devices: none -> 120 us  [the longest x32 86.5 us: along(): return lax.ppermute(array, 'tp', pairs)]
    pallas_call x0 -> x2, Pallas kernels: none -> 85.6 us  [the longest x1 54.5 us: attention_backward(): pl.pallas_call(backward_kernel, grid=(pairs,), in_specs=[pl.BlockSpec((ro...]
    psum x1 -> x0, blocking collectives: 40.3 us -> none  [per_device(): gain_sums = lax.psum((grad_gain_one, grad_gain_two), ('seq', 'tp'))]
  transfers between devices with their start and end apart: 9 -> 87, of which waited for: 9 -> 31; matrix products, arithmetic and copies ran while one was open for 2% -> 19% of each run, Pallas kernels for 0% -> 4%
where the time goes in v1:
time: 746 us; the launch traced here: 739 us
  waiting for transfers between devices  232 us (31%)
  matrix products  137 us (18%)
  starting transfers between devices  120 us (16%)
  Pallas kernels  85.6 us (11%)
  local copies, waits for them, and re-layouts  82.1 us (11%)
  other arithmetic  75.3 us (10%)
    ppermute x32, waiting for transfers between devices, along(): return lax.ppermute(array, 'tp', pairs)  149 us
    dot_general x23, matrix products, mm(): return lax.dot_general(a, b, dims, preferred_element_type=F32).astype(out)  137 us
    ppermute x32, starting transfers between devices, along(): return lax.ppermute(array, 'tp', pairs)  86.5 us
    ppermute x55, waiting for transfers between devices, swap(): return lax.ppermute(array, 'seq', [(i, i ^ bit) for i in range(self.size)])  83.2 us
    pallas_call x1, Pallas kernels, attention_backward(): pl.pallas_call(backward_kernel, grid=(pairs,), in_specs=[pl.BlockSpec((ro...  54.5 us
    unnamed x147, local copies, waits for them, and re-layouts  34.6 us
    ppermute x55, starting transfers between devices, swap(): return lax.ppermute(array, 'seq', [(i, i ^ bit) for i in range(self.size)])  33.3 us
    pallas_call x1, Pallas kernels, attention_forward(): pl.pallas_call(forward_kernel, grid=(pairs,), in_specs=[pl.BlockSpec((row...  31.1 us
  transfers between devices with their start and end apart: 87, of which 31 were waited for; matrix products, arithmetic and copies ran while one was open for 19% of the time, Pallas kernels for 4%

profile of v1, /device:TPU:0, one launch (start us, length us, event | category | flops | bytes accessed | tf_op | source)
XLA Modules:
  0.0 739.2 jit_solution(12229939261693048019)
XLA Ops:
  12.0 3.7 collective-permute-start.19
  28.6 5.8 collective-permute-done.3
  37.4 23.7 %collective-permute-done.4 = bf16[128,1024]{1,0:T(8,128)(2,1)} collective-permute-done((bf16[128,1024]{1,0:T(8,128)(2,1)}, bf16[128,1024]{1,0:T(8,128)(2,1)}, u32[]{:S(2)}, u32[]{:S(2)}) %collective-permute-start.4) | collective-permute-done | bytes 262176 | tf_op jit(solution)/shard_map/ppermute | solution.py:31
  71.6 11.0 %collective-permute-done.22 = bf16[256,1024]{1,0:T(8,128)(2,1)} collective-permute-done((bf16[256,1024]{1,0:T(8,128)(2,1)}, bf16[256,1024]{1,0:T(8,128)(2,1)}, u32[]{:S(2)}, u32[]{:S(2)}) %collective-permute-start.22) | collective-permute-done | bytes 524320 | tf_op jit(solution)/shard_map/ppermute | solution.py:31
  103.2 10.3 %collective-permute-done.17 = bf16[512,1024]{1,0:T(8,128)(2,1)S(1)} collective-permute-done((bf16[512,1024]{1,0:T(8,128)(2,1)}, bf16[512,1024]{1,0:T(8,128)(2,1)S(1)}, u32[]{:S(2)}, u32[]{:S(2)}) %collective-permute-start.17) | collective-permute-done | bytes 1048608 | tf_op jit(solution)/shard_map/ppermute | solution.py:31
  122.0 4.2 pad_maximum_fusion.2
  132.5 11.6 %collective-permute-done.18 = bf16[512,1024]{1,0:T(8,128)(2,1)} collective-permute-done((bf16[512,1024]{1,0:T(8,128)(2,1)}, bf16[512,1024]{1,0:T(8,128)(2,1)}, u32[]{:S(2)}, u32[]{:S(2)}) %collective-permute-start.18) | collective-permute-done | bytes 1048608 | tf_op jit(solution)/shard_map/ppermute | solution.py:31
  146.4 13.5 %convolution_convert_fusion.k_ref.v_ref = bf16[2048,2048]{1,0:T(8,128)(2,1)} fusion(bf16[2048,1024]{1,0:T(8,128)(2,1)} %bitcast.351, bf16[512,1024]{1,0:T(8,128)(2,1)S(1)} %broadcast_select_fusion, bf16[512,1024]{1,0:T(8,128)(2,1)S(1)} %copy-done.25, bf16[512,1024]{1,0:T(8,128)(2,1)} %collective-permute-done.14, bf16[512,1024]{1,0:T(8,128)(2,1)} %param.10), kind=kOutput, calls=%fused_computation.61 | convolution fusion | flops 8610906112 | bytes 16777216 | tf_op jit(solution)/shard_map/dot_general | solution.py:27
  160.0 31.1 %attention_forward.1 = (bf16[512,1024]{1,0:T(8,128)(2,1)S(1)}, f32[8,2,512]{2,1,0:T(2,128)S(1)}) custom-call(bf16[512,1024]{1,0:T(8,128)(2,1)S(1)} %fusion.46.q_ref, bf16[2048,2048]{1,0:T(8,128)(2,1)} %convolution_convert_fusion.k_ref.v_ref, bf16[2048,2048]{1,0:T(8,128)(2,1)} %convolution_convert_fusion.k_ref.v_ref, f32[1,2048]{1,0:T(1,128)S(1)} %add_select_fusion.bias_ref), custom_call_target="tpu_custom_call" | custom-call | flops 17179869184 | bytes 20971520 | tf_op jit(solution)/shard_map/attention_forward/pallas_call | solution.py:137
  203.3 12.2 %collective-permute-done.29 = bf16[384,1024]{1,0:T(8,128)(2,1)S(1)} collective-permute-done((bf16[384,1024]{1,0:T(8,128)(2,1)S(1)}, bf16[384,1024]{1,0:T(8,128)(2,1)S(1)}, u32[]{:S(2)}, u32[]{:S(2)}) %collective-permute-start.29) | collective-permute-done | bytes 786464 | tf_op jit(solution)/shard_map/ppermute | solution.py:67
  230.6 6.6 copy.42
  237.2 4.5 pad_maximum_fusion
  241.7 25.9 %multiply_convert_fusion.1 = (bf16[512,4096]{1,0:T(8,128)(2,1)}, f32[512,4096]{1,0:T(8,128)}, f32[512,4096]{1,0:T(8,128)}) fusion(bf16[2,4096,1024]{2,1,0:T(8,128)(2,1)S(1)} %pad_maximum_fusion, f32[512,1024]{1,0:T(8,128)S(1)} %copy-done.14, f32[1024]{0:T(1024)S(1)} %copy-done.32, f32[512]{0:T(512)S(1)} %add_rsqrt_fusion.1, f32[512]{0:T(512)S(1)} %broadcast_multiply_fusion.5), kind=kOutput, calls=%fused_computation.47 | convolution fusion | flops 4431282176 | bytes 31465472 | tf_op jit(solution)/shard_map/dot_general | solution.py:27
  267.6 7.0 fusion.97
  277.1 13.3 %multiply_convert_fusion = bf16[512,4096]{1,0:T(8,128)(2,1)} fusion(bf16[2,4096,1024]{2,1,0:T(8,128)(2,1)} %copy-done.8, f32[512,4096]{1,0:T(8,128)} %get-tuple-element.45, f32[512,4096]{1,0:T(8,128)} %get-tuple-element.86, bf16[512,1024]{1,0:T(8,128)(2,1)S(1)} %copy-done.29, f32[512,1024]{1,0:T(8,128)S(1)} %get-tuple-element.88, ...), kind=kOutput, calls=%fused_computation.46 | convolution fusion | flops 4318560256 | bytes 32518144 | tf_op jit(solution)/shard_map/dot_general | solution.py:27
  290.3 11.3 %multiply_reduce_fusion = (f32[1024]{0:T(1024)S(1)}, f32[512]{0:T(512)S(1)}, f32[512]{0:T(512)S(1)}, f32[512,1024]{1,0:T(8,128)}) fusion(f32[512,1024]{1,0:T(8,128)S(1)} %copy-done.14, f32[512]{0:T(512)S(1)} %add_rsqrt_fusion.1, f32[512]{0:T(512)S(1)} %broadcast_multiply_fusion.5, f32[1024]{0:T(1024)S(1)} %copy-done.32, ...), kind=kOutput, calls=%fused_computation.120 | convolution fusion | flops 4303878144 | bytes 19951616 | tf_op jit(solution)/shard_map/dot_general | solution.py:27
  301.6 7.4 convert_bitcast_fusion.2
  309.0 7.4 convert_bitcast_fusion.1
  318.8 5.6 pad_maximum_fusion.1
  328.2 4.2 convert_multiply_fusion.2
  337.7 54.5 %attention_backward.1 = (bf16[512,1024]{1,0:T(8,128)(2,1)S(1)}, bf16[2048,1024]{1,0:T(8,128)(2,1)}, bf16[2048,1024]{1,0:T(8,128)(2,1)}) custom-call(bf16[512,1024]{1,0:T(8,128)(2,1)S(1)} %copy-done.3, bf16[2048,2048]{1,0:T(8,128)(2,1)} %convolution_convert_fusion.k_ref.v_ref, bf16[2048,2048]{1,0:T(8,128)(2,1)} %convolution_convert_fusion.k_ref.v_ref, ...), custom_call_target="tpu_custom_call" | custom-call | flops 42949672960 | bytes 29360128 | tf_op jit(solution)/shard_map/attention_backward/pallas_call | solution.py:203
  395.4 6.5 convert_bitcast_fusion.5
  401.9 6.3 convert_bitcast_fusion.6
  427.8 7.3 fusion.25
  437.2 6.7 copy.44
  443.9 3.9 fusion.53
  460.3 15.0 %collective-permute-done.36 = bf16[512,1024]{1,0:T(8,128)(2,1)S(1)} collective-permute-done((bf16[512,1024]{1,0:T(8,128)(2,1)S(1)}, bf16[512,1024]{1,0:T(8,128)(2,1)S(1)}, u32[]{:S(2)}, u32[]{:S(2)}) %collective-permute-start.36) | collective-permute-done | bytes 1048608 | tf_op jit(solution)/shard_map/ppermute | solution.py:31
  482.1 10.8 %collective-permute-done.41 = bf16[4,64,1024]{2,1,0:T(8,128)(2,1)S(1)} collective-permute-done((bf16[4,64,1024]{2,1,0:T(8,128)(2,1)S(1)}, bf16[4,64,1024]{2,1,0:T(8,128)(2,1)S(1)}, u32[]{:S(2)}, u32[]{:S(2)}) %collective-permute-start.41) | collective-permute-done | bytes 524320 | tf_op jit(solution)/shard_map/ppermute | solution.py:67
  505.2 13.6 %collective-permute-done.42 = bf16[4,128,1024]{2,1,0:T(8,128)(2,1)S(1)} collective-permute-done((bf16[4,128,1024]{2,1,0:T(8,128)(2,1)S(1)}, bf16[4,128,1024]{2,1,0:T(8,128)(2,1)S(1)}, u32[]{:S(2)}, u32[]{:S(2)}) %collective-permute-start.42) | collective-permute-done | bytes 1048608 | tf_op jit(solution)/shard_map/ppermute | solution.py:67
  525.1 4.4 collective-permute-start.46
  533.4 4.4 collective-permute-start.33
  537.9 5.1 collective-permute-done.63
  543.0 4.4 collective-permute-start.49
  549.6 13.1 %collective-permute-done.49 = bf16[128,1024]{1,0:T(8,128)(2,1)S(1)} collective-permute-done((bf16[128,1024]{1,0:T(8,128)(2,1)S(1)}, bf16[128,1024]{1,0:T(8,128)(2,1)S(1)}, u32[]{:S(2)}, u32[]{:S(2)}) %collective-permute-start.49) | collective-permute-done | bytes 262176 | tf_op jit(solution)/shard_map/ppermute | solution.py:31
  574.1 3.8 fusion.50
  578.0 19.9 %collective-permute-start.86 = (f32[2,1024]{1,0:T(2,128)S(1)}, f32[2,1024]{1,0:T(2,128)S(1)}, u32[]{:S(2)}, u32[]{:S(2)}) collective-permute-start(f32[2,1024]{1,0:T(2,128)S(1)} %add.277), channel_id=1, source_target_pairs={{0,2},{1,3},{2,0},{3,1},{4,6},{5,7},{6,4},{7,5},{8,10},{9,11},{10,... | collective-permute-start | bytes 24584 | tf_op jit(solution)/shard_map/ppermute | solution.py:31
  603.0 10.6 %collective-permute-done.54 = bf16[128,1024]{1,0:T(8,128)(2,1)S(1)} collective-permute-done((bf16[128,1024]{1,0:T(8,128)(2,1)S(1)}, bf16[128,1024]{1,0:T(8,128)(2,1)S(1)}, u32[]{:S(2)}, u32[]{:S(2)}) %collective-permute-start.54) | collective-permute-done | bytes 262176 | tf_op jit(solution)/shard_map/ppermute | solution.py:67
  615.4 5.9 collective-permute-done.52
  627.7 4.3 collective-permute-start.68
  632.9 10.9 %collective-permute-done.68 = bf16[256,1024]{1,0:T(8,128)(2,1)S(1)} collective-permute-done((bf16[256,1024]{1,0:T(8,128)(2,1)S(1)}, bf16[256,1024]{1,0:T(8,128)(2,1)S(1)}, u32[]{:S(2)}, u32[]{:S(2)}) %collective-permute-start.68) | collective-permute-done | bytes 524320 | tf_op jit(solution)/shard_map/ppermute | solution.py:31
  643.8 4.4 collective-permute-start.71
  651.9 8.6 %collective-permute-done.71 = bf16[256,1024]{1,0:T(8,128)(2,1)S(1)} collective-permute-done((bf16[256,1024]{1,0:T(8,128)(2,1)S(1)}, bf16[256,1024]{1,0:T(8,128)(2,1)S(1)}, u32[]{:S(2)}, u32[]{:S(2)}) %collective-permute-start.71) | collective-permute-done | bytes 524320 | tf_op jit(solution)/shard_map/ppermute | solution.py:31
  665.1 27.8 %collective-permute-done.70 = bf16[256,1024]{1,0:T(8,128)(2,1)S(1)} collective-permute-done((bf16[256,1024]{1,0:T(8,128)(2,1)S(1)}, bf16[256,1024]{1,0:T(8,128)(2,1)S(1)}, u32[]{:S(2)}, u32[]{:S(2)}) %collective-permute-start.70) | collective-permute-done | bytes 524320 | tf_op jit(solution)/shard_map/ppermute | solution.py:31
  706.7 5.7 add_convert_fusion.4
  712.4 5.3 collective-permute-done.76
  718.5 7.2 collective-permute-done.78
  729.1 4.3 fusion.91
  733.4 5.3 copy.47
  (419 shorter events, 231.9 us)
Async XLA Ops:
  12.0 23.9 %collective-permute-start.19 = (bf16[256,1024]{1,0:T(8,128)(2,1)}, bf16[256,1024]{1,0:T(8,128)(2,1)}, u32[]{:S(2)}, u32[]{:S(2)}) collective-permute-start(bf16[256,1024]{1,0:T(8,128)(2,1)} %bitcast.32), channel_id=1, source_target_pairs={{0,1},{1,0},{2,3},{3,2},{4,5},{5,4},{6,7},{7,6},{8,9},{9,8},{10,11... | collective-permute-start | bytes 1572872 | tf_op jit(solution)/shard_map/ppermute | solution.py:31
  18.4 48.4 %collective-permute-start.14 = (bf16[512,1024]{1,0:T(8,128)(2,1)}, bf16[512,1024]{1,0:T(8,128)(2,1)}, u32[]{:S(2)}, u32[]{:S(2)}) collective-permute-start(bf16[512,1024]{1,0:T(8,128)(2,1)} %param.10), channel_id=1, source_target_pairs={{0,1},{1,0},{2,3},{3,2},{4,5},{5,4},{6,7},{7,6},{8,9},{9,8},{10,11... | collective-permute-start | bytes 3145736 | tf_op jit(solution)/shard_map/ppermute | solution.py:31
  21.1 49.3 %collective-permute-start.16 = (bf16[512,1024]{1,0:T(8,128)(2,1)}, bf16[512,1024]{1,0:T(8,128)(2,1)}, u32[]{:S(2)}, u32[]{:S(2)}) collective-permute-start(bf16[512,1024]{1,0:T(8,128)(2,1)} %param.10), channel_id=1, source_target_pairs={{1,2},{2,1},{5,6},{6,5},{9,10},{10,9},{13,14},{14,13},{17,18},{18,... | collective-permute-start | bytes 3145736 | tf_op jit(solution)/shard_map/ppermute | solution.py:31
  25.3 35.8 %collective-permute-start.4 = (bf16[128,1024]{1,0:T(8,128)(2,1)}, bf16[128,1024]{1,0:T(8,128)(2,1)}, u32[]{:S(2)}, u32[]{:S(2)}) collective-permute-start(bf16[128,1024]{1,0:T(8,128)(2,1)} %collective-permute-done.1), channel_id=1, source_target_pairs={{1,0},{2,3},{5,4},{6,7},{9,8},{10,11},{13,12},{14,15},{17,16},{18,... | collective-permute-start | bytes 786440 | tf_op jit(solution)/shard_map/ppermute | solution.py:31
  34.4 31.1 %collective-permute-start.21 = (bf16[256,1024]{1,0:T(8,128)(2,1)}, bf16[256,1024]{1,0:T(8,128)(2,1)}, u32[]{:S(2)}, u32[]{:S(2)}) collective-permute-start(bf16[256,1024]{1,0:T(8,128)(2,1)} %bitcast.32), channel_id=1, source_target_pairs={{1,2},{2,1},{5,6},{6,5},{9,10},{10,9},{13,14},{14,13},{17,18},{18,... | collective-permute-start | bytes 1572872 | tf_op jit(solution)/shard_map/ppermute | solution.py:31
  35.9 32.6 %collective-permute-start.20 = (bf16[256,1024]{1,0:T(8,128)(2,1)}, bf16[256,1024]{1,0:T(8,128)(2,1)}, u32[]{:S(2)}, u32[]{:S(2)}) collective-permute-start(bf16[256,1024]{1,0:T(8,128)(2,1)} %collective-permute-done.19), channel_id=1, source_target_pairs={{1,2},{2,1},{5,6},{6,5},{9,10},{10,9},{13,14},{14,13},{17,18},{18,... | collective-permute-start | bytes 1572872 | tf_op jit(solution)/shard_map/ppermute | solution.py:31
  64.0 20.3 %collective-permute-start.8 = (bf16[384,1024]{1,0:T(8,128)(2,1)}, bf16[384,1024]{1,0:T(8,128)(2,1)}, u32[]{:S(2)}, u32[]{:S(2)}) collective-permute-start(bf16[384,1024]{1,0:T(8,128)(2,1)} %pad_maximum_fusion.18), channel_id=1, source_target_pairs={{0,16},{4,20},{8,24},{12,28},{16,0},{20,4},{24,8},{28,12},{1,17},{... | collective-permute-start | bytes 2359304 | tf_op jit(solution)/shard_map/ppermute | solution.py:67
  66.8 20.8 %collective-permute-start.6 = (bf16[384,1024]{1,0:T(8,128)(2,1)}, bf16[384,1024]{1,0:T(8,128)(2,1)}, u32[]{:S(2)}, u32[]{:S(2)}) collective-permute-start(bf16[384,1024]{1,0:T(8,128)(2,1)} %pad_maximum_fusion.18), channel_id=1, source_target_pairs={{0,8},{4,12},{8,0},{12,4},{16,24},{20,28},{24,16},{28,20},{1,9},{5... | collective-permute-start | bytes 2359304 | tf_op jit(solution)/shard_map/ppermute | solution.py:67
  68.4 25.4 %collective-permute-start.23 = (bf16[256,1024]{1,0:T(8,128)(2,1)}, bf16[256,1024]{1,0:T(8,128)(2,1)}, u32[]{:S(2)}, u32[]{:S(2)}) collective-permute-start(bf16[256,1024]{1,0:T(8,128)(2,1)} %collective-permute-done.20), channel_id=1, source_target_pairs={{1,0},{2,3},{5,4},{6,7},{9,8},{10,11},{13,12},{14,15},{17,16},{18,... | collective-permute-start | bytes 1572872 | tf_op jit(solution)/shard_map/ppermute | solution.py:31
  70.4 26.2 %collective-permute-start.5 = (bf16[384,1024]{1,0:T(8,128)(2,1)}, bf16[384,1024]{1,0:T(8,128)(2,1)S(1)}, u32[]{:S(2)}, u32[]{:S(2)}) collective-permute-start(bf16[384,1024]{1,0:T(8,128)(2,1)} %pad_maximum_fusion.18), channel_id=1, source_target_pairs={{0,4},{4,0},{8,12},{12,8},{16,20},{20,16},{24,28},{28,24},{1,5},{5... | collective-permute-start | bytes 2359304 | tf_op jit(solution)/shard_map/ppermute | solution.py:67
  82.6 19.1 %collective-permute-start.15 = (bf16[512,1024]{1,0:T(8,128)(2,1)}, bf16[512,1024]{1,0:T(8,128)(2,1)}, u32[]{:S(2)}, u32[]{:S(2)}) collective-permute-start(bf16[512,1024]{1,0:T(8,128)(2,1)} %collective-permute-done.14), channel_id=1, source_target_pairs={{1,2},{2,1},{5,6},{6,5},{9,10},{10,9},{13,14},{14,13},{17,18},{18,... | collective-permute-start | bytes 3145736 | tf_op jit(solution)/shard_map/ppermute | solution.py:31
  84.2 29.3 %collective-permute-start.17 = (bf16[512,1024]{1,0:T(8,128)(2,1)}, bf16[512,1024]{1,0:T(8,128)(2,1)S(1)}, u32[]{:S(2)}, u32[]{:S(2)}) collective-permute-start(bf16[512,1024]{1,0:T(8,128)(2,1)} %collective-permute-done.16), channel_id=1, source_target_pairs={{1,0},{2,3},{5,4},{6,7},{9,8},{10,11},{13,12},{14,15},{17,16},{18,... | collective-permute-start | bytes 3145736 | tf_op jit(solution)/shard_map/ppermute | solution.py:31
  96.6 18.0 %collective-permute-start.7 = (bf16[384,1024]{1,0:T(8,128)(2,1)}, bf16[384,1024]{1,0:T(8,128)(2,1)S(1)}, u32[]{:S(2)}, u32[]{:S(2)}) collective-permute-start(bf16[384,1024]{1,0:T(8,128)(2,1)} %collective-permute-done.6), channel_id=1, source_target_pairs={{0,4},{4,0},{8,12},{12,8},{16,20},{20,16},{24,28},{28,24},{1,5},{5... | collective-permute-start | bytes 2359304 | tf_op jit(solution)/shard_map/ppermute | solution.py:67
  98.0 18.4 %collective-permute-start.9 = (bf16[384,1024]{1,0:T(8,128)(2,1)}, bf16[384,1024]{1,0:T(8,128)(2,1)S(1)}, u32[]{:S(2)}, u32[]{:S(2)}) collective-permute-start(bf16[384,1024]{1,0:T(8,128)(2,1)} %collective-permute-done.8), channel_id=1, source_target_pairs={{0,4},{4,0},{8,12},{12,8},{16,20},{20,16},{24,28},{28,24},{1,5},{5... | collective-permute-start | bytes 2359304 | tf_op jit(solution)/shard_map/ppermute | solution.py:67
  101.6 98.6 %collective-permute-start.24 = (bf16[768,1024]{1,0:T(8,128)(2,1)S(1)}, bf16[768,1024]{1,0:T(8,128)(2,1)}, u32[]{:S(2)}, u32[]{:S(2)}) collective-permute-start(bf16[768,1024]{1,0:T(8,128)(2,1)S(1)} %pad_maximum_fusion.12), channel_id=1, source_target_pairs={{0,4},{4,0},{8,12},{12,8},{16,20},{20,16},{24,28},{28,24},{1,5},{5... | collective-permute-start | bytes 4718600 | tf_op jit(solution)/shard_map/ppermute | solution.py:67
  101.7 43.8 %collective-permute-start.25 = (bf16[768,1024]{1,0:T(8,128)(2,1)S(1)}, bf16[768,1024]{1,0:T(8,128)(2,1)}, u32[]{:S(2)}, u32[]{:S(2)}) collective-permute-start(bf16[768,1024]{1,0:T(8,128)(2,1)S(1)} %pad_maximum_fusion.12), channel_id=1, source_target_pairs={{0,8},{4,12},{8,0},{12,4},{16,24},{20,28},{24,16},{28,20},{1,9},{5... | collective-permute-start | bytes 4718600 | tf_op jit(solution)/shard_map/ppermute | solution.py:67
  116.4 74.7 %collective-permute-start.27 = (bf16[768,1024]{1,0:T(8,128)(2,1)S(1)}, bf16[768,1024]{1,0:T(8,128)(2,1)}, u32[]{:S(2)}, u32[]{:S(2)}) collective-permute-start(bf16[768,1024]{1,0:T(8,128)(2,1)S(1)} %pad_maximum_fusion.12), channel_id=1, source_target_pairs={{0,16},{4,20},{8,24},{12,28},{16,0},{20,4},{24,8},{28,12},{1,17},{... | collective-permute-start | bytes 4718600 | tf_op jit(solution)/shard_map/ppermute | solution.py:67
  117.1 27.0 %collective-permute-start.18 = (bf16[512,1024]{1,0:T(8,128)(2,1)}, bf16[512,1024]{1,0:T(8,128)(2,1)}, u32[]{:S(2)}, u32[]{:S(2)}) collective-permute-start(bf16[512,1024]{1,0:T(8,128)(2,1)} %collective-permute-done.15), channel_id=1, source_target_pairs={{1,0},{2,3},{5,4},{6,7},{9,8},{10,11},{13,12},{14,15},{17,16},{18,... | collective-permute-start | bytes 3145736 | tf_op jit(solution)/shard_map/ppermute | solution.py:31
  145.5 75.5 %collective-permute-start.26 = (bf16[768,1024]{1,0:T(8,128)(2,1)}, bf16[768,1024]{1,0:T(8,128)(2,1)}, u32[]{:S(2)}, u32[]{:S(2)}) collective-permute-start(bf16[768,1024]{1,0:T(8,128)(2,1)} %collective-permute-done.25), channel_id=1, source_target_pairs={{0,4},{4,0},{8,12},{12,8},{16,20},{20,16},{24,28},{28,24},{1,5},{5... | collective-permute-start | bytes 4718600 | tf_op jit(solution)/shard_map/ppermute | solution.py:67
  191.1 35.5 %collective-permute-start.28 = (bf16[768,1024]{1,0:T(8,128)(2,1)}, bf16[768,1024]{1,0:T(8,128)(2,1)S(1)}, u32[]{:S(2)}, u32[]{:S(2)}) collective-permute-start(bf16[768,1024]{1,0:T(8,128)(2,1)} %collective-permute-done.27), channel_id=1, source_target_pairs={{0,4},{4,0},{8,12},{12,8},{16,20},{20,16},{24,28},{28,24},{1,5},{5... | collective-permute-start | bytes 4718600 | tf_op jit(solution)/shard_map/ppermute | solution.py:67
  195.8 19.7 %collective-permute-start.29 = (bf16[384,1024]{1,0:T(8,128)(2,1)S(1)}, bf16[384,1024]{1,0:T(8,128)(2,1)S(1)}, u32[]{:S(2)}, u32[]{:S(2)}) collective-permute-start(bf16[384,1024]{1,0:T(8,128)(2,1)S(1)} %slice.323), channel_id=1, source_target_pairs={{0,8},{4,12},{8,0},{12,4},{16,24},{20,28},{24,16},{28,20},{1,9},{5... | collective-permute-start | bytes 2359304 | tf_op jit(solution)/shard_map/ppermute | solution.py:67
  198.6 19.4 %collective-permute-start.30 = (bf16[384,1024]{1,0:T(8,128)(2,1)S(1)}, bf16[384,1024]{1,0:T(8,128)(2,1)S(1)}, u32[]{:S(2)}, u32[]{:S(2)}) collective-permute-start(bf16[384,1024]{1,0:T(8,128)(2,1)S(1)} %slice.324), channel_id=1, source_target_pairs={{0,16},{4,20},{8,24},{12,28},{16,0},{20,4},{24,8},{28,12},{1,17},{... | collective-permute-start | bytes 2359304 | tf_op jit(solution)/shard_map/ppermute | solution.py:67
  422.6 29.8 %collective-permute-start.82 = (f32[2,1024]{1,0:T(2,128)S(1)}, f32[2,1024]{1,0:T(2,128)S(1)}, u32[]{:S(2)}, u32[]{:S(2)}) collective-permute-start(f32[2,1024]{1,0:T(2,128)S(1)} %pad_maximum_fusion.21), channel_id=1, source_target_pairs={{0,4},{4,0},{8,12},{12,8},{16,20},{20,16},{24,28},{28,24},{1,5},{5... | collective-permute-start | bytes 24584 | tf_op jit(solution)/shard_map/ppermute | solution.py:67
  435.1 61.3 %collective-permute-start.61 = (bf16[4,256,1024]{2,1,0:T(8,128)(2,1)}, bf16[4,256,1024]{2,1,0:T(8,128)(2,1)}, u32[]{:S(2)}, u32[]{:S(2)}) collective-permute-start(bf16[4,256,1024]{2,1,0:T(8,128)(2,1)} %bitcast.109), channel_id=1, source_target_pairs={{0,4},{4,0},{8,12},{12,8},{16,20},{20,16},{24,28},{28,24},{1,5},{5... | collective-permute-start | bytes 6291464 | tf_op jit(solution)/shard_map/ppermute | solution.py:67
  435.2 64.5 %collective-permute-start.62 = (bf16[4,256,1024]{2,1,0:T(8,128)(2,1)}, bf16[4,256,1024]{2,1,0:T(8,128)(2,1)}, u32[]{:S(2)}, u32[]{:S(2)}) collective-permute-start(bf16[4,256,1024]{2,1,0:T(8,128)(2,1)} %bitcast.111), channel_id=1, source_target_pairs={{0,4},{4,0},{8,12},{12,8},{16,20},{20,16},{24,28},{28,24},{1,5},{5... | collective-permute-start | bytes 6291464 | tf_op jit(solution)/shard_map/ppermute | solution.py:67
  447.9 30.1 %collective-permute-start.40 = (bf16[4,128,1024]{2,1,0:T(8,128)(2,1)S(1)}, bf16[4,128,1024]{2,1,0:T(8,128)(2,1)S(1)}, u32[]{:S(2)}, u32[]{:S(2)}) collective-permute-start(bf16[4,128,1024]{2,1,0:T(8,128)(2,1)S(1)} %bitcast.365), channel_id=1, source_target_pairs={{0,4},{4,0},{8,12},{12,8},{16,20},{20,16},{24,28},{28,24},{1,5},{5... | collective-permute-start | bytes 3145736 | tf_op jit(solution)/shard_map/ppermute | solution.py:67
  450.7 24.6 %collective-permute-start.36 = (bf16[512,1024]{1,0:T(8,128)(2,1)S(1)}, bf16[512,1024]{1,0:T(8,128)(2,1)S(1)}, u32[]{:S(2)}, u32[]{:S(2)}) collective-permute-start(bf16[512,1024]{1,0:T(8,128)(2,1)S(1)} %add_convert_fusion.9), channel_id=1, source_target_pairs={{0,1},{3,2},{4,5},{7,6},{8,9},{11,10},{12,13},{15,14},{16,17},{19,... | collective-permute-start | bytes 3145736 | tf_op jit(solution)/shard_map/ppermute | solution.py:31
  460.3 18.6 %collective-permute-start.39 = (bf16[4,128,1024]{2,1,0:T(8,128)(2,1)S(1)}, bf16[4,128,1024]{2,1,0:T(8,128)(2,1)S(1)}, u32[]{:S(2)}, u32[]{:S(2)}) collective-permute-start(bf16[4,128,1024]{2,1,0:T(8,128)(2,1)S(1)} %bitcast.364), channel_id=1, source_target_pairs={{0,4},{4,0},{8,12},{12,8},{16,20},{20,16},{24,28},{28,24},{1,5},{5... | collective-permute-start | bytes 3145736 | tf_op jit(solution)/shard_map/ppermute | solution.py:67
  478.0 47.1 %collective-permute-start.65 = (bf16[4,256,1024]{2,1,0:T(8,128)(2,1)S(1)}, bf16[4,256,1024]{2,1,0:T(8,128)(2,1)S(1)}, u32[]{:S(2)}, u32[]{:S(2)}) collective-permute-start(bf16[4,256,1024]{2,1,0:T(8,128)(2,1)S(1)} %bitcast.358), channel_id=1, source_target_pairs={{0,4},{4,0},{8,12},{12,8},{16,20},{20,16},{24,28},{28,24},{1,5},{5... | collective-permute-start | bytes 6291464 | tf_op jit(solution)/shard_map/ppermute | solution.py:67
  494.6 24.2 %collective-permute-start.42 = (bf16[4,128,1024]{2,1,0:T(8,128)(2,1)S(1)}, bf16[4,128,1024]{2,1,0:T(8,128)(2,1)S(1)}, u32[]{:S(2)}, u32[]{:S(2)}) collective-permute-start(bf16[4,128,1024]{2,1,0:T(8,128)(2,1)S(1)} %pad_maximum_fusion.16), channel_id=1, source_target_pairs={{0,8},{4,12},{8,0},{12,4},{16,24},{20,28},{24,16},{28,20},{1,9},{5... | collective-permute-start | bytes 3145736 | tf_op jit(solution)/shard_map/ppermute | solution.py:67
  496.4 24.1 %collective-permute-start.45 = (bf16[4,128,1024]{2,1,0:T(8,128)(2,1)}, bf16[4,128,1024]{2,1,0:T(8,128)(2,1)S(1)}, u32[]{:S(2)}, u32[]{:S(2)}) collective-permute-start(bf16[4,128,1024]{2,1,0:T(8,128)(2,1)} %pad_maximum_fusion.17), channel_id=1, source_target_pairs={{0,16},{4,20},{8,24},{12,28},{16,0},{20,4},{24,8},{28,12},{1,17},{... | collective-permute-start | bytes 3145736 | tf_op jit(solution)/shard_map/ppermute | solution.py:67
  499.7 124.0 %collective-permute-start.60 = (bf16[4,256,1024]{2,1,0:T(8,128)(2,1)S(1)}, bf16[4,256,1024]{2,1,0:T(8,128)(2,1)S(1)}, u32[]{:S(2)}, u32[]{:S(2)}) collective-permute-start(bf16[4,256,1024]{2,1,0:T(8,128)(2,1)S(1)} %bitcast.357), channel_id=1, source_target_pairs={{0,4},{4,0},{8,12},{12,8},{16,20},{20,16},{24,28},{28,24},{1,5},{5... | collective-permute-start | bytes 6291464 | tf_op jit(solution)/shard_map/ppermute | solution.py:67
  502.7 66.8 %collective-permute-start.85 = (f32[2,1024]{1,0:T(2,128)S(1)}, f32[2,1024]{1,0:T(2,128)S(1)}, u32[]{:S(2)}, u32[]{:S(2)}) collective-permute-start(f32[2,1024]{1,0:T(2,128)S(1)} %add.276), channel_id=1, source_target_pairs={{0,1},{1,0},{2,3},{3,2},{4,5},{5,4},{6,7},{7,6},{8,9},{9,8},{10,11... | collective-permute-start | bytes 24584 | tf_op jit(solution)/shard_map/ppermute | solution.py:31
  518.8 24.2 %collective-permute-start.63 = (bf16[4,128,1024]{2,1,0:T(8,128)(2,1)S(1)}, bf16[4,128,1024]{2,1,0:T(8,128)(2,1)S(1)}, u32[]{:S(2)}, u32[]{:S(2)}) collective-permute-start(bf16[4,128,1024]{2,1,0:T(8,128)(2,1)S(1)} %get-tuple-element.69), channel_id=1, source_target_pairs={{0,16},{4,20},{8,24},{12,28},{16,0},{20,4},{24,8},{28,12},{1,17},{... | collective-permute-start | bytes 3145736 | tf_op jit(solution)/shard_map/ppermute | solution.py:67
  520.5 27.3 %collective-permute-start.66 = (bf16[4,128,1024]{2,1,0:T(8,128)(2,1)S(1)}, bf16[4,128,1024]{2,1,0:T(8,128)(2,1)S(1)}, u32[]{:S(2)}, u32[]{:S(2)}) collective-permute-start(bf16[4,128,1024]{2,1,0:T(8,128)(2,1)S(1)} %get-tuple-element.70), channel_id=1, source_target_pairs={{0,8},{4,12},{8,0},{12,4},{16,24},{20,28},{24,16},{28,20},{1,9},{5... | collective-permute-start | bytes 3145736 | tf_op jit(solution)/shard_map/ppermute | solution.py:67
  533.4 33.2 %collective-permute-start.33 = (bf16[512,1024]{1,0:T(8,128)(2,1)}, bf16[512,1024]{1,0:T(8,128)(2,1)S(1)}, u32[]{:S(2)}, u32[]{:S(2)}) collective-permute-start(bf16[512,1024]{1,0:T(8,128)(2,1)} %get-tuple-element.93), channel_id=1, source_target_pairs={{0,1},{3,2},{4,5},{7,6},{8,9},{11,10},{12,13},{15,14},{16,17},{19,... | collective-permute-start | bytes 3145736 | tf_op jit(solution)/shard_map/ppermute | solution.py:31
  543.0 19.7 %collective-permute-start.49 = (bf16[128,1024]{1,0:T(8,128)(2,1)S(1)}, bf16[128,1024]{1,0:T(8,128)(2,1)S(1)}, u32[]{:S(2)}, u32[]{:S(2)}) collective-permute-start(bf16[128,1024]{1,0:T(8,128)(2,1)S(1)} %get-tuple-element.77), channel_id=1, source_target_pairs={{0,1},{3,2},{4,5},{7,6},{8,9},{11,10},{12,13},{15,14},{16,17},{19,... | collective-permute-start | bytes 786440 | tf_op jit(solution)/shard_map/ppermute | solution.py:31
  562.7 62.8 %collective-permute-start.64 = (bf16[4,256,1024]{2,1,0:T(8,128)(2,1)S(1)}, bf16[4,256,1024]{2,1,0:T(8,128)(2,1)S(1)}, u32[]{:S(2)}, u32[]{:S(2)}) collective-permute-start(bf16[4,256,1024]{2,1,0:T(8,128)(2,1)S(1)} %pad_maximum_fusion.10), channel_id=1, source_target_pairs={{0,8},{4,12},{8,0},{12,4},{16,24},{20,28},{24,16},{28,20},{1,9},{5... | collective-permute-start | bytes 6291464 | tf_op jit(solution)/shard_map/ppermute | solution.py:67
  563.5 62.0 %collective-permute-start.67 = (bf16[4,256,1024]{2,1,0:T(8,128)(2,1)S(1)}, bf16[4,256,1024]{2,1,0:T(8,128)(2,1)S(1)}, u32[]{:S(2)}, u32[]{:S(2)}) collective-permute-start(bf16[4,256,1024]{2,1,0:T(8,128)(2,1)S(1)} %pad_maximum_fusion.11), channel_id=1, source_target_pairs={{0,16},{4,20},{8,24},{12,28},{16,0},{20,4},{24,8},{28,12},{1,17},{... | collective-permute-start | bytes 6291464 | tf_op jit(solution)/shard_map/ppermute | solution.py:67
  569.5 33.4 %collective-permute-start.34 = (bf16[512,1024]{1,0:T(8,128)(2,1)S(1)}, bf16[512,1024]{1,0:T(8,128)(2,1)S(1)}, u32[]{:S(2)}, u32[]{:S(2)}) collective-permute-start(bf16[512,1024]{1,0:T(8,128)(2,1)S(1)} %add_convert_fusion.7), channel_id=1, source_target_pairs={{1,2},{2,1},{5,6},{6,5},{9,10},{10,9},{13,14},{14,13},{17,18},{18,... | collective-permute-start | bytes 3145736 | tf_op jit(solution)/shard_map/ppermute | solution.py:31
  578.0 21.5 %collective-permute-start.86 = (f32[2,1024]{1,0:T(2,128)S(1)}, f32[2,1024]{1,0:T(2,128)S(1)}, u32[]{:S(2)}, u32[]{:S(2)}) collective-permute-start(f32[2,1024]{1,0:T(2,128)S(1)} %add.277), channel_id=1, source_target_pairs={{0,2},{1,3},{2,0},{3,1},{4,6},{5,7},{6,4},{7,5},{8,10},{9,11},{10,... | collective-permute-start | bytes 24584 | tf_op jit(solution)/shard_map/ppermute | solution.py:31
  603.0 20.1 %collective-permute-start.51 = (bf16[128,1024]{1,0:T(8,128)(2,1)S(1)}, bf16[128,1024]{1,0:T(8,128)(2,1)S(1)}, u32[]{:S(2)}, u32[]{:S(2)}) collective-permute-start(bf16[128,1024]{1,0:T(8,128)(2,1)S(1)} %get-tuple-element.43), channel_id=1, source_target_pairs={{0,4},{4,0},{8,12},{12,8},{16,20},{20,16},{24,28},{28,24},{1,5},{5... | collective-permute-start | bytes 786440 | tf_op jit(solution)/shard_map/ppermute | solution.py:67
  621.4 85.3 %collective-permute-start.37 = (bf16[512,1024]{1,0:T(8,128)(2,1)}, bf16[512,1024]{1,0:T(8,128)(2,1)}, u32[]{:S(2)}, u32[]{:S(2)}) collective-permute-start(bf16[512,1024]{1,0:T(8,128)(2,1)} %get-tuple-element.92), channel_id=1, source_target_pairs={{1,2},{2,1},{5,6},{6,5},{9,10},{10,9},{13,14},{14,13},{17,18},{18,... | collective-permute-start | bytes 3145736 | tf_op jit(solution)/shard_map/ppermute | solution.py:31
  632.6 19.2 %collective-permute-start.59 = (bf16[64,1024]{1,0:T(8,128)(2,1)S(1)}, bf16[64,1024]{1,0:T(8,128)(2,1)S(1)}, u32[]{:S(2)}, u32[]{:S(2)}) collective-permute-start(bf16[64,1024]{1,0:T(8,128)(2,1)S(1)} %collective-permute-done.57), channel_id=1, source_target_pairs={{0,4},{4,0},{8,12},{12,8},{16,20},{20,16},{24,28},{28,24},{1,5},{5... | collective-permute-start | bytes 393224 | tf_op jit(solution)/shard_map/ppermute | solution.py:67
  649.2 57.5 %collective-permute-start.35 = (bf16[512,1024]{1,0:T(8,128)(2,1)}, bf16[512,1024]{1,0:T(8,128)(2,1)}, u32[]{:S(2)}, u32[]{:S(2)}) collective-permute-start(bf16[512,1024]{1,0:T(8,128)(2,1)} %add_convert_fusion.6), channel_id=1, source_target_pairs={{0,1},{1,0},{2,3},{3,2},{4,5},{5,4},{6,7},{7,6},{8,9},{9,8},{10,11... | collective-permute-start | bytes 3145736 | tf_op jit(solution)/shard_map/ppermute | solution.py:31
  660.9 32.0 %collective-permute-start.70 = (bf16[256,1024]{1,0:T(8,128)(2,1)S(1)}, bf16[256,1024]{1,0:T(8,128)(2,1)S(1)}, u32[]{:S(2)}, u32[]{:S(2)}) collective-permute-start(bf16[256,1024]{1,0:T(8,128)(2,1)S(1)} %get-tuple-element.65), channel_id=1, source_target_pairs={{0,1},{1,0},{2,3},{3,2},{4,5},{5,4},{6,7},{7,6},{8,9},{9,8},{10,11... | collective-permute-start | bytes 1572872 | tf_op jit(solution)/shard_map/ppermute | solution.py:31
  664.0 29.0 %collective-permute-start.72 = (bf16[256,1024]{1,0:T(8,128)(2,1)S(1)}, bf16[256,1024]{1,0:T(8,128)(2,1)S(1)}, u32[]{:S(2)}, u32[]{:S(2)}) collective-permute-start(bf16[256,1024]{1,0:T(8,128)(2,1)S(1)} %get-tuple-element.66), channel_id=1, source_target_pairs={{1,2},{2,1},{5,6},{6,5},{9,10},{10,9},{13,14},{14,13},{17,18},{18,... | collective-permute-start | bytes 1572872 | tf_op jit(solution)/shard_map/ppermute | solution.py:31
  706.7 19.6 %collective-permute-start.75 = (bf16[256,1024]{1,0:T(8,128)(2,1)S(1)}, bf16[256,1024]{1,0:T(8,128)(2,1)S(1)}, u32[]{:S(2)}, u32[]{:S(2)}) collective-permute-start(bf16[256,1024]{1,0:T(8,128)(2,1)S(1)} %collective-permute-done.74), channel_id=1, source_target_pairs={{0,4},{4,0},{8,12},{12,8},{16,20},{20,16},{24,28},{28,24},{1,5},{5... | collective-permute-start | bytes 1572872 | tf_op jit(solution)/shard_map/ppermute | solution.py:67
  (84 other events, 766.2 us)

commit v2 on v1

v2 whole, which is shorter than its diff:
```python
import functools

import jax
import jax.numpy as jnp
from jax import lax
from jax.experimental import pallas as pl
from jax.experimental.pallas import tpu as pltpu
from jax.sharding import PartitionSpec as P

HEAD = 64
SLOTS = 4
BF = jnp.bfloat16
F32 = jnp.float32
LOG2E = 1.4426950408889634
LN_EPS = 1e-5
LIGHT = pl.CostEstimate(flops=10**9, bytes_accessed=10**6, transcendentals=0)
NT = (((1,), (1,)), ((), ()))
NN = (((1,), (0,)), ((), ()))
TN = (((0,), (0,)), ((), ()))

PAIR = [(0, 1), (1, 0), (2, 3), (3, 2)]
MIDDLE = [(1, 2), (2, 1)]
OUTWARD = [(1, 0), (2, 3)]


def mm(a, b, dims, out=F32):
    return lax.dot_general(a, b, dims, preferred_element_type=F32).astype(out)


def along(array, pairs):
    return lax.ppermute(array, "tp", pairs)


def fence(*arrays):
    return lax.optimization_barrier(arrays)


class Plane:
    def __init__(self, size):
        self.size = size

    def swap(self, array, bit):
        return lax.ppermute(array, "seq", [(i, i ^ bit) for i in range(self.size)])

    def higher(self, total):
        bit = 8
        while bit < self.size:
            total = (total.astype(F32) + self.swap(total, bit).astype(F32)).astype(BF)
            bit *= 2
        return total


def forward_kernel(q_ref, *refs):
    blocks = (len(refs) - 5) // 2
    k_refs, v_refs = refs[:blocks], refs[blocks : 2 * blocks]
    bias_ref, out_ref, lse_ref = refs[2 * blocks], refs[-2], refs[-1]
    scale = HEAD**-0.5 * LOG2E
    rows = q_ref.shape[0]
    lane = lax.broadcasted_iota(jnp.int32, (1, 2 * HEAD), 1)
    zero = jnp.zeros((), BF)
    keys = jnp.concatenate([ref[...] for ref in k_refs])
    values = jnp.concatenate([ref[...] for ref in v_refs])
    bias = bias_ref[...]
    sub = 256
    mine = [(lane < HEAD) == (head == 0) for head in range(2)]
    k = [jnp.where(m, keys, zero) for m in mine]
    v = [jnp.where(m, values, zero) for m in mine]
    for at in range(rows // sub):
        span = pl.ds(at * sub, sub)
        q = q_ref[span, :]
        outs, lses = [], []
        for head in range(2):
            s = lax.dot_general(q, k[head], NT, preferred_element_type=F32)
            s = s * scale + bias
            top = jnp.max(s, axis=1, keepdims=True)
            p = jnp.exp2(s - top)
            total = jnp.sum(p, axis=1, keepdims=True)
            o = lax.dot_general(p.astype(BF), v[head], NN, preferred_element_type=F32)
            outs.append(o / total)
            lses.append(top + jnp.log2(total))
        out_ref[span, :] = (outs[0] + outs[1]).astype(BF)
        wide = jnp.where(lane < HEAD, lses[0], lses[1])
        flat = jnp.transpose(wide)
        lse_ref[0, :, span] = jnp.concatenate(
            [flat[0:1], flat[HEAD : HEAD + 1]], axis=0
        )


def attention_forward(q, kvs, bias, first, count, held):
    rows, width = q.shape
    keys = bias.shape[1]
    pairs = width // (2 * HEAD)
    wide = 2 * HEAD
    at = lambda shift: lambda h: (0, h + first + shift)
    return pl.pallas_call(
        forward_kernel,
        grid=(count,),
        in_specs=[pl.BlockSpec((rows, wide), at(0))]
        + [pl.BlockSpec((kv.shape[0], wide), at(0)) for kv in kvs]
        + [pl.BlockSpec((kv.shape[0], wide), at(pairs)) for kv in kvs]
        + [pl.BlockSpec((1, keys), lambda h: (0, 0))]
        + [pl.BlockSpec(memory_space=pl.ANY)] * 2,
        out_specs=[
            pl.BlockSpec((rows, wide), at(0)),
            pl.BlockSpec((1, 2, rows), lambda h: (h + first, 0, 0)),
        ],
        out_shape=[
            jax.ShapeDtypeStruct((rows, width), BF),
            jax.ShapeDtypeStruct((pairs, 2, rows), F32),
        ],
        input_output_aliases={2 * len(kvs) + 2: 0, 2 * len(kvs) + 3: 1},
        compiler_params=pltpu.CompilerParams(vmem_limit_bytes=48 * 2**20),
        cost_estimate=LIGHT,
        name="attention_forward",
    )(q, *kvs, *kvs, bias, *held)


def backward_kernel(
    q_ref, k_ref, v_ref, go_ref, lse_ref, inner_ref, bias_ref, wkv_ref, *refs
):
    add_ref = refs[0] if len(refs) == 9 else None
    gq_ref, keep_k_ref, keep_v_ref, send_ref, part_ref, all_ref = refs[-6:]
    step, pairs = pl.program_id(0), pl.num_programs(0)
    scale = HEAD**-0.5
    wide = 2 * HEAD
    keys = k_ref.shape[0]
    lane = lax.broadcasted_iota(jnp.int32, (1, wide), 1)
    q, go = q_ref[...], go_ref[...]
    zero = jnp.zeros((), BF)
    mine = [(lane < HEAD) == (head == 0) for head in range(2)]
    qs = [jnp.where(m, q, zero) for m in mine]
    gos = [jnp.where(m, go, zero) for m in mine]
    total_q = [0.0, 0.0]
    gks, gvs = [], []
    sub = 512
    for at in range(keys // sub):
        span = pl.ds(at * sub, sub)
        bias = bias_ref[span, 0:1]
        keys_t = k_ref[span, :].T
        total_k, total_v = 0.0, 0.0
        for head in range(2):
            k = jnp.where(mine[head], k_ref[span, :], zero)
            v = jnp.where(mine[head], v_ref[span, :], zero)
            s = lax.dot_general(k, q, NT, preferred_element_type=F32)
            p = jnp.exp2(s * (scale * LOG2E) + (bias - lse_ref[0, head : head + 1, :]))
            gp = lax.dot_general(v, go, NT, preferred_element_type=F32)
            gs = (p * (gp - inner_ref[0, head : head + 1, :])).astype(BF)
            total_v += lax.dot_general(p.astype(BF), gos[head], NN, preferred_element_type=F32)
            total_k += lax.dot_general(gs, qs[head], NN, preferred_element_type=F32)
            own_keys = keys_t[head * HEAD : (head + 1) * HEAD]
            total_q[head] += lax.dot_general(own_keys, gs, NN, preferred_element_type=F32)
        gks.append((total_k * scale).astype(BF))
        gvs.append(total_v.astype(BF))
    gk, gv = jnp.concatenate(gks), jnp.concatenate(gvs)
    gq = jnp.concatenate(total_q).T * scale
    gq_ref[...] = gq if add_ref is None else gq + add_ref[...]
    half = pairs // 2

    @pl.when(step < half)
    def _():
        keep_k_ref[...] = gk
        keep_v_ref[...] = gv

    @pl.when(step >= half)
    def _():
        send_ref[0] = gk
        send_ref[1] = gv

    lanes = pl.multiple_of(step * wide, wide)
    all_ref[:, pl.ds(lanes, wide)] = gk
    all_ref[:, pl.ds(pl.multiple_of(lanes + q_width(part_ref), wide), wide)] = gv

    @pl.when(step == pairs - 1)
    def _():
        for at in range(keys // 256):
            span = pl.ds(at * 256, 256)
            part = lax.dot_general(
                all_ref[span, :], wkv_ref[...], NN, preferred_element_type=F32
            )
            part_ref[span, :] = part.astype(BF)


def q_width(part_ref):
    return part_ref.shape[1]


def attention_backward(q, kv, go, lse, inner, bias, wkv, block, blocks, held):
    rows, width = q.shape
    keys = kv.shape[0]
    pairs = width // (2 * HEAD)
    wide = 2 * HEAD
    half = pairs // 2
    by_pair = pl.BlockSpec((rows, wide), lambda h: (0, h))
    stats = pl.BlockSpec((1, 2, rows), lambda h: (h, 0, 0))
    whole = pl.BlockSpec(memory_space=pl.ANY)
    keep = pl.BlockSpec((keys, wide), lambda h: (block, jnp.minimum(h, half - 1)))
    send = pl.BlockSpec((2, keys, wide), lambda h: (0, 0, jnp.maximum(h - half, 0)))
    return pl.pallas_call(
        backward_kernel,
        grid=(pairs,),
        in_specs=[
            by_pair,
            pl.BlockSpec((keys, wide), lambda h: (0, h)),
            pl.BlockSpec((keys, wide), lambda h: (0, h + pairs)),
            by_pair,
            stats,
            stats,
            pl.BlockSpec((keys, 128), lambda h: (0, 0)),
            pl.BlockSpec((2 * width, width), lambda h: (0, 0)),
        ]
        + ([by_pair, whole, whole] if held else []),
        out_specs=[by_pair, keep, keep, send, pl.BlockSpec((keys, width), lambda h: (0, 0))],
        out_shape=[
            jax.ShapeDtypeStruct((rows, width), F32),
            jax.ShapeDtypeStruct((blocks * keys, width // 2), BF),
            jax.ShapeDtypeStruct((blocks * keys, width // 2), BF),
            jax.ShapeDtypeStruct((2, keys, width // 2), BF),
            jax.ShapeDtypeStruct((keys, width), BF),
        ],
        scratch_shapes=[pltpu.VMEM((keys, 2 * width), BF)],
        input_output_aliases={9: 1, 10: 2} if held else {},
        compiler_params=pltpu.CompilerParams(vmem_limit_bytes=48 * 2**20),
        cost_estimate=LIGHT,
        name="attention_backward",
    )(q, kv, kv, go, lse, inner, bias, wkv, *(held or ()))


def gelu_tile(x):
    size = jnp.abs(x)
    t = 1.0 / (1.0 + size * (0.3275911 * 0.5**0.5))
    poly = t * (
        0.127414796
        + t * (-0.142248368 + t * (0.7107068705 + t * (-0.7265760135 + t * 0.5307027145)))
    )
    bell = jnp.exp2(x * x * (-0.5 * LOG2E))
    tail = poly * bell
    cdf = jnp.where(x >= 0, 1.0 - tail, tail)
    return (x * cdf).astype(BF), (cdf + x * (bell * 0.3989422804014327)).astype(BF)


def head_grads_kernel(
    first, big_ref, came_ref, came_two_ref, small_ref, small_peer_ref,
    rows_ref, rows_two_ref, peer_ref, peer_two_ref, right_ref, right_peer_ref, *out_refs
):
    def outer(left, right):
        return lax.dot_general(left, right[...], TN, preferred_element_type=F32)

    keys = rows_ref.shape[0]
    total = outer(big_ref[:keys, :], rows_ref) + outer(big_ref[keys:, :], rows_two_ref)
    total += outer(came_ref[0], peer_ref) + outer(came_two_ref[0], peer_two_ref)
    total = total.astype(BF)
    other = outer(small_ref[...], right_ref) + outer(small_peer_ref[...], right_peer_ref)
    kinds = [total, other.astype(BF)] if first else [other.astype(BF), total]
    size = HEAD // 2
    for at in range(total.shape[0] // (4 * size)):
        for kind in range(2):
            for chunk in range(4):
                source = (at * 4 + (chunk & 1) * 2 + (chunk >> 1)) * size
                place = (at * 2 + kind) * size
                out_refs[chunk][place : place + size, :] = kinds[kind][source : source + size, :]


def head_grads(first, big, came, small, small_peer, rows, peer, right, right_peer):
    keys, width = rows[0].shape
    own = right.shape[0]
    core = width // 2
    wide = core // 2
    which = 1 if first else 0
    whole = lambda a: pl.BlockSpec(a.shape, lambda g: (0, 0))
    columns = lambda n: pl.BlockSpec((n, wide), lambda g: (0, g))
    arrived = pl.BlockSpec((1, keys, wide), lambda g: (which, 0, g))
    return pl.pallas_call(
        functools.partial(head_grads_kernel, first),
        grid=(core // wide,),
        in_specs=[columns(2 * keys), arrived, arrived, columns(own), columns(own)]
        + [whole(a) for a in (*rows, *peer, right, right_peer)],
        out_specs=[pl.BlockSpec((wide // 2, width), lambda g: (g, 0))] * 4,
        out_shape=[jax.ShapeDtypeStruct((core // 2, width), BF)] * 4,
        compiler_params=pltpu.CompilerParams(vmem_limit_bytes=48 * 2**20),
        cost_estimate=LIGHT,
        name="head_grads",
    )(big, *came, small, small_peer, *rows, *peer, right, right_peer)


def rows_kernel(moves, n_held, n_out, *refs):
    n_in = len(refs) - n_held - n_out - 1
    ins, outs, sems = refs[:n_in], refs[-1 - n_out : -1], refs[-1]
    copies = []
    for n, (source, at, count, out, place) in enumerate(moves):
        copies.append(
            pltpu.make_async_copy(
                ins[source].at[pl.ds(at, count), :],
                outs[out].at[pl.ds(place, count), :],
                sems.at[n],
            )
        )
    for copy in copies:
        copy.start()
    for copy in copies:
        copy.wait()


def put_rows(moves, shape, n_out, held=()):
    arrays, listed = [], []
    for array, at, count, out, place in moves:
        known = [n for n, a in enumerate(arrays) if a is array]
        if not known:
            arrays.append(array)
        listed.append((known[0] if known else len(arrays) - 1, at, count, out, place))
    whole = pl.BlockSpec(memory_space=pl.ANY)
    return pl.pallas_call(
        functools.partial(rows_kernel, listed, len(held), n_out),
        in_specs=[pl.BlockSpec(memory_space=pltpu.VMEM)] * len(arrays) + [whole] * len(held),
        out_specs=[whole] * n_out,
        out_shape=[jax.ShapeDtypeStruct(shape, BF)] * n_out,
        scratch_shapes=[pltpu.SemaphoreType.DMA((len(listed),))],
        input_output_aliases={len(arrays) + n: n for n in range(len(held))},
        compiler_params=pltpu.CompilerParams(vmem_limit_bytes=32 * 2**20),
        cost_estimate=LIGHT,
        name="put_rows",
    )(*arrays, *held)


def totals_kernel(at_ref, *refs):
    *ins, out_ref = refs
    size = ins[0].shape[0]
    for n in range(2):
        a, b, c = [ref[...].astype(F32) for ref in ins[3 * n : 3 * n + 3]]
        out_ref[n * size : (n + 1) * size, :] = (a + b + c).astype(BF)


def totals(ones, twos, t):
    rows, width = ones[0].shape
    size = rows // 4
    return pl.pallas_call(
        totals_kernel,
        grid_spec=pltpu.PrefetchScalarGridSpec(
            num_scalar_prefetch=1,
            grid=(4,),
            in_specs=[pl.BlockSpec((size, width), lambda u, at: (at[0] ^ u, 0))] * 6,
            out_specs=pl.BlockSpec((2 * size, width), lambda u, at: (u, 0)),
        ),
        out_shape=jax.ShapeDtypeStruct((2 * rows, width), BF),
        cost_estimate=LIGHT,
        name="totals",
    )(t[None].astype(jnp.int32), *ones, *twos)


def outer_kernel(left_ref, right_ref, left_two_ref, right_two_ref, *out_refs):
    total = lax.dot_general(left_ref[...], right_ref[...], TN, preferred_element_type=F32)
    total += lax.dot_general(
        left_two_ref[...], right_two_ref[...], TN, preferred_element_type=F32
    )
    total = total.astype(BF)
    each = pl.num_programs(0) // len(out_refs)
    for n, out_ref in enumerate(out_refs):

        @pl.when(pl.program_id(0) // each == n)
        def _():
            out_ref[...] = total


def outer_four(left, right, left_two, right_two):
    rows, hidden = left.shape
    width = right.shape[1]
    tile = 256
    each = hidden // (4 * tile)
    columns = pl.BlockSpec((rows, tile), lambda i: (0, i))
    whole = pl.BlockSpec((rows, width), lambda i: (0, 0))
    place = lambda n: lambda i: (jnp.clip(i - n * each, 0, each - 1), 0)
    return pl.pallas_call(
        outer_kernel,
        grid=(hidden // tile,),
        in_specs=[columns, whole, columns, whole],
        out_specs=[pl.BlockSpec((tile, width), place(n)) for n in range(4)],
        out_shape=[jax.ShapeDtypeStruct((hidden // 4, width), BF)] * 4,
        compiler_params=pltpu.CompilerParams(vmem_limit_bytes=32 * 2**20),
        cost_estimate=LIGHT,
        name="outer_four",
    )(left, right, left_two, right_two)


def reverse(i):
    return ((i & 1) << 2) | (i & 2) | (i >> 2)


def placed_kernel(flips, order, at_ref, *refs):
    *pieces, out_ref, whole_ref = refs
    for i, piece in enumerate(pieces):
        place = order(at_ref[0] ^ i)
        size = piece.shape[0]
        whole_ref[pl.ds(pl.multiple_of(place * size, size), size), :] = piece[...].astype(F32)
    out = whole_ref[...]
    out = out.T if flips else out
    out_ref[...] = out.reshape(out_ref.shape)


def placed(pieces, kinds, size, order, s8, flips):
    width = pieces[0][0].shape[1]
    tile = 256
    rows = 8 * size
    if kinds > 1:
        out_shape = (kinds, width, rows)
        out_spec = pl.BlockSpec((1, tile, rows), lambda n, c: (n, c, 0))
    elif flips:
        out_shape, out_spec = (width, rows), pl.BlockSpec((tile, rows), lambda n, c: (c, 0))
    else:
        out_shape, out_spec = (rows, width), pl.BlockSpec((rows, tile), lambda n, c: (0, c))
    part = lambda first: pl.BlockSpec((size, tile), lambda n, c: (n + first, c))
    return pl.pallas_call(
        functools.partial(placed_kernel, flips, order),
        grid=(kinds, width // tile),
        in_specs=[pl.BlockSpec(memory_space=pltpu.SMEM)] + [part(first) for _, first in pieces],
        out_specs=out_spec,
        out_shape=jax.ShapeDtypeStruct(out_shape, F32),
        scratch_shapes=[pltpu.VMEM((rows, tile), F32)],
        compiler_params=pltpu.CompilerParams(vmem_limit_bytes=32 * 2**20),
        name="placed",
    )(s8[None].astype(jnp.int32), *[array for array, _ in pieces])


def centred(values):
    centre = values - jnp.mean(values, axis=-1, keepdims=True)
    root = lax.rsqrt(jnp.mean(centre * centre, axis=-1, keepdims=True) + LN_EPS)
    return centre * root, root


def norm_pull(grad, gain, unit, root):
    scaled = grad * gain
    mean = jnp.mean(scaled, axis=-1, keepdims=True)
    slope = jnp.mean(scaled * unit, axis=-1, keepdims=True)
    return root * (scaled - mean - unit * slope), jnp.sum(grad * unit, axis=0)


def per_device(
    seq_size, tokens, w_qkv, w_out, w_up, w_down, gain_one, gain_two, cotangent, bucket, lengths
):
    rows, width = tokens.shape
    t = lax.axis_index("tp")
    middle = (t == 1) | (t == 2)
    s8 = lax.axis_index("seq") % 8
    plane = Plane(seq_size)
    swap = plane.swap
    hid = w_out.shape[0]
    ff = w_down.shape[0]
    qp, fp = hid // 8, ff // 8
    up = lambda a: a.astype(F32)
    across = lambda a, j: along(a, [(i, i ^ j) for i in range(4)])

    w_attn_own = jnp.concatenate([w_qkv.transpose(1, 2, 0), w_out[None]])

    def attn_piece(i):
        return lax.dynamic_slice_in_dim(w_attn_own, reverse(s8 ^ i) * qp, qp, axis=1)

    def up_piece(i):
        return lax.dynamic_slice_in_dim(w_up, (s8 ^ i) * fp, fp, axis=1).T

    def down_piece(i):
        return lax.dynamic_slice_in_dim(w_down, (s8 ^ i) * fp, fp, axis=0)

    attn_own = attn_piece(0).reshape(4 * qp, width)
    up_own = jnp.concatenate([up_piece(2 * i) for i in range(4)])
    down_own = jnp.concatenate([down_piece(2 * i) for i in range(4)])
    ff_own = jnp.concatenate([up_own[:fp], down_own[:fp]])

    upper = rows // 2
    gathered = [
        lax.all_gather(tokens[n * upper : (n + 1) * upper], "tp", axis=0, tiled=True)
        for n in range(2)
    ]
    a_far = [across(attn_own, j) for j in (1, 2, 3)]
    a_far = fence(*a_far)
    attn_three = jnp.concatenate(a_far)
    half = attn_three.shape[0] // 2
    a_x, a_y = swap(attn_three, 2), swap(attn_three, 4)
    attn_three, a_x, a_y = fence(attn_three, a_x, a_y)
    a_d1, a_d2 = swap(a_y[:half], 2), swap(a_x[half:], 4)
    others = [swap(attn_three, 1), swap(a_x, 1), swap(a_y, 1)]
    a_d1, a_d2, *others = fence(a_d1, a_d2, *others)
    others += fence(swap(a_d1, 1), swap(a_d2, 1))

    four = [attn_three, a_x, a_y, a_d1, a_d2]
    pieces = []
    for i in range(8):
        part = others if i & 1 else four
        far = part[i >> 1] if i < 6 else jnp.concatenate(part[3:])
        pieces.append(jnp.concatenate([attn_piece(i)[None], far.reshape(3, 4, qp, width)]))
    w_attn = jnp.stack(pieces).reshape(2, 2, 2, 4, 4, qp, width).transpose(4, 2, 3, 1, 0, 5, 6)
    w_attn = w_attn.reshape(4, width, width)
    wq, wk, wv, wo = [w_attn[n] for n in range(4)]
    wkv = w_attn[1:3].reshape(2 * width, width)

    whole = bucket[0] == 1
    place = jnp.arange(rows, dtype=jnp.int32)
    seen = []
    for u in range(4):
        alone = jnp.where(t == u, lengths[0, u], 0)
        limit = jnp.where(whole, lengths[0, 0] - u * rows, alone)
        seen.append((place < limit).reshape(2, upper))
    bias = jnp.where(jnp.stack(seen, axis=1), 0.0, -1e9).astype(F32).reshape(4 * rows)
    bias_cols = jnp.broadcast_to(bias[:, None], (4 * rows, 128))

    q = mm(tokens, wq, NT, BF)
    tokens_peer = swap(tokens, 1)
    upper_kv = mm(gathered[0], wkv, NT, BF)
    upper_kv, q, tokens_peer, ff_own, up_own, down_own, *gathered = fence(
        upper_kv, q, tokens_peer, ff_own, up_own, down_own, *gathered
    )
    f_one, f_far = along(ff_own, PAIR), along(ff_own, MIDDLE)
    kvs = fence(upper_kv, mm(gathered[1], wkv, NT, BF))
    held = (jnp.zeros((rows, width), BF), jnp.zeros((width // (2 * HEAD), 2, rows), F32))
    bias_row = bias[None]
    held = attention_forward(q, kvs, bias_row, 0, 2, held)
    f_one, f_far, *held = fence(f_one, f_far, *held)
    f_two, f_two_end = along(f_one, MIDDLE), along(f_far, OUTWARD)
    one_x, one_y = swap(f_one, 2), swap(f_one, 4)
    held = attention_forward(q, kvs, bias_row, 2, 2, held)
    f_two, f_two_end, one_x, one_y, *held = fence(f_two, f_two_end, one_x, one_y, *held)
    f_three_end = along(f_two, OUTWARD)
    f_two = jnp.where(middle, f_two, f_two_end)
    one_d1, one_d2 = swap(one_y[:fp], 2), swap(one_x[fp:], 4)
    two_x, two_y = swap(f_two, 2), swap(f_two, 4)
    held = attention_forward(q, kvs, bias_row, 4, 2, held)
    f_three_end, one_d1, one_d2, two_x, two_y, *held = fence(
        f_three_end, one_d1, one_d2, two_x, two_y, *held
    )
    f_three = jnp.where(middle, f_far, f_three_end)
    two_d1, two_d2 = swap(two_y[:fp], 2), swap(two_x[fp:], 4)
    three_x, three_y = swap(f_three, 2), swap(f_three, 4)

    def moves(j, block):
        own, by_x, by_y, d1, d2 = block
        for i, (a, b, at) in enumerate(((own,) * 2 + (fp,), (by_x,) * 2 + (fp,), (by_y,) * 2 + (fp,), (d1, d2, 0))):
            yield (a, 0, fp, 0, (4 * i + j) * fp)
            yield (b, at, fp, 1, (4 * i + j) * fp)

    own = []
    for i in range(4):
        own.append((up_own, i * fp, fp, 0, 4 * i * fp))
        own.append((down_own, i * fp, fp, 1, 4 * i * fp))
    one = moves(1, (f_one, one_x, one_y, one_d1, one_d2))
    w_ff = put_rows([*own, *one], (ff * 2, width), 2)
    w_ff = fence(*w_ff, *held)
    w_ff, held = w_ff[:2], w_ff[2:]
    held = attention_forward(q, kvs, bias_row, 6, 2, held)
    two_d1, two_d2, three_x, three_y, *held = fence(two_d1, two_d2, three_x, three_y, *held)
    three_d1, three_d2 = swap(three_y[:fp], 2), swap(three_x[fp:], 4)
    attended, lse = held
    first_sum = up(tokens) + mm(attended, wo, NN)
    unit_one, root_one = centred(first_sum)
    normed = unit_one * gain_one
    normed_low = normed.astype(BF)

    two = moves(2, (f_two, two_x, two_y, two_d1, two_d2))
    three = moves(3, (f_three, three_x, three_y, three_d1, three_d2))
    wu, wd = put_rows([*two, *three], (ff * 2, width), 2, w_ff)

    normed_peer = swap(normed_low, 1)
    gathered_peer = [swap(part, 1) for part in gathered]
    attended_peer = swap(attended[:, width // 2 :], 1)
    act, slope = gelu_tile(mm(normed_low, wu, NT))
    act_peer, slope_peer = gelu_tile(mm(normed_peer, wu, NT))
    shrunk_peer = swap(mm(act_peer, wd, NN, BF), 1)
    unit_two, root_two = centred(normed + mm(act, wd, NN) + up(shrunk_peer))
    mixed = (unit_two * gain_two).astype(BF)

    grad_second, gain_grad_two = norm_pull(up(cotangent), gain_two, unit_two, root_two)
    second_low = grad_second.astype(BF)
    second_peer = swap(second_low, 1)
    grad_exp = (mm(second_low, wd, NT) * up(slope)).astype(BF)
    grad_exp_peer = (mm(second_peer, wd, NT) * up(slope_peer)).astype(BF)
    normed_part_peer = swap(mm(grad_exp_peer, wu, NN, BF), 1)
    normed_part = mm(grad_exp, wu, NN)
    twos = outer_four(act, second_low, act_peer, second_peer)
    normed_part, normed_part_peer, *twos = fence(normed_part, normed_part_peer, *twos)
    diag_y, two_y = swap(twos[3], 4), swap(twos[2], 4)
    ones = outer_four(grad_exp, normed_low, grad_exp_peer, normed_peer)
    grad_normed = grad_second + normed_part + up(normed_part_peer)
    normed_part, *ones = fence(normed_part, *ones)
    diag_x, one_x = swap(ones[3], 2), swap(ones[1], 2)
    grad_first, gain_grad_one = norm_pull(grad_normed, gain_one, unit_one, root_one)
    first_low = grad_first.astype(BF)
    first_peer = swap(first_low, 1)
    go = mm(first_low, wo, NT, BF)
    inner = (up(go) * up(attended)).reshape(rows, width // HEAD, HEAD).sum(-1)
    inner = inner.T.reshape(width // (2 * HEAD), 2, rows)
    core = width // 2
    inner, go, first_peer, attended_peer, *gathered_peer = fence(
        inner, go, first_peer, attended_peer, *gathered_peer
    )

    def pull(n, held):
        keys = bias_cols[2 * n * rows : 2 * (n + 1) * rows]
        *held, send, part = attention_backward(
            q, kvs[n], go, lse, inner, keys, wkv, n, 2, held
        )
        return held, send, part

    def line_sum(part):
        return lax.psum_scatter(part, "tp", scatter_dimension=0, tiled=True)

    gains = jnp.stack([gain_grad_one, gain_grad_two])
    gains_came = swap(gains, 1)
    held, send, part = pull(0, None)
    diag_x, diag_y, one_x, two_y, send, part, gains_came, *held = fence(
        diag_x, diag_y, one_x, two_y, send, part, gains_came, *held
    )
    upper_sum = line_sum(part)
    came = [swap(send, 1)]
    gains = gains + gains_came
    gains_came = swap(gains, 2)
    two_x = (up(twos[1]) + up(diag_y)).astype(BF)
    one_y = (up(ones[2]) + up(diag_x)).astype(BF)
    two_x, one_y, *held = fence(two_x, one_y, *held)
    two_x, one_y = swap(two_x, 2), swap(one_y, 4)
    held, send, part = pull(1, held)
    two_x, one_y, came[0], send, part, gains_came, upper_sum, *held = fence(
        two_x, one_y, came[0], send, part, gains_came, upper_sum, *held
    )
    gq, gk, gv = held
    gq = gq.astype(BF)
    came.append(swap(send, 1))
    gq_peer = swap(gq[:, core:], 1)
    gains = gains + gains_came
    gains_came = swap(gains, 4)
    ff_total = line_sum(
        plane.higher(totals((ones[0], one_x, one_y), (twos[0], two_x, two_y), t))
    )
    first = mm(gq, wq, NN) + grad_first
    came[1], gq_peer, gains_came, first = fence(came[1], gq_peer, gains_came, first)
    gains = gains + gains_came
    gains_came = across(gains, 1)
    a_twos = fence(
        *head_grads(
            True, gv, came, attended, attended_peer, gathered, gathered_peer, first_low, first_peer
        )
    )
    a_diag_y, a_two_y = swap(a_twos[3], 4), swap(a_twos[2], 4)
    a_ones = head_grads(
        False, gk, came, gq, gq_peer, gathered, gathered_peer, tokens, tokens_peer
    )
    a_diag_y, gains_came, *a_ones = fence(a_diag_y, gains_came, *a_ones)
    gains = gains + gains_came
    gains_came = across(gains, 2)
    a_diag_x, a_one_x = swap(a_ones[3], 2), swap(a_ones[1], 2)
    a_two_x = (up(a_twos[1]) + up(a_diag_y)).astype(BF)
    a_two_x, a_diag_x, gains_came = fence(a_two_x, a_diag_x, gains_came)
    gains = gains + gains_came
    bit = 8
    while bit < seq_size:
        gains = gains + swap(gains, bit)
        bit *= 2
    a_two_x = swap(a_two_x, 2)
    a_one_y = swap((up(a_ones[2]) + up(a_diag_x)).astype(BF), 4)
    ff_total, part = fence(ff_total.astype(BF), part)
    lower_sum = line_sum(part)
    a_two_x, a_one_y, a_one_x, a_two_y = fence(a_two_x, a_one_y, a_one_x, a_two_y)
    vo_mine = plane.higher((up(a_twos[0]) + up(a_two_x) + up(a_two_y)).astype(BF))
    qk_mine = plane.higher((up(a_ones[0]) + up(a_one_x) + up(a_one_y)).astype(BF))
    qk_mine, vo_mine = qk_mine.reshape(4, 2 * qp, width), vo_mine.reshape(4, 2 * qp, width)
    a_mine = fence(*[jnp.concatenate([qk_mine[j], vo_mine[j]]) for j in range(4)])
    a_came = [across(a_mine[j], j) for j in (1, 2, 3)]
    f_x, f_y = swap(ff_total, 2), swap(ff_total, 4)
    f_core = [swap(ff_total, 1)]
    f_x, f_y, *f_core = fence(f_x, f_y, *f_core)
    f_d1, f_d2 = swap(f_y[:fp], 2), swap(f_x[fp:], 4)
    f_core += [swap(f_x, 1), swap(f_y, 1)]
    a_came = fence(*a_came)
    a_total = fence(sum((up(a) for a in a_came), up(a_mine[0])).astype(BF))[0]
    a_four = [a_total, swap(a_total, 2), swap(a_total, 4), swap(a_total, 6)]
    a_core = [swap(a_total, 1)]
    f_core += [swap(f_d1, 1), swap(f_d2, 1)]
    f_four = [ff_total, f_x, f_y, f_d1, f_d2]
    ups, downs = [], []
    for i in range(8):
        part = f_core if i & 1 else f_four
        ups.append((part[i >> 1], 0))
        downs.append((part[i >> 1], 1) if i < 6 else (part[4], 0))
    plain = lambda i: i
    grad_up = placed(ups, 1, fp, plain, s8, True)
    grad_down = placed(downs, 1, fp, plain, s8, False)
    grad_up, grad_down, *a_four = fence(grad_up, grad_down, *a_four)
    a_core += [swap(a, 1) for a in a_four[1:]]
    a_all = [(a_core if i & 1 else a_four)[i >> 1] for i in range(8)]
    grad_qkv = placed([(a, 0) for a in a_all], 3, qp, reverse, s8, True)
    grad_out = placed([(a, 3) for a in a_all], 1, qp, reverse, s8, False)

    tokens_grad = (first + up(jnp.concatenate([upper_sum, lower_sum]))).astype(BF)
    return (
        mixed,
        tokens_grad,
        grad_qkv.transpose(1, 0, 2),
        grad_out,
        grad_up,
        grad_down,
        gains[0],
        gains[1],
    )


def solution(mesh):
    rows = P(("seq", "tp"), None)
    weights = (P(None, None, "tp"), P("tp", None), P(None, "tp"), P("tp", None), P(), P())
    return jax.shard_map(
        functools.partial(per_device, mesh.shape["seq"]),
        mesh=mesh,
        in_specs=(rows,) + weights + (rows, P("seq"), P("seq", None)),
        out_specs=(rows, rows) + weights,
        check_vma=False,
    )
```

time: 746 us -> 548 us (0.73)
  the two profiles are of different devices: /device:TPU:0 before, /device:TPU:25 now
where the time goes in v2:
time: 548 us; the launch traced here: 539 us
  Pallas kernels  166 us (30%)
  waiting for transfers between devices  127 us (23%)
  starting transfers between devices  82.9 us (15%)
  matrix products  60.4 us (11%)
  local copies, waits for them, and re-layouts  47.6 us (9%)
  other arithmetic  34.7 us (6%)
  between operations  21.4 us (4%)
    pallas_call x2, Pallas kernels, attention_backward(): pl.pallas_call(backward_kernel, grid=(pairs,), in_specs=[by_pair, pl.Bloc...  72.2 us
    ppermute x64, starting transfers between devices, swap(): return lax.ppermute(array, 'seq', [(i, i ^ bit) for i in range(self.size)])  64.1 us
    dot_general x14, matrix products, mm(): return lax.dot_general(a, b, dims, preferred_element_type=F32).astype(out)  60.4 us
    ppermute x64, waiting for transfers between devices, swap(): return lax.ppermute(array, 'seq', [(i, i ^ bit) for i in range(self.size)])  59.1 us
    ppermute x13, waiting for transfers between devices, along(): return lax.ppermute(array, 'tp', pairs)  38.8 us
    pallas_call x4, Pallas kernels, attention_forward(): pl.pallas_call(forward_kernel, grid=(count,), in_specs=[pl.BlockSpec((row...  33.6 us
    unnamed x128, local copies, waits for them, and re-layouts  21.6 us
    pallas_call x2, Pallas kernels, head_grads(): pl.pallas_call(functools.partial(head_grads_kernel, first), grid=(core //...  21.2 us
  transfers between devices with their start and end apart: 82, of which 25 were waited for; matrix products, arithmetic and copies ran while one was open for 20% of the time, Pallas kernels for 30%

profile of v2, /device:TPU:25, one launch (start us, length us, event | category | flops | bytes accessed | tf_op | source)
XLA Modules:
  0.0 539.4 jit_solution(2461859122585321148)
XLA Ops:
  13.2 2.8 collective-permute-start.2
  16.1 11.8 %collective-permute-done = bf16[128,1024]{1,0:T(8,128)(2,1)S(1)} collective-permute-done((bf16[128,1024]{1,0:T(8,128)(2,1)S(1)}, bf16[128,1024]{1,0:T(8,128)(2,1)S(1)}, u32[]{:S(2)}, u32[]{:S(2)}) %collective-permute-start) | collective-permute-done | bytes 262176 | tf_op jit(solution)/shard_map/ppermute | solution.py:31
  27.8 12.8 %collective-permute-done.2 = bf16[128,1024]{1,0:T(8,128)(2,1)S(1)} collective-permute-done((bf16[128,1024]{1,0:T(8,128)(2,1)S(1)}, bf16[128,1024]{1,0:T(8,128)(2,1)S(1)}, u32[]{:S(2)}, u32[]{:S(2)}) %collective-permute-start.2) | collective-permute-done | bytes 262176 | tf_op jit(solution)/shard_map/ppermute | solution.py:31
  58.2 5.8 %collective-permute-start.7 = (bf16[384,1024]{1,0:T(8,128)(2,1)}, bf16[384,1024]{1,0:T(8,128)(2,1)}, u32[]{:S(2)}, u32[]{:S(2)}) collective-permute-start(bf16[384,1024]{1,0:T(8,128)(2,1)} %constant_dynamic-update-slice_fusion), channel_id=1, source_target_pairs={{0,4},{4,0},{8,12},{12,8},{16,20},{20,16},{24,28},{28,24},{1,5},{5... | collective-permute-start | bytes 2359304 | tf_op jit(solution)/shard_map/ppermute | solution.py:43
  73.6 7.1 %collective-permute-done.5 = bf16[192,1024]{1,0:T(8,128)(2,1)} collective-permute-done((bf16[192,1024]{1,0:T(8,128)(2,1)}, bf16[192,1024]{1,0:T(8,128)(2,1)}, u32[]{:S(2)}, u32[]{:S(2)}) %collective-permute-start.5) | collective-permute-done | bytes 393248 | tf_op jit(solution)/shard_map/ppermute | solution.py:43
  98.5 9.4 %convert_bitcast_fusion.refs_0_.refs_2_.k_ref.v_ref = bf16[1024,2048]{1,0:T(8,128)(2,1)} fusion(bf16[2048,1024]{1,0:T(8,128)(2,1)} %bitcast.121, bf16[1024,1024]{1,0:T(8,128)(2,1)} %all-gather.3.cloned.1.call-done.rows_ref), kind=kOutput, calls=%fused_computation.20 | convolution fusion | flops 4297064448 | bytes 10485760 | tf_op jit(solution)/shard_map/dot_general | solution.py:27
  108.9 10.2 %all-gather.5.cloned.1.call-done.rows_two_ref = bf16[1024,1024]{1,0:T(8,128)(2,1)} async-done(((bf16[256,1024]{1,0:T(8,128)(2,1)}), bf16[1024,1024]{1,0:T(8,128)(2,1)}) %all-gather.5.cloned.1.call-update) | async-done | bytes 2097168 | tf_op jit(solution)/shard_map/all_gather | solution.py:468
  123.6 9.5 %convolution_convert_fusion.refs_1_.refs_3_.k_ref.v_ref = bf16[1024,2048]{1,0:T(8,128)(2,1)} fusion(bf16[1024,1024]{1,0:T(8,128)(2,1)} %all-gather.5.cloned.1.call-done.rows_two_ref, bf16[2048,1024]{1,0:T(8,128)(2,1)} %bitcast.122), kind=kOutput, calls=%fused_computation.21 | convolution fusion | flops 4297064448 | bytes 10485760 | tf_op jit(solution)/shard_map/dot_general | solution.py:27
  133.2 8.4 %attention_forward.4 = (bf16[512,1024]{1,0:T(8,128)(2,1)S(1)}, f32[8,2,512]{2,1,0:T(2,128)S(1)}) custom-call(bf16[512,1024]{1,0:T(8,128)(2,1)S(1)} %fusion.7.q_ref, bf16[1024,2048]{1,0:T(8,128)(2,1)} %convert_bitcast_fusion.refs_0_.refs_2_.k_ref.v_ref, ...), custom_call_target="tpu_custom_call", output_to_operand_aliasing={{0}: (6, {}), {1}: (7, {})} | custom-call | flops 1000000000 | bytes 1000000 | tf_op jit(solution)/shard_map/attention_forward/pallas_call | solution.py:95
  146.8 8.4 %attention_forward.5 = (bf16[512,1024]{1,0:T(8,128)(2,1)S(1)}, f32[8,2,512]{2,1,0:T(2,128)S(1)}) custom-call(bf16[512,1024]{1,0:T(8,128)(2,1)S(1)} %fusion.7.q_ref, bf16[1024,2048]{1,0:T(8,128)(2,1)} %convert_bitcast_fusion.refs_0_.refs_2_.k_ref.v_ref, ...), custom_call_target="tpu_custom_call", output_to_operand_aliasing={{0}: (6, {}), {1}: (7, {})} | custom-call | flops 1000000000 | bytes 1000000 | tf_op jit(solution)/shard_map/attention_forward/pallas_call | solution.py:95
  155.1 3.3 collective-permute-done.16
  166.1 8.4 %attention_forward.6 = (bf16[512,1024]{1,0:T(8,128)(2,1)S(1)}, f32[8,2,512]{2,1,0:T(2,128)S(1)}) custom-call(bf16[512,1024]{1,0:T(8,128)(2,1)S(1)} %fusion.7.q_ref, bf16[1024,2048]{1,0:T(8,128)(2,1)} %convert_bitcast_fusion.refs_0_.refs_2_.k_ref.v_ref, ...), custom_call_target="tpu_custom_call", output_to_operand_aliasing={{0}: (6, {}), {1}: (7, {})} | custom-call | flops 1000000000 | bytes 1000000 | tf_op jit(solution)/shard_map/attention_forward/pallas_call | solution.py:95
  174.5 3.9 collective-permute-done.20.refs_5_
  188.3 8.5 %attention_forward.7 = (bf16[512,1024]{1,0:T(8,128)(2,1)S(1)}, f32[8,2,512]{2,1,0:T(2,128)S(1)}) custom-call(bf16[512,1024]{1,0:T(8,128)(2,1)S(1)} %fusion.7.q_ref, bf16[1024,2048]{1,0:T(8,128)(2,1)} %convert_bitcast_fusion.refs_0_.refs_2_.k_ref.v_ref, ...), custom_call_target="tpu_custom_call", output_to_operand_aliasing={{0}: (6, {}), {1}: (7, {})} | custom-call | flops 1000000000 | bytes 1000000 | tf_op jit(solution)/shard_map/attention_forward/pallas_call | solution.py:95
  199.3 3.9 collective-permute-start.30
  207.2 4.9 collective-permute-done.28.refs_8_
  215.3 5.5 %multiply_convert_fusion.2 = (bf16[512,2048]{1,0:T(8,128)(2,1)S(1)}, f32[512,2048]{1,0:T(8,128)S(1)}) fusion(bf16[512,1024]{1,0:T(8,128)(2,1)S(1)} %collective-permute-done.30.right_two_ref, bf16[2048,1024]{1,0:T(8,128)(2,1)S(1)} %get-tuple-element.229), kind=kOutput, calls=%fused_computation.14 | convolution fusion | flops 2169503744 | bytes 11534336 | tf_op jit(solution)/shard_map/dot_general | solution.py:27
  224.3 6.5 %multiply_convert_fusion.3 = (bf16[512,2048]{1,0:T(8,128)(2,1)S(1)}, f32[512,2048]{1,0:T(8,128)}) fusion(bf16[512,1024]{1,0:T(8,128)(2,1)S(1)} %multiply_convert_fusion.5.right_ref, bf16[2048,1024]{1,0:T(8,128)(2,1)S(1)} %get-tuple-element.229), kind=kOutput, calls=%fused_computation.17 | convolution fusion | flops 2169503744 | bytes 11534336 | tf_op jit(solution)/shard_map/dot_general | solution.py:27
  240.1 5.7 %multiply_convert_fusion.left_two_ref = bf16[512,2048]{1,0:T(8,128)(2,1)S(1)} fusion(bf16[512,1024]{1,0:T(8,128)(2,1)S(1)} %collective-permute-done.32.right_two_ref, bf16[2048,1024]{1,0:T(8,128)(2,1)S(1)} %get-tuple-element.230, f32[512,2048]{1,0:T(8,128)S(1)} %get-tuple-element.387), kind=kOutput, calls=%fused_computation.10 | convolution fusion | flops 2174746624 | bytes 11534336 | tf_op jit(solution)/shard_map/dot_general | solution.py:27
  245.9 3.3 convolution_convert_fusion.3
  249.3 5.3 multiply_convert_fusion.1.left_ref
  257.0 8.3 %outer_four.2 = (bf16[512,1024]{1,0:T(8,128)(2,1)S(1)}, bf16[512,1024]{1,0:T(8,128)(2,1)S(1)}, bf16[512,1024]{1,0:T(8,128)(2,1)}, bf16[512,1024]{1,0:T(8,128)(2,1)}) custom-call(bf16[512,2048]{1,0:T(8,128)(2,1)S(1)} %get-tuple-element.388.left_ref, bf16[512,1024]{1,0:T(8,128)(2,1)S(1)} %fusion.32.right_ref, ...), custom_call_target="tpu_custom_call" | custom-call | flops 1000000000 | bytes 1000000 | tf_op jit(solution)/shard_map/outer_four/pallas_call | solution.py:371
  265.3 2.9 multiply_reduce_fusion
  270.5 8.3 %outer_four.3 = (bf16[512,1024]{1,0:T(8,128)(2,1)S(1)}, bf16[512,1024]{1,0:T(8,128)(2,1)}, bf16[512,1024]{1,0:T(8,128)(2,1)S(1)}, bf16[512,1024]{1,0:T(8,128)(2,1)}) custom-call(bf16[512,2048]{1,0:T(8,128)(2,1)S(1)} %multiply_convert_fusion.1.left_ref, bf16[512,1024]{1,0:T(8,128)(2,1)S(1)} %multiply_convert_fusion.5.right_ref, ...), custom_call_target="tpu_custom_call" | custom-call | flops 1000000000 | bytes 1000000 | tf_op jit(solution)/shard_map/outer_four/pallas_call | solution.py:371
  281.9 3.0 convert_multiply_fusion.2
  284.8 2.9 copy.68
  292.5 35.8 %attention_backward.2 = (f32[512,1024]{1,0:T(8,128)S(1)}, bf16[2048,512]{1,0:T(8,128)(2,1)}, bf16[2048,512]{1,0:T(8,128)(2,1)}, bf16[2,1024,512]{2,1,0:T(8,128)(2,1)}, bf16[1024,1024]{1,0:T(8,128)(2,1)}) custom-call(bf16[512,1024]{1,0:T(8,128)(2,1)S(1)} %fusion.7.q_ref, bf16[1024,2048]{1,0:T(8,128)(2,1)} %convert_bitcast_fusion.refs_0_.refs_2_.k_ref.v_ref, ...), custom_call_target="tpu_custom_call" | custom-call | flops 1000000000 | bytes 1000000 | tf_op jit(solution)/shard_map/attention_backward/pallas_call | solution.py:198
  336.7 36.4 %attention_backward.3 = (f32[512,1024]{1,0:T(8,128)S(1)}, bf16[2048,512]{1,0:T(8,128)(2,1)}, bf16[2048,512]{1,0:T(8,128)(2,1)}, bf16[2,1024,512]{2,1,0:T(8,128)(2,1)}, bf16[1024,1024]{1,0:T(8,128)(2,1)}) custom-call(bf16[512,1024]{1,0:T(8,128)(2,1)S(1)} %fusion.7.q_ref, ...), custom_call_target="tpu_custom_call", output_to_operand_aliasing={{1}: (9, {}), {2}: (10, {})} | custom-call | flops 1000000000 | bytes 1000000 | tf_op jit(solution)/shard_map/attention_backward/pallas_call | solution.py:198
  374.7 4.8 totals.1
  383.9 2.6 convolution_add_fusion
  388.6 11.1 %head_grads.2 = (bf16[256,1024]{1,0:T(8,128)(2,1)S(1)}, bf16[256,1024]{1,0:T(8,128)(2,1)S(1)}, bf16[256,1024]{1,0:T(8,128)(2,1)S(1)}, bf16[256,1024]{1,0:T(8,128)(2,1)}) custom-call(bf16[2048,512]{1,0:T(8,128)(2,1)} %get-tuple-element.291.big_ref, bf16[2,1024,512]{2,1,0:T(8,128)(2,1)} %collective-permute-done.45.came_ref, bf16[2,1024,512]{2,1,0:T(8,128)(2,1)} %copy-done.37, ...), custom_call_target="tpu_custom_call" | custom-call | flops 1000000000 | bytes 1000000 | tf_op jit(solution)/shard_map/head_grads/pallas_call | solution.py:272
  402.9 3.4 collective-permute-start.60
  406.3 18.1 %reduce-scatter.6.cloned.1.call-done.refs_0_ = bf16[256,1024]{1,0:T(8,128)(2,1)} async-done(((bf16[1024,1024]{1,0:T(8,128)(2,1)}), bf16[256,1024]{1,0:T(8,128)(2,1)}) %reduce-scatter.6.cloned.1.call-update) | async-done | bytes 524304 | tf_op jit(solution)/shard_map/reduce_scatter | solution.py:600
  425.5 10.0 %head_grads.3 = (bf16[256,1024]{1,0:T(8,128)(2,1)S(1)}, bf16[256,1024]{1,0:T(8,128)(2,1)S(1)}, bf16[256,1024]{1,0:T(8,128)(2,1)S(1)}, bf16[256,1024]{1,0:T(8,128)(2,1)S(1)}) custom-call(bf16[2048,512]{1,0:T(8,128)(2,1)} %get-tuple-element.300.big_ref, bf16[2,1024,512]{2,1,0:T(8,128)(2,1)} %collective-permute-done.45.came_ref, ...), custom_call_target="tpu_custom_call" | custom-call | flops 1000000000 | bytes 1000000 | tf_op jit(solution)/shard_map/head_grads/pallas_call | solution.py:272
  439.7 3.8 collective-permute-done.62
  443.5 5.3 collective-permute-done.61
  451.3 8.7 %collective-permute-done.65 = bf16[256,1024]{1,0:T(8,128)(2,1)S(1)} collective-permute-done((bf16[256,1024]{1,0:T(8,128)(2,1)S(1)}, bf16[256,1024]{1,0:T(8,128)(2,1)S(1)}, u32[]{:S(2)}, u32[]{:S(2)}) %collective-permute-start.65) | collective-permute-done | bytes 524320 | tf_op jit(solution)/shard_map/ppermute | solution.py:43
  460.0 11.1 %collective-permute-done.63 = bf16[256,1024]{1,0:T(8,128)(2,1)S(1)} collective-permute-done((bf16[256,1024]{1,0:T(8,128)(2,1)S(1)}, bf16[256,1024]{1,0:T(8,128)(2,1)S(1)}, u32[]{:S(2)}, u32[]{:S(2)}) %collective-permute-start.63) | collective-permute-done | bytes 524320 | tf_op jit(solution)/shard_map/ppermute | solution.py:43
  478.9 5.7 %collective-permute-done.50.refs_2_ = bf16[256,1024]{1,0:T(8,128)(2,1)S(1)} collective-permute-done((bf16[256,1024]{1,0:T(8,128)(2,1)S(1)}, bf16[256,1024]{1,0:T(8,128)(2,1)S(1)}, u32[]{:S(2)}, u32[]{:S(2)}) %collective-permute-start.50) | collective-permute-done | bytes 524320 | tf_op jit(solution)/shard_map/ppermute | solution.py:43
  485.2 2.7 collective-permute-start.53
  489.7 2.7 collective-permute-done.68
  492.7 4.5 collective-permute-done.69
  497.1 3.0 collective-permute-start.56
  500.8 5.4 %collective-permute-start.58 = (bf16[128,1024]{1,0:T(8,128)(2,1)S(1)}, bf16[128,1024]{1,0:T(8,128)(2,1)S(1)}, u32[]{:S(2)}, u32[]{:S(2)}) collective-permute-start(bf16[128,1024]{1,0:T(8,128)(2,1)S(1)} %collective-permute-done.57.refs_6_), channel_id=1, source_target_pairs={{0,4},{4,0},{8,12},{12,8},{16,20},{20,16},{24,28},{28,24},{1,5},{5... | collective-permute-start | bytes 786440 | tf_op jit(solution)/shard_map/ppermute | solution.py:43
  508.2 3.4 placed.4
  511.6 2.8 placed.5
  514.5 5.3 collective-permute-done.71.refs_4_
  522.5 5.7 %placed.6 = f32[3,1024,256]{2,1,0:T(8,128)} custom-call(s32[1]{0:T(128)} %bitcast.49.at_ref, bf16[128,1024]{1,0:T(8,128)(2,1)S(1)} %add_convert_fusion.9.refs_0_, bf16[128,1024]{1,0:T(8,128)(2,1)S(1)} %collective-permute-done.73.refs_1_, bf16[128,1024]{1,0:T(8,128)(2,1)S(1)} %collective-permute-done.70.refs_2_, ...), custom_call_target="tpu_custom_call" | custom-call | tf_op jit(solution)/shard_map/placed/pallas_call | solution.py:410
  (367 shorter events, 154.7 us)
Async XLA Ops:
  7.2 91.3 %all-gather.3.cloned.1.call-start = ((), (), s32[]{:S(2)}) async-start(), calls=%async_computation.3 | async-start | bytes 2621440 | tf_op jit(solution)/shard_map/all_gather | solution.py:468
  9.5 109.7 %all-gather.5.cloned.1.call-start = ((), (), s32[]{:S(2)}) async-start(), calls=%async_computation.4 | async-start | bytes 2621440 | tf_op jit(solution)/shard_map/all_gather | solution.py:468
  12.5 15.3 %collective-permute-start = (bf16[128,1024]{1,0:T(8,128)(2,1)S(1)}, bf16[128,1024]{1,0:T(8,128)(2,1)S(1)}, u32[]{:S(2)}, u32[]{:S(2)}) collective-permute-start(bf16[128,1024]{1,0:T(8,128)(2,1)S(1)} %bitcast.143), channel_id=1, source_target_pairs={{0,1},{1,0},{2,3},{3,2},{4,5},{5,4},{6,7},{7,6},{8,9},{9,8},{10,11... | collective-permute-start | bytes 786440 | tf_op jit(solution)/shard_map/ppermute | solution.py:31
  12.7 15.1 %collective-permute-start.1 = (bf16[128,1024]{1,0:T(8,128)(2,1)S(1)}, bf16[128,1024]{1,0:T(8,128)(2,1)S(1)}, u32[]{:S(2)}, u32[]{:S(2)}) collective-permute-start(bf16[128,1024]{1,0:T(8,128)(2,1)S(1)} %bitcast.144), channel_id=1, source_target_pairs={{0,2},{1,3},{2,0},{3,1},{4,6},{5,7},{6,4},{7,5},{8,10},{9,11},{10,... | collective-permute-start | bytes 786440 | tf_op jit(solution)/shard_map/ppermute | solution.py:31
  13.2 27.4 %collective-permute-start.2 = (bf16[128,1024]{1,0:T(8,128)(2,1)S(1)}, bf16[128,1024]{1,0:T(8,128)(2,1)S(1)}, u32[]{:S(2)}, u32[]{:S(2)}) collective-permute-start(bf16[128,1024]{1,0:T(8,128)(2,1)S(1)} %bitcast.145), channel_id=1, source_target_pairs={{0,3},{1,2},{2,1},{3,0},{4,7},{5,6},{6,5},{7,4},{8,11},{9,10},{10,... | collective-permute-start | bytes 786440 | tf_op jit(solution)/shard_map/ppermute | solution.py:31
  42.8 14.9 %collective-permute-start.3 = (bf16[384,1024]{1,0:T(8,128)(2,1)}, bf16[384,1024]{1,0:T(8,128)(2,1)}, u32[]{:S(2)}, u32[]{:S(2)}) collective-permute-start(bf16[384,1024]{1,0:T(8,128)(2,1)} %constant_dynamic-update-slice_fusion), channel_id=1, source_target_pairs={{0,8},{4,12},{8,0},{12,4},{16,24},{20,28},{24,16},{28,20},{1,9},{5... | collective-permute-start | bytes 2359304 | tf_op jit(solution)/shard_map/ppermute | solution.py:43
  43.8 14.4 %collective-permute-start.4 = (bf16[384,1024]{1,0:T(8,128)(2,1)}, bf16[384,1024]{1,0:T(8,128)(2,1)}, u32[]{:S(2)}, u32[]{:S(2)}) collective-permute-start(bf16[384,1024]{1,0:T(8,128)(2,1)} %constant_dynamic-update-slice_fusion), channel_id=1, source_target_pairs={{0,16},{4,20},{8,24},{12,28},{16,0},{20,4},{24,8},{28,12},{1,17},{... | collective-permute-start | bytes 2359304 | tf_op jit(solution)/shard_map/ppermute | solution.py:43
  45.1 329.6 %reduce-scatter.4.cloned.1.call-start = ((), (), s32[]{:S(2)}) async-start(), calls=%async_computation.5 | async-start | bytes 2621440 | tf_op jit(solution)/shard_map/reduce_scatter | solution.py:600
  58.2 23.2 %collective-permute-start.7 = (bf16[384,1024]{1,0:T(8,128)(2,1)}, bf16[384,1024]{1,0:T(8,128)(2,1)}, u32[]{:S(2)}, u32[]{:S(2)}) collective-permute-start(bf16[384,1024]{1,0:T(8,128)(2,1)} %constant_dynamic-update-slice_fusion), channel_id=1, source_target_pairs={{0,4},{4,0},{8,12},{12,8},{16,20},{20,16},{24,28},{28,24},{1,5},{5... | collective-permute-start | bytes 2359304 | tf_op jit(solution)/shard_map/ppermute | solution.py:43
  64.1 17.4 %collective-permute-start.8 = (bf16[384,1024]{1,0:T(8,128)(2,1)}, bf16[384,1024]{1,0:T(8,128)(2,1)}, u32[]{:S(2)}, u32[]{:S(2)}) collective-permute-start(bf16[384,1024]{1,0:T(8,128)(2,1)} %collective-permute-done.3), channel_id=1, source_target_pairs={{0,4},{4,0},{8,12},{12,8},{16,20},{20,16},{24,28},{28,24},{1,5},{5... | collective-permute-start | bytes 2359304 | tf_op jit(solution)/shard_map/ppermute | solution.py:43
  64.1 17.4 %collective-permute-start.9 = (bf16[384,1024]{1,0:T(8,128)(2,1)}, bf16[384,1024]{1,0:T(8,128)(2,1)}, u32[]{:S(2)}, u32[]{:S(2)}) collective-permute-start(bf16[384,1024]{1,0:T(8,128)(2,1)} %collective-permute-done.4), channel_id=1, source_target_pairs={{0,4},{4,0},{8,12},{12,8},{16,20},{20,16},{24,28},{28,24},{1,5},{5... | collective-permute-start | bytes 2359304 | tf_op jit(solution)/shard_map/ppermute | solution.py:43
  80.7 27.2 %collective-permute-start.12 = (bf16[512,1024]{1,0:T(8,128)(2,1)S(1)}, bf16[512,1024]{1,0:T(8,128)(2,1)S(1)}, u32[]{:S(2)}, u32[]{:S(2)}) collective-permute-start(bf16[512,1024]{1,0:T(8,128)(2,1)S(1)} %copy-done.2), channel_id=1, source_target_pairs={{0,4},{4,0},{8,12},{12,8},{16,20},{20,16},{24,28},{28,24},{1,5},{5... | collective-permute-start | bytes 3145736 | tf_op jit(solution)/shard_map/ppermute | solution.py:43
  119.1 22.4 %collective-permute-start.13 = (bf16[256,1024]{1,0:T(8,128)(2,1)}, bf16[256,1024]{1,0:T(8,128)(2,1)}, u32[]{:S(2)}, u32[]{:S(2)}) collective-permute-start(bf16[256,1024]{1,0:T(8,128)(2,1)} %pad_maximum_fusion.4), channel_id=1, source_target_pairs={{0,1},{1,0},{2,3},{3,2},{4,5},{5,4},{6,7},{7,6},{8,9},{9,8},{10,11... | collective-permute-start | bytes 1572872 | tf_op jit(solution)/shard_map/ppermute | solution.py:31
  121.7 19.9 %collective-permute-start.14 = (bf16[256,1024]{1,0:T(8,128)(2,1)}, bf16[256,1024]{1,0:T(8,128)(2,1)}, u32[]{:S(2)}, u32[]{:S(2)}) collective-permute-start(bf16[256,1024]{1,0:T(8,128)(2,1)} %pad_maximum_fusion.4), channel_id=1, source_target_pairs={{1,2},{2,1},{5,6},{6,5},{9,10},{10,9},{13,14},{14,13},{17,18},{18,... | collective-permute-start | bytes 1572872 | tf_op jit(solution)/shard_map/ppermute | solution.py:31
  143.1 15.3 %collective-permute-start.16 = (bf16[256,1024]{1,0:T(8,128)(2,1)}, bf16[256,1024]{1,0:T(8,128)(2,1)}, u32[]{:S(2)}, u32[]{:S(2)}) collective-permute-start(bf16[256,1024]{1,0:T(8,128)(2,1)} %collective-permute-done.14), channel_id=1, source_target_pairs={{1,0},{2,3},{5,4},{6,7},{9,8},{10,11},{13,12},{14,15},{17,16},{18,... | collective-permute-start | bytes 1572872 | tf_op jit(solution)/shard_map/ppermute | solution.py:31
  158.4 20.7 %collective-permute-start.19 = (bf16[256,1024]{1,0:T(8,128)(2,1)}, bf16[256,1024]{1,0:T(8,128)(2,1)S(1)}, u32[]{:S(2)}, u32[]{:S(2)}) collective-permute-start(bf16[256,1024]{1,0:T(8,128)(2,1)} %collective-permute-done.15), channel_id=1, source_target_pairs={{1,0},{2,3},{5,4},{6,7},{9,8},{10,11},{13,12},{14,15},{17,16},{18,... | collective-permute-start | bytes 1572872 | tf_op jit(solution)/shard_map/ppermute | solution.py:31
  161.0 18.2 %collective-permute-start.22 = (bf16[256,1024]{1,0:T(8,128)(2,1)S(1)}, bf16[256,1024]{1,0:T(8,128)(2,1)S(1)}, u32[]{:S(2)}, u32[]{:S(2)}) collective-permute-start(bf16[256,1024]{1,0:T(8,128)(2,1)S(1)} %broadcast_select_fusion.1.refs_0_), channel_id=1, source_target_pairs={{0,8},{4,12},{8,0},{12,4},{16,24},{20,28},{24,16},{28,20},{1,9},{5... | collective-permute-start | bytes 1572872 | tf_op jit(solution)/shard_map/ppermute | solution.py:43
  162.0 17.2 %collective-permute-start.23 = (bf16[256,1024]{1,0:T(8,128)(2,1)S(1)}, bf16[256,1024]{1,0:T(8,128)(2,1)S(1)}, u32[]{:S(2)}, u32[]{:S(2)}) collective-permute-start(bf16[256,1024]{1,0:T(8,128)(2,1)S(1)} %broadcast_select_fusion.1.refs_0_), channel_id=1, source_target_pairs={{0,16},{4,20},{8,24},{12,28},{16,0},{20,4},{24,8},{28,12},{1,17},{... | collective-permute-start | bytes 1572872 | tf_op jit(solution)/shard_map/ppermute | solution.py:43
  179.3 17.6 %collective-permute-start.26 = (bf16[256,1024]{1,0:T(8,128)(2,1)S(1)}, bf16[256,1024]{1,0:T(8,128)(2,1)}, u32[]{:S(2)}, u32[]{:S(2)}) collective-permute-start(bf16[256,1024]{1,0:T(8,128)(2,1)S(1)} %broadcast_select_fusion.refs_5_), channel_id=1, source_target_pairs={{0,8},{4,12},{8,0},{12,4},{16,24},{20,28},{24,16},{28,20},{1,9},{5... | collective-permute-start | bytes 1572872 | tf_op jit(solution)/shard_map/ppermute | solution.py:43
  180.3 16.6 %collective-permute-start.27 = (bf16[256,1024]{1,0:T(8,128)(2,1)S(1)}, bf16[256,1024]{1,0:T(8,128)(2,1)}, u32[]{:S(2)}, u32[]{:S(2)}) collective-permute-start(bf16[256,1024]{1,0:T(8,128)(2,1)S(1)} %broadcast_select_fusion.refs_5_), channel_id=1, source_target_pairs={{0,16},{4,20},{8,24},{12,28},{16,0},{20,4},{24,8},{28,12},{1,17},{... | collective-permute-start | bytes 1572872 | tf_op jit(solution)/shard_map/ppermute | solution.py:43
  181.6 15.3 %collective-permute-start.24 = (bf16[128,1024]{1,0:T(8,128)(2,1)S(1)}, bf16[128,1024]{1,0:T(8,128)(2,1)S(1)}, u32[]{:S(2)}, u32[]{:S(2)}) collective-permute-start(bf16[128,1024]{1,0:T(8,128)(2,1)S(1)} %slice.136), channel_id=1, source_target_pairs={{0,8},{4,12},{8,0},{12,4},{16,24},{20,28},{24,16},{28,20},{1,9},{5... | collective-permute-start | bytes 786440 | tf_op jit(solution)/shard_map/ppermute | solution.py:43
  199.3 16.0 %collective-permute-start.30 = (bf16[512,1024]{1,0:T(8,128)(2,1)S(1)}, bf16[512,1024]{1,0:T(8,128)(2,1)S(1)}, u32[]{:S(2)}, u32[]{:S(2)}) collective-permute-start(bf16[512,1024]{1,0:T(8,128)(2,1)S(1)} %multiply_convert_fusion.5.right_ref), channel_id=1, source_target_pairs={{0,4},{4,0},{8,12},{12,8},{16,20},{20,16},{24,28},{28,24},{1,5},{5... | collective-permute-start | bytes 3145736 | tf_op jit(solution)/shard_map/ppermute | solution.py:43
  236.8 44.1 %collective-permute-start.41 = (bf16[1024,1024]{1,0:T(8,128)(2,1)}, bf16[1024,1024]{1,0:T(8,128)(2,1)}, u32[]{:S(2)}, u32[]{:S(2)}) collective-permute-start(bf16[1024,1024]{1,0:T(8,128)(2,1)} %all-gather.5.cloned.1.call-done.rows_two_ref), channel_id=1, source_target_pairs={{0,4},{4,0},{8,12},{12,8},{16,20},{20,16},{24,28},{28,24},{1,5},{5... | collective-permute-start | bytes 6291464 | tf_op jit(solution)/shard_map/ppermute | solution.py:43
  237.3 42.4 %collective-permute-start.40 = (bf16[1024,1024]{1,0:T(8,128)(2,1)}, bf16[1024,1024]{1,0:T(8,128)(2,1)}, u32[]{:S(2)}, u32[]{:S(2)}) collective-permute-start(bf16[1024,1024]{1,0:T(8,128)(2,1)} %all-gather.3.cloned.1.call-done.rows_ref), channel_id=1, source_target_pairs={{0,4},{4,0},{8,12},{12,8},{16,20},{20,16},{24,28},{28,24},{1,5},{5... | collective-permute-start | bytes 6291464 | tf_op jit(solution)/shard_map/ppermute | solution.py:43
  238.2 43.4 %collective-permute-start.39 = (bf16[512,512]{1,0:T(8,128)(2,1)}, bf16[512,512]{1,0:T(8,128)(2,1)S(1)}, u32[]{:S(2)}, u32[]{:S(2)}) collective-permute-start(bf16[512,512]{1,0:T(8,128)(2,1)} %slice.141), channel_id=1, source_target_pairs={{0,4},{4,0},{8,12},{12,8},{16,20},{20,16},{24,28},{28,24},{1,5},{5... | collective-permute-start | bytes 1572872 | tf_op jit(solution)/shard_map/ppermute | solution.py:43
  249.2 16.1 %collective-permute-start.33 = (bf16[512,1024]{1,0:T(8,128)(2,1)}, bf16[512,1024]{1,0:T(8,128)(2,1)S(1)}, u32[]{:S(2)}, u32[]{:S(2)}) collective-permute-start(bf16[512,1024]{1,0:T(8,128)(2,1)} %convolution_convert_fusion.3), channel_id=1, source_target_pairs={{0,4},{4,0},{8,12},{12,8},{16,20},{20,16},{24,28},{28,24},{1,5},{5... | collective-permute-start | bytes 3145736 | tf_op jit(solution)/shard_map/ppermute | solution.py:43
  270.2 19.5 %collective-permute-start.38 = (bf16[512,1024]{1,0:T(8,128)(2,1)S(1)}, bf16[512,1024]{1,0:T(8,128)(2,1)}, u32[]{:S(2)}, u32[]{:S(2)}) collective-permute-start(bf16[512,1024]{1,0:T(8,128)(2,1)S(1)} %get-tuple-element.342.right_ref), channel_id=1, source_target_pairs={{0,4},{4,0},{8,12},{12,8},{16,20},{20,16},{24,28},{28,24},{1,5},{5... | collective-permute-start | bytes 3145736 | tf_op jit(solution)/shard_map/ppermute | solution.py:43
  278.9 50.7 %collective-permute-start.34 = (bf16[512,1024]{1,0:T(8,128)(2,1)}, bf16[512,1024]{1,0:T(8,128)(2,1)}, u32[]{:S(2)}, u32[]{:S(2)}) collective-permute-start(bf16[512,1024]{1,0:T(8,128)(2,1)} %get-tuple-element.241), channel_id=1, source_target_pairs={{0,8},{4,12},{8,0},{12,4},{16,24},{20,28},{24,16},{28,20},{1,9},{5... | collective-permute-start | bytes 3145736 | tf_op jit(solution)/shard_map/ppermute | solution.py:43
  279.7 49.9 %collective-permute-start.35 = (bf16[512,1024]{1,0:T(8,128)(2,1)}, bf16[512,1024]{1,0:T(8,128)(2,1)}, u32[]{:S(2)}, u32[]{:S(2)}) collective-permute-start(bf16[512,1024]{1,0:T(8,128)(2,1)} %get-tuple-element.242), channel_id=1, source_target_pairs={{0,16},{4,20},{8,24},{12,28},{16,0},{20,4},{24,8},{28,12},{1,17},{... | collective-permute-start | bytes 3145736 | tf_op jit(solution)/shard_map/ppermute | solution.py:43
  280.9 48.7 %collective-permute-start.36 = (bf16[512,1024]{1,0:T(8,128)(2,1)}, bf16[512,1024]{1,0:T(8,128)(2,1)}, u32[]{:S(2)}, u32[]{:S(2)}) collective-permute-start(bf16[512,1024]{1,0:T(8,128)(2,1)} %get-tuple-element.243), channel_id=1, source_target_pairs={{0,8},{4,12},{8,0},{12,4},{16,24},{20,28},{24,16},{28,20},{1,9},{5... | collective-permute-start | bytes 3145736 | tf_op jit(solution)/shard_map/ppermute | solution.py:43
  281.7 48.0 %collective-permute-start.37 = (bf16[512,1024]{1,0:T(8,128)(2,1)}, bf16[512,1024]{1,0:T(8,128)(2,1)}, u32[]{:S(2)}, u32[]{:S(2)}) collective-permute-start(bf16[512,1024]{1,0:T(8,128)(2,1)} %get-tuple-element.244), channel_id=1, source_target_pairs={{0,16},{4,20},{8,24},{12,28},{16,0},{20,4},{24,8},{28,12},{1,17},{... | collective-permute-start | bytes 3145736 | tf_op jit(solution)/shard_map/ppermute | solution.py:43
  289.7 39.9 %collective-permute-start.42 = (f32[2,1024]{1,0:T(2,128)S(1)}, f32[2,1024]{1,0:T(2,128)S(1)}, u32[]{:S(2)}, u32[]{:S(2)}) collective-permute-start(f32[2,1024]{1,0:T(2,128)S(1)} %pad_maximum_fusion.9), channel_id=1, source_target_pairs={{0,4},{4,0},{8,12},{12,8},{16,20},{20,16},{24,28},{28,24},{1,5},{5... | collective-permute-start | bytes 24584 | tf_op jit(solution)/shard_map/ppermute | solution.py:43
  329.7 94.8 %reduce-scatter.6.cloned.1.call-start = ((), (), s32[]{:S(2)}) async-start(), calls=%async_computation.6 | async-start | bytes 2621440 | tf_op jit(solution)/shard_map/reduce_scatter | solution.py:600
  329.7 44.6 %collective-permute-start.45 = (bf16[2,1024,512]{2,1,0:T(8,128)(2,1)}, bf16[2,1024,512]{2,1,0:T(8,128)(2,1)}, u32[]{:S(2)}, u32[]{:S(2)}) collective-permute-start(bf16[2,1024,512]{2,1,0:T(8,128)(2,1)} %get-tuple-element.263), channel_id=1, source_target_pairs={{0,4},{4,0},{8,12},{12,8},{16,20},{20,16},{24,28},{28,24},{1,5},{5... | collective-permute-start | bytes 6291464 | tf_op jit(solution)/shard_map/ppermute | solution.py:43
  333.6 40.8 %collective-permute-start.43 = (bf16[512,1024]{1,0:T(8,128)(2,1)S(1)}, bf16[512,1024]{1,0:T(8,128)(2,1)}, u32[]{:S(2)}, u32[]{:S(2)}) collective-permute-start(bf16[512,1024]{1,0:T(8,128)(2,1)S(1)} %add_convert_fusion.4), channel_id=1, source_target_pairs={{0,8},{4,12},{8,0},{12,4},{16,24},{20,28},{24,16},{28,20},{1,9},{5... | collective-permute-start | bytes 3145736 | tf_op jit(solution)/shard_map/ppermute | solution.py:43
  334.4 40.0 %collective-permute-start.44 = (bf16[512,1024]{1,0:T(8,128)(2,1)S(1)}, bf16[512,1024]{1,0:T(8,128)(2,1)}, u32[]{:S(2)}, u32[]{:S(2)}) collective-permute-start(bf16[512,1024]{1,0:T(8,128)(2,1)S(1)} %add_convert_fusion.3), channel_id=1, source_target_pairs={{0,16},{4,20},{8,24},{12,28},{16,0},{20,4},{24,8},{28,12},{1,17},{... | collective-permute-start | bytes 3145736 | tf_op jit(solution)/shard_map/ppermute | solution.py:43
  335.7 38.7 %collective-permute-start.46 = (f32[2,1024]{1,0:T(2,128)S(1)}, f32[2,1024]{1,0:T(2,128)S(1)}, u32[]{:S(2)}, u32[]{:S(2)}) collective-permute-start(f32[2,1024]{1,0:T(2,128)S(1)} %fusion.31), channel_id=1, source_target_pairs={{0,8},{4,12},{8,0},{12,4},{16,24},{20,28},{24,16},{28,20},{1,9},{5... | collective-permute-start | bytes 24584 | tf_op jit(solution)/shard_map/ppermute | solution.py:43
  379.6 150.3 %reduce-scatter.8.cloned.1.call-start = ((), (), s32[]{:S(2)}) async-start(), calls=%async_computation.7 | async-start | bytes 2621440 | tf_op jit(solution)/shard_map/reduce_scatter | solution.py:600
  402.2 33.4 %collective-permute-start.59 = (bf16[256,1024]{1,0:T(8,128)(2,1)}, bf16[256,1024]{1,0:T(8,128)(2,1)}, u32[]{:S(2)}, u32[]{:S(2)}) collective-permute-start(bf16[256,1024]{1,0:T(8,128)(2,1)} %get-tuple-element.298), channel_id=1, source_target_pairs={{0,16},{4,20},{8,24},{12,28},{16,0},{20,4},{24,8},{28,12},{1,17},{... | collective-permute-start | bytes 1572872 | tf_op jit(solution)/shard_map/ppermute | solution.py:43
  402.9 32.6 %collective-permute-start.60 = (f32[2,1024]{1,0:T(2,128)S(1)}, f32[2,1024]{1,0:T(2,128)S(1)}, u32[]{:S(2)}, u32[]{:S(2)}) collective-permute-start(f32[2,1024]{1,0:T(2,128)S(1)} %add.236), channel_id=1, source_target_pairs={{0,1},{1,0},{2,3},{3,2},{4,5},{5,4},{6,7},{7,6},{8,9},{9,8},{10,11... | collective-permute-start | bytes 24584 | tf_op jit(solution)/shard_map/ppermute | solution.py:31
  436.9 14.4 %collective-permute-start.66 = (bf16[256,1024]{1,0:T(8,128)(2,1)S(1)}, bf16[256,1024]{1,0:T(8,128)(2,1)S(1)}, u32[]{:S(2)}, u32[]{:S(2)}) collective-permute-start(bf16[256,1024]{1,0:T(8,128)(2,1)S(1)} %copy-done.33), channel_id=1, source_target_pairs={{0,16},{4,20},{8,24},{12,28},{16,0},{20,4},{24,8},{28,12},{1,17},{... | collective-permute-start | bytes 1572872 | tf_op jit(solution)/shard_map/ppermute | solution.py:43
  438.1 21.9 %collective-permute-start.65 = (bf16[256,1024]{1,0:T(8,128)(2,1)S(1)}, bf16[256,1024]{1,0:T(8,128)(2,1)S(1)}, u32[]{:S(2)}, u32[]{:S(2)}) collective-permute-start(bf16[256,1024]{1,0:T(8,128)(2,1)S(1)} %get-tuple-element.315), channel_id=1, source_target_pairs={{0,8},{4,12},{8,0},{12,4},{16,24},{20,28},{24,16},{28,20},{1,9},{5... | collective-permute-start | bytes 1572872 | tf_op jit(solution)/shard_map/ppermute | solution.py:43
  448.8 22.4 %collective-permute-start.63 = (bf16[256,1024]{1,0:T(8,128)(2,1)S(1)}, bf16[256,1024]{1,0:T(8,128)(2,1)S(1)}, u32[]{:S(2)}, u32[]{:S(2)}) collective-permute-start(bf16[256,1024]{1,0:T(8,128)(2,1)S(1)} %add_convert_fusion.8), channel_id=1, source_target_pairs={{0,8},{4,12},{8,0},{12,4},{16,24},{20,28},{24,16},{28,20},{1,9},{5... | collective-permute-start | bytes 1572872 | tf_op jit(solution)/shard_map/ppermute | solution.py:43
  450.0 21.1 %collective-permute-start.64 = (bf16[256,1024]{1,0:T(8,128)(2,1)S(1)}, bf16[256,1024]{1,0:T(8,128)(2,1)S(1)}, u32[]{:S(2)}, u32[]{:S(2)}) collective-permute-start(bf16[256,1024]{1,0:T(8,128)(2,1)S(1)} %add_convert_fusion.7), channel_id=1, source_target_pairs={{0,16},{4,20},{8,24},{12,28},{16,0},{20,4},{24,8},{28,12},{1,17},{... | collective-permute-start | bytes 1572872 | tf_op jit(solution)/shard_map/ppermute | solution.py:43
  478.2 14.2 %collective-permute-start.68 = (bf16[128,1024]{1,0:T(8,128)(2,1)S(1)}, bf16[128,1024]{1,0:T(8,128)(2,1)S(1)}, u32[]{:S(2)}, u32[]{:S(2)}) collective-permute-start(bf16[128,1024]{1,0:T(8,128)(2,1)S(1)} %pad_maximum_fusion.7), channel_id=1, source_target_pairs={{0,2},{1,3},{2,0},{3,1},{4,6},{5,7},{6,4},{7,5},{8,10},{9,11},{10,... | collective-permute-start | bytes 786440 | tf_op jit(solution)/shard_map/ppermute | solution.py:31
  485.2 21.0 %collective-permute-start.53 = (bf16[256,1024]{1,0:T(8,128)(2,1)S(1)}, bf16[256,1024]{1,0:T(8,128)(2,1)S(1)}, u32[]{:S(2)}, u32[]{:S(2)}) collective-permute-start(bf16[256,1024]{1,0:T(8,128)(2,1)S(1)} %collective-permute-done.50.refs_2_), channel_id=1, source_target_pairs={{0,4},{4,0},{8,12},{12,8},{16,20},{20,16},{24,28},{28,24},{1,5},{5... | collective-permute-start | bytes 1572872 | tf_op jit(solution)/shard_map/ppermute | solution.py:43
  487.9 18.3 %collective-permute-start.54 = (bf16[256,1024]{1,0:T(8,128)(2,1)S(1)}, bf16[256,1024]{1,0:T(8,128)(2,1)S(1)}, u32[]{:S(2)}, u32[]{:S(2)}) collective-permute-start(bf16[256,1024]{1,0:T(8,128)(2,1)S(1)} %collective-permute-done.51.refs_4_), channel_id=1, source_target_pairs={{0,4},{4,0},{8,12},{12,8},{16,20},{20,16},{24,28},{28,24},{1,5},{5... | collective-permute-start | bytes 1572872 | tf_op jit(solution)/shard_map/ppermute | solution.py:43
  500.3 14.2 %collective-permute-start.70 = (bf16[128,1024]{1,0:T(8,128)(2,1)S(1)}, bf16[128,1024]{1,0:T(8,128)(2,1)S(1)}, u32[]{:S(2)}, u32[]{:S(2)}) collective-permute-start(bf16[128,1024]{1,0:T(8,128)(2,1)S(1)} %add_convert_fusion.9.refs_0_), channel_id=1, source_target_pairs={{0,8},{4,12},{8,0},{12,4},{16,24},{20,28},{24,16},{28,20},{1,9},{5... | collective-permute-start | bytes 786440 | tf_op jit(solution)/shard_map/ppermute | solution.py:43
  (93 other events, 676.8 us)
Sparse Core Ops, SparseCore 0:
  10.1 62.6 all-gather.2
  74.4 44.7 all-gather.4
  329.8 44.9 reduce-scatter.3
  379.7 44.6 reduce-scatter.5
  426.6 43.3 reduce-scatter.7

commit v3 on v2

--- a/solution.py
+++ b/solution.py
@@ -50,8 +50,7 @@
         return total
 
 
-def forward_kernel(q_ref, *refs):
-    blocks = (len(refs) - 5) // 2
+def forward_kernel(blocks, q_ref, *refs):
     k_refs, v_refs = refs[:blocks], refs[blocks : 2 * blocks]
     bias_ref, out_ref, lse_ref = refs[2 * blocks], refs[-2], refs[-1]
     scale = HEAD**-0.5 * LOG2E
@@ -86,20 +85,20 @@
         )
 
 
-def attention_forward(q, kvs, bias, first, count, held):
+def attention_forward(q, kvs, bias, first, count, held=()):
     rows, width = q.shape
     keys = bias.shape[1]
     pairs = width // (2 * HEAD)
     wide = 2 * HEAD
     at = lambda shift: lambda h: (0, h + first + shift)
     return pl.pallas_call(
-        forward_kernel,
+        functools.partial(forward_kernel, len(kvs)),
         grid=(count,),
         in_specs=[pl.BlockSpec((rows, wide), at(0))]
         + [pl.BlockSpec((kv.shape[0], wide), at(0)) for kv in kvs]
         + [pl.BlockSpec((kv.shape[0], wide), at(pairs)) for kv in kvs]
         + [pl.BlockSpec((1, keys), lambda h: (0, 0))]
-        + [pl.BlockSpec(memory_space=pl.ANY)] * 2,
+        + [pl.BlockSpec(memory_space=pl.ANY)] * len(held),
         out_specs=[
             pl.BlockSpec((rows, wide), at(0)),
             pl.BlockSpec((1, 2, rows), lambda h: (h + first, 0, 0)),
@@ -108,15 +107,15 @@
             jax.ShapeDtypeStruct((rows, width), BF),
             jax.ShapeDtypeStruct((pairs, 2, rows), F32),
         ],
-        input_output_aliases={2 * len(kvs) + 2: 0, 2 * len(kvs) + 3: 1},
-        compiler_params=pltpu.CompilerParams(vmem_limit_bytes=48 * 2**20),
+        input_output_aliases={2 * len(kvs) + 2 + n: n for n in range(len(held))},
+        compiler_params=pltpu.CompilerParams(vmem_limit_bytes=24 * 2**20),
         cost_estimate=LIGHT,
         name="attention_forward",
     )(q, *kvs, *kvs, bias, *held)
 
 
 def backward_kernel(
-    q_ref, k_ref, v_ref, go_ref, lse_ref, inner_ref, bias_ref, wkv_ref, *refs
+    q_ref, k_ref, v_ref, go_ref, att_ref, lse_ref, bias_ref, wkv_ref, *refs
 ):
     add_ref = refs[0] if len(refs) == 9 else None
     gq_ref, keep_k_ref, keep_v_ref, send_ref, part_ref, all_ref = refs[-6:]
@@ -130,6 +129,11 @@
     mine = [(lane < HEAD) == (head == 0) for head in range(2)]
     qs = [jnp.where(m, q, zero) for m in mine]
     gos = [jnp.where(m, go, zero) for m in mine]
+    product = go.T.astype(F32) * att_ref[...].T.astype(F32)
+    inner = [
+        jnp.sum(product[head * HEAD : (head + 1) * HEAD], axis=0, keepdims=True)
+        for head in range(2)
+    ]
     total_q = [0.0, 0.0]
     gks, gvs = [], []
     sub = 512
@@ -144,7 +148,7 @@
             s = lax.dot_general(k, q, NT, preferred_element_type=F32)
             p = jnp.exp2(s * (scale * LOG2E) + (bias - lse_ref[0, head : head + 1, :]))
             gp = lax.dot_general(v, go, NT, preferred_element_type=F32)
-            gs = (p * (gp - inner_ref[0, head : head + 1, :])).astype(BF)
+            gs = (p * (gp - inner[head])).astype(BF)
             total_v += lax.dot_general(p.astype(BF), gos[head], NN, preferred_element_type=F32)
             total_k += lax.dot_general(gs, qs[head], NN, preferred_element_type=F32)
             own_keys = keys_t[head * HEAD : (head + 1) * HEAD]
@@ -153,7 +157,7 @@
         gvs.append(total_v.astype(BF))
     gk, gv = jnp.concatenate(gks), jnp.concatenate(gvs)
     gq = jnp.concatenate(total_q).T * scale
-    gq_ref[...] = gq if add_ref is None else gq + add_ref[...]
+    gq_ref[...] = (gq if add_ref is None else gq + add_ref[...]).astype(gq_ref.dtype)
     half = pairs // 2
 
     @pl.when(step < half)
@@ -184,7 +188,7 @@
     return part_ref.shape[1]
 
 
-def attention_backward(q, kv, go, lse, inner, bias, wkv, block, blocks, held):
+def attention_backward(q, kv, go, attended, lse, bias, wkv, block, blocks, held):
     rows, width = q.shape
     keys = kv.shape[0]
     pairs = width // (2 * HEAD)
@@ -203,15 +207,15 @@
             pl.BlockSpec((keys, wide), lambda h: (0, h)),
             pl.BlockSpec((keys, wide), lambda h: (0, h + pairs)),
             by_pair,
-            stats,
+            by_pair,
             stats,
             pl.BlockSpec((keys, 128), lambda h: (0, 0)),
-            pl.BlockSpec((2 * width, width), lambda h: (0, 0)),
+            pl.BlockSpec((2 * width, width), lambda h: (0, 0), pipeline_mode=pl.Buffered(1)),
         ]
         + ([by_pair, whole, whole] if held else []),
         out_specs=[by_pair, keep, keep, send, pl.BlockSpec((keys, width), lambda h: (0, 0))],
         out_shape=[
-            jax.ShapeDtypeStruct((rows, width), F32),
+            jax.ShapeDtypeStruct((rows, width), BF if held else F32),
             jax.ShapeDtypeStruct((blocks * keys, width // 2), BF),
             jax.ShapeDtypeStruct((blocks * keys, width // 2), BF),
             jax.ShapeDtypeStruct((2, keys, width // 2), BF),
@@ -222,7 +226,7 @@
         compiler_params=pltpu.CompilerParams(vmem_limit_bytes=48 * 2**20),
         cost_estimate=LIGHT,
         name="attention_backward",
-    )(q, kv, kv, go, lse, inner, bias, wkv, *(held or ()))
+    )(q, kv, kv, go, attended, lse, bias, wkv, *(held or ()))
 
 
 def gelu_tile(x):
@@ -266,7 +270,7 @@
     core = width // 2
     wide = core // 2
     which = 1 if first else 0
-    whole = lambda a: pl.BlockSpec(a.shape, lambda g: (0, 0))
+    whole = lambda a: pl.BlockSpec(a.shape, lambda g: (0, 0), pipeline_mode=pl.Buffered(1))
     columns = lambda n: pl.BlockSpec((n, wide), lambda g: (0, g))
     arrived = pl.BlockSpec((1, keys, wide), lambda g: (which, 0, g))
     return pl.pallas_call(
@@ -363,7 +367,7 @@
 def outer_four(left, right, left_two, right_two):
     rows, hidden = left.shape
     width = right.shape[1]
-    tile = 256
+    tile = 512
     each = hidden // (4 * tile)
     columns = pl.BlockSpec((rows, tile), lambda i: (0, i))
     whole = pl.BlockSpec((rows, width), lambda i: (0, 0))
@@ -384,37 +388,76 @@
     return ((i & 1) << 2) | (i & 2) | (i >> 2)
 
 
-def placed_kernel(flips, order, at_ref, *refs):
+def heads_placed_kernel(at_ref, *refs):
+    *pieces, turned_ref, plain_ref, whole_ref = refs
+    step, last = pl.program_id(0), pl.num_programs(0) - 1
+    for i, piece in enumerate(pieces):
+        place = reverse(at_ref[0] ^ i)
+        size = piece.shape[0]
+        whole_ref[pl.ds(pl.multiple_of(place * size, size), size), :] = piece[...]
+
+    @pl.when(step < last)
+    def _():
+        turned_ref[0] = whole_ref[...].T.astype(F32)
+
+    @pl.when(step == last)
+    def _():
+        plain_ref[...] = whole_ref[...].astype(F32)
+
+
+def heads_placed(pieces, s8):
+    width = pieces[0].shape[1]
+    size = pieces[0].shape[0] // 4
+    rows = 8 * size
+    return pl.pallas_call(
+        heads_placed_kernel,
+        grid=(4,),
+        in_specs=[pl.BlockSpec(memory_space=pltpu.SMEM)]
+        + [pl.BlockSpec((size, width), lambda n: (n, 0)) for _ in pieces],
+        out_specs=[
+            pl.BlockSpec((1, width, rows), lambda n: (jnp.minimum(n, 2), 0, 0)),
+            pl.BlockSpec((rows, width), lambda n: (0, 0)),
+        ],
+        out_shape=[
+            jax.ShapeDtypeStruct((3, width, rows), F32),
+            jax.ShapeDtypeStruct((rows, width), F32),
+        ],
+        scratch_shapes=[pltpu.VMEM((rows, width), BF)],
+        compiler_params=pltpu.CompilerParams(vmem_limit_bytes=32 * 2**20),
+        cost_estimate=LIGHT,
+        name="heads_placed",
+    )(s8[None].astype(jnp.int32), *pieces)
+
+
+def placed_kernel(flips, at_ref, *refs):
     *pieces, out_ref, whole_ref = refs
     for i, piece in enumerate(pieces):
-        place = order(at_ref[0] ^ i)
+        place = at_ref[0] ^ i
         size = piece.shape[0]
-        whole_ref[pl.ds(pl.multiple_of(place * size, size), size), :] = piece[...].astype(F32)
+        whole_ref[pl.ds(pl.multiple_of(place * size, size), size), :] = piece[...]
     out = whole_ref[...]
     out = out.T if flips else out
-    out_ref[...] = out.reshape(out_ref.shape)
-
-
-def placed(pieces, kinds, size, order, s8, flips):
+    out_ref[...] = out.astype(F32)
+
+
+def placed(pieces, size, s8, flips):
     width = pieces[0][0].shape[1]
-    tile = 256
+    tile = 512
     rows = 8 * size
-    if kinds > 1:
-        out_shape = (kinds, width, rows)
-        out_spec = pl.BlockSpec((1, tile, rows), lambda n, c: (n, c, 0))
-    elif flips:
-        out_shape, out_spec = (width, rows), pl.BlockSpec((tile, rows), lambda n, c: (c, 0))
+    if flips:
+        out_shape, out_spec = (width, rows), pl.BlockSpec((tile, rows), lambda c: (c, 0))
     else:
-        out_shape, out_spec = (rows, width), pl.BlockSpec((rows, tile), lambda n, c: (0, c))
-    part = lambda first: pl.BlockSpec((size, tile), lambda n, c: (n + first, c))
+        out_shape, out_spec = (rows, width), pl.BlockSpec((rows, tile), lambda c: (0, c))
+    part = lambda first: pl.BlockSpec((size, tile), lambda c: (first, c))
     return pl.pallas_call(
-        functools.partial(placed_kernel, flips, order),
-        grid=(kinds, width // tile),
+        functools.partial(placed_kernel, flips),
+        grid=(width // tile,),
         in_specs=[pl.BlockSpec(memory_space=pltpu.SMEM)] + [part(first) for _, first in pieces],
         out_specs=out_spec,
         out_shape=jax.ShapeDtypeStruct(out_shape, F32),
-        scratch_shapes=[pltpu.VMEM((rows, tile), F32)],
+        scratch_shapes=[pltpu.VMEM((rows, tile), BF)],
         compiler_params=pltpu.CompilerParams(vmem_limit_bytes=32 * 2**20),
+        cost_estimate=LIGHT,
         name="placed",
     )(s8[None].astype(jnp.int32), *[array for array, _ in pieces])
 
@@ -469,7 +512,17 @@
         for n in range(2)
     ]
     a_far = [across(attn_own, j) for j in (1, 2, 3)]
-    a_far = fence(*a_far)
+    whole = bucket[0] == 1
+    place = jnp.arange(rows, dtype=jnp.int32)
+    seen = []
+    for u in range(4):
+        alone = jnp.where(t == u, lengths[0, u], 0)
+        limit = jnp.where(whole, lengths[0, 0] - u * rows, alone)
+        seen.append((place < limit).reshape(2, upper))
+    bias = jnp.where(jnp.stack(seen, axis=1), 0.0, -1e9).astype(F32).reshape(4 * rows)
+    bias, *a_far = fence(bias, *a_far)
+    bias_cols = jnp.broadcast_to(bias[:, None], (4 * rows, 128))
+
     attn_three = jnp.concatenate(a_far)
     half = attn_three.shape[0] // 2
     a_x, a_y = swap(attn_three, 2), swap(attn_three, 4)
@@ -490,16 +543,6 @@
     wq, wk, wv, wo = [w_attn[n] for n in range(4)]
     wkv = w_attn[1:3].reshape(2 * width, width)
 
-    whole = bucket[0] == 1
-    place = jnp.arange(rows, dtype=jnp.int32)
-    seen = []
-    for u in range(4):
-        alone = jnp.where(t == u, lengths[0, u], 0)
-        limit = jnp.where(whole, lengths[0, 0] - u * rows, alone)
-        seen.append((place < limit).reshape(2, upper))
-    bias = jnp.where(jnp.stack(seen, axis=1), 0.0, -1e9).astype(F32).reshape(4 * rows)
-    bias_cols = jnp.broadcast_to(bias[:, None], (4 * rows, 128))
-
     q = mm(tokens, wq, NT, BF)
     tokens_peer = swap(tokens, 1)
     upper_kv = mm(gathered[0], wkv, NT, BF)
@@ -507,30 +550,29 @@
         upper_kv, q, tokens_peer, ff_own, up_own, down_own, *gathered
     )
     f_one, f_far = along(ff_own, PAIR), along(ff_own, MIDDLE)
-    kvs = fence(upper_kv, mm(gathered[1], wkv, NT, BF))
-    held = (jnp.zeros((rows, width), BF), jnp.zeros((width // (2 * HEAD), 2, rows), F32))
+    f_one, f_far, *kvs = fence(f_one, f_far, upper_kv, mm(gathered[1], wkv, NT, BF))
     bias_row = bias[None]
-    held = attention_forward(q, kvs, bias_row, 0, 2, held)
-    f_one, f_far, *held = fence(f_one, f_far, *held)
     f_two, f_two_end = along(f_one, MIDDLE), along(f_far, OUTWARD)
     one_x, one_y = swap(f_one, 2), swap(f_one, 4)
-    held = attention_forward(q, kvs, bias_row, 2, 2, held)
+    held = attention_forward(q, kvs, bias_row, 0, 2)
     f_two, f_two_end, one_x, one_y, *held = fence(f_two, f_two_end, one_x, one_y, *held)
     f_three_end = along(f_two, OUTWARD)
     f_two = jnp.where(middle, f_two, f_two_end)
+    two_x, two_y = swap(f_two, 2), swap(f_two, 4)
     one_d1, one_d2 = swap(one_y[:fp], 2), swap(one_x[fp:], 4)
-    two_x, two_y = swap(f_two, 2), swap(f_two, 4)
-    held = attention_forward(q, kvs, bias_row, 4, 2, held)
+    held = attention_forward(q, kvs, bias_row, 2, 2, held)
     f_three_end, one_d1, one_d2, two_x, two_y, *held = fence(
         f_three_end, one_d1, one_d2, two_x, two_y, *held
     )
     f_three = jnp.where(middle, f_far, f_three_end)
+    three_x, three_y = swap(f_three, 2), swap(f_three, 4)
     two_d1, two_d2 = swap(two_y[:fp], 2), swap(two_x[fp:], 4)
-    three_x, three_y = swap(f_three, 2), swap(f_three, 4)
 
     def moves(j, block):
         own, by_x, by_y, d1, d2 = block
-        for i, (a, b, at) in enumerate(((own,) * 2 + (fp,), (by_x,) * 2 + (fp,), (by_y,) * 2 + (fp,), (d1, d2, 0))):
+        last = (d1, d2, fp if d1 is d2 else 0)
+        sources = [(own, own, fp), (by_x, by_x, fp), (by_y, by_y, fp), last]
+        for i, (a, b, at) in enumerate(sources):
             yield (a, 0, fp, 0, (4 * i + j) * fp)
             yield (b, at, fp, 1, (4 * i + j) * fp)
 
@@ -542,9 +584,11 @@
     w_ff = put_rows([*own, *one], (ff * 2, width), 2)
     w_ff = fence(*w_ff, *held)
     w_ff, held = w_ff[:2], w_ff[2:]
-    held = attention_forward(q, kvs, bias_row, 6, 2, held)
+    held = attention_forward(q, kvs, bias_row, 4, 2, held)
     two_d1, two_d2, three_x, three_y, *held = fence(two_d1, two_d2, three_x, three_y, *held)
     three_d1, three_d2 = swap(three_y[:fp], 2), swap(three_x[fp:], 4)
+    held = attention_forward(q, kvs, bias_row, 6, 2, held)
+    three_d1, three_d2, *held = fence(three_d1, three_d2, *held)
     attended, lse = held
     first_sum = up(tokens) + mm(attended, wo, NN)
     unit_one, root_one = centred(first_sum)
@@ -582,17 +626,15 @@
     first_low = grad_first.astype(BF)
     first_peer = swap(first_low, 1)
     go = mm(first_low, wo, NT, BF)
-    inner = (up(go) * up(attended)).reshape(rows, width // HEAD, HEAD).sum(-1)
-    inner = inner.T.reshape(width // (2 * HEAD), 2, rows)
     core = width // 2
-    inner, go, first_peer, attended_peer, *gathered_peer = fence(
-        inner, go, first_peer, attended_peer, *gathered_peer
+    go, first_peer, attended_peer, *gathered_peer = fence(
+        go, first_peer, attended_peer, *gathered_peer
     )
 
     def pull(n, held):
         keys = bias_cols[2 * n * rows : 2 * (n + 1) * rows]
         *held, send, part = attention_backward(
-            q, kvs[n], go, lse, inner, keys, wkv, n, 2, held
+            q, kvs[n], go, attended, lse, keys, wkv, n, 2, held
         )
         return held, send, part
 
@@ -600,7 +642,7 @@
         return lax.psum_scatter(part, "tp", scatter_dimension=0, tiled=True)
 
     gains = jnp.stack([gain_grad_one, gain_grad_two])
-    gains_came = swap(gains, 1)
+    gains_came = across(gains, 1)
     held, send, part = pull(0, None)
     diag_x, diag_y, one_x, two_y, send, part, gains_came, *held = fence(
         diag_x, diag_y, one_x, two_y, send, part, gains_came, *held
@@ -608,28 +650,26 @@
     upper_sum = line_sum(part)
     came = [swap(send, 1)]
     gains = gains + gains_came
-    gains_came = swap(gains, 2)
+    gains_came = across(gains, 2)
     two_x = (up(twos[1]) + up(diag_y)).astype(BF)
     one_y = (up(ones[2]) + up(diag_x)).astype(BF)
     two_x, one_y, *held = fence(two_x, one_y, *held)
     two_x, one_y = swap(two_x, 2), swap(one_y, 4)
     held, send, part = pull(1, held)
-    two_x, one_y, came[0], send, part, gains_came, upper_sum, *held = fence(
-        two_x, one_y, came[0], send, part, gains_came, upper_sum, *held
+    two_x, one_y, came[0], send, part, gains_came, *held = fence(
+        two_x, one_y, came[0], send, part, gains_came, *held
     )
     gq, gk, gv = held
-    gq = gq.astype(BF)
     came.append(swap(send, 1))
     gq_peer = swap(gq[:, core:], 1)
     gains = gains + gains_came
-    gains_came = swap(gains, 4)
-    ff_total = line_sum(
-        plane.higher(totals((ones[0], one_x, one_y), (twos[0], two_x, two_y), t))
-    )
-    first = mm(gq, wq, NN) + grad_first
-    came[1], gq_peer, gains_came, first = fence(came[1], gq_peer, gains_came, first)
+    gains_came = swap(gains, 1)
+    lower_sum = line_sum(part)
+    ff_total = plane.higher(totals((ones[0], one_x, one_y), (twos[0], two_x, two_y), t))
+    upper_sum, ff_total = fence(upper_sum, ff_total)
+    ff_total = line_sum(ff_total)
+    came[1], gq_peer, gains_came = fence(came[1], gq_peer, gains_came)
     gains = gains + gains_came
-    gains_came = across(gains, 1)
     a_twos = fence(
         *head_grads(
             True, gv, came, attended, attended_peer, gathered, gathered_peer, first_low, first_peer
@@ -639,33 +679,36 @@
     a_ones = head_grads(
         False, gk, came, gq, gq_peer, gathered, gathered_peer, tokens, tokens_peer
     )
-    a_diag_y, gains_came, *a_ones = fence(a_diag_y, gains_came, *a_ones)
+    a_diag_y, gq, *a_ones = fence(a_diag_y, gq, *a_ones)
+    a_diag_x, a_one_x = swap(a_ones[3], 2), swap(a_ones[1], 2)
+    gains_came = swap(gains, 2)
+    a_two_x = (up(a_twos[1]) + up(a_diag_y)).astype(BF)
+    first = mm(gq, wq, NN) + grad_first
+    a_two_x, a_diag_x, first = fence(a_two_x, a_diag_x, first)
+    a_one_y = (up(a_ones[2]) + up(a_diag_x)).astype(BF)
+    a_two_x, a_one_y, ff_total = fence(a_two_x, a_one_y, ff_total)
+    a_two_x, a_one_y = swap(a_two_x, 2), swap(a_one_y, 4)
+    f_x, f_y = swap(ff_total, 2), swap(ff_total, 4)
+    a_two_x, a_one_y, a_one_x, a_two_y, gains_came = fence(
+        a_two_x, a_one_y, a_one_x, a_two_y, gains_came
+    )
     gains = gains + gains_came
-    gains_came = across(gains, 2)
-    a_diag_x, a_one_x = swap(a_ones[3], 2), swap(a_ones[1], 2)
-    a_two_x = (up(a_twos[1]) + up(a_diag_y)).astype(BF)
-    a_two_x, a_diag_x, gains_came = fence(a_two_x, a_diag_x, gains_came)
+    gains_came = swap(gains, 4)
+    vo_mine = plane.higher((up(a_twos[0]) + up(a_two_x) + up(a_two_y)).astype(BF))
+    qk_mine = plane.higher((up(a_ones[0]) + up(a_one_x) + up(a_one_y)).astype(BF))
+    qk_mine, vo_mine = qk_mine.reshape(4, 2 * qp, width), vo_mine.reshape(4, 2 * qp, width)
+    a_mine = fence(*[jnp.concatenate([qk_mine[j], vo_mine[j]]) for j in range(4)])
+    a_came = [across(a_mine[j], j) for j in (1, 2, 3)]
+    f_core = [swap(ff_total, 1)]
+    f_d1, f_d2 = swap(f_y[:fp], 2), swap(f_x[fp:], 4)
+    f_core += [swap(f_x, 1), swap(f_y, 1)]
+    *a_came, f_d1, f_d2, b0, b1, b2, gains_came = fence(*a_came, f_d1, f_d2, *f_core, gains_came)
+    f_core = [b0, b1, b2]
     gains = gains + gains_came
     bit = 8
     while bit < seq_size:
         gains = gains + swap(gains, bit)
         bit *= 2
-    a_two_x = swap(a_two_x, 2)
-    a_one_y = swap((up(a_ones[2]) + up(a_diag_x)).astype(BF), 4)
-    ff_total, part = fence(ff_total.astype(BF), part)
-    lower_sum = line_sum(part)
-    a_two_x, a_one_y, a_one_x, a_two_y = fence(a_two_x, a_one_y, a_one_x, a_two_y)
-    vo_mine = plane.higher((up(a_twos[0]) + up(a_two_x) + up(a_two_y)).astype(BF))
-    qk_mine = plane.higher((up(a_ones[0]) + up(a_one_x) + up(a_one_y)).astype(BF))
-    qk_mine, vo_mine = qk_mine.reshape(4, 2 * qp, width), vo_mine.reshape(4, 2 * qp, width)
-    a_mine = fence(*[jnp.concatenate([qk_mine[j], vo_mine[j]]) for j in range(4)])
-    a_came = [across(a_mine[j], j) for j in (1, 2, 3)]
-    f_x, f_y = swap(ff_total, 2), swap(ff_total, 4)
-    f_core = [swap(ff_total, 1)]
-    f_x, f_y, *f_core = fence(f_x, f_y, *f_core)
-    f_d1, f_d2 = swap(f_y[:fp], 2), swap(f_x[fp:], 4)
-    f_core += [swap(f_x, 1), swap(f_y, 1)]
-    a_came = fence(*a_came)
     a_total = fence(sum((up(a) for a in a_came), up(a_mine[0])).astype(BF))[0]
     a_four = [a_total, swap(a_total, 2), swap(a_total, 4), swap(a_total, 6)]
     a_core = [swap(a_total, 1)]
@@ -676,16 +719,13 @@
         part = f_core if i & 1 else f_four
         ups.append((part[i >> 1], 0))
         downs.append((part[i >> 1], 1) if i < 6 else (part[4], 0))
-    plain = lambda i: i
-    grad_up = placed(ups, 1, fp, plain, s8, True)
-    grad_down = placed(downs, 1, fp, plain, s8, False)
-    grad_up, grad_down, *a_four = fence(grad_up, grad_down, *a_four)
+    grad_up = placed(ups, fp, s8, True)
+    grad_down = placed(downs, fp, s8, False)
+    tokens_grad = (first + up(jnp.concatenate([upper_sum, lower_sum]))).astype(BF)
+    grad_up, grad_down, tokens_grad, *a_four = fence(grad_up, grad_down, tokens_grad, *a_four)
     a_core += [swap(a, 1) for a in a_four[1:]]
     a_all = [(a_core if i & 1 else a_four)[i >> 1] for i in range(8)]
-    grad_qkv = placed([(a, 0) for a in a_all], 3, qp, reverse, s8, True)
-    grad_out = placed([(a, 3) for a in a_all], 1, qp, reverse, s8, False)
-
-    tokens_grad = (first + up(jnp.concatenate([upper_sum, lower_sum]))).astype(BF)
+    grad_qkv, grad_out = heads_placed(a_all, s8)
     return (
         mixed,
         tokens_grad,

time: 548 us -> 518 us (0.945)
  the two profiles are of different devices: /device:TPU:25 before, /device:TPU:9 now
where the time goes in v3:
time: 518 us; the launch traced here: 509 us
  Pallas kernels  156 us (30%)
  waiting for transfers between devices  114 us (22%)
  starting transfers between devices  80.6 us (16%)
  matrix products  60 us (12%)
  local copies, waits for them, and re-layouts  42.9 us (8%)
  other arithmetic  33.6 us (6%)
  between operations  21.4 us (4%)
    pallas_call x2, Pallas kernels, attention_backward(): pl.pallas_call(backward_kernel, grid=(pairs,), in_specs=[by_pair, pl.Bloc...  72.9 us
    ppermute x64, waiting for transfers between devices, swap(): return lax.ppermute(array, 'seq', [(i, i ^ bit) for i in range(self.size)])  63.1 us
    ppermute x64, starting transfers between devices, swap(): return lax.ppermute(array, 'seq', [(i, i ^ bit) for i in range(self.size)])  62.8 us
    dot_general x14, matrix products, mm(): return lax.dot_general(a, b, dims, preferred_element_type=F32).astype(out)  60 us
    ppermute x13, waiting for transfers between devices, along(): return lax.ppermute(array, 'tp', pairs)  50.8 us
    pallas_call x4, Pallas kernels, attention_forward(): pl.pallas_call(functools.partial(forward_kernel, len(kvs)), grid=(count,)...  31.3 us
    unnamed x128, local copies, waits for them, and re-layouts  24.6 us
    pallas_call x2, Pallas kernels, head_grads(): pl.pallas_call(functools.partial(head_grads_kernel, first), grid=(core //...  21.8 us
  transfers between devices with their start and end apart: 82, of which 25 were waited for; matrix products, arithmetic and copies ran while one was open for 19% of the time, Pallas kernels for 30%

profile of v3, /device:TPU:9, one launch (start us, length us, event | category | flops | bytes accessed | tf_op | source)
XLA Modules:
  0.0 508.7 jit_solution(8676613858734895682)
XLA Ops:
  12.5 2.5 collective-permute-start.1
  21.6 2.9 collective-permute-done
  24.5 5.0 collective-permute-done.1
  29.6 22.5 %collective-permute-done.2 = bf16[128,1024]{1,0:T(8,128)(2,1)S(1)} collective-permute-done((bf16[128,1024]{1,0:T(8,128)(2,1)S(1)}, bf16[128,1024]{1,0:T(8,128)(2,1)S(1)}, u32[]{:S(2)}, u32[]{:S(2)}) %collective-permute-start.2) | collective-permute-done | bytes 262176 | tf_op jit(solution)/shard_map/ppermute | solution.py:31
  56.8 9.4 %collective-permute-done.3 = bf16[384,1024]{1,0:T(8,128)(2,1)} collective-permute-done((bf16[384,1024]{1,0:T(8,128)(2,1)}, bf16[384,1024]{1,0:T(8,128)(2,1)}, u32[]{:S(2)}, u32[]{:S(2)}) %collective-permute-start.3) | collective-permute-done | bytes 786464 | tf_op jit(solution)/shard_map/ppermute | solution.py:43
  67.0 8.7 %collective-permute-start.7 = (bf16[384,1024]{1,0:T(8,128)(2,1)}, bf16[384,1024]{1,0:T(8,128)(2,1)}, u32[]{:S(2)}, u32[]{:S(2)}) collective-permute-start(bf16[384,1024]{1,0:T(8,128)(2,1)} %constant_dynamic-update-slice_fusion), channel_id=1, source_target_pairs={{0,4},{4,0},{8,12},{12,8},{16,20},{20,16},{24,28},{28,24},{1,5},{5... | collective-permute-start | bytes 2359304 | tf_op jit(solution)/shard_map/ppermute | solution.py:43
  89.1 4.9 collective-permute-done.5
  108.4 2.5 copy.44
  110.8 9.4 %convert_bitcast_fusion.refs_0_.refs_2_.k_ref.v_ref = bf16[1024,2048]{1,0:T(8,128)(2,1)} fusion(bf16[2048,1024]{1,0:T(8,128)(2,1)} %bitcast.121, bf16[1024,1024]{1,0:T(8,128)(2,1)} %all-gather.3.cloned.1.call-done.rows_ref), kind=kOutput, calls=%fused_computation.20 | convolution fusion | flops 4297064448 | bytes 10485760 | tf_op jit(solution)/shard_map/dot_general | solution.py:27
  121.5 3.6 collective-permute-start.14
  125.1 9.4 %convolution_convert_fusion.refs_1_.refs_3_.k_ref.v_ref = bf16[1024,2048]{1,0:T(8,128)(2,1)} fusion(bf16[1024,1024]{1,0:T(8,128)(2,1)} %all-gather.5.cloned.1.call-done.rows_two_ref, bf16[2048,1024]{1,0:T(8,128)(2,1)} %bitcast.122), kind=kOutput, calls=%fused_computation.21 | convolution fusion | flops 4297064448 | bytes 10485760 | tf_op jit(solution)/shard_map/dot_general | solution.py:27
  136.2 3.8 collective-permute-start.15
  148.6 7.7 %attention_forward.4 = (bf16[512,1024]{1,0:T(8,128)(2,1)S(1)}, f32[8,2,512]{2,1,0:T(2,128)S(1)}) custom-call(bf16[512,1024]{1,0:T(8,128)(2,1)S(1)} %fusion.7.q_ref, bf16[1024,2048]{1,0:T(8,128)(2,1)S(1)} %copy-done.2, bf16[1024,2048]{1,0:T(8,128)(2,1)S(1)} %copy-done, bf16[1024,2048]{1,0:T(8,128)(2,1)S(1)} %copy-done.2, bf16[1024,2048]{1,0:T(8,128)(2,1)S(1)} %copy-done, ...), custom_call_target="tpu_custom_call" | custom-call | flops 1000000000 | bytes 1000000 | tf_op jit(solution)/shard_map/attention_forward/pallas_call | solution.py:94
  164.1 7.8 %attention_forward.5 = (bf16[512,1024]{1,0:T(8,128)(2,1)S(1)}, f32[8,2,512]{2,1,0:T(2,128)S(1)}) custom-call(bf16[512,1024]{1,0:T(8,128)(2,1)S(1)} %fusion.7.q_ref, bf16[1024,2048]{1,0:T(8,128)(2,1)S(1)} %copy-done.2, bf16[1024,2048]{1,0:T(8,128)(2,1)S(1)} %copy-done, ...), custom_call_target="tpu_custom_call", output_to_operand_aliasing={{0}: (6, {}), {1}: (7, {})} | custom-call | flops 1000000000 | bytes 1000000 | tf_op jit(solution)/shard_map/attention_forward/pallas_call | solution.py:94
  171.9 4.1 collective-permute-done.20.refs_5_
  182.8 7.8 %attention_forward.6 = (bf16[512,1024]{1,0:T(8,128)(2,1)S(1)}, f32[8,2,512]{2,1,0:T(2,128)S(1)}) custom-call(bf16[512,1024]{1,0:T(8,128)(2,1)S(1)} %fusion.7.q_ref, bf16[1024,2048]{1,0:T(8,128)(2,1)S(1)} %copy-done.3, bf16[1024,2048]{1,0:T(8,128)(2,1)S(1)} %copy-done.1, ...), custom_call_target="tpu_custom_call", output_to_operand_aliasing={{0}: (6, {}), {1}: (7, {})} | custom-call | flops 1000000000 | bytes 1000000 | tf_op jit(solution)/shard_map/attention_forward/pallas_call | solution.py:94
  190.6 3.2 collective-permute-done.24.refs_3_
  195.5 8.0 %attention_forward.7 = (bf16[512,1024]{1,0:T(8,128)(2,1)S(1)}, f32[8,2,512]{2,1,0:T(2,128)S(1)}) custom-call(bf16[512,1024]{1,0:T(8,128)(2,1)S(1)} %fusion.7.q_ref, bf16[1024,2048]{1,0:T(8,128)(2,1)S(1)} %copy-done.3, bf16[1024,2048]{1,0:T(8,128)(2,1)S(1)} %copy-done.1, ...), custom_call_target="tpu_custom_call", output_to_operand_aliasing={{0}: (6, {}), {1}: (7, {})} | custom-call | flops 1000000000 | bytes 1000000 | tf_op jit(solution)/shard_map/attention_forward/pallas_call | solution.py:94
  205.9 5.5 %collective-permute-start.30 = (bf16[512,1024]{1,0:T(8,128)(2,1)S(1)}, bf16[512,1024]{1,0:T(8,128)(2,1)S(1)}, u32[]{:S(2)}, u32[]{:S(2)}) collective-permute-start(bf16[512,1024]{1,0:T(8,128)(2,1)S(1)} %multiply_convert_fusion.5.right_ref), channel_id=1, source_target_pairs={{0,4},{4,0},{8,12},{12,8},{16,20},{20,16},{24,28},{28,24},{1,5},{5... | collective-permute-start | bytes 3145736 | tf_op jit(solution)/shard_map/ppermute | solution.py:43
  213.7 6.5 %multiply_convert_fusion.2 = (bf16[512,2048]{1,0:T(8,128)(2,1)S(1)}, f32[512,2048]{1,0:T(8,128)}) fusion(bf16[512,1024]{1,0:T(8,128)(2,1)S(1)} %collective-permute-done.30.right_two_ref, bf16[2048,1024]{1,0:T(8,128)(2,1)S(1)} %get-tuple-element.242), kind=kOutput, calls=%fused_computation.14 | convolution fusion | flops 2169503744 | bytes 11534336 | tf_op jit(solution)/shard_map/dot_general | solution.py:27
  220.2 2.3 convolution_convert_fusion.4
  223.0 6.9 %multiply_convert_fusion.3 = (bf16[512,2048]{1,0:T(8,128)(2,1)S(1)}, f32[512,2048]{1,0:T(8,128)}) fusion(bf16[512,1024]{1,0:T(8,128)(2,1)S(1)} %multiply_convert_fusion.5.right_ref, bf16[2048,1024]{1,0:T(8,128)(2,1)S(1)} %get-tuple-element.242), kind=kOutput, calls=%fused_computation.17 | convolution fusion | flops 2169503744 | bytes 11534336 | tf_op jit(solution)/shard_map/dot_general | solution.py:27
  229.8 2.6 fusion.42
  238.0 5.3 %multiply_convert_fusion.left_two_ref = bf16[512,2048]{1,0:T(8,128)(2,1)S(1)} fusion(bf16[512,1024]{1,0:T(8,128)(2,1)S(1)} %collective-permute-done.32.right_two_ref, bf16[2048,1024]{1,0:T(8,128)(2,1)S(1)} %get-tuple-element.243, f32[512,2048]{1,0:T(8,128)S(1)} %copy-done.58), kind=kOutput, calls=%fused_computation.10 | convolution fusion | flops 2174746624 | bytes 11534336 | tf_op jit(solution)/shard_map/dot_general | solution.py:27
  243.3 3.3 convolution_convert_fusion.3
  246.8 5.5 %multiply_convert_fusion.1.left_ref = bf16[512,2048]{1,0:T(8,128)(2,1)S(1)} fusion(bf16[512,1024]{1,0:T(8,128)(2,1)S(1)} %fusion.32.right_ref, bf16[2048,1024]{1,0:T(8,128)(2,1)S(1)} %get-tuple-element.243, f32[512,2048]{1,0:T(8,128)S(1)} %copy-done.59), kind=kOutput, calls=%fused_computation.12 | convolution fusion | flops 2174746624 | bytes 11534336 | tf_op jit(solution)/shard_map/dot_general | solution.py:27
  252.3 2.3 fusion.43
  254.6 5.9 %outer_four.2 = (bf16[512,1024]{1,0:T(8,128)(2,1)S(1)}, bf16[512,1024]{1,0:T(8,128)(2,1)S(1)}, bf16[512,1024]{1,0:T(8,128)(2,1)S(1)}, bf16[512,1024]{1,0:T(8,128)(2,1)S(1)}) custom-call(bf16[512,2048]{1,0:T(8,128)(2,1)S(1)} %get-tuple-element.406.left_ref, bf16[512,1024]{1,0:T(8,128)(2,1)S(1)} %fusion.32.right_ref, ...), custom_call_target="tpu_custom_call" | custom-call | flops 1000000000 | bytes 1000000 | tf_op jit(solution)/shard_map/outer_four/pallas_call | solution.py:375
  260.6 3.0 multiply_reduce_fusion
  265.9 5.9 %outer_four.3 = (bf16[512,1024]{1,0:T(8,128)(2,1)S(1)}, bf16[512,1024]{1,0:T(8,128)(2,1)S(1)}, bf16[512,1024]{1,0:T(8,128)(2,1)S(1)}, bf16[512,1024]{1,0:T(8,128)(2,1)S(1)}) custom-call(bf16[512,2048]{1,0:T(8,128)(2,1)S(1)} %multiply_convert_fusion.1.left_ref, bf16[512,1024]{1,0:T(8,128)(2,1)S(1)} %multiply_convert_fusion.5.right_ref, ...), custom_call_target="tpu_custom_call" | custom-call | flops 1000000000 | bytes 1000000 | tf_op jit(solution)/shard_map/outer_four/pallas_call | solution.py:375
  278.2 36.5 %attention_backward.2 = (f32[512,1024]{1,0:T(8,128)S(1)}, bf16[2048,512]{1,0:T(8,128)(2,1)}, bf16[2048,512]{1,0:T(8,128)(2,1)}, bf16[2,1024,512]{2,1,0:T(8,128)(2,1)}, bf16[1024,1024]{1,0:T(8,128)(2,1)}) custom-call(bf16[512,1024]{1,0:T(8,128)(2,1)S(1)} %fusion.7.q_ref, bf16[1024,2048]{1,0:T(8,128)(2,1)} %convert_bitcast_fusion.refs_0_.refs_2_.k_ref.v_ref, ...), custom_call_target="tpu_custom_call" | custom-call | flops 1000000000 | bytes 1000000 | tf_op jit(solution)/shard_map/attention_backward/pallas_call | solution.py:202
  316.1 2.8 collective-permute-done.36.refs_1_
  326.8 36.4 %attention_backward.3 = (bf16[512,1024]{1,0:T(8,128)(2,1)S(1)}, bf16[2048,512]{1,0:T(8,128)(2,1)}, bf16[2048,512]{1,0:T(8,128)(2,1)}, bf16[2,1024,512]{2,1,0:T(8,128)(2,1)}, bf16[1024,1024]{1,0:T(8,128)(2,1)}) custom-call(bf16[512,1024]{1,0:T(8,128)(2,1)S(1)} %fusion.7.q_ref, ...), custom_call_target="tpu_custom_call", output_to_operand_aliasing={{1}: (9, {}), {2}: (10, {})} | custom-call | flops 1000000000 | bytes 1000000 | tf_op jit(solution)/shard_map/attention_backward/pallas_call | solution.py:202
  364.2 4.8 totals.1
  371.2 3.3 collective-permute-done.49
  378.9 10.9 %head_grads.2 = (bf16[256,1024]{1,0:T(8,128)(2,1)S(1)}, bf16[256,1024]{1,0:T(8,128)(2,1)S(1)}, bf16[256,1024]{1,0:T(8,128)(2,1)S(1)}, bf16[256,1024]{1,0:T(8,128)(2,1)}) custom-call(bf16[2048,512]{1,0:T(8,128)(2,1)} %get-tuple-element.285.big_ref, bf16[2,1024,512]{2,1,0:T(8,128)(2,1)} %collective-permute-done.45.came_ref, bf16[2,1024,512]{2,1,0:T(8,128)(2,1)} %copy-done.37, ...), custom_call_target="tpu_custom_call" | custom-call | flops 1000000000 | bytes 1000000 | tf_op jit(solution)/shard_map/head_grads/pallas_call | solution.py:276
  394.9 10.8 %head_grads.3 = (bf16[256,1024]{1,0:T(8,128)(2,1)S(1)}, bf16[256,1024]{1,0:T(8,128)(2,1)}, bf16[256,1024]{1,0:T(8,128)(2,1)S(1)}, bf16[256,1024]{1,0:T(8,128)(2,1)S(1)}) custom-call(bf16[2048,512]{1,0:T(8,128)(2,1)} %get-tuple-element.297.big_ref, bf16[2,1024,512]{2,1,0:T(8,128)(2,1)} %collective-permute-done.45.came_ref, bf16[2,1024,512]{2,1,0:T(8,128)(2,1)} %copy-done.37, ...), custom_call_target="tpu_custom_call" | custom-call | flops 1000000000 | bytes 1000000 | tf_op jit(solution)/shard_map/head_grads/pallas_call | solution.py:276
  408.5 2.6 convolution_add_fusion
  411.1 6.2 %collective-permute-done.51 = bf16[256,1024]{1,0:T(8,128)(2,1)S(1)} collective-permute-done((bf16[256,1024]{1,0:T(8,128)(2,1)S(1)}, bf16[256,1024]{1,0:T(8,128)(2,1)S(1)}, u32[]{:S(2)}, u32[]{:S(2)}) %collective-permute-start.51) | collective-permute-done | bytes 524320 | tf_op jit(solution)/shard_map/ppermute | solution.py:43
  420.3 19.7 %collective-permute-done.56 = f32[2,1024]{1,0:T(2,128)S(1)} collective-permute-done((f32[2,1024]{1,0:T(2,128)S(1)}, f32[2,1024]{1,0:T(2,128)S(1)}, u32[]{:S(2)}, u32[]{:S(2)}) %collective-permute-start.56) | collective-permute-done | bytes 8224 | tf_op jit(solution)/shard_map/ppermute | solution.py:43
  441.6 3.3 collective-permute-start.64
  451.2 3.8 collective-permute-start.65
  458.2 8.0 %collective-permute-done.57 = bf16[128,1024]{1,0:T(8,128)(2,1)S(1)} collective-permute-done((bf16[128,1024]{1,0:T(8,128)(2,1)S(1)}, bf16[128,1024]{1,0:T(8,128)(2,1)S(1)}, u32[]{:S(2)}, u32[]{:S(2)}) %collective-permute-start.57) | collective-permute-done | bytes 262176 | tf_op jit(solution)/shard_map/ppermute | solution.py:31
  470.6 8.6 %collective-permute-done.59 = bf16[128,1024]{1,0:T(8,128)(2,1)S(1)} collective-permute-done((bf16[128,1024]{1,0:T(8,128)(2,1)S(1)}, bf16[128,1024]{1,0:T(8,128)(2,1)S(1)}, u32[]{:S(2)}, u32[]{:S(2)}) %collective-permute-start.59) | collective-permute-done | bytes 262176 | tf_op jit(solution)/shard_map/ppermute | solution.py:31
  483.5 3.2 add_convert_fusion.2
  487.2 3.5 placed.2
  490.7 3.3 placed.3
  497.3 4.5 heads_placed.1
  (359 shorter events, 137.0 us)
Async XLA Ops:
  7.2 103.7 %all-gather.3.cloned.1.call-start = ((), (), s32[]{:S(2)}) async-start(), calls=%async_computation.3 | async-start | bytes 2621440 | tf_op jit(solution)/shard_map/all_gather | solution.py:511
  9.5 110.8 %all-gather.5.cloned.1.call-start = ((), (), s32[]{:S(2)}) async-start(), calls=%async_computation.4 | async-start | bytes 2621440 | tf_op jit(solution)/shard_map/all_gather | solution.py:511
  12.5 17.1 %collective-permute-start.1 = (bf16[128,1024]{1,0:T(8,128)(2,1)S(1)}, bf16[128,1024]{1,0:T(8,128)(2,1)S(1)}, u32[]{:S(2)}, u32[]{:S(2)}) collective-permute-start(bf16[128,1024]{1,0:T(8,128)(2,1)S(1)} %bitcast.143), channel_id=1, source_target_pairs={{0,2},{1,3},{2,0},{3,1},{4,6},{5,7},{6,4},{7,5},{8,10},{9,11},{10,... | collective-permute-start | bytes 786440 | tf_op jit(solution)/shard_map/ppermute | solution.py:31
  14.9 37.2 %collective-permute-start.2 = (bf16[128,1024]{1,0:T(8,128)(2,1)S(1)}, bf16[128,1024]{1,0:T(8,128)(2,1)S(1)}, u32[]{:S(2)}, u32[]{:S(2)}) collective-permute-start(bf16[128,1024]{1,0:T(8,128)(2,1)S(1)} %bitcast.144), channel_id=1, source_target_pairs={{0,3},{1,2},{2,1},{3,0},{4,7},{5,6},{6,5},{7,4},{8,11},{9,10},{10,... | collective-permute-start | bytes 786440 | tf_op jit(solution)/shard_map/ppermute | solution.py:31
  56.7 312.4 %reduce-scatter.4.cloned.1.call-start = ((), (), s32[]{:S(2)}) async-start(), calls=%async_computation.5 | async-start | bytes 2621440 | tf_op jit(solution)/shard_map/reduce_scatter | solution.py:642
  67.0 27.8 %collective-permute-start.7 = (bf16[384,1024]{1,0:T(8,128)(2,1)}, bf16[384,1024]{1,0:T(8,128)(2,1)}, u32[]{:S(2)}, u32[]{:S(2)}) collective-permute-start(bf16[384,1024]{1,0:T(8,128)(2,1)} %constant_dynamic-update-slice_fusion), channel_id=1, source_target_pairs={{0,4},{4,0},{8,12},{12,8},{16,20},{20,16},{24,28},{28,24},{1,5},{5... | collective-permute-start | bytes 2359304 | tf_op jit(solution)/shard_map/ppermute | solution.py:43
  75.7 19.1 %collective-permute-start.8 = (bf16[384,1024]{1,0:T(8,128)(2,1)}, bf16[384,1024]{1,0:T(8,128)(2,1)}, u32[]{:S(2)}, u32[]{:S(2)}) collective-permute-start(bf16[384,1024]{1,0:T(8,128)(2,1)} %collective-permute-done.3), channel_id=1, source_target_pairs={{0,4},{4,0},{8,12},{12,8},{16,20},{20,16},{24,28},{28,24},{1,5},{5... | collective-permute-start | bytes 2359304 | tf_op jit(solution)/shard_map/ppermute | solution.py:43
  75.7 19.1 %collective-permute-start.9 = (bf16[384,1024]{1,0:T(8,128)(2,1)}, bf16[384,1024]{1,0:T(8,128)(2,1)}, u32[]{:S(2)}, u32[]{:S(2)}) collective-permute-start(bf16[384,1024]{1,0:T(8,128)(2,1)} %collective-permute-done.4), channel_id=1, source_target_pairs={{0,4},{4,0},{8,12},{12,8},{16,20},{20,16},{24,28},{28,24},{1,5},{5... | collective-permute-start | bytes 2359304 | tf_op jit(solution)/shard_map/ppermute | solution.py:43
  94.0 26.3 %collective-permute-start.12 = (bf16[512,1024]{1,0:T(8,128)(2,1)S(1)}, bf16[512,1024]{1,0:T(8,128)(2,1)S(1)}, u32[]{:S(2)}, u32[]{:S(2)}) collective-permute-start(bf16[512,1024]{1,0:T(8,128)(2,1)S(1)} %copy-done.4), channel_id=1, source_target_pairs={{0,4},{4,0},{8,12},{12,8},{16,20},{20,16},{24,28},{28,24},{1,5},{5... | collective-permute-start | bytes 3145736 | tf_op jit(solution)/shard_map/ppermute | solution.py:43
  120.3 14.2 %collective-permute-start.13 = (bf16[256,1024]{1,0:T(8,128)(2,1)}, bf16[256,1024]{1,0:T(8,128)(2,1)}, u32[]{:S(2)}, u32[]{:S(2)}) collective-permute-start(bf16[256,1024]{1,0:T(8,128)(2,1)} %pad_maximum_fusion.4), channel_id=1, source_target_pairs={{0,1},{1,0},{2,3},{3,2},{4,5},{5,4},{6,7},{7,6},{8,9},{9,8},{10,11... | collective-permute-start | bytes 1572872 | tf_op jit(solution)/shard_map/ppermute | solution.py:31
  121.5 14.7 %collective-permute-start.14 = (bf16[256,1024]{1,0:T(8,128)(2,1)}, bf16[256,1024]{1,0:T(8,128)(2,1)}, u32[]{:S(2)}, u32[]{:S(2)}) collective-permute-start(bf16[256,1024]{1,0:T(8,128)(2,1)} %pad_maximum_fusion.4), channel_id=1, source_target_pairs={{1,2},{2,1},{5,6},{6,5},{9,10},{10,9},{13,14},{14,13},{17,18},{18,... | collective-permute-start | bytes 1572872 | tf_op jit(solution)/shard_map/ppermute | solution.py:31
  136.2 20.2 %collective-permute-start.15 = (bf16[256,1024]{1,0:T(8,128)(2,1)}, bf16[256,1024]{1,0:T(8,128)(2,1)}, u32[]{:S(2)}, u32[]{:S(2)}) collective-permute-start(bf16[256,1024]{1,0:T(8,128)(2,1)} %collective-permute-done.13.refs_2_), channel_id=1, source_target_pairs={{1,2},{2,1},{5,6},{6,5},{9,10},{10,9},{13,14},{14,13},{17,18},{18,... | collective-permute-start | bytes 1572872 | tf_op jit(solution)/shard_map/ppermute | solution.py:31
  140.0 16.4 %collective-permute-start.16 = (bf16[256,1024]{1,0:T(8,128)(2,1)}, bf16[256,1024]{1,0:T(8,128)(2,1)}, u32[]{:S(2)}, u32[]{:S(2)}) collective-permute-start(bf16[256,1024]{1,0:T(8,128)(2,1)} %collective-permute-done.14), channel_id=1, source_target_pairs={{1,0},{2,3},{5,4},{6,7},{9,8},{10,11},{13,12},{14,15},{17,16},{18,... | collective-permute-start | bytes 1572872 | tf_op jit(solution)/shard_map/ppermute | solution.py:31
  142.1 14.3 %collective-permute-start.17 = (bf16[256,1024]{1,0:T(8,128)(2,1)}, bf16[256,1024]{1,0:T(8,128)(2,1)}, u32[]{:S(2)}, u32[]{:S(2)}) collective-permute-start(bf16[256,1024]{1,0:T(8,128)(2,1)} %collective-permute-done.13.refs_2_), channel_id=1, source_target_pairs={{0,8},{4,12},{8,0},{12,4},{16,24},{20,28},{24,16},{28,20},{1,9},{5... | collective-permute-start | bytes 1572872 | tf_op jit(solution)/shard_map/ppermute | solution.py:43
  156.4 20.3 %collective-permute-start.19 = (bf16[256,1024]{1,0:T(8,128)(2,1)}, bf16[256,1024]{1,0:T(8,128)(2,1)S(1)}, u32[]{:S(2)}, u32[]{:S(2)}) collective-permute-start(bf16[256,1024]{1,0:T(8,128)(2,1)} %collective-permute-done.15), channel_id=1, source_target_pairs={{1,0},{2,3},{5,4},{6,7},{9,8},{10,11},{13,12},{14,15},{17,16},{18,... | collective-permute-start | bytes 1572872 | tf_op jit(solution)/shard_map/ppermute | solution.py:31
  159.0 17.6 %collective-permute-start.22 = (bf16[256,1024]{1,0:T(8,128)(2,1)S(1)}, bf16[256,1024]{1,0:T(8,128)(2,1)S(1)}, u32[]{:S(2)}, u32[]{:S(2)}) collective-permute-start(bf16[256,1024]{1,0:T(8,128)(2,1)S(1)} %broadcast_select_fusion.1.refs_0_), channel_id=1, source_target_pairs={{0,8},{4,12},{8,0},{12,4},{16,24},{20,28},{24,16},{28,20},{1,9},{5... | collective-permute-start | bytes 1572872 | tf_op jit(solution)/shard_map/ppermute | solution.py:43
  159.8 16.9 %collective-permute-start.23 = (bf16[256,1024]{1,0:T(8,128)(2,1)S(1)}, bf16[256,1024]{1,0:T(8,128)(2,1)S(1)}, u32[]{:S(2)}, u32[]{:S(2)}) collective-permute-start(bf16[256,1024]{1,0:T(8,128)(2,1)S(1)} %broadcast_select_fusion.1.refs_0_), channel_id=1, source_target_pairs={{0,16},{4,20},{8,24},{12,28},{16,0},{20,4},{24,8},{28,12},{1,17},{... | collective-permute-start | bytes 1572872 | tf_op jit(solution)/shard_map/ppermute | solution.py:43
  160.8 15.2 %collective-permute-start.20 = (bf16[128,1024]{1,0:T(8,128)(2,1)S(1)}, bf16[128,1024]{1,0:T(8,128)(2,1)S(1)}, u32[]{:S(2)}, u32[]{:S(2)}) collective-permute-start(bf16[128,1024]{1,0:T(8,128)(2,1)S(1)} %slice.127), channel_id=1, source_target_pairs={{0,8},{4,12},{8,0},{12,4},{16,24},{20,28},{24,16},{28,20},{1,9},{5... | collective-permute-start | bytes 786440 | tf_op jit(solution)/shard_map/ppermute | solution.py:43
  177.8 16.1 %collective-permute-start.26 = (bf16[256,1024]{1,0:T(8,128)(2,1)S(1)}, bf16[256,1024]{1,0:T(8,128)(2,1)S(1)}, u32[]{:S(2)}, u32[]{:S(2)}) collective-permute-start(bf16[256,1024]{1,0:T(8,128)(2,1)S(1)} %broadcast_select_fusion.refs_5_), channel_id=1, source_target_pairs={{0,8},{4,12},{8,0},{12,4},{16,24},{20,28},{24,16},{28,20},{1,9},{5... | collective-permute-start | bytes 1572872 | tf_op jit(solution)/shard_map/ppermute | solution.py:43
  178.4 15.4 %collective-permute-start.27 = (bf16[256,1024]{1,0:T(8,128)(2,1)S(1)}, bf16[256,1024]{1,0:T(8,128)(2,1)S(1)}, u32[]{:S(2)}, u32[]{:S(2)}) collective-permute-start(bf16[256,1024]{1,0:T(8,128)(2,1)S(1)} %broadcast_select_fusion.refs_5_), channel_id=1, source_target_pairs={{0,16},{4,20},{8,24},{12,28},{16,0},{20,4},{24,8},{28,12},{1,17},{... | collective-permute-start | bytes 1572872 | tf_op jit(solution)/shard_map/ppermute | solution.py:43
  178.4 15.4 %collective-permute-start.24 = (bf16[128,1024]{1,0:T(8,128)(2,1)S(1)}, bf16[128,1024]{1,0:T(8,128)(2,1)S(1)}, u32[]{:S(2)}, u32[]{:S(2)}) collective-permute-start(bf16[128,1024]{1,0:T(8,128)(2,1)S(1)} %slice.129), channel_id=1, source_target_pairs={{0,8},{4,12},{8,0},{12,4},{16,24},{20,28},{24,16},{28,20},{1,9},{5... | collective-permute-start | bytes 786440 | tf_op jit(solution)/shard_map/ppermute | solution.py:43
  179.4 14.4 %collective-permute-start.25 = (bf16[128,1024]{1,0:T(8,128)(2,1)S(1)}, bf16[128,1024]{1,0:T(8,128)(2,1)S(1)}, u32[]{:S(2)}, u32[]{:S(2)}) collective-permute-start(bf16[128,1024]{1,0:T(8,128)(2,1)S(1)} %slice.130), channel_id=1, source_target_pairs={{0,16},{4,20},{8,24},{12,28},{16,0},{20,4},{24,8},{28,12},{1,17},{... | collective-permute-start | bytes 786440 | tf_op jit(solution)/shard_map/ppermute | solution.py:43
  235.4 38.4 %collective-permute-start.41 = (bf16[1024,1024]{1,0:T(8,128)(2,1)}, bf16[1024,1024]{1,0:T(8,128)(2,1)}, u32[]{:S(2)}, u32[]{:S(2)}) collective-permute-start(bf16[1024,1024]{1,0:T(8,128)(2,1)} %all-gather.5.cloned.1.call-done.rows_two_ref), channel_id=1, source_target_pairs={{0,4},{4,0},{8,12},{12,8},{16,20},{20,16},{24,28},{28,24},{1,5},{5... | collective-permute-start | bytes 6291464 | tf_op jit(solution)/shard_map/ppermute | solution.py:43
  235.8 36.1 %collective-permute-start.40 = (bf16[1024,1024]{1,0:T(8,128)(2,1)}, bf16[1024,1024]{1,0:T(8,128)(2,1)}, u32[]{:S(2)}, u32[]{:S(2)}) collective-permute-start(bf16[1024,1024]{1,0:T(8,128)(2,1)} %all-gather.3.cloned.1.call-done.rows_ref), channel_id=1, source_target_pairs={{0,4},{4,0},{8,12},{12,8},{16,20},{20,16},{24,28},{28,24},{1,5},{5... | collective-permute-start | bytes 6291464 | tf_op jit(solution)/shard_map/ppermute | solution.py:43
  236.0 38.9 %collective-permute-start.39 = (bf16[512,512]{1,0:T(8,128)(2,1)S(1)}, bf16[512,512]{1,0:T(8,128)(2,1)S(1)}, u32[]{:S(2)}, u32[]{:S(2)}) collective-permute-start(bf16[512,512]{1,0:T(8,128)(2,1)S(1)} %slice.134), channel_id=1, source_target_pairs={{0,4},{4,0},{8,12},{12,8},{16,20},{20,16},{24,28},{28,24},{1,5},{5... | collective-permute-start | bytes 1572872 | tf_op jit(solution)/shard_map/ppermute | solution.py:43
  271.8 44.3 %collective-permute-start.34 = (bf16[512,1024]{1,0:T(8,128)(2,1)S(1)}, bf16[512,1024]{1,0:T(8,128)(2,1)S(1)}, u32[]{:S(2)}, u32[]{:S(2)}) collective-permute-start(bf16[512,1024]{1,0:T(8,128)(2,1)S(1)} %get-tuple-element.254), channel_id=1, source_target_pairs={{0,8},{4,12},{8,0},{12,4},{16,24},{20,28},{24,16},{28,20},{1,9},{5... | collective-permute-start | bytes 3145736 | tf_op jit(solution)/shard_map/ppermute | solution.py:43
  271.9 44.2 %collective-permute-start.35 = (bf16[512,1024]{1,0:T(8,128)(2,1)S(1)}, bf16[512,1024]{1,0:T(8,128)(2,1)S(1)}, u32[]{:S(2)}, u32[]{:S(2)}) collective-permute-start(bf16[512,1024]{1,0:T(8,128)(2,1)S(1)} %get-tuple-element.255), channel_id=1, source_target_pairs={{0,16},{4,20},{8,24},{12,28},{16,0},{20,4},{24,8},{28,12},{1,17},{... | collective-permute-start | bytes 3145736 | tf_op jit(solution)/shard_map/ppermute | solution.py:43
  273.8 45.2 %collective-permute-start.36 = (bf16[512,1024]{1,0:T(8,128)(2,1)S(1)}, bf16[512,1024]{1,0:T(8,128)(2,1)S(1)}, u32[]{:S(2)}, u32[]{:S(2)}) collective-permute-start(bf16[512,1024]{1,0:T(8,128)(2,1)S(1)} %get-tuple-element.256), channel_id=1, source_target_pairs={{0,8},{4,12},{8,0},{12,4},{16,24},{20,28},{24,16},{28,20},{1,9},{5... | collective-permute-start | bytes 3145736 | tf_op jit(solution)/shard_map/ppermute | solution.py:43
  275.6 43.8 %collective-permute-start.37 = (bf16[512,1024]{1,0:T(8,128)(2,1)S(1)}, bf16[512,1024]{1,0:T(8,128)(2,1)S(1)}, u32[]{:S(2)}, u32[]{:S(2)}) collective-permute-start(bf16[512,1024]{1,0:T(8,128)(2,1)S(1)} %get-tuple-element.257), channel_id=1, source_target_pairs={{0,16},{4,20},{8,24},{12,28},{16,0},{20,4},{24,8},{28,12},{1,17},{... | collective-permute-start | bytes 3145736 | tf_op jit(solution)/shard_map/ppermute | solution.py:43
  278.1 38.0 %collective-permute-start.42 = (f32[2,1024]{1,0:T(2,128)S(1)}, f32[2,1024]{1,0:T(2,128)S(1)}, u32[]{:S(2)}, u32[]{:S(2)}) collective-permute-start(f32[2,1024]{1,0:T(2,128)S(1)} %pad_maximum_fusion.9), channel_id=1, source_target_pairs={{0,1},{1,0},{2,3},{3,2},{4,5},{5,4},{6,7},{7,6},{8,9},{9,8},{10,11... | collective-permute-start | bytes 24584 | tf_op jit(solution)/shard_map/ppermute | solution.py:31
  321.0 97.3 %reduce-scatter.6.cloned.1.call-start = ((), (), s32[]{:S(2)}) async-start(), calls=%async_computation.6 | async-start | bytes 2621440 | tf_op jit(solution)/shard_map/reduce_scatter | solution.py:642
  321.1 43.2 %collective-permute-start.45 = (bf16[2,1024,512]{2,1,0:T(8,128)(2,1)}, bf16[2,1024,512]{2,1,0:T(8,128)(2,1)}, u32[]{:S(2)}, u32[]{:S(2)}) collective-permute-start(bf16[2,1024,512]{2,1,0:T(8,128)(2,1)} %get-tuple-element.275), channel_id=1, source_target_pairs={{0,4},{4,0},{8,12},{12,8},{16,20},{20,16},{24,28},{28,24},{1,5},{5... | collective-permute-start | bytes 6291464 | tf_op jit(solution)/shard_map/ppermute | solution.py:43
  324.5 39.8 %collective-permute-start.43 = (bf16[512,1024]{1,0:T(8,128)(2,1)S(1)}, bf16[512,1024]{1,0:T(8,128)(2,1)}, u32[]{:S(2)}, u32[]{:S(2)}) collective-permute-start(bf16[512,1024]{1,0:T(8,128)(2,1)S(1)} %add_convert_fusion.4), channel_id=1, source_target_pairs={{0,8},{4,12},{8,0},{12,4},{16,24},{20,28},{24,16},{28,20},{1,9},{5... | collective-permute-start | bytes 3145736 | tf_op jit(solution)/shard_map/ppermute | solution.py:43
  325.1 39.2 %collective-permute-start.44 = (bf16[512,1024]{1,0:T(8,128)(2,1)S(1)}, bf16[512,1024]{1,0:T(8,128)(2,1)}, u32[]{:S(2)}, u32[]{:S(2)}) collective-permute-start(bf16[512,1024]{1,0:T(8,128)(2,1)S(1)} %add_convert_fusion.3), channel_id=1, source_target_pairs={{0,16},{4,20},{8,24},{12,28},{16,0},{20,4},{24,8},{28,12},{1,17},{... | collective-permute-start | bytes 3145736 | tf_op jit(solution)/shard_map/ppermute | solution.py:43
  326.5 37.7 %collective-permute-start.46 = (f32[2,1024]{1,0:T(2,128)S(1)}, f32[2,1024]{1,0:T(2,128)S(1)}, u32[]{:S(2)}, u32[]{:S(2)}) collective-permute-start(f32[2,1024]{1,0:T(2,128)S(1)} %fusion.31), channel_id=1, source_target_pairs={{0,2},{1,3},{2,0},{3,1},{4,6},{5,7},{6,4},{7,5},{8,10},{9,11},{10,... | collective-permute-start | bytes 24584 | tf_op jit(solution)/shard_map/ppermute | solution.py:31
  369.2 114.4 %reduce-scatter.8.cloned.1.call-start = ((), (), s32[]{:S(2)}) async-start(), calls=%async_computation.7 | async-start | bytes 2621440 | tf_op jit(solution)/shard_map/reduce_scatter | solution.py:642
  392.7 47.8 %collective-permute-start.55 = (bf16[256,1024]{1,0:T(8,128)(2,1)}, bf16[256,1024]{1,0:T(8,128)(2,1)}, u32[]{:S(2)}, u32[]{:S(2)}) collective-permute-start(bf16[256,1024]{1,0:T(8,128)(2,1)} %copy-done.33), channel_id=1, source_target_pairs={{0,16},{4,20},{8,24},{12,28},{16,0},{20,4},{24,8},{28,12},{1,17},{... | collective-permute-start | bytes 1572872 | tf_op jit(solution)/shard_map/ppermute | solution.py:43
  406.7 34.8 %collective-permute-start.54 = (bf16[256,1024]{1,0:T(8,128)(2,1)}, bf16[256,1024]{1,0:T(8,128)(2,1)}, u32[]{:S(2)}, u32[]{:S(2)}) collective-permute-start(bf16[256,1024]{1,0:T(8,128)(2,1)} %get-tuple-element.322), channel_id=1, source_target_pairs={{0,8},{4,12},{8,0},{12,4},{16,24},{20,28},{24,16},{28,20},{1,9},{5... | collective-permute-start | bytes 1572872 | tf_op jit(solution)/shard_map/ppermute | solution.py:43
  418.3 26.5 %collective-permute-start.52 = (bf16[256,1024]{1,0:T(8,128)(2,1)S(1)}, bf16[256,1024]{1,0:T(8,128)(2,1)S(1)}, u32[]{:S(2)}, u32[]{:S(2)}) collective-permute-start(bf16[256,1024]{1,0:T(8,128)(2,1)S(1)} %add_convert_fusion.8), channel_id=1, source_target_pairs={{0,8},{4,12},{8,0},{12,4},{16,24},{20,28},{24,16},{28,20},{1,9},{5... | collective-permute-start | bytes 1572872 | tf_op jit(solution)/shard_map/ppermute | solution.py:43
  419.3 25.5 %collective-permute-start.53 = (bf16[256,1024]{1,0:T(8,128)(2,1)}, bf16[256,1024]{1,0:T(8,128)(2,1)S(1)}, u32[]{:S(2)}, u32[]{:S(2)}) collective-permute-start(bf16[256,1024]{1,0:T(8,128)(2,1)} %add_convert_fusion.7), channel_id=1, source_target_pairs={{0,16},{4,20},{8,24},{12,28},{16,0},{20,4},{24,8},{28,12},{1,17},{... | collective-permute-start | bytes 1572872 | tf_op jit(solution)/shard_map/ppermute | solution.py:43
  419.9 20.1 %collective-permute-start.56 = (f32[2,1024]{1,0:T(2,128)S(1)}, f32[2,1024]{1,0:T(2,128)S(1)}, u32[]{:S(2)}, u32[]{:S(2)}) collective-permute-start(f32[2,1024]{1,0:T(2,128)S(1)} %add.237), channel_id=1, source_target_pairs={{0,8},{4,12},{8,0},{12,4},{16,24},{20,28},{24,16},{28,20},{1,9},{5... | collective-permute-start | bytes 24584 | tf_op jit(solution)/shard_map/ppermute | solution.py:43
  440.0 15.1 %collective-permute-start.60 = (bf16[256,1024]{1,0:T(8,128)(2,1)}, bf16[256,1024]{1,0:T(8,128)(2,1)S(1)}, u32[]{:S(2)}, u32[]{:S(2)}) collective-permute-start(bf16[256,1024]{1,0:T(8,128)(2,1)} %reduce-scatter.6.cloned.1.call-done.refs_0_), channel_id=1, source_target_pairs={{0,16},{4,20},{8,24},{12,28},{16,0},{20,4},{24,8},{28,12},{1,17},{... | collective-permute-start | bytes 1572872 | tf_op jit(solution)/shard_map/ppermute | solution.py:43
  447.7 18.5 %collective-permute-start.57 = (bf16[128,1024]{1,0:T(8,128)(2,1)S(1)}, bf16[128,1024]{1,0:T(8,128)(2,1)S(1)}, u32[]{:S(2)}, u32[]{:S(2)}) collective-permute-start(bf16[128,1024]{1,0:T(8,128)(2,1)S(1)} %pad_maximum_fusion.6), channel_id=1, source_target_pairs={{0,1},{1,0},{2,3},{3,2},{4,5},{5,4},{6,7},{7,6},{8,9},{9,8},{10,11... | collective-permute-start | bytes 786440 | tf_op jit(solution)/shard_map/ppermute | solution.py:31
  449.2 20.2 %collective-permute-start.58 = (bf16[128,1024]{1,0:T(8,128)(2,1)S(1)}, bf16[128,1024]{1,0:T(8,128)(2,1)S(1)}, u32[]{:S(2)}, u32[]{:S(2)}) collective-permute-start(bf16[128,1024]{1,0:T(8,128)(2,1)S(1)} %pad_maximum_fusion.7), channel_id=1, source_target_pairs={{0,2},{1,3},{2,0},{3,1},{4,6},{5,7},{6,4},{7,5},{8,10},{9,11},{10,... | collective-permute-start | bytes 786440 | tf_op jit(solution)/shard_map/ppermute | solution.py:31
  451.2 28.0 %collective-permute-start.65 = (bf16[256,1024]{1,0:T(8,128)(2,1)S(1)}, bf16[256,1024]{1,0:T(8,128)(2,1)S(1)}, u32[]{:S(2)}, u32[]{:S(2)}) collective-permute-start(bf16[256,1024]{1,0:T(8,128)(2,1)S(1)} %collective-permute-done.62.refs_2_), channel_id=1, source_target_pairs={{0,4},{4,0},{8,12},{12,8},{16,20},{20,16},{24,28},{28,24},{1,5},{5... | collective-permute-start | bytes 1572872 | tf_op jit(solution)/shard_map/ppermute | solution.py:43
  455.0 24.2 %collective-permute-start.66 = (bf16[256,1024]{1,0:T(8,128)(2,1)S(1)}, bf16[256,1024]{1,0:T(8,128)(2,1)S(1)}, u32[]{:S(2)}, u32[]{:S(2)}) collective-permute-start(bf16[256,1024]{1,0:T(8,128)(2,1)S(1)} %collective-permute-done.60.refs_4_), channel_id=1, source_target_pairs={{0,4},{4,0},{8,12},{12,8},{16,20},{20,16},{24,28},{28,24},{1,5},{5... | collective-permute-start | bytes 1572872 | tf_op jit(solution)/shard_map/ppermute | solution.py:43
  458.0 21.2 %collective-permute-start.59 = (bf16[128,1024]{1,0:T(8,128)(2,1)S(1)}, bf16[128,1024]{1,0:T(8,128)(2,1)S(1)}, u32[]{:S(2)}, u32[]{:S(2)}) collective-permute-start(bf16[128,1024]{1,0:T(8,128)(2,1)S(1)} %pad_maximum_fusion.8), channel_id=1, source_target_pairs={{0,3},{1,2},{2,1},{3,0},{4,7},{5,6},{6,5},{7,4},{8,11},{9,10},{10,... | collective-permute-start | bytes 786440 | tf_op jit(solution)/shard_map/ppermute | solution.py:31
  479.4 14.6 %collective-permute-start.70 = (bf16[128,1024]{1,0:T(8,128)(2,1)S(1)}, bf16[128,1024]{1,0:T(8,128)(2,1)}, u32[]{:S(2)}, u32[]{:S(2)}) collective-permute-start(bf16[128,1024]{1,0:T(8,128)(2,1)S(1)} %add_convert_fusion.9.refs_0_), channel_id=1, source_target_pairs={{0,8},{4,12},{8,0},{12,4},{16,24},{20,28},{24,16},{28,20},{1,9},{5... | collective-permute-start | bytes 786440 | tf_op jit(solution)/shard_map/ppermute | solution.py:43
  (94 other events, 719.5 us)
Sparse Core Ops, SparseCore 0:
  10.1 61.5 all-gather.2
  73.3 46.0 all-gather.4
  321.1 40.7 reduce-scatter.3
  369.3 41.7 reduce-scatter.5
  413.2 46.5 reduce-scatter.7

commit v4 on v3

--- a/solution.py
+++ b/solution.py
@@ -21,6 +21,10 @@
 PAIR = [(0, 1), (1, 0), (2, 3), (3, 2)]
 MIDDLE = [(1, 2), (2, 1)]
 OUTWARD = [(1, 0), (2, 3)]
+
+
+def in_hbm(*arrays):
+    return [pltpu.with_memory_space_constraint(a, pltpu.HBM) for a in arrays]
 
 
 def mm(a, b, dims, out=F32):
@@ -226,7 +230,7 @@
         compiler_params=pltpu.CompilerParams(vmem_limit_bytes=48 * 2**20),
         cost_estimate=LIGHT,
         name="attention_backward",
-    )(q, kv, kv, go, attended, lse, bias, wkv, *(held or ()))
+    )(*in_hbm(q, kv, kv, go, attended), lse, bias, *in_hbm(wkv, *(held or ())))
 
 
 def gelu_tile(x):
@@ -242,48 +246,79 @@
     return (x * cdf).astype(BF), (cdf + x * (bell * 0.3989422804014327)).astype(BF)
 
 
-def head_grads_kernel(
-    first, big_ref, came_ref, came_two_ref, small_ref, small_peer_ref,
-    rows_ref, rows_two_ref, peer_ref, peer_two_ref, right_ref, right_peer_ref, *out_refs
-):
+def head_grads_kernel(many, *refs):
+    ins, (x_ref, y_ref, near_x_ref, near_y_ref, own_ref) = refs[:-5], refs[-5:]
+
     def outer(left, right):
-        return lax.dot_general(left, right[...], TN, preferred_element_type=F32)
-
-    keys = rows_ref.shape[0]
-    total = outer(big_ref[:keys, :], rows_ref) + outer(big_ref[keys:, :], rows_two_ref)
-    total += outer(came_ref[0], peer_ref) + outer(came_two_ref[0], peer_two_ref)
-    total = total.astype(BF)
-    other = outer(small_ref[...], right_ref) + outer(small_peer_ref[...], right_peer_ref)
-    kinds = [total, other.astype(BF)] if first else [other.astype(BF), total]
+        return lax.dot_general(left, right, TN, preferred_element_type=F32)
+
+    if many:
+        big_refs, came_refs, row_refs = ins[:2], ins[2:4], ins[4:]
+        keys = row_refs[0].shape[0]
+        totals_of = []
+        for kind in range(2):
+            total = 0.0
+            for n in range(2):
+                part = slice(n * keys, (n + 1) * keys)
+                total += outer(big_refs[kind][part, :], row_refs[n][...])
+                total += outer(came_refs[n][kind], row_refs[2 + n][...])
+            totals_of.append(total.astype(BF))
+    else:
+        totals_of = []
+        for kind in range(2):
+            left, left_peer, right, right_peer = [ref[...] for ref in ins[4 * kind : 4 * kind + 4]]
+            totals_of.append((outer(left, right) + outer(left_peer, right_peer)).astype(BF))
     size = HEAD // 2
-    for at in range(total.shape[0] // (4 * size)):
-        for kind in range(2):
-            for chunk in range(4):
-                source = (at * 4 + (chunk & 1) * 2 + (chunk >> 1)) * size
-                place = (at * 2 + kind) * size
-                out_refs[chunk][place : place + size, :] = kinds[kind][source : source + size, :]
-
-
-def head_grads(first, big, came, small, small_peer, rows, peer, right, right_peer):
-    keys, width = rows[0].shape
-    own = right.shape[0]
-    core = width // 2
-    wide = core // 2
-    which = 1 if first else 0
-    whole = lambda a: pl.BlockSpec(a.shape, lambda g: (0, 0), pipeline_mode=pl.Buffered(1))
-    columns = lambda n: pl.BlockSpec((n, wide), lambda g: (0, g))
-    arrived = pl.BlockSpec((1, keys, wide), lambda g: (which, 0, g))
+
+    def chunk(n):
+        rows = []
+        for at in range(totals_of[0].shape[0] // (4 * size)):
+            source = (at * 4 + (n & 1) * 2 + (n >> 1)) * size
+            rows += [total[source : source + size] for total in totals_of]
+        return jnp.concatenate(rows)
+
+    half = own_ref.shape[0]
+    own_ref[...] = chunk(0)
+
+    @pl.when(pl.program_id(0) == 0)
+    def _():
+        x_ref[:half, :] = chunk(3)
+        x_ref[half:, :] = chunk(1)
+        near_y_ref[...] = chunk(2)
+
+    @pl.when(pl.program_id(0) == 1)
+    def _():
+        y_ref[:half, :] = chunk(3)
+        y_ref[half:, :] = chunk(2)
+        near_x_ref[...] = chunk(1)
+
+
+def head_grads(columns, arrived, whole_arrays, many, order=None):
+    width = whole_arrays[0].shape[1]
+    wide = width // 4
+    half = wide // 2
+    by_column = [pl.BlockSpec((a.shape[0], wide), lambda g: (0, g)) for a in columns]
+    by_kind = [pl.BlockSpec((2, a.shape[1], wide), lambda g: (0, 0, g)) for a in arrived]
+    whole = [
+        pl.BlockSpec(a.shape, lambda g: (0, 0), pipeline_mode=pl.Buffered(1))
+        for a in whole_arrays
+    ]
+    args, specs = [*columns, *arrived, *whole_arrays], by_column + by_kind + whole
+    if order:
+        args, specs = [args[n] for n in order], [specs[n] for n in order]
+    fixed = lambda rows: pl.BlockSpec((rows, width), lambda g: (0, 0))
+    shape = lambda rows: jax.ShapeDtypeStruct((rows, width), BF)
     return pl.pallas_call(
-        functools.partial(head_grads_kernel, first),
-        grid=(core // wide,),
-        in_specs=[columns(2 * keys), arrived, arrived, columns(own), columns(own)]
-        + [whole(a) for a in (*rows, *peer, right, right_peer)],
-        out_specs=[pl.BlockSpec((wide // 2, width), lambda g: (g, 0))] * 4,
-        out_shape=[jax.ShapeDtypeStruct((core // 2, width), BF)] * 4,
+        functools.partial(head_grads_kernel, many),
+        grid=(2,),
+        in_specs=specs,
+        out_specs=[fixed(wide), fixed(wide), fixed(half), fixed(half)]
+        + [pl.BlockSpec((half, width), lambda g: (g, 0))],
+        out_shape=[shape(wide), shape(wide), shape(half), shape(half), shape(wide)],
         compiler_params=pltpu.CompilerParams(vmem_limit_bytes=48 * 2**20),
         cost_estimate=LIGHT,
         name="head_grads",
-    )(big, *came, small, small_peer, *rows, *peer, right, right_peer)
+    )(*in_hbm(*args))
 
 
 def rows_kernel(moves, n_held, n_out, *refs):
@@ -406,6 +441,7 @@
 
 
 def heads_placed(pieces, s8):
+    kind_at = lambda n: jnp.where(n == 0, 0, jnp.where(n == 3, 1, n + 1))
     width = pieces[0].shape[1]
     size = pieces[0].shape[0] // 4
     rows = 8 * size
@@ -413,7 +449,7 @@
         heads_placed_kernel,
         grid=(4,),
         in_specs=[pl.BlockSpec(memory_space=pltpu.SMEM)]
-        + [pl.BlockSpec((size, width), lambda n: (n, 0)) for _ in pieces],
+        + [pl.BlockSpec((size, width), lambda n: (kind_at(n), 0)) for _ in pieces],
         out_specs=[
             pl.BlockSpec((1, width, rows), lambda n: (jnp.minimum(n, 2), 0, 0)),
             pl.BlockSpec((rows, width), lambda n: (0, 0)),
@@ -660,56 +696,72 @@
         two_x, one_y, came[0], send, part, gains_came, *held
     )
     gq, gk, gv = held
-    came.append(swap(send, 1))
     gq_peer = swap(gq[:, core:], 1)
     gains = gains + gains_came
     gains_came = swap(gains, 1)
-    lower_sum = line_sum(part)
+    part = part.reshape(4, 2, upper // 2, width)
+    part_one, part_two = [part[:, n].reshape(rows, width) for n in range(2)]
+    lower_one = line_sum(part_one)
     ff_total = plane.higher(totals((ones[0], one_x, one_y), (twos[0], two_x, two_y), t))
     upper_sum, ff_total = fence(upper_sum, ff_total)
     ff_total = line_sum(ff_total)
-    came[1], gq_peer, gains_came = fence(came[1], gq_peer, gains_came)
+    gq_peer, gains_came, send = fence(gq_peer, gains_came, send)
+    came.append(swap(send, 1))
     gains = gains + gains_came
-    a_twos = fence(
-        *head_grads(
-            True, gv, came, attended, attended_peer, gathered, gathered_peer, first_low, first_peer
-        )
-    )
-    a_diag_y, a_two_y = swap(a_twos[3], 4), swap(a_twos[2], 4)
-    a_ones = head_grads(
-        False, gk, came, gq, gq_peer, gathered, gathered_peer, tokens, tokens_peer
-    )
-    a_diag_y, gq, *a_ones = fence(a_diag_y, gq, *a_ones)
-    a_diag_x, a_one_x = swap(a_ones[3], 2), swap(a_ones[1], 2)
+    light = head_grads(
+        [gq, gq_peer, attended, attended_peer],
+        [],
+        [tokens, tokens_peer, first_low, first_peer],
+        False,
+        (0, 1, 4, 5, 2, 3, 6, 7),
+    )
+    came[1], *light = fence(came[1], *light)
+    to_x, to_y = swap(light[0], 2), swap(light[1], 4)
+    heavy = head_grads([gk, gv], came, [*gathered, *gathered_peer], True)
+    to_x, to_y, gq, *heavy = fence(to_x, to_y, gq, *heavy)
+    half = 4 * qp
+    add = lambda *arrays: sum(up(a) for a in arrays).astype(BF)
+
+    def second_hop(parts, to_x, to_y):
+        return add(parts[2], to_y[:half]), add(parts[3], to_x[:half])
+
+    def mine_of(parts, to_x, to_y, on_x, on_y):
+        own = parts[4]
+        total = [add(own[:half], to_x[half:], on_y), add(own[half:], to_y[half:], on_x)]
+        return plane.higher(jnp.concatenate(total)).reshape(4, 2 * qp, width)
+
+    next_x, next_y = second_hop(light, to_x, to_y)
+    next_x, next_y, *heavy = fence(next_x, next_y, *heavy)
+    on_x, on_y = swap(next_x, 2), swap(next_y, 4)
+    far_x, far_y = swap(heavy[0], 2), swap(heavy[1], 4)
     gains_came = swap(gains, 2)
-    a_two_x = (up(a_twos[1]) + up(a_diag_y)).astype(BF)
     first = mm(gq, wq, NN) + grad_first
-    a_two_x, a_diag_x, first = fence(a_two_x, a_diag_x, first)
-    a_one_y = (up(a_ones[2]) + up(a_diag_x)).astype(BF)
-    a_two_x, a_one_y, ff_total = fence(a_two_x, a_one_y, ff_total)
-    a_two_x, a_one_y = swap(a_two_x, 2), swap(a_one_y, 4)
+    on_x, on_y, far_x, far_y, first = fence(on_x, on_y, far_x, far_y, first)
+    next_x, next_y = second_hop(heavy, far_x, far_y)
+    next_x, next_y, ff_total = fence(next_x, next_y, ff_total)
+    last_x, last_y = swap(next_x, 2), swap(next_y, 4)
     f_x, f_y = swap(ff_total, 2), swap(ff_total, 4)
-    a_two_x, a_one_y, a_one_x, a_two_y, gains_came = fence(
-        a_two_x, a_one_y, a_one_x, a_two_y, gains_came
-    )
+    light_mine = mine_of(light, to_x, to_y, on_x, on_y)
+    last_x, last_y, light_mine, gains_came = fence(last_x, last_y, light_mine, gains_came)
     gains = gains + gains_came
-    gains_came = swap(gains, 4)
-    vo_mine = plane.higher((up(a_twos[0]) + up(a_two_x) + up(a_two_y)).astype(BF))
-    qk_mine = plane.higher((up(a_ones[0]) + up(a_one_x) + up(a_one_y)).astype(BF))
-    qk_mine, vo_mine = qk_mine.reshape(4, 2 * qp, width), vo_mine.reshape(4, 2 * qp, width)
-    a_mine = fence(*[jnp.concatenate([qk_mine[j], vo_mine[j]]) for j in range(4)])
-    a_came = [across(a_mine[j], j) for j in (1, 2, 3)]
+    heavy_mine = mine_of(heavy, far_x, far_y, last_x, last_y)
+    a_mine = jnp.concatenate([light_mine, heavy_mine], axis=1)
+    pairs = a_mine.reshape(2, 2, 4 * qp, width)
+    pairs = jnp.where((t & 1) == 1, pairs[:, ::-1], pairs)
+    a_mine = fence(jnp.where((t & 2) == 2, pairs[::-1], pairs).reshape(a_mine.shape))[0]
+    a_came = lax.all_to_all(a_mine, "tp", split_axis=0, concat_axis=0, tiled=True)
     f_core = [swap(ff_total, 1)]
     f_d1, f_d2 = swap(f_y[:fp], 2), swap(f_x[fp:], 4)
     f_core += [swap(f_x, 1), swap(f_y, 1)]
-    *a_came, f_d1, f_d2, b0, b1, b2, gains_came = fence(*a_came, f_d1, f_d2, *f_core, gains_came)
+    a_came, part_two, f_d1, f_d2, b0, b1, b2 = fence(a_came, part_two, f_d1, f_d2, *f_core)
     f_core = [b0, b1, b2]
-    gains = gains + gains_came
+    lower_two = line_sum(part_two)
+    a_total, gains = fence(jnp.sum(up(a_came), axis=0).astype(BF), gains)
+    gains = gains + swap(gains, 4)
     bit = 8
     while bit < seq_size:
         gains = gains + swap(gains, bit)
         bit *= 2
-    a_total = fence(sum((up(a) for a in a_came), up(a_mine[0])).astype(BF))[0]
     a_four = [a_total, swap(a_total, 2), swap(a_total, 4), swap(a_total, 6)]
     a_core = [swap(a_total, 1)]
     f_core += [swap(f_d1, 1), swap(f_d2, 1)]
@@ -721,11 +773,11 @@
         downs.append((part[i >> 1], 1) if i < 6 else (part[4], 0))
     grad_up = placed(ups, fp, s8, True)
     grad_down = placed(downs, fp, s8, False)
-    tokens_grad = (first + up(jnp.concatenate([upper_sum, lower_sum]))).astype(BF)
-    grad_up, grad_down, tokens_grad, *a_four = fence(grad_up, grad_down, tokens_grad, *a_four)
+    grad_up, grad_down, *a_four = fence(grad_up, grad_down, *a_four)
     a_core += [swap(a, 1) for a in a_four[1:]]
     a_all = [(a_core if i & 1 else a_four)[i >> 1] for i in range(8)]
     grad_qkv, grad_out = heads_placed(a_all, s8)
+    tokens_grad = (first + up(jnp.concatenate([upper_sum, lower_one, lower_two]))).astype(BF)
     return (
         mixed,
         tokens_grad,

time: 518 us -> 512 us (0.988)
  the two profiles are of different devices: /device:TPU:9 before, /device:TPU:0 now
where the time goes in v4:
time: 512 us; the launch traced here: 504 us
  Pallas kernels  154 us (30%)
  waiting for transfers between devices  108 us (21%)
  starting transfers between devices  75.5 us (15%)
  matrix products  65.9 us (13%)
  local copies, waits for them, and re-layouts  40.3 us (8%)
  other arithmetic  37.8 us (7%)
  between operations  21.6 us (4%)
    pallas_call x2, Pallas kernels, attention_backward(): pl.pallas_call(backward_kernel, grid=(pairs,), in_specs=[by_pair, pl.Bloc...  71.6 us
    ppermute x66, waiting for transfers between devices, swap(): return lax.ppermute(array, 'seq', [(i, i ^ bit) for i in range(self.size)])  70 us
    dot_general x14, matrix products, mm(): return lax.dot_general(a, b, dims, preferred_element_type=F32).astype(out)  65.9 us
    ppermute x66, starting transfers between devices, swap(): return lax.ppermute(array, 'seq', [(i, i ^ bit) for i in range(self.size)])  48.7 us
    pallas_call x4, Pallas kernels, attention_forward(): pl.pallas_call(functools.partial(forward_kernel, len(kvs)), grid=(count,)...  31.2 us
    ppermute x10, waiting for transfers between devices, along(): return lax.ppermute(array, 'tp', pairs)  27.1 us
    ppermute x10, starting transfers between devices, along(): return lax.ppermute(array, 'tp', pairs)  22.3 us
    pallas_call x2, Pallas kernels, head_grads(): pl.pallas_call(functools.partial(head_grads_kernel, many), grid=(2,), in_...  22 us
  transfers between devices with their start and end apart: 83, of which 29 were waited for; matrix products, arithmetic and copies ran while one was open for 22% of the time, Pallas kernels for 31%

profile of v4, /device:TPU:0, one launch (start us, length us, event | category | flops | bytes accessed | tf_op | source)
XLA Modules:
  0.0 503.5 jit_solution(716598504615183414)
XLA Ops:
  12.5 3.0 collective-permute-start
  15.5 2.6 collective-permute-start.1
  24.6 6.7 %collective-permute-done = bf16[128,1024]{1,0:T(8,128)(2,1)S(1)} collective-permute-done((bf16[128,1024]{1,0:T(8,128)(2,1)S(1)}, bf16[128,1024]{1,0:T(8,128)(2,1)S(1)}, u32[]{:S(2)}, u32[]{:S(2)}) %collective-permute-start) | collective-permute-done | bytes 262176 | tf_op jit(solution)/shard_map/ppermute | solution.py:35
  31.3 9.3 %collective-permute-done.1 = bf16[128,1024]{1,0:T(8,128)(2,1)S(1)} collective-permute-done((bf16[128,1024]{1,0:T(8,128)(2,1)S(1)}, bf16[128,1024]{1,0:T(8,128)(2,1)S(1)}, u32[]{:S(2)}, u32[]{:S(2)}) %collective-permute-start.1) | collective-permute-done | bytes 262176 | tf_op jit(solution)/shard_map/ppermute | solution.py:35
  40.6 5.8 %collective-permute-done.2 = bf16[128,1024]{1,0:T(8,128)(2,1)S(1)} collective-permute-done((bf16[128,1024]{1,0:T(8,128)(2,1)S(1)}, bf16[128,1024]{1,0:T(8,128)(2,1)S(1)}, u32[]{:S(2)}, u32[]{:S(2)}) %collective-permute-start.2) | collective-permute-done | bytes 262176 | tf_op jit(solution)/shard_map/ppermute | solution.py:35
  51.8 13.2 %collective-permute-done.3 = bf16[384,1024]{1,0:T(8,128)(2,1)} collective-permute-done((bf16[384,1024]{1,0:T(8,128)(2,1)}, bf16[384,1024]{1,0:T(8,128)(2,1)}, u32[]{:S(2)}, u32[]{:S(2)}) %collective-permute-start.3) | collective-permute-done | bytes 786464 | tf_op jit(solution)/shard_map/ppermute | solution.py:47
  81.2 5.6 %collective-permute-done.5 = bf16[192,1024]{1,0:T(8,128)(2,1)} collective-permute-done((bf16[192,1024]{1,0:T(8,128)(2,1)}, bf16[192,1024]{1,0:T(8,128)(2,1)}, u32[]{:S(2)}, u32[]{:S(2)}) %collective-permute-start.5) | collective-permute-done | bytes 393248 | tf_op jit(solution)/shard_map/ppermute | solution.py:47
  99.3 3.2 fusion.7.q_ref
  103.2 2.5 copy.48
  105.7 9.5 %convert_bitcast_fusion.refs_0_.refs_2_.k_ref.v_ref = bf16[1024,2048]{1,0:T(8,128)(2,1)} fusion(bf16[2048,1024]{1,0:T(8,128)(2,1)} %bitcast.133, bf16[1024,1024]{1,0:T(8,128)(2,1)} %all-gather.3.cloned.1.call-done.refs_4_), kind=kOutput, calls=%fused_computation.20 | convolution fusion | flops 4297064448 | bytes 10485760 | tf_op jit(solution)/shard_map/dot_general | solution.py:31
  115.2 8.2 %all-gather.5.cloned.1.call-done.refs_5_ = bf16[1024,1024]{1,0:T(8,128)(2,1)} async-done(((bf16[256,1024]{1,0:T(8,128)(2,1)}), bf16[1024,1024]{1,0:T(8,128)(2,1)}) %all-gather.5.cloned.1.call-update) | async-done | bytes 2097168 | tf_op jit(solution)/shard_map/all_gather | solution.py:547
  123.4 3.8 collective-permute-start.13
  128.8 9.4 %convolution_convert_fusion.refs_1_.refs_3_.k_ref.v_ref = bf16[1024,2048]{1,0:T(8,128)(2,1)} fusion(bf16[1024,1024]{1,0:T(8,128)(2,1)} %all-gather.5.cloned.1.call-done.refs_5_, bf16[2048,1024]{1,0:T(8,128)(2,1)} %bitcast.134), kind=kOutput, calls=%fused_computation.21 | convolution fusion | flops 4297064448 | bytes 10485760 | tf_op jit(solution)/shard_map/dot_general | solution.py:31
  149.1 7.7 %attention_forward.4 = (bf16[512,1024]{1,0:T(8,128)(2,1)S(1)}, f32[8,2,512]{2,1,0:T(2,128)S(1)}) custom-call(bf16[512,1024]{1,0:T(8,128)(2,1)S(1)} %fusion.7.q_ref, bf16[1024,2048]{1,0:T(8,128)(2,1)S(1)} %copy-done.2, bf16[1024,2048]{1,0:T(8,128)(2,1)S(1)} %copy-done, bf16[1024,2048]{1,0:T(8,128)(2,1)S(1)} %copy-done.2, bf16[1024,2048]{1,0:T(8,128)(2,1)S(1)} %copy-done, ...), custom_call_target="tpu_custom_call" | custom-call | flops 1000000000 | bytes 1000000 | tf_op jit(solution)/shard_map/attention_forward/pallas_call | solution.py:98
  156.9 3.7 collective-permute-done.16
  168.5 7.7 %attention_forward.5 = (bf16[512,1024]{1,0:T(8,128)(2,1)S(1)}, f32[8,2,512]{2,1,0:T(2,128)S(1)}) custom-call(bf16[512,1024]{1,0:T(8,128)(2,1)S(1)} %fusion.7.q_ref, bf16[1024,2048]{1,0:T(8,128)(2,1)S(1)} %copy-done.2, bf16[1024,2048]{1,0:T(8,128)(2,1)S(1)} %copy-done, ...), custom_call_target="tpu_custom_call", output_to_operand_aliasing={{0}: (6, {}), {1}: (7, {})} | custom-call | flops 1000000000 | bytes 1000000 | tf_op jit(solution)/shard_map/attention_forward/pallas_call | solution.py:98
  176.3 4.0 collective-permute-done.20.refs_5_
  187.6 7.8 %attention_forward.6 = (bf16[512,1024]{1,0:T(8,128)(2,1)S(1)}, f32[8,2,512]{2,1,0:T(2,128)S(1)}) custom-call(bf16[512,1024]{1,0:T(8,128)(2,1)S(1)} %fusion.7.q_ref, bf16[1024,2048]{1,0:T(8,128)(2,1)S(1)} %copy-done.3, bf16[1024,2048]{1,0:T(8,128)(2,1)S(1)} %copy-done.1, ...), custom_call_target="tpu_custom_call", output_to_operand_aliasing={{0}: (6, {}), {1}: (7, {})} | custom-call | flops 1000000000 | bytes 1000000 | tf_op jit(solution)/shard_map/attention_forward/pallas_call | solution.py:98
  195.4 2.5 collective-permute-done.24.refs_3_
  202.1 8.0 %attention_forward.7 = (bf16[512,1024]{1,0:T(8,128)(2,1)S(1)}, f32[8,2,512]{2,1,0:T(2,128)S(1)}) custom-call(bf16[512,1024]{1,0:T(8,128)(2,1)S(1)} %fusion.7.q_ref, bf16[1024,2048]{1,0:T(8,128)(2,1)S(1)} %copy-done.3, bf16[1024,2048]{1,0:T(8,128)(2,1)S(1)} %copy-done.1, ...), custom_call_target="tpu_custom_call", output_to_operand_aliasing={{0}: (6, {}), {1}: (7, {})} | custom-call | flops 1000000000 | bytes 1000000 | tf_op jit(solution)/shard_map/attention_forward/pallas_call | solution.py:98
  210.1 2.9 fusion.40
  216.7 6.5 %multiply_convert_fusion.2 = (bf16[512,2048]{1,0:T(8,128)(2,1)S(1)}, f32[512,2048]{1,0:T(8,128)}) fusion(bf16[512,1024]{1,0:T(8,128)(2,1)S(1)} %collective-permute-done.30.right_two_ref, bf16[2048,1024]{1,0:T(8,128)(2,1)S(1)} %get-tuple-element.255), kind=kOutput, calls=%fused_computation.14 | convolution fusion | flops 2169503744 | bytes 11534336 | tf_op jit(solution)/shard_map/dot_general | solution.py:31
  225.8 6.7 %multiply_convert_fusion.3 = (bf16[512,2048]{1,0:T(8,128)(2,1)S(1)}, f32[512,2048]{1,0:T(8,128)}) fusion(bf16[512,1024]{1,0:T(8,128)(2,1)S(1)} %multiply_convert_fusion.5.right_ref, bf16[2048,1024]{1,0:T(8,128)(2,1)S(1)} %get-tuple-element.255), kind=kOutput, calls=%fused_computation.17 | convolution fusion | flops 2169503744 | bytes 11534336 | tf_op jit(solution)/shard_map/dot_general | solution.py:31
  232.4 2.6 fusion.41
  240.7 5.3 %multiply_convert_fusion.left_two_ref = bf16[512,2048]{1,0:T(8,128)(2,1)S(1)} fusion(bf16[512,1024]{1,0:T(8,128)(2,1)S(1)} %collective-permute-done.32.right_two_ref, bf16[2048,1024]{1,0:T(8,128)(2,1)S(1)} %get-tuple-element.256, f32[512,2048]{1,0:T(8,128)S(1)} %copy-done.47), kind=kOutput, calls=%fused_computation.10 | convolution fusion | flops 2174746624 | bytes 11534336 | tf_op jit(solution)/shard_map/dot_general | solution.py:31
  246.1 2.3 convolution_convert_fusion.3
  248.9 5.7 %multiply_convert_fusion.1.left_ref = bf16[512,2048]{1,0:T(8,128)(2,1)S(1)} fusion(bf16[512,1024]{1,0:T(8,128)(2,1)S(1)} %fusion.32.right_ref, bf16[2048,1024]{1,0:T(8,128)(2,1)S(1)} %get-tuple-element.256, f32[512,2048]{1,0:T(8,128)S(1)} %copy-done.48), kind=kOutput, calls=%fused_computation.12 | convolution fusion | flops 2174746624 | bytes 11534336 | tf_op jit(solution)/shard_map/dot_general | solution.py:31
  256.9 5.9 %outer_four.2 = (bf16[512,1024]{1,0:T(8,128)(2,1)S(1)}, bf16[512,1024]{1,0:T(8,128)(2,1)S(1)}, bf16[512,1024]{1,0:T(8,128)(2,1)S(1)}, bf16[512,1024]{1,0:T(8,128)(2,1)S(1)}) custom-call(bf16[512,2048]{1,0:T(8,128)(2,1)S(1)} %get-tuple-element.430.left_ref, bf16[512,1024]{1,0:T(8,128)(2,1)S(1)} %fusion.32.right_ref, ...), custom_call_target="tpu_custom_call" | custom-call | flops 1000000000 | bytes 1000000 | tf_op jit(solution)/shard_map/outer_four/pallas_call | solution.py:410
  262.9 2.9 multiply_reduce_fusion
  267.9 5.9 %outer_four.3 = (bf16[512,1024]{1,0:T(8,128)(2,1)S(1)}, bf16[512,1024]{1,0:T(8,128)(2,1)S(1)}, bf16[512,1024]{1,0:T(8,128)(2,1)S(1)}, bf16[512,1024]{1,0:T(8,128)(2,1)S(1)}) custom-call(bf16[512,2048]{1,0:T(8,128)(2,1)S(1)} %multiply_convert_fusion.1.left_ref, bf16[512,1024]{1,0:T(8,128)(2,1)S(1)} %multiply_convert_fusion.5.right_ref, ...), custom_call_target="tpu_custom_call" | custom-call | flops 1000000000 | bytes 1000000 | tf_op jit(solution)/shard_map/outer_four/pallas_call | solution.py:410
  280.3 3.9 collective-permute-start.42
  284.4 36.2 %attention_backward.2 = (f32[512,1024]{1,0:T(8,128)S(1)}, bf16[2048,512]{1,0:T(8,128)(2,1)S(1)}, bf16[2048,512]{1,0:T(8,128)(2,1)}, bf16[2,1024,512]{2,1,0:T(8,128)(2,1)}, bf16[1024,1024]{1,0:T(8,128)(2,1)}) custom-call(bf16[512,1024]{1,0:T(8,128)(2,1)} %copy-done.5, bf16[1024,2048]{1,0:T(8,128)(2,1)} %convert_bitcast_fusion.refs_0_.refs_2_.k_ref.v_ref, ...), custom_call_target="tpu_custom_call" | custom-call | flops 1000000000 | bytes 1000000 | tf_op jit(solution)/shard_map/attention_backward/pallas_call | solution.py:206
  329.2 3.6 collective-permute-start.46
  333.1 35.4 %attention_backward.3 = (bf16[512,1024]{1,0:T(8,128)(2,1)S(1)}, bf16[2048,512]{1,0:T(8,128)(2,1)}, bf16[2048,512]{1,0:T(8,128)(2,1)}, bf16[2,1024,512]{2,1,0:T(8,128)(2,1)S(1)}, bf16[1024,1024]{1,0:T(8,128)(2,1)S(1)}) custom-call(bf16[512,1024]{1,0:T(8,128)(2,1)} %copy-done.5, ...), custom_call_target="tpu_custom_call", output_to_operand_aliasing={{1}: (9, {}), {2}: (10, {})} | custom-call | flops 1000000000 | bytes 1000000 | tf_op jit(solution)/shard_map/attention_backward/pallas_call | solution.py:206
  369.8 5.2 %totals.1 = bf16[1024,1024]{1,0:T(8,128)(2,1)} custom-call(s32[1]{0:T(128)} %bitcast.47.at_ref, bf16[512,1024]{1,0:T(8,128)(2,1)} %copy-done.13, bf16[512,1024]{1,0:T(8,128)(2,1)} %copy-done.31, bf16[512,1024]{1,0:T(8,128)(2,1)} %collective-permute-done.44.refs_2_, bf16[512,1024]{1,0:T(8,128)(2,1)} %copy-done.12, ...), custom_call_target="tpu_custom_call" | custom-call | flops 1000000000 | bytes 1000000 | tf_op jit(solution)/shard_map/totals/pallas_call | solution.py:374
  377.9 6.8 %head_grads.2 = (bf16[256,1024]{1,0:T(8,128)(2,1)}, bf16[256,1024]{1,0:T(8,128)(2,1)S(1)}, bf16[128,1024]{1,0:T(8,128)(2,1)S(1)}, bf16[128,1024]{1,0:T(8,128)(2,1)S(1)}, bf16[256,1024]{1,0:T(8,128)(2,1)S(1)}) custom-call(bf16[512,1024]{1,0:T(8,128)(2,1)} %copy-done.8, bf16[512,512]{1,0:T(8,128)(2,1)} %copy-done.42, bf16[512,1024]{1,0:T(8,128)(2,1)} %refs_2_.1, ...), custom_call_target="tpu_custom_call" | custom-call | flops 1000000000 | bytes 1000000 | tf_op jit(solution)/shard_map/head_grads/pallas_call | solution.py:311
  387.5 15.3 %head_grads.3 = (bf16[256,1024]{1,0:T(8,128)(2,1)}, bf16[256,1024]{1,0:T(8,128)(2,1)}, bf16[128,1024]{1,0:T(8,128)(2,1)S(1)}, bf16[128,1024]{1,0:T(8,128)(2,1)S(1)}, bf16[256,1024]{1,0:T(8,128)(2,1)S(1)}) custom-call(bf16[2048,512]{1,0:T(8,128)(2,1)} %get-tuple-element.314.refs_0_, bf16[2048,512]{1,0:T(8,128)(2,1)} %get-tuple-element.315.refs_1_, ...), custom_call_target="tpu_custom_call" | custom-call | flops 1000000000 | bytes 1000000 | tf_op jit(solution)/shard_map/head_grads/pallas_call | solution.py:311
  413.4 4.9 convolution_add_fusion
  418.4 7.5 %collective-permute-done.52 = bf16[128,1024]{1,0:T(8,128)(2,1)S(1)} collective-permute-done((bf16[128,1024]{1,0:T(8,128)(2,1)}, bf16[128,1024]{1,0:T(8,128)(2,1)S(1)}, u32[]{:S(2)}, u32[]{:S(2)}) %collective-permute-start.52) | collective-permute-done | bytes 262176 | tf_op jit(solution)/shard_map/ppermute | solution.py:47
  432.8 3.3 collective-permute-done.56
  439.7 4.3 all-to-all-start
  446.7 9.1 %collective-permute-done.61.refs_2_ = bf16[256,1024]{1,0:T(8,128)(2,1)S(1)} collective-permute-done((bf16[256,1024]{1,0:T(8,128)(2,1)S(1)}, bf16[256,1024]{1,0:T(8,128)(2,1)S(1)}, u32[]{:S(2)}, u32[]{:S(2)}) %collective-permute-start.61) | collective-permute-done | bytes 524320 | tf_op jit(solution)/shard_map/ppermute | solution.py:47
  458.9 6.4 %collective-permute-done.60.refs_6_ = bf16[128,1024]{1,0:T(8,128)(2,1)} collective-permute-done((bf16[128,1024]{1,0:T(8,128)(2,1)S(1)}, bf16[128,1024]{1,0:T(8,128)(2,1)}, u32[]{:S(2)}, u32[]{:S(2)}) %collective-permute-start.60) | collective-permute-done | bytes 262176 | tf_op jit(solution)/shard_map/ppermute | solution.py:47
  473.7 3.5 placed.2
  477.2 3.3 placed.3
  480.5 4.5 collective-permute-done.69.refs_4_
  489.8 3.1 heads_placed.1
  494.0 2.4 add_convert_fusion.2
  (342 shorter events, 152.5 us)
Async XLA Ops:
  7.2 98.6 %all-gather.3.cloned.1.call-start = ((), (), s32[]{:S(2)}) async-start(), calls=%async_computation.5 | async-start | bytes 2621440 | tf_op jit(solution)/shard_map/all_gather | solution.py:547
  9.5 113.9 %all-gather.5.cloned.1.call-start = ((), (), s32[]{:S(2)}) async-start(), calls=%async_computation.6 | async-start | bytes 2621440 | tf_op jit(solution)/shard_map/all_gather | solution.py:547
  12.5 18.8 %collective-permute-start = (bf16[128,1024]{1,0:T(8,128)(2,1)S(1)}, bf16[128,1024]{1,0:T(8,128)(2,1)S(1)}, u32[]{:S(2)}, u32[]{:S(2)}) collective-permute-start(bf16[128,1024]{1,0:T(8,128)(2,1)S(1)} %bitcast.156), channel_id=1, source_target_pairs={{0,1},{1,0},{2,3},{3,2},{4,5},{5,4},{6,7},{7,6},{8,9},{9,8},{10,11... | collective-permute-start | bytes 786440 | tf_op jit(solution)/shard_map/ppermute | solution.py:35
  15.5 25.1 %collective-permute-start.1 = (bf16[128,1024]{1,0:T(8,128)(2,1)S(1)}, bf16[128,1024]{1,0:T(8,128)(2,1)S(1)}, u32[]{:S(2)}, u32[]{:S(2)}) collective-permute-start(bf16[128,1024]{1,0:T(8,128)(2,1)S(1)} %bitcast.157), channel_id=1, source_target_pairs={{0,2},{1,3},{2,0},{3,1},{4,6},{5,7},{6,4},{7,5},{8,10},{9,11},{10,... | collective-permute-start | bytes 786440 | tf_op jit(solution)/shard_map/ppermute | solution.py:35
  18.1 28.3 %collective-permute-start.2 = (bf16[128,1024]{1,0:T(8,128)(2,1)S(1)}, bf16[128,1024]{1,0:T(8,128)(2,1)S(1)}, u32[]{:S(2)}, u32[]{:S(2)}) collective-permute-start(bf16[128,1024]{1,0:T(8,128)(2,1)S(1)} %bitcast.158), channel_id=1, source_target_pairs={{0,3},{1,2},{2,1},{3,0},{4,7},{5,6},{6,5},{7,4},{8,11},{9,10},{10,... | collective-permute-start | bytes 786440 | tf_op jit(solution)/shard_map/ppermute | solution.py:35
  48.6 16.4 %collective-permute-start.3 = (bf16[384,1024]{1,0:T(8,128)(2,1)}, bf16[384,1024]{1,0:T(8,128)(2,1)}, u32[]{:S(2)}, u32[]{:S(2)}) collective-permute-start(bf16[384,1024]{1,0:T(8,128)(2,1)} %constant_dynamic-update-slice_fusion), channel_id=1, source_target_pairs={{0,8},{4,12},{8,0},{12,4},{16,24},{20,28},{24,16},{28,20},{1,9},{5... | collective-permute-start | bytes 2359304 | tf_op jit(solution)/shard_map/ppermute | solution.py:47
  50.1 16.1 %collective-permute-start.4 = (bf16[384,1024]{1,0:T(8,128)(2,1)}, bf16[384,1024]{1,0:T(8,128)(2,1)}, u32[]{:S(2)}, u32[]{:S(2)}) collective-permute-start(bf16[384,1024]{1,0:T(8,128)(2,1)} %constant_dynamic-update-slice_fusion), channel_id=1, source_target_pairs={{0,16},{4,20},{8,24},{12,28},{16,0},{20,4},{24,8},{28,12},{1,17},{... | collective-permute-start | bytes 2359304 | tf_op jit(solution)/shard_map/ppermute | solution.py:47
  51.7 323.3 %reduce-scatter.5.cloned.1.call-start = ((), (), s32[]{:S(2)}) async-start(), calls=%async_computation.7 | async-start | bytes 2621440 | tf_op jit(solution)/shard_map/reduce_scatter | solution.py:678
  66.2 20.7 %collective-permute-start.7 = (bf16[384,1024]{1,0:T(8,128)(2,1)}, bf16[384,1024]{1,0:T(8,128)(2,1)}, u32[]{:S(2)}, u32[]{:S(2)}) collective-permute-start(bf16[384,1024]{1,0:T(8,128)(2,1)} %constant_dynamic-update-slice_fusion), channel_id=1, source_target_pairs={{0,4},{4,0},{8,12},{12,8},{16,20},{20,16},{24,28},{28,24},{1,5},{5... | collective-permute-start | bytes 2359304 | tf_op jit(solution)/shard_map/ppermute | solution.py:47
  66.2 20.7 %collective-permute-start.8 = (bf16[384,1024]{1,0:T(8,128)(2,1)}, bf16[384,1024]{1,0:T(8,128)(2,1)}, u32[]{:S(2)}, u32[]{:S(2)}) collective-permute-start(bf16[384,1024]{1,0:T(8,128)(2,1)} %collective-permute-done.3), channel_id=1, source_target_pairs={{0,4},{4,0},{8,12},{12,8},{16,20},{20,16},{24,28},{28,24},{1,5},{5... | collective-permute-start | bytes 2359304 | tf_op jit(solution)/shard_map/ppermute | solution.py:47
  66.7 20.2 %collective-permute-start.9 = (bf16[384,1024]{1,0:T(8,128)(2,1)}, bf16[384,1024]{1,0:T(8,128)(2,1)}, u32[]{:S(2)}, u32[]{:S(2)}) collective-permute-start(bf16[384,1024]{1,0:T(8,128)(2,1)} %collective-permute-done.4), channel_id=1, source_target_pairs={{0,4},{4,0},{8,12},{12,8},{16,20},{20,16},{24,28},{28,24},{1,5},{5... | collective-permute-start | bytes 2359304 | tf_op jit(solution)/shard_map/ppermute | solution.py:47
  86.7 28.4 %collective-permute-start.12 = (bf16[512,1024]{1,0:T(8,128)(2,1)}, bf16[512,1024]{1,0:T(8,128)(2,1)S(1)}, u32[]{:S(2)}, u32[]{:S(2)}) collective-permute-start(bf16[512,1024]{1,0:T(8,128)(2,1)} %refs_2_.1), channel_id=1, source_target_pairs={{0,4},{4,0},{8,12},{12,8},{16,20},{20,16},{24,28},{28,24},{1,5},{5... | collective-permute-start | bytes 3145736 | tf_op jit(solution)/shard_map/ppermute | solution.py:47
  123.4 16.4 %collective-permute-start.13 = (bf16[256,1024]{1,0:T(8,128)(2,1)}, bf16[256,1024]{1,0:T(8,128)(2,1)}, u32[]{:S(2)}, u32[]{:S(2)}) collective-permute-start(bf16[256,1024]{1,0:T(8,128)(2,1)} %pad_maximum_fusion.5), channel_id=1, source_target_pairs={{0,1},{1,0},{2,3},{3,2},{4,5},{5,4},{6,7},{7,6},{8,9},{9,8},{10,11... | collective-permute-start | bytes 1572872 | tf_op jit(solution)/shard_map/ppermute | solution.py:35
  139.8 17.0 %collective-permute-start.15 = (bf16[256,1024]{1,0:T(8,128)(2,1)}, bf16[256,1024]{1,0:T(8,128)(2,1)S(1)}, u32[]{:S(2)}, u32[]{:S(2)}) collective-permute-start(bf16[256,1024]{1,0:T(8,128)(2,1)} %collective-permute-done.13.refs_2_), channel_id=1, source_target_pairs={{1,2},{2,1},{5,6},{6,5},{9,10},{10,9},{13,14},{14,13},{17,18},{18,... | collective-permute-start | bytes 1572872 | tf_op jit(solution)/shard_map/ppermute | solution.py:35
  140.5 20.1 %collective-permute-start.16 = (bf16[256,1024]{1,0:T(8,128)(2,1)}, bf16[256,1024]{1,0:T(8,128)(2,1)S(1)}, u32[]{:S(2)}, u32[]{:S(2)}) collective-permute-start(bf16[256,1024]{1,0:T(8,128)(2,1)} %collective-permute-done.14), channel_id=1, source_target_pairs={{1,0},{2,3},{5,4},{6,7},{9,8},{10,11},{13,12},{14,15},{17,16},{18,... | collective-permute-start | bytes 1572872 | tf_op jit(solution)/shard_map/ppermute | solution.py:35
  141.8 18.8 %collective-permute-start.17 = (bf16[256,1024]{1,0:T(8,128)(2,1)}, bf16[256,1024]{1,0:T(8,128)(2,1)}, u32[]{:S(2)}, u32[]{:S(2)}) collective-permute-start(bf16[256,1024]{1,0:T(8,128)(2,1)} %collective-permute-done.13.refs_2_), channel_id=1, source_target_pairs={{0,8},{4,12},{8,0},{12,4},{16,24},{20,28},{24,16},{28,20},{1,9},{5... | collective-permute-start | bytes 1572872 | tf_op jit(solution)/shard_map/ppermute | solution.py:47
  143.2 17.4 %collective-permute-start.18 = (bf16[256,1024]{1,0:T(8,128)(2,1)}, bf16[256,1024]{1,0:T(8,128)(2,1)}, u32[]{:S(2)}, u32[]{:S(2)}) collective-permute-start(bf16[256,1024]{1,0:T(8,128)(2,1)} %collective-permute-done.13.refs_2_), channel_id=1, source_target_pairs={{0,16},{4,20},{8,24},{12,28},{16,0},{20,4},{24,8},{28,12},{1,17},{... | collective-permute-start | bytes 1572872 | tf_op jit(solution)/shard_map/ppermute | solution.py:47
  160.6 20.5 %collective-permute-start.19 = (bf16[256,1024]{1,0:T(8,128)(2,1)S(1)}, bf16[256,1024]{1,0:T(8,128)(2,1)S(1)}, u32[]{:S(2)}, u32[]{:S(2)}) collective-permute-start(bf16[256,1024]{1,0:T(8,128)(2,1)S(1)} %collective-permute-done.15), channel_id=1, source_target_pairs={{1,0},{2,3},{5,4},{6,7},{9,8},{10,11},{13,12},{14,15},{17,16},{18,... | collective-permute-start | bytes 1572872 | tf_op jit(solution)/shard_map/ppermute | solution.py:35
  162.3 18.7 %collective-permute-start.22 = (bf16[256,1024]{1,0:T(8,128)(2,1)S(1)}, bf16[256,1024]{1,0:T(8,128)(2,1)S(1)}, u32[]{:S(2)}, u32[]{:S(2)}) collective-permute-start(bf16[256,1024]{1,0:T(8,128)(2,1)S(1)} %broadcast_select_fusion.1.refs_0_), channel_id=1, source_target_pairs={{0,8},{4,12},{8,0},{12,4},{16,24},{20,28},{24,16},{28,20},{1,9},{5... | collective-permute-start | bytes 1572872 | tf_op jit(solution)/shard_map/ppermute | solution.py:47
  163.6 17.5 %collective-permute-start.23 = (bf16[256,1024]{1,0:T(8,128)(2,1)S(1)}, bf16[256,1024]{1,0:T(8,128)(2,1)S(1)}, u32[]{:S(2)}, u32[]{:S(2)}) collective-permute-start(bf16[256,1024]{1,0:T(8,128)(2,1)S(1)} %broadcast_select_fusion.1.refs_0_), channel_id=1, source_target_pairs={{0,16},{4,20},{8,24},{12,28},{16,0},{20,4},{24,8},{28,12},{1,17},{... | collective-permute-start | bytes 1572872 | tf_op jit(solution)/shard_map/ppermute | solution.py:47
  166.1 14.2 %collective-permute-start.20 = (bf16[128,1024]{1,0:T(8,128)(2,1)S(1)}, bf16[128,1024]{1,0:T(8,128)(2,1)S(1)}, u32[]{:S(2)}, u32[]{:S(2)}) collective-permute-start(bf16[128,1024]{1,0:T(8,128)(2,1)S(1)} %slice.137), channel_id=1, source_target_pairs={{0,8},{4,12},{8,0},{12,4},{16,24},{20,28},{24,16},{28,20},{1,9},{5... | collective-permute-start | bytes 786440 | tf_op jit(solution)/shard_map/ppermute | solution.py:47
  181.1 18.3 %collective-permute-start.26 = (bf16[256,1024]{1,0:T(8,128)(2,1)S(1)}, bf16[256,1024]{1,0:T(8,128)(2,1)S(1)}, u32[]{:S(2)}, u32[]{:S(2)}) collective-permute-start(bf16[256,1024]{1,0:T(8,128)(2,1)S(1)} %broadcast_select_fusion.refs_5_), channel_id=1, source_target_pairs={{0,8},{4,12},{8,0},{12,4},{16,24},{20,28},{24,16},{28,20},{1,9},{5... | collective-permute-start | bytes 1572872 | tf_op jit(solution)/shard_map/ppermute | solution.py:47
  182.2 17.2 %collective-permute-start.27 = (bf16[256,1024]{1,0:T(8,128)(2,1)S(1)}, bf16[256,1024]{1,0:T(8,128)(2,1)S(1)}, u32[]{:S(2)}, u32[]{:S(2)}) collective-permute-start(bf16[256,1024]{1,0:T(8,128)(2,1)S(1)} %broadcast_select_fusion.refs_5_), channel_id=1, source_target_pairs={{0,16},{4,20},{8,24},{12,28},{16,0},{20,4},{24,8},{28,12},{1,17},{... | collective-permute-start | bytes 1572872 | tf_op jit(solution)/shard_map/ppermute | solution.py:47
  184.9 14.5 %collective-permute-start.25 = (bf16[128,1024]{1,0:T(8,128)(2,1)S(1)}, bf16[128,1024]{1,0:T(8,128)(2,1)S(1)}, u32[]{:S(2)}, u32[]{:S(2)}) collective-permute-start(bf16[128,1024]{1,0:T(8,128)(2,1)S(1)} %slice.140), channel_id=1, source_target_pairs={{0,16},{4,20},{8,24},{12,28},{16,0},{20,4},{24,8},{28,12},{1,17},{... | collective-permute-start | bytes 786440 | tf_op jit(solution)/shard_map/ppermute | solution.py:47
  238.3 37.4 %collective-permute-start.41 = (bf16[1024,1024]{1,0:T(8,128)(2,1)}, bf16[1024,1024]{1,0:T(8,128)(2,1)}, u32[]{:S(2)}, u32[]{:S(2)}) collective-permute-start(bf16[1024,1024]{1,0:T(8,128)(2,1)} %all-gather.5.cloned.1.call-done.refs_5_), channel_id=1, source_target_pairs={{0,4},{4,0},{8,12},{12,8},{16,20},{20,16},{24,28},{28,24},{1,5},{5... | collective-permute-start | bytes 6291464 | tf_op jit(solution)/shard_map/ppermute | solution.py:47
  238.4 37.1 %collective-permute-start.40 = (bf16[1024,1024]{1,0:T(8,128)(2,1)}, bf16[1024,1024]{1,0:T(8,128)(2,1)}, u32[]{:S(2)}, u32[]{:S(2)}) collective-permute-start(bf16[1024,1024]{1,0:T(8,128)(2,1)} %all-gather.3.cloned.1.call-done.refs_4_), channel_id=1, source_target_pairs={{0,4},{4,0},{8,12},{12,8},{16,20},{20,16},{24,28},{28,24},{1,5},{5... | collective-permute-start | bytes 6291464 | tf_op jit(solution)/shard_map/ppermute | solution.py:47
  239.6 36.5 %collective-permute-start.39 = (bf16[512,512]{1,0:T(8,128)(2,1)}, bf16[512,512]{1,0:T(8,128)(2,1)S(1)}, u32[]{:S(2)}, u32[]{:S(2)}) collective-permute-start(bf16[512,512]{1,0:T(8,128)(2,1)} %slice.144), channel_id=1, source_target_pairs={{0,4},{4,0},{8,12},{12,8},{16,20},{20,16},{24,28},{28,24},{1,5},{5... | collective-permute-start | bytes 1572872 | tf_op jit(solution)/shard_map/ppermute | solution.py:47
  248.4 14.5 %collective-permute-start.33 = (bf16[512,1024]{1,0:T(8,128)(2,1)S(1)}, bf16[512,1024]{1,0:T(8,128)(2,1)S(1)}, u32[]{:S(2)}, u32[]{:S(2)}) collective-permute-start(bf16[512,1024]{1,0:T(8,128)(2,1)S(1)} %convolution_convert_fusion.3), channel_id=1, source_target_pairs={{0,4},{4,0},{8,12},{12,8},{16,20},{20,16},{24,28},{28,24},{1,5},{5... | collective-permute-start | bytes 3145736 | tf_op jit(solution)/shard_map/ppermute | solution.py:47
  273.9 49.5 %collective-permute-start.34 = (bf16[512,1024]{1,0:T(8,128)(2,1)S(1)}, bf16[512,1024]{1,0:T(8,128)(2,1)}, u32[]{:S(2)}, u32[]{:S(2)}) collective-permute-start(bf16[512,1024]{1,0:T(8,128)(2,1)S(1)} %get-tuple-element.267), channel_id=1, source_target_pairs={{0,8},{4,12},{8,0},{12,4},{16,24},{20,28},{24,16},{28,20},{1,9},{5... | collective-permute-start | bytes 3145736 | tf_op jit(solution)/shard_map/ppermute | solution.py:47
  275.6 47.8 %collective-permute-start.35 = (bf16[512,1024]{1,0:T(8,128)(2,1)S(1)}, bf16[512,1024]{1,0:T(8,128)(2,1)}, u32[]{:S(2)}, u32[]{:S(2)}) collective-permute-start(bf16[512,1024]{1,0:T(8,128)(2,1)S(1)} %get-tuple-element.268), channel_id=1, source_target_pairs={{0,16},{4,20},{8,24},{12,28},{16,0},{20,4},{24,8},{28,12},{1,17},{... | collective-permute-start | bytes 3145736 | tf_op jit(solution)/shard_map/ppermute | solution.py:47
  275.7 47.6 %collective-permute-start.36 = (bf16[512,1024]{1,0:T(8,128)(2,1)S(1)}, bf16[512,1024]{1,0:T(8,128)(2,1)S(1)}, u32[]{:S(2)}, u32[]{:S(2)}) collective-permute-start(bf16[512,1024]{1,0:T(8,128)(2,1)S(1)} %get-tuple-element.269), channel_id=1, source_target_pairs={{0,8},{4,12},{8,0},{12,4},{16,24},{20,28},{24,16},{28,20},{1,9},{5... | collective-permute-start | bytes 3145736 | tf_op jit(solution)/shard_map/ppermute | solution.py:47
  276.1 47.2 %collective-permute-start.37 = (bf16[512,1024]{1,0:T(8,128)(2,1)S(1)}, bf16[512,1024]{1,0:T(8,128)(2,1)}, u32[]{:S(2)}, u32[]{:S(2)}) collective-permute-start(bf16[512,1024]{1,0:T(8,128)(2,1)S(1)} %get-tuple-element.270), channel_id=1, source_target_pairs={{0,16},{4,20},{8,24},{12,28},{16,0},{20,4},{24,8},{28,12},{1,17},{... | collective-permute-start | bytes 3145736 | tf_op jit(solution)/shard_map/ppermute | solution.py:47
  280.3 43.0 %collective-permute-start.42 = (f32[2,1024]{1,0:T(2,128)S(1)}, f32[2,1024]{1,0:T(2,128)S(1)}, u32[]{:S(2)}, u32[]{:S(2)}) collective-permute-start(f32[2,1024]{1,0:T(2,128)S(1)} %pad_maximum_fusion.8), channel_id=1, source_target_pairs={{0,1},{1,0},{2,3},{3,2},{4,5},{5,4},{6,7},{7,6},{8,9},{9,8},{10,11... | collective-permute-start | bytes 24584 | tf_op jit(solution)/shard_map/ppermute | solution.py:35
  323.4 105.8 %reduce-scatter.9.cloned.1.call-start = ((), (), s32[]{:S(2)}) async-start(), calls=%async_computation.9 | async-start | bytes 2621440 | tf_op jit(solution)/shard_map/reduce_scatter | solution.py:678
  323.5 46.4 %collective-permute-start.45 = (bf16[2,1024,512]{2,1,0:T(8,128)(2,1)}, bf16[2,1024,512]{2,1,0:T(8,128)(2,1)}, u32[]{:S(2)}, u32[]{:S(2)}) collective-permute-start(bf16[2,1024,512]{2,1,0:T(8,128)(2,1)} %get-tuple-element.288), channel_id=1, source_target_pairs={{0,4},{4,0},{8,12},{12,8},{16,20},{20,16},{24,28},{28,24},{1,5},{5... | collective-permute-start | bytes 6291464 | tf_op jit(solution)/shard_map/ppermute | solution.py:47
  327.0 42.8 %collective-permute-start.43 = (bf16[512,1024]{1,0:T(8,128)(2,1)S(1)}, bf16[512,1024]{1,0:T(8,128)(2,1)}, u32[]{:S(2)}, u32[]{:S(2)}) collective-permute-start(bf16[512,1024]{1,0:T(8,128)(2,1)S(1)} %add_convert_fusion.4), channel_id=1, source_target_pairs={{0,8},{4,12},{8,0},{12,4},{16,24},{20,28},{24,16},{28,20},{1,9},{5... | collective-permute-start | bytes 3145736 | tf_op jit(solution)/shard_map/ppermute | solution.py:47
  327.4 42.4 %collective-permute-start.44 = (bf16[512,1024]{1,0:T(8,128)(2,1)S(1)}, bf16[512,1024]{1,0:T(8,128)(2,1)}, u32[]{:S(2)}, u32[]{:S(2)}) collective-permute-start(bf16[512,1024]{1,0:T(8,128)(2,1)S(1)} %add_convert_fusion.3), channel_id=1, source_target_pairs={{0,16},{4,20},{8,24},{12,28},{16,0},{20,4},{24,8},{28,12},{1,17},{... | collective-permute-start | bytes 3145736 | tf_op jit(solution)/shard_map/ppermute | solution.py:47
  329.2 40.6 %collective-permute-start.46 = (f32[2,1024]{1,0:T(2,128)S(1)}, f32[2,1024]{1,0:T(2,128)S(1)}, u32[]{:S(2)}, u32[]{:S(2)}) collective-permute-start(f32[2,1024]{1,0:T(2,128)S(1)} %fusion.31), channel_id=1, source_target_pairs={{0,2},{1,3},{2,0},{3,1},{4,6},{5,7},{6,4},{7,5},{8,10},{9,11},{10,... | collective-permute-start | bytes 24584 | tf_op jit(solution)/shard_map/ppermute | solution.py:35
  375.0 117.8 %reduce-scatter.7.cloned.1.call-start = ((), (), s32[]{:S(2)}) async-start(), calls=%async_computation.8 | async-start | bytes 1310720 | tf_op jit(solution)/shard_map/reduce_scatter | solution.py:678
  386.8 16.0 %collective-permute-start.50 = (bf16[256,1024]{1,0:T(8,128)(2,1)}, bf16[256,1024]{1,0:T(8,128)(2,1)}, u32[]{:S(2)}, u32[]{:S(2)}) collective-permute-start(bf16[256,1024]{1,0:T(8,128)(2,1)} %get-tuple-element.312), channel_id=1, source_target_pairs={{0,8},{4,12},{8,0},{12,4},{16,24},{20,28},{24,16},{28,20},{1,9},{5... | collective-permute-start | bytes 1572872 | tf_op jit(solution)/shard_map/ppermute | solution.py:47
  387.1 15.7 %collective-permute-start.51 = (bf16[256,1024]{1,0:T(8,128)(2,1)S(1)}, bf16[256,1024]{1,0:T(8,128)(2,1)}, u32[]{:S(2)}, u32[]{:S(2)}) collective-permute-start(bf16[256,1024]{1,0:T(8,128)(2,1)S(1)} %get-tuple-element.313), channel_id=1, source_target_pairs={{0,16},{4,20},{8,24},{12,28},{16,0},{20,4},{24,8},{28,12},{1,17},{... | collective-permute-start | bytes 1572872 | tf_op jit(solution)/shard_map/ppermute | solution.py:47
  406.5 20.6 %collective-permute-start.54 = (bf16[256,1024]{1,0:T(8,128)(2,1)}, bf16[256,1024]{1,0:T(8,128)(2,1)}, u32[]{:S(2)}, u32[]{:S(2)}) collective-permute-start(bf16[256,1024]{1,0:T(8,128)(2,1)} %get-tuple-element.335), channel_id=1, source_target_pairs={{0,8},{4,12},{8,0},{12,4},{16,24},{20,28},{24,16},{28,20},{1,9},{5... | collective-permute-start | bytes 1572872 | tf_op jit(solution)/shard_map/ppermute | solution.py:47
  407.8 19.3 %collective-permute-start.55 = (bf16[256,1024]{1,0:T(8,128)(2,1)}, bf16[256,1024]{1,0:T(8,128)(2,1)}, u32[]{:S(2)}, u32[]{:S(2)}) collective-permute-start(bf16[256,1024]{1,0:T(8,128)(2,1)} %get-tuple-element.336), channel_id=1, source_target_pairs={{0,16},{4,20},{8,24},{12,28},{16,0},{20,4},{24,8},{28,12},{1,17},{... | collective-permute-start | bytes 1572872 | tf_op jit(solution)/shard_map/ppermute | solution.py:47
  411.3 21.5 %collective-permute-start.58 = (f32[2,1024]{1,0:T(2,128)S(1)}, f32[2,1024]{1,0:T(2,128)S(1)}, u32[]{:S(2)}, u32[]{:S(2)}) collective-permute-start(f32[2,1024]{1,0:T(2,128)S(1)} %add.254), channel_id=1, source_target_pairs={{0,8},{4,12},{8,0},{12,4},{16,24},{20,28},{24,16},{28,20},{1,9},{5... | collective-permute-start | bytes 24584 | tf_op jit(solution)/shard_map/ppermute | solution.py:47
  411.7 14.2 %collective-permute-start.52 = (bf16[128,1024]{1,0:T(8,128)(2,1)}, bf16[128,1024]{1,0:T(8,128)(2,1)S(1)}, u32[]{:S(2)}, u32[]{:S(2)}) collective-permute-start(bf16[128,1024]{1,0:T(8,128)(2,1)} %add_convert_fusion.12), channel_id=1, source_target_pairs={{0,8},{4,12},{8,0},{12,4},{16,24},{20,28},{24,16},{28,20},{1,9},{5... | collective-permute-start | bytes 786440 | tf_op jit(solution)/shard_map/ppermute | solution.py:47
  439.7 28.4 %all-to-all-start = ((bf16[4,128,1024]{2,1,0:T(8,128)(2,1)}), bf16[4,128,1024]{2,1,0:T(8,128)(2,1)}, u32[]{:S(2)}, u32[]{:S(2)}) async-start(bf16[4,128,1024]{2,1,0:T(8,128)(2,1)} %bitcast.53), calls=%async_computation.3 | async-start | bytes 2097152 | tf_op jit(solution)/shard_map/all_to_all | solution.py:752
  443.9 50.0 %reduce-scatter.11.cloned.1.call-start = ((), (), s32[]{:S(2)}) async-start(), calls=%async_computation.10 | async-start | bytes 1310720 | tf_op jit(solution)/shard_map/reduce_scatter | solution.py:678
  473.7 16.1 %collective-permute-start.71 = (bf16[128,1024]{1,0:T(8,128)(2,1)S(1)}, bf16[128,1024]{1,0:T(8,128)(2,1)S(1)}, u32[]{:S(2)}, u32[]{:S(2)}) collective-permute-start(bf16[128,1024]{1,0:T(8,128)(2,1)S(1)} %reduce_sum.112.refs_0_), channel_id=1, source_target_pairs={{0,4},{4,0},{8,12},{12,8},{16,20},{20,16},{24,28},{28,24},{1,5},{5... | collective-permute-start | bytes 786440 | tf_op jit(solution)/shard_map/ppermute | solution.py:47
  (84 other events, 808.5 us)
Sparse Core Ops, SparseCore 0:
  10.1 64.9 all-gather.2
  77.3 46.0 all-gather.4
  323.5 44.5 reduce-scatter.4
  375.1 41.9 reduce-scatter.8
  419.9 26.4 reduce-scatter.6
  468.2 25.6 reduce-scatter.10

commit v5 on v4

--- a/solution.py
+++ b/solution.py
@@ -45,6 +45,13 @@
 
     def swap(self, array, bit):
         return lax.ppermute(array, "seq", [(i, i ^ bit) for i in range(self.size)])
+
+    def higher_exact(self, total):
+        bit = 8
+        while bit < self.size:
+            total = total + self.swap(total, bit)
+            bit *= 2
+        return total
 
     def higher(self, total):
         bit = 8
@@ -678,7 +685,7 @@
         return lax.psum_scatter(part, "tp", scatter_dimension=0, tiled=True)
 
     gains = jnp.stack([gain_grad_one, gain_grad_two])
-    gains_came = across(gains, 1)
+    gains_came = swap(gains, 1)
     held, send, part = pull(0, None)
     diag_x, diag_y, one_x, two_y, send, part, gains_came, *held = fence(
         diag_x, diag_y, one_x, two_y, send, part, gains_came, *held
@@ -686,7 +693,7 @@
     upper_sum = line_sum(part)
     came = [swap(send, 1)]
     gains = gains + gains_came
-    gains_came = across(gains, 2)
+    gains_came = swap(gains, 2)
     two_x = (up(twos[1]) + up(diag_y)).astype(BF)
     one_y = (up(ones[2]) + up(diag_x)).astype(BF)
     two_x, one_y, *held = fence(two_x, one_y, *held)
@@ -698,7 +705,7 @@
     gq, gk, gv = held
     gq_peer = swap(gq[:, core:], 1)
     gains = gains + gains_came
-    gains_came = swap(gains, 1)
+    gains_came = swap(gains, 4)
     part = part.reshape(4, 2, upper // 2, width)
     part_one, part_two = [part[:, n].reshape(rows, width) for n in range(2)]
     lower_one = line_sum(part_one)
@@ -707,7 +714,9 @@
     ff_total = line_sum(ff_total)
     gq_peer, gains_came, send = fence(gq_peer, gains_came, send)
     came.append(swap(send, 1))
-    gains = gains + gains_came
+    gains = plane.higher_exact(gains + gains_came)
+    coarse = lax.reduce_precision(gains, exponent_bits=8, mantissa_bits=7)
+    gains = jnp.concatenate([coarse, gains - coarse, jnp.zeros((12, width), F32)]).astype(BF)
     light = head_grads(
         [gq, gq_peer, attended, attended_peer],
         [],
@@ -734,7 +743,6 @@
     next_x, next_y, *heavy = fence(next_x, next_y, *heavy)
     on_x, on_y = swap(next_x, 2), swap(next_y, 4)
     far_x, far_y = swap(heavy[0], 2), swap(heavy[1], 4)
-    gains_came = swap(gains, 2)
     first = mm(gq, wq, NN) + grad_first
     on_x, on_y, far_x, far_y, first = fence(on_x, on_y, far_x, far_y, first)
     next_x, next_y = second_hop(heavy, far_x, far_y)
@@ -742,13 +750,14 @@
     last_x, last_y = swap(next_x, 2), swap(next_y, 4)
     f_x, f_y = swap(ff_total, 2), swap(ff_total, 4)
     light_mine = mine_of(light, to_x, to_y, on_x, on_y)
-    last_x, last_y, light_mine, gains_came = fence(last_x, last_y, light_mine, gains_came)
-    gains = gains + gains_came
+    last_x, last_y, light_mine = fence(last_x, last_y, light_mine)
     heavy_mine = mine_of(heavy, far_x, far_y, last_x, last_y)
     a_mine = jnp.concatenate([light_mine, heavy_mine], axis=1)
     pairs = a_mine.reshape(2, 2, 4 * qp, width)
     pairs = jnp.where((t & 1) == 1, pairs[:, ::-1], pairs)
-    a_mine = fence(jnp.where((t & 2) == 2, pairs[::-1], pairs).reshape(a_mine.shape))[0]
+    a_mine = jnp.where((t & 2) == 2, pairs[::-1], pairs).reshape(a_mine.shape)
+    gains = jnp.broadcast_to(gains[None], (4, 16, width))
+    a_mine = fence(jnp.concatenate([a_mine, gains], axis=1))[0]
     a_came = lax.all_to_all(a_mine, "tp", split_axis=0, concat_axis=0, tiled=True)
     f_core = [swap(ff_total, 1)]
     f_d1, f_d2 = swap(f_y[:fp], 2), swap(f_x[fp:], 4)
@@ -756,12 +765,9 @@
     a_came, part_two, f_d1, f_d2, b0, b1, b2 = fence(a_came, part_two, f_d1, f_d2, *f_core)
     f_core = [b0, b1, b2]
     lower_two = line_sum(part_two)
-    a_total, gains = fence(jnp.sum(up(a_came), axis=0).astype(BF), gains)
-    gains = gains + swap(gains, 4)
-    bit = 8
-    while bit < seq_size:
-        gains = gains + swap(gains, bit)
-        bit *= 2
+    a_total = fence(jnp.sum(up(a_came[:, : 4 * qp]), axis=0).astype(BF))[0]
+    gains = jnp.sum(up(a_came[:, 4 * qp : 4 * qp + 4]), axis=0)
+    gains = gains[:2] + gains[2:]
     a_four = [a_total, swap(a_total, 2), swap(a_total, 4), swap(a_total, 6)]
     a_core = [swap(a_total, 1)]
     f_core += [swap(f_d1, 1), swap(f_d2, 1)]

time: 512 us -> 515 us (level)
  waiting for transfers between devices: 108 us -> 126 us
  starting transfers between devices: 75.5 us -> 69.1 us
    ppermute x66, waiting for transfers between devices: 70 us -> 78.3 us  [swap(): return lax.ppermute(array, 'seq', [(i, i ^ bit) for i in range(self.size)])]
    ppermute x10 -> x8, starting transfers between devices: 22.3 us -> 15 us  [along(): return lax.ppermute(array, 'tp', pairs)]
    all_to_all x1, waiting for transfers between devices: 1.8 us -> 8.16 us  [per_device(): lax.all_to_all(a_mine, 'tp', split_axis=0, concat_axis=0, tiled=True)]
    unnamed x106 -> x118, local copies, waits for them, and re-layouts: 18.4 us -> 19.8 us
    ppermute x10 -> x8, waiting for transfers between devices: 27.1 us -> 26.4 us  [along(): return lax.ppermute(array, 'tp', pairs)]
  transfers between devices with their start and end apart: 83 -> 81, of which waited for: 29 -> 33; matrix products, arithmetic and copies ran while one was open for 22% -> 20% of each run, Pallas kernels for 31% -> 30%
where the time goes in v5:
time: 515 us; the launch traced here: 506 us
  Pallas kernels  153 us (30%)
  waiting for transfers between devices  126 us (24%)
  starting transfers between devices  69.1 us (13%)
  matrix products  62.9 us (12%)
  local copies, waits for them, and re-layouts  40.7 us (8%)
  other arithmetic  33.9 us (7%)
  between operations  21.6 us (4%)
    ppermute x66, waiting for transfers between devices, swap(): return lax.ppermute(array, 'seq', [(i, i ^ bit) for i in range(self.size)])  78.3 us
    pallas_call x2, Pallas kernels, attention_backward(): pl.pallas_call(backward_kernel, grid=(pairs,), in_specs=[by_pair, pl.Bloc...  71.9 us
    dot_general x14, matrix products, mm(): return lax.dot_general(a, b, dims, preferred_element_type=F32).astype(out)  62.9 us
    ppermute x66, starting transfers between devices, swap(): return lax.ppermute(array, 'seq', [(i, i ^ bit) for i in range(self.size)])  48.2 us
    pallas_call x4, Pallas kernels, attention_forward(): pl.pallas_call(functools.partial(forward_kernel, len(kvs)), grid=(count,)...  31.3 us
    ppermute x8, waiting for transfers between devices, along(): return lax.ppermute(array, 'tp', pairs)  26.4 us
    pallas_call x2, Pallas kernels, head_grads(): pl.pallas_call(functools.partial(head_grads_kernel, many), grid=(2,), in_...  20.9 us
    unnamed x118, local copies, waits for them, and re-layouts  19.8 us
  transfers between devices with their start and end apart: 81, of which 33 were waited for; matrix products, arithmetic and copies ran while one was open for 20% of the time, Pallas kernels for 30%

profile of v5, /device:TPU:0, one launch (start us, length us, event | category | flops | bytes accessed | tf_op | source)
XLA Modules:
  0.0 506.4 jit_solution(12568971363396364393)
XLA Ops:
  12.5 3.0 collective-permute-start
  15.5 2.6 collective-permute-start.1
  24.7 6.7 %collective-permute-done = bf16[128,1024]{1,0:T(8,128)(2,1)S(1)} collective-permute-done((bf16[128,1024]{1,0:T(8,128)(2,1)S(1)}, bf16[128,1024]{1,0:T(8,128)(2,1)S(1)}, u32[]{:S(2)}, u32[]{:S(2)}) %collective-permute-start) | collective-permute-done | bytes 262176 | tf_op jit(solution)/shard_map/ppermute | solution.py:35
  31.3 9.2 %collective-permute-done.1 = bf16[128,1024]{1,0:T(8,128)(2,1)S(1)} collective-permute-done((bf16[128,1024]{1,0:T(8,128)(2,1)S(1)}, bf16[128,1024]{1,0:T(8,128)(2,1)S(1)}, u32[]{:S(2)}, u32[]{:S(2)}) %collective-permute-start.1) | collective-permute-done | bytes 262176 | tf_op jit(solution)/shard_map/ppermute | solution.py:35
  40.6 5.9 %collective-permute-done.2 = bf16[128,1024]{1,0:T(8,128)(2,1)S(1)} collective-permute-done((bf16[128,1024]{1,0:T(8,128)(2,1)S(1)}, bf16[128,1024]{1,0:T(8,128)(2,1)S(1)}, u32[]{:S(2)}, u32[]{:S(2)}) %collective-permute-start.2) | collective-permute-done | bytes 262176 | tf_op jit(solution)/shard_map/ppermute | solution.py:35
  51.8 13.2 %collective-permute-done.3 = bf16[384,1024]{1,0:T(8,128)(2,1)} collective-permute-done((bf16[384,1024]{1,0:T(8,128)(2,1)}, bf16[384,1024]{1,0:T(8,128)(2,1)}, u32[]{:S(2)}, u32[]{:S(2)}) %collective-permute-start.3) | collective-permute-done | bytes 786464 | tf_op jit(solution)/shard_map/ppermute | solution.py:47
  81.3 5.5 %collective-permute-done.5 = bf16[192,1024]{1,0:T(8,128)(2,1)} collective-permute-done((bf16[192,1024]{1,0:T(8,128)(2,1)}, bf16[192,1024]{1,0:T(8,128)(2,1)}, u32[]{:S(2)}, u32[]{:S(2)}) %collective-permute-start.5) | collective-permute-done | bytes 393248 | tf_op jit(solution)/shard_map/ppermute | solution.py:47
  99.4 2.6 fusion.7.q_ref
  102.8 2.5 copy.48
  105.2 9.4 %convert_bitcast_fusion.refs_0_.refs_2_.k_ref.v_ref = bf16[1024,2048]{1,0:T(8,128)(2,1)} fusion(bf16[2048,1024]{1,0:T(8,128)(2,1)} %bitcast.133, bf16[1024,1024]{1,0:T(8,128)(2,1)} %all-gather.3.cloned.1.call-done.refs_4_), kind=kOutput, calls=%fused_computation.20 | convolution fusion | flops 4297064448 | bytes 10485760 | tf_op jit(solution)/shard_map/dot_general | solution.py:31
  114.7 8.8 %all-gather.5.cloned.1.call-done.refs_5_ = bf16[1024,1024]{1,0:T(8,128)(2,1)} async-done(((bf16[256,1024]{1,0:T(8,128)(2,1)}), bf16[1024,1024]{1,0:T(8,128)(2,1)}) %all-gather.5.cloned.1.call-update) | async-done | bytes 2097168 | tf_op jit(solution)/shard_map/all_gather | solution.py:554
  123.4 3.3 collective-permute-start.13
  128.3 9.4 %convolution_convert_fusion.refs_1_.refs_3_.k_ref.v_ref = bf16[1024,2048]{1,0:T(8,128)(2,1)} fusion(bf16[1024,1024]{1,0:T(8,128)(2,1)} %all-gather.5.cloned.1.call-done.refs_5_, bf16[2048,1024]{1,0:T(8,128)(2,1)} %bitcast.134), kind=kOutput, calls=%fused_computation.21 | convolution fusion | flops 4297064448 | bytes 10485760 | tf_op jit(solution)/shard_map/dot_general | solution.py:31
  149.3 7.7 %attention_forward.4 = (bf16[512,1024]{1,0:T(8,128)(2,1)S(1)}, f32[8,2,512]{2,1,0:T(2,128)S(1)}) custom-call(bf16[512,1024]{1,0:T(8,128)(2,1)S(1)} %fusion.7.q_ref, bf16[1024,2048]{1,0:T(8,128)(2,1)S(1)} %copy-done.2, bf16[1024,2048]{1,0:T(8,128)(2,1)S(1)} %copy-done, bf16[1024,2048]{1,0:T(8,128)(2,1)S(1)} %copy-done.2, bf16[1024,2048]{1,0:T(8,128)(2,1)S(1)} %copy-done, ...), custom_call_target="tpu_custom_call" | custom-call | flops 1000000000 | bytes 1000000 | tf_op jit(solution)/shard_map/attention_forward/pallas_call | solution.py:105
  157.1 3.1 collective-permute-done.16
  169.2 7.8 %attention_forward.5 = (bf16[512,1024]{1,0:T(8,128)(2,1)S(1)}, f32[8,2,512]{2,1,0:T(2,128)S(1)}) custom-call(bf16[512,1024]{1,0:T(8,128)(2,1)S(1)} %fusion.7.q_ref, bf16[1024,2048]{1,0:T(8,128)(2,1)S(1)} %copy-done.2, bf16[1024,2048]{1,0:T(8,128)(2,1)S(1)} %copy-done, ...), custom_call_target="tpu_custom_call", output_to_operand_aliasing={{0}: (6, {}), {1}: (7, {})} | custom-call | flops 1000000000 | bytes 1000000 | tf_op jit(solution)/shard_map/attention_forward/pallas_call | solution.py:105
  177.0 4.0 collective-permute-done.20.refs_5_
  188.3 7.8 %attention_forward.6 = (bf16[512,1024]{1,0:T(8,128)(2,1)S(1)}, f32[8,2,512]{2,1,0:T(2,128)S(1)}) custom-call(bf16[512,1024]{1,0:T(8,128)(2,1)S(1)} %fusion.7.q_ref, bf16[1024,2048]{1,0:T(8,128)(2,1)S(1)} %copy-done.3, bf16[1024,2048]{1,0:T(8,128)(2,1)S(1)} %copy-done.1, ...), custom_call_target="tpu_custom_call", output_to_operand_aliasing={{0}: (6, {}), {1}: (7, {})} | custom-call | flops 1000000000 | bytes 1000000 | tf_op jit(solution)/shard_map/attention_forward/pallas_call | solution.py:105
  196.1 2.5 collective-permute-done.24.refs_3_
  202.7 8.0 %attention_forward.7 = (bf16[512,1024]{1,0:T(8,128)(2,1)S(1)}, f32[8,2,512]{2,1,0:T(2,128)S(1)}) custom-call(bf16[512,1024]{1,0:T(8,128)(2,1)S(1)} %fusion.7.q_ref, bf16[1024,2048]{1,0:T(8,128)(2,1)S(1)} %copy-done.3, bf16[1024,2048]{1,0:T(8,128)(2,1)S(1)} %copy-done.1, ...), custom_call_target="tpu_custom_call", output_to_operand_aliasing={{0}: (6, {}), {1}: (7, {})} | custom-call | flops 1000000000 | bytes 1000000 | tf_op jit(solution)/shard_map/attention_forward/pallas_call | solution.py:105
  210.7 2.9 fusion.41
  217.3 6.5 %multiply_convert_fusion.2 = (bf16[512,2048]{1,0:T(8,128)(2,1)S(1)}, f32[512,2048]{1,0:T(8,128)}) fusion(bf16[512,1024]{1,0:T(8,128)(2,1)S(1)} %collective-permute-done.30.right_two_ref, bf16[2048,1024]{1,0:T(8,128)(2,1)S(1)} %get-tuple-element.252), kind=kOutput, calls=%fused_computation.14 | convolution fusion | flops 2169503744 | bytes 11534336 | tf_op jit(solution)/shard_map/dot_general | solution.py:31
  226.3 6.7 %multiply_convert_fusion.3 = (bf16[512,2048]{1,0:T(8,128)(2,1)S(1)}, f32[512,2048]{1,0:T(8,128)}) fusion(bf16[512,1024]{1,0:T(8,128)(2,1)S(1)} %multiply_convert_fusion.5.right_ref, bf16[2048,1024]{1,0:T(8,128)(2,1)S(1)} %get-tuple-element.252), kind=kOutput, calls=%fused_computation.17 | convolution fusion | flops 2169503744 | bytes 11534336 | tf_op jit(solution)/shard_map/dot_general | solution.py:31
  233.0 2.6 fusion.42
  241.3 5.3 %multiply_convert_fusion.left_two_ref = bf16[512,2048]{1,0:T(8,128)(2,1)S(1)} fusion(bf16[512,1024]{1,0:T(8,128)(2,1)S(1)} %collective-permute-done.32.right_two_ref, bf16[2048,1024]{1,0:T(8,128)(2,1)S(1)} %get-tuple-element.253, f32[512,2048]{1,0:T(8,128)S(1)} %copy-done.53), kind=kOutput, calls=%fused_computation.10 | convolution fusion | flops 2174746624 | bytes 11534336 | tf_op jit(solution)/shard_map/dot_general | solution.py:31
  246.6 2.3 convolution_convert_fusion.3
  249.4 5.7 %multiply_convert_fusion.1.left_ref = bf16[512,2048]{1,0:T(8,128)(2,1)S(1)} fusion(bf16[512,1024]{1,0:T(8,128)(2,1)S(1)} %fusion.33.right_ref, bf16[2048,1024]{1,0:T(8,128)(2,1)S(1)} %get-tuple-element.253, f32[512,2048]{1,0:T(8,128)S(1)} %copy-done.54), kind=kOutput, calls=%fused_computation.12 | convolution fusion | flops 2174746624 | bytes 11534336 | tf_op jit(solution)/shard_map/dot_general | solution.py:31
  257.5 5.9 %outer_four.2 = (bf16[512,1024]{1,0:T(8,128)(2,1)S(1)}, bf16[512,1024]{1,0:T(8,128)(2,1)S(1)}, bf16[512,1024]{1,0:T(8,128)(2,1)S(1)}, bf16[512,1024]{1,0:T(8,128)(2,1)S(1)}) custom-call(bf16[512,2048]{1,0:T(8,128)(2,1)S(1)} %get-tuple-element.426.left_ref, bf16[512,1024]{1,0:T(8,128)(2,1)S(1)} %fusion.33.right_ref, ...), custom_call_target="tpu_custom_call" | custom-call | flops 1000000000 | bytes 1000000 | tf_op jit(solution)/shard_map/outer_four/pallas_call | solution.py:417
  263.4 2.9 multiply_reduce_fusion
  268.4 5.9 %outer_four.3 = (bf16[512,1024]{1,0:T(8,128)(2,1)S(1)}, bf16[512,1024]{1,0:T(8,128)(2,1)S(1)}, bf16[512,1024]{1,0:T(8,128)(2,1)S(1)}, bf16[512,1024]{1,0:T(8,128)(2,1)S(1)}) custom-call(bf16[512,2048]{1,0:T(8,128)(2,1)S(1)} %multiply_convert_fusion.1.left_ref, bf16[512,1024]{1,0:T(8,128)(2,1)S(1)} %multiply_convert_fusion.5.right_ref, ...), custom_call_target="tpu_custom_call" | custom-call | flops 1000000000 | bytes 1000000 | tf_op jit(solution)/shard_map/outer_four/pallas_call | solution.py:417
  282.0 36.2 %attention_backward.2 = (f32[512,1024]{1,0:T(8,128)S(1)}, bf16[2048,512]{1,0:T(8,128)(2,1)S(1)}, bf16[2048,512]{1,0:T(8,128)(2,1)}, bf16[2,1024,512]{2,1,0:T(8,128)(2,1)}, bf16[1024,1024]{1,0:T(8,128)(2,1)}) custom-call(bf16[512,1024]{1,0:T(8,128)(2,1)} %copy-done.5, bf16[1024,2048]{1,0:T(8,128)(2,1)} %convert_bitcast_fusion.refs_0_.refs_2_.k_ref.v_ref, ...), custom_call_target="tpu_custom_call" | custom-call | flops 1000000000 | bytes 1000000 | tf_op jit(solution)/shard_map/attention_backward/pallas_call | solution.py:213
  329.7 35.7 %attention_backward.3 = (bf16[512,1024]{1,0:T(8,128)(2,1)S(1)}, bf16[2048,512]{1,0:T(8,128)(2,1)}, bf16[2048,512]{1,0:T(8,128)(2,1)}, bf16[2,1024,512]{2,1,0:T(8,128)(2,1)S(1)}, bf16[1024,1024]{1,0:T(8,128)(2,1)S(1)}) custom-call(bf16[512,1024]{1,0:T(8,128)(2,1)} %copy-done.5, ...), custom_call_target="tpu_custom_call", output_to_operand_aliasing={{1}: (9, {}), {2}: (10, {})} | custom-call | flops 1000000000 | bytes 1000000 | tf_op jit(solution)/shard_map/attention_backward/pallas_call | solution.py:213
  366.7 5.2 %totals.1 = bf16[1024,1024]{1,0:T(8,128)(2,1)} custom-call(s32[1]{0:T(128)} %bitcast.47.at_ref, bf16[512,1024]{1,0:T(8,128)(2,1)} %copy-done.13, bf16[512,1024]{1,0:T(8,128)(2,1)} %copy-done.29, bf16[512,1024]{1,0:T(8,128)(2,1)} %collective-permute-done.44.refs_2_, bf16[512,1024]{1,0:T(8,128)(2,1)} %copy-done.12, ...), custom_call_target="tpu_custom_call" | custom-call | flops 1000000000 | bytes 1000000 | tf_op jit(solution)/shard_map/totals/pallas_call | solution.py:381
  375.9 6.5 %head_grads.2 = (bf16[256,1024]{1,0:T(8,128)(2,1)}, bf16[256,1024]{1,0:T(8,128)(2,1)}, bf16[128,1024]{1,0:T(8,128)(2,1)S(1)}, bf16[128,1024]{1,0:T(8,128)(2,1)S(1)}, bf16[256,1024]{1,0:T(8,128)(2,1)S(1)}) custom-call(bf16[512,1024]{1,0:T(8,128)(2,1)} %copy-done.8, bf16[512,512]{1,0:T(8,128)(2,1)} %collective-permute-done.47.refs_1_, ...), custom_call_target="tpu_custom_call" | custom-call | flops 1000000000 | bytes 1000000 | tf_op jit(solution)/shard_map/head_grads/pallas_call | solution.py:318
  387.1 14.5 %head_grads.3 = (bf16[256,1024]{1,0:T(8,128)(2,1)S(1)}, bf16[256,1024]{1,0:T(8,128)(2,1)S(1)}, bf16[128,1024]{1,0:T(8,128)(2,1)S(1)}, bf16[128,1024]{1,0:T(8,128)(2,1)S(1)}, bf16[256,1024]{1,0:T(8,128)(2,1)S(1)}) custom-call(bf16[2048,512]{1,0:T(8,128)(2,1)} %get-tuple-element.311.refs_0_, bf16[2048,512]{1,0:T(8,128)(2,1)} %get-tuple-element.312.refs_1_, ...), custom_call_target="tpu_custom_call" | custom-call | flops 1000000000 | bytes 1000000 | tf_op jit(solution)/shard_map/head_grads/pallas_call | solution.py:318
  407.8 2.6 convolution_add_fusion
  410.4 12.7 %collective-permute-done.52 = bf16[128,1024]{1,0:T(8,128)(2,1)S(1)} collective-permute-done((bf16[128,1024]{1,0:T(8,128)(2,1)S(1)}, bf16[128,1024]{1,0:T(8,128)(2,1)S(1)}, u32[]{:S(2)}, u32[]{:S(2)}) %collective-permute-start.52) | collective-permute-done | bytes 262176 | tf_op jit(solution)/shard_map/ppermute | solution.py:47
  427.8 4.1 collective-permute-done.56
  434.8 5.7 %all-to-all-start = ((bf16[4,144,1024]{2,1,0:T(8,128)(2,1)}), bf16[4,144,1024]{2,1,0:T(8,128)(2,1)}, u32[]{:S(2)}, u32[]{:S(2)}) async-start(bf16[4,144,1024]{2,1,0:T(8,128)(2,1)} %pad_maximum_fusion), calls=%async_computation.3 | async-start | bytes 2359296 | tf_op jit(solution)/shard_map/all_to_all | solution.py:761
  442.7 9.2 %collective-permute-done.60.refs_2_ = bf16[256,1024]{1,0:T(8,128)(2,1)S(1)} collective-permute-done((bf16[256,1024]{1,0:T(8,128)(2,1)S(1)}, bf16[256,1024]{1,0:T(8,128)(2,1)S(1)}, u32[]{:S(2)}, u32[]{:S(2)}) %collective-permute-start.60) | collective-permute-done | bytes 524320 | tf_op jit(solution)/shard_map/ppermute | solution.py:47
  455.1 6.4 %collective-permute-done.59.refs_6_ = bf16[128,1024]{1,0:T(8,128)(2,1)} collective-permute-done((bf16[128,1024]{1,0:T(8,128)(2,1)S(1)}, bf16[128,1024]{1,0:T(8,128)(2,1)}, u32[]{:S(2)}, u32[]{:S(2)}) %collective-permute-start.59) | collective-permute-done | bytes 262176 | tf_op jit(solution)/shard_map/ppermute | solution.py:47
  462.3 8.2 %all-to-all-done = bf16[4,144,1024]{2,1,0:T(8,128)(2,1)} async-done(((bf16[4,144,1024]{2,1,0:T(8,128)(2,1)}), bf16[4,144,1024]{2,1,0:T(8,128)(2,1)}, u32[]{:S(2)}, u32[]{:S(2)}) %all-to-all-start) | async-done | bytes 1179680 | tf_op jit(solution)/shard_map/all_to_all | solution.py:761
  477.0 3.5 placed.2
  480.4 2.4 placed.3
  482.8 4.8 collective-permute-done.68.refs_4_
  489.9 3.0 heads_placed.1
  492.9 3.9 reduce-scatter.11.cloned.1.call-done
  496.8 2.4 add_convert_fusion.2
  (355 shorter events, 148.3 us)
Async XLA Ops:
  7.2 98.1 %all-gather.3.cloned.1.call-start = ((), (), s32[]{:S(2)}) async-start(), calls=%async_computation.5 | async-start | bytes 2621440 | tf_op jit(solution)/shard_map/all_gather | solution.py:554
  9.5 113.9 %all-gather.5.cloned.1.call-start = ((), (), s32[]{:S(2)}) async-start(), calls=%async_computation.6 | async-start | bytes 2621440 | tf_op jit(solution)/shard_map/all_gather | solution.py:554
  12.5 18.8 %collective-permute-start = (bf16[128,1024]{1,0:T(8,128)(2,1)S(1)}, bf16[128,1024]{1,0:T(8,128)(2,1)S(1)}, u32[]{:S(2)}, u32[]{:S(2)}) collective-permute-start(bf16[128,1024]{1,0:T(8,128)(2,1)S(1)} %bitcast.159), channel_id=1, source_target_pairs={{0,1},{1,0},{2,3},{3,2},{4,5},{5,4},{6,7},{7,6},{8,9},{9,8},{10,11... | collective-permute-start | bytes 786440 | tf_op jit(solution)/shard_map/ppermute | solution.py:35
  15.5 25.1 %collective-permute-start.1 = (bf16[128,1024]{1,0:T(8,128)(2,1)S(1)}, bf16[128,1024]{1,0:T(8,128)(2,1)S(1)}, u32[]{:S(2)}, u32[]{:S(2)}) collective-permute-start(bf16[128,1024]{1,0:T(8,128)(2,1)S(1)} %bitcast.160), channel_id=1, source_target_pairs={{0,2},{1,3},{2,0},{3,1},{4,6},{5,7},{6,4},{7,5},{8,10},{9,11},{10,... | collective-permute-start | bytes 786440 | tf_op jit(solution)/shard_map/ppermute | solution.py:35
  18.1 28.3 %collective-permute-start.2 = (bf16[128,1024]{1,0:T(8,128)(2,1)S(1)}, bf16[128,1024]{1,0:T(8,128)(2,1)S(1)}, u32[]{:S(2)}, u32[]{:S(2)}) collective-permute-start(bf16[128,1024]{1,0:T(8,128)(2,1)S(1)} %bitcast.161), channel_id=1, source_target_pairs={{0,3},{1,2},{2,1},{3,0},{4,7},{5,6},{6,5},{7,4},{8,11},{9,10},{10,... | collective-permute-start | bytes 786440 | tf_op jit(solution)/shard_map/ppermute | solution.py:35
  48.6 16.4 %collective-permute-start.3 = (bf16[384,1024]{1,0:T(8,128)(2,1)}, bf16[384,1024]{1,0:T(8,128)(2,1)}, u32[]{:S(2)}, u32[]{:S(2)}) collective-permute-start(bf16[384,1024]{1,0:T(8,128)(2,1)} %constant_dynamic-update-slice_fusion), channel_id=1, source_target_pairs={{0,8},{4,12},{8,0},{12,4},{16,24},{20,28},{24,16},{28,20},{1,9},{5... | collective-permute-start | bytes 2359304 | tf_op jit(solution)/shard_map/ppermute | solution.py:47
  50.1 16.2 %collective-permute-start.4 = (bf16[384,1024]{1,0:T(8,128)(2,1)}, bf16[384,1024]{1,0:T(8,128)(2,1)}, u32[]{:S(2)}, u32[]{:S(2)}) collective-permute-start(bf16[384,1024]{1,0:T(8,128)(2,1)} %constant_dynamic-update-slice_fusion), channel_id=1, source_target_pairs={{0,16},{4,20},{8,24},{12,28},{16,0},{20,4},{24,8},{28,12},{1,17},{... | collective-permute-start | bytes 2359304 | tf_op jit(solution)/shard_map/ppermute | solution.py:47
  51.7 320.2 %reduce-scatter.5.cloned.1.call-start = ((), (), s32[]{:S(2)}) async-start(), calls=%async_computation.7 | async-start | bytes 2621440 | tf_op jit(solution)/shard_map/reduce_scatter | solution.py:685
  66.3 20.7 %collective-permute-start.7 = (bf16[384,1024]{1,0:T(8,128)(2,1)}, bf16[384,1024]{1,0:T(8,128)(2,1)}, u32[]{:S(2)}, u32[]{:S(2)}) collective-permute-start(bf16[384,1024]{1,0:T(8,128)(2,1)} %constant_dynamic-update-slice_fusion), channel_id=1, source_target_pairs={{0,4},{4,0},{8,12},{12,8},{16,20},{20,16},{24,28},{28,24},{1,5},{5... | collective-permute-start | bytes 2359304 | tf_op jit(solution)/shard_map/ppermute | solution.py:47
  66.3 20.7 %collective-permute-start.8 = (bf16[384,1024]{1,0:T(8,128)(2,1)}, bf16[384,1024]{1,0:T(8,128)(2,1)}, u32[]{:S(2)}, u32[]{:S(2)}) collective-permute-start(bf16[384,1024]{1,0:T(8,128)(2,1)} %collective-permute-done.3), channel_id=1, source_target_pairs={{0,4},{4,0},{8,12},{12,8},{16,20},{20,16},{24,28},{28,24},{1,5},{5... | collective-permute-start | bytes 2359304 | tf_op jit(solution)/shard_map/ppermute | solution.py:47
  66.8 20.2 %collective-permute-start.9 = (bf16[384,1024]{1,0:T(8,128)(2,1)}, bf16[384,1024]{1,0:T(8,128)(2,1)}, u32[]{:S(2)}, u32[]{:S(2)}) collective-permute-start(bf16[384,1024]{1,0:T(8,128)(2,1)} %collective-permute-done.4), channel_id=1, source_target_pairs={{0,4},{4,0},{8,12},{12,8},{16,20},{20,16},{24,28},{28,24},{1,5},{5... | collective-permute-start | bytes 2359304 | tf_op jit(solution)/shard_map/ppermute | solution.py:47
  86.8 27.9 %collective-permute-start.12 = (bf16[512,1024]{1,0:T(8,128)(2,1)}, bf16[512,1024]{1,0:T(8,128)(2,1)S(1)}, u32[]{:S(2)}, u32[]{:S(2)}) collective-permute-start(bf16[512,1024]{1,0:T(8,128)(2,1)} %refs_2_.1), channel_id=1, source_target_pairs={{0,4},{4,0},{8,12},{12,8},{16,20},{20,16},{24,28},{28,24},{1,5},{5... | collective-permute-start | bytes 3145736 | tf_op jit(solution)/shard_map/ppermute | solution.py:47
  123.4 15.9 %collective-permute-start.13 = (bf16[256,1024]{1,0:T(8,128)(2,1)}, bf16[256,1024]{1,0:T(8,128)(2,1)}, u32[]{:S(2)}, u32[]{:S(2)}) collective-permute-start(bf16[256,1024]{1,0:T(8,128)(2,1)} %pad_maximum_fusion.6), channel_id=1, source_target_pairs={{0,1},{1,0},{2,3},{3,2},{4,5},{5,4},{6,7},{7,6},{8,9},{9,8},{10,11... | collective-permute-start | bytes 1572872 | tf_op jit(solution)/shard_map/ppermute | solution.py:35
  139.3 17.8 %collective-permute-start.15 = (bf16[256,1024]{1,0:T(8,128)(2,1)}, bf16[256,1024]{1,0:T(8,128)(2,1)}, u32[]{:S(2)}, u32[]{:S(2)}) collective-permute-start(bf16[256,1024]{1,0:T(8,128)(2,1)} %collective-permute-done.13.refs_2_), channel_id=1, source_target_pairs={{1,2},{2,1},{5,6},{6,5},{9,10},{10,9},{13,14},{14,13},{17,18},{18,... | collective-permute-start | bytes 1572872 | tf_op jit(solution)/shard_map/ppermute | solution.py:35
  140.8 19.4 %collective-permute-start.16 = (bf16[256,1024]{1,0:T(8,128)(2,1)}, bf16[256,1024]{1,0:T(8,128)(2,1)}, u32[]{:S(2)}, u32[]{:S(2)}) collective-permute-start(bf16[256,1024]{1,0:T(8,128)(2,1)} %collective-permute-done.14), channel_id=1, source_target_pairs={{1,0},{2,3},{5,4},{6,7},{9,8},{10,11},{13,12},{14,15},{17,16},{18,... | collective-permute-start | bytes 1572872 | tf_op jit(solution)/shard_map/ppermute | solution.py:35
  142.0 18.2 %collective-permute-start.17 = (bf16[256,1024]{1,0:T(8,128)(2,1)}, bf16[256,1024]{1,0:T(8,128)(2,1)}, u32[]{:S(2)}, u32[]{:S(2)}) collective-permute-start(bf16[256,1024]{1,0:T(8,128)(2,1)} %collective-permute-done.13.refs_2_), channel_id=1, source_target_pairs={{0,8},{4,12},{8,0},{12,4},{16,24},{20,28},{24,16},{28,20},{1,9},{5... | collective-permute-start | bytes 1572872 | tf_op jit(solution)/shard_map/ppermute | solution.py:47
  143.4 16.8 %collective-permute-start.18 = (bf16[256,1024]{1,0:T(8,128)(2,1)}, bf16[256,1024]{1,0:T(8,128)(2,1)}, u32[]{:S(2)}, u32[]{:S(2)}) collective-permute-start(bf16[256,1024]{1,0:T(8,128)(2,1)} %collective-permute-done.13.refs_2_), channel_id=1, source_target_pairs={{0,16},{4,20},{8,24},{12,28},{16,0},{20,4},{24,8},{28,12},{1,17},{... | collective-permute-start | bytes 1572872 | tf_op jit(solution)/shard_map/ppermute | solution.py:47
  160.2 21.5 %collective-permute-start.19 = (bf16[256,1024]{1,0:T(8,128)(2,1)}, bf16[256,1024]{1,0:T(8,128)(2,1)S(1)}, u32[]{:S(2)}, u32[]{:S(2)}) collective-permute-start(bf16[256,1024]{1,0:T(8,128)(2,1)} %collective-permute-done.15), channel_id=1, source_target_pairs={{1,0},{2,3},{5,4},{6,7},{9,8},{10,11},{13,12},{14,15},{17,16},{18,... | collective-permute-start | bytes 1572872 | tf_op jit(solution)/shard_map/ppermute | solution.py:35
  163.0 18.7 %collective-permute-start.22 = (bf16[256,1024]{1,0:T(8,128)(2,1)S(1)}, bf16[256,1024]{1,0:T(8,128)(2,1)S(1)}, u32[]{:S(2)}, u32[]{:S(2)}) collective-permute-start(bf16[256,1024]{1,0:T(8,128)(2,1)S(1)} %broadcast_select_fusion.1.refs_0_), channel_id=1, source_target_pairs={{0,8},{4,12},{8,0},{12,4},{16,24},{20,28},{24,16},{28,20},{1,9},{5... | collective-permute-start | bytes 1572872 | tf_op jit(solution)/shard_map/ppermute | solution.py:47
  164.3 17.5 %collective-permute-start.23 = (bf16[256,1024]{1,0:T(8,128)(2,1)S(1)}, bf16[256,1024]{1,0:T(8,128)(2,1)S(1)}, u32[]{:S(2)}, u32[]{:S(2)}) collective-permute-start(bf16[256,1024]{1,0:T(8,128)(2,1)S(1)} %broadcast_select_fusion.1.refs_0_), channel_id=1, source_target_pairs={{0,16},{4,20},{8,24},{12,28},{16,0},{20,4},{24,8},{28,12},{1,17},{... | collective-permute-start | bytes 1572872 | tf_op jit(solution)/shard_map/ppermute | solution.py:47
  166.8 14.2 %collective-permute-start.20 = (bf16[128,1024]{1,0:T(8,128)(2,1)S(1)}, bf16[128,1024]{1,0:T(8,128)(2,1)S(1)}, u32[]{:S(2)}, u32[]{:S(2)}) collective-permute-start(bf16[128,1024]{1,0:T(8,128)(2,1)S(1)} %slice.149), channel_id=1, source_target_pairs={{0,8},{4,12},{8,0},{12,4},{16,24},{20,28},{24,16},{28,20},{1,9},{5... | collective-permute-start | bytes 786440 | tf_op jit(solution)/shard_map/ppermute | solution.py:47
  181.8 18.3 %collective-permute-start.26 = (bf16[256,1024]{1,0:T(8,128)(2,1)S(1)}, bf16[256,1024]{1,0:T(8,128)(2,1)S(1)}, u32[]{:S(2)}, u32[]{:S(2)}) collective-permute-start(bf16[256,1024]{1,0:T(8,128)(2,1)S(1)} %broadcast_select_fusion.refs_5_), channel_id=1, source_target_pairs={{0,8},{4,12},{8,0},{12,4},{16,24},{20,28},{24,16},{28,20},{1,9},{5... | collective-permute-start | bytes 1572872 | tf_op jit(solution)/shard_map/ppermute | solution.py:47
  182.9 17.2 %collective-permute-start.27 = (bf16[256,1024]{1,0:T(8,128)(2,1)S(1)}, bf16[256,1024]{1,0:T(8,128)(2,1)S(1)}, u32[]{:S(2)}, u32[]{:S(2)}) collective-permute-start(bf16[256,1024]{1,0:T(8,128)(2,1)S(1)} %broadcast_select_fusion.refs_5_), channel_id=1, source_target_pairs={{0,16},{4,20},{8,24},{12,28},{16,0},{20,4},{24,8},{28,12},{1,17},{... | collective-permute-start | bytes 1572872 | tf_op jit(solution)/shard_map/ppermute | solution.py:47
  184.7 13.9 %collective-permute-start.24 = (bf16[128,1024]{1,0:T(8,128)(2,1)S(1)}, bf16[128,1024]{1,0:T(8,128)(2,1)S(1)}, u32[]{:S(2)}, u32[]{:S(2)}) collective-permute-start(bf16[128,1024]{1,0:T(8,128)(2,1)S(1)} %slice.151), channel_id=1, source_target_pairs={{0,8},{4,12},{8,0},{12,4},{16,24},{20,28},{24,16},{28,20},{1,9},{5... | collective-permute-start | bytes 786440 | tf_op jit(solution)/shard_map/ppermute | solution.py:47
  185.6 14.6 %collective-permute-start.25 = (bf16[128,1024]{1,0:T(8,128)(2,1)S(1)}, bf16[128,1024]{1,0:T(8,128)(2,1)S(1)}, u32[]{:S(2)}, u32[]{:S(2)}) collective-permute-start(bf16[128,1024]{1,0:T(8,128)(2,1)S(1)} %slice.152), channel_id=1, source_target_pairs={{0,16},{4,20},{8,24},{12,28},{16,0},{20,4},{24,8},{28,12},{1,17},{... | collective-permute-start | bytes 786440 | tf_op jit(solution)/shard_map/ppermute | solution.py:47
  238.8 37.5 %collective-permute-start.41 = (bf16[1024,1024]{1,0:T(8,128)(2,1)}, bf16[1024,1024]{1,0:T(8,128)(2,1)}, u32[]{:S(2)}, u32[]{:S(2)}) collective-permute-start(bf16[1024,1024]{1,0:T(8,128)(2,1)} %all-gather.5.cloned.1.call-done.refs_5_), channel_id=1, source_target_pairs={{0,4},{4,0},{8,12},{12,8},{16,20},{20,16},{24,28},{28,24},{1,5},{5... | collective-permute-start | bytes 6291464 | tf_op jit(solution)/shard_map/ppermute | solution.py:47
  239.0 37.1 %collective-permute-start.40 = (bf16[1024,1024]{1,0:T(8,128)(2,1)}, bf16[1024,1024]{1,0:T(8,128)(2,1)}, u32[]{:S(2)}, u32[]{:S(2)}) collective-permute-start(bf16[1024,1024]{1,0:T(8,128)(2,1)} %all-gather.3.cloned.1.call-done.refs_4_), channel_id=1, source_target_pairs={{0,4},{4,0},{8,12},{12,8},{16,20},{20,16},{24,28},{28,24},{1,5},{5... | collective-permute-start | bytes 6291464 | tf_op jit(solution)/shard_map/ppermute | solution.py:47
  240.2 36.4 %collective-permute-start.39 = (bf16[512,512]{1,0:T(8,128)(2,1)}, bf16[512,512]{1,0:T(8,128)(2,1)S(1)}, u32[]{:S(2)}, u32[]{:S(2)}) collective-permute-start(bf16[512,512]{1,0:T(8,128)(2,1)} %slice.156), channel_id=1, source_target_pairs={{0,4},{4,0},{8,12},{12,8},{16,20},{20,16},{24,28},{28,24},{1,5},{5... | collective-permute-start | bytes 1572872 | tf_op jit(solution)/shard_map/ppermute | solution.py:47
  249.0 14.5 %collective-permute-start.33 = (bf16[512,1024]{1,0:T(8,128)(2,1)S(1)}, bf16[512,1024]{1,0:T(8,128)(2,1)S(1)}, u32[]{:S(2)}, u32[]{:S(2)}) collective-permute-start(bf16[512,1024]{1,0:T(8,128)(2,1)S(1)} %convolution_convert_fusion.3), channel_id=1, source_target_pairs={{0,4},{4,0},{8,12},{12,8},{16,20},{20,16},{24,28},{28,24},{1,5},{5... | collective-permute-start | bytes 3145736 | tf_op jit(solution)/shard_map/ppermute | solution.py:47
  274.4 46.6 %collective-permute-start.34 = (bf16[512,1024]{1,0:T(8,128)(2,1)S(1)}, bf16[512,1024]{1,0:T(8,128)(2,1)S(1)}, u32[]{:S(2)}, u32[]{:S(2)}) collective-permute-start(bf16[512,1024]{1,0:T(8,128)(2,1)S(1)} %get-tuple-element.264), channel_id=1, source_target_pairs={{0,8},{4,12},{8,0},{12,4},{16,24},{20,28},{24,16},{28,20},{1,9},{5... | collective-permute-start | bytes 3145736 | tf_op jit(solution)/shard_map/ppermute | solution.py:47
  276.1 44.8 %collective-permute-start.35 = (bf16[512,1024]{1,0:T(8,128)(2,1)S(1)}, bf16[512,1024]{1,0:T(8,128)(2,1)S(1)}, u32[]{:S(2)}, u32[]{:S(2)}) collective-permute-start(bf16[512,1024]{1,0:T(8,128)(2,1)S(1)} %get-tuple-element.265), channel_id=1, source_target_pairs={{0,16},{4,20},{8,24},{12,28},{16,0},{20,4},{24,8},{28,12},{1,17},{... | collective-permute-start | bytes 3145736 | tf_op jit(solution)/shard_map/ppermute | solution.py:47
  276.4 46.0 %collective-permute-start.36 = (bf16[512,1024]{1,0:T(8,128)(2,1)S(1)}, bf16[512,1024]{1,0:T(8,128)(2,1)S(1)}, u32[]{:S(2)}, u32[]{:S(2)}) collective-permute-start(bf16[512,1024]{1,0:T(8,128)(2,1)S(1)} %get-tuple-element.266), channel_id=1, source_target_pairs={{0,8},{4,12},{8,0},{12,4},{16,24},{20,28},{24,16},{28,20},{1,9},{5... | collective-permute-start | bytes 3145736 | tf_op jit(solution)/shard_map/ppermute | solution.py:47
  276.6 47.1 %collective-permute-start.37 = (bf16[512,1024]{1,0:T(8,128)(2,1)S(1)}, bf16[512,1024]{1,0:T(8,128)(2,1)S(1)}, u32[]{:S(2)}, u32[]{:S(2)}) collective-permute-start(bf16[512,1024]{1,0:T(8,128)(2,1)S(1)} %get-tuple-element.267), channel_id=1, source_target_pairs={{0,16},{4,20},{8,24},{12,28},{16,0},{20,4},{24,8},{28,12},{1,17},{... | collective-permute-start | bytes 3145736 | tf_op jit(solution)/shard_map/ppermute | solution.py:47
  280.8 40.1 %collective-permute-start.42 = (f32[2,1024]{1,0:T(2,128)S(1)}, f32[2,1024]{1,0:T(2,128)S(1)}, u32[]{:S(2)}, u32[]{:S(2)}) collective-permute-start(f32[2,1024]{1,0:T(2,128)S(1)} %pad_maximum_fusion.9), channel_id=1, source_target_pairs={{0,4},{4,0},{8,12},{12,8},{16,20},{20,16},{24,28},{28,24},{1,5},{5... | collective-permute-start | bytes 24584 | tf_op jit(solution)/shard_map/ppermute | solution.py:47
  324.8 100.1 %reduce-scatter.9.cloned.1.call-start = ((), (), s32[]{:S(2)}) async-start(), calls=%async_computation.9 | async-start | bytes 2621440 | tf_op jit(solution)/shard_map/reduce_scatter | solution.py:685
  324.8 41.9 %collective-permute-start.45 = (bf16[2,1024,512]{2,1,0:T(8,128)(2,1)}, bf16[2,1024,512]{2,1,0:T(8,128)(2,1)}, u32[]{:S(2)}, u32[]{:S(2)}) collective-permute-start(bf16[2,1024,512]{2,1,0:T(8,128)(2,1)} %get-tuple-element.285), channel_id=1, source_target_pairs={{0,4},{4,0},{8,12},{12,8},{16,20},{20,16},{24,28},{28,24},{1,5},{5... | collective-permute-start | bytes 6291464 | tf_op jit(solution)/shard_map/ppermute | solution.py:47
  327.0 39.6 %collective-permute-start.43 = (bf16[512,1024]{1,0:T(8,128)(2,1)S(1)}, bf16[512,1024]{1,0:T(8,128)(2,1)}, u32[]{:S(2)}, u32[]{:S(2)}) collective-permute-start(bf16[512,1024]{1,0:T(8,128)(2,1)S(1)} %add_convert_fusion.4), channel_id=1, source_target_pairs={{0,8},{4,12},{8,0},{12,4},{16,24},{20,28},{24,16},{28,20},{1,9},{5... | collective-permute-start | bytes 3145736 | tf_op jit(solution)/shard_map/ppermute | solution.py:47
  328.3 38.3 %collective-permute-start.44 = (bf16[512,1024]{1,0:T(8,128)(2,1)S(1)}, bf16[512,1024]{1,0:T(8,128)(2,1)}, u32[]{:S(2)}, u32[]{:S(2)}) collective-permute-start(bf16[512,1024]{1,0:T(8,128)(2,1)S(1)} %add_convert_fusion.3), channel_id=1, source_target_pairs={{0,16},{4,20},{8,24},{12,28},{16,0},{20,4},{24,8},{28,12},{1,17},{... | collective-permute-start | bytes 3145736 | tf_op jit(solution)/shard_map/ppermute | solution.py:47
  328.6 38.0 %collective-permute-start.46 = (f32[2,1024]{1,0:T(2,128)S(1)}, f32[2,1024]{1,0:T(2,128)S(1)}, u32[]{:S(2)}, u32[]{:S(2)}) collective-permute-start(f32[2,1024]{1,0:T(2,128)S(1)} %fusion.32), channel_id=1, source_target_pairs={{0,8},{4,12},{8,0},{12,4},{16,24},{20,28},{24,16},{28,20},{1,9},{5... | collective-permute-start | bytes 24584 | tf_op jit(solution)/shard_map/ppermute | solution.py:47
  371.9 121.0 %reduce-scatter.7.cloned.1.call-start = ((), (), s32[]{:S(2)}) async-start(), calls=%async_computation.8 | async-start | bytes 1310720 | tf_op jit(solution)/shard_map/reduce_scatter | solution.py:685
  382.4 19.1 %collective-permute-start.50 = (bf16[256,1024]{1,0:T(8,128)(2,1)}, bf16[256,1024]{1,0:T(8,128)(2,1)}, u32[]{:S(2)}, u32[]{:S(2)}) collective-permute-start(bf16[256,1024]{1,0:T(8,128)(2,1)} %get-tuple-element.309), channel_id=1, source_target_pairs={{0,8},{4,12},{8,0},{12,4},{16,24},{20,28},{24,16},{28,20},{1,9},{5... | collective-permute-start | bytes 1572872 | tf_op jit(solution)/shard_map/ppermute | solution.py:47
  383.5 18.0 %collective-permute-start.51 = (bf16[256,1024]{1,0:T(8,128)(2,1)}, bf16[256,1024]{1,0:T(8,128)(2,1)}, u32[]{:S(2)}, u32[]{:S(2)}) collective-permute-start(bf16[256,1024]{1,0:T(8,128)(2,1)} %get-tuple-element.310), channel_id=1, source_target_pairs={{0,16},{4,20},{8,24},{12,28},{16,0},{20,4},{24,8},{28,12},{1,17},{... | collective-permute-start | bytes 1572872 | tf_op jit(solution)/shard_map/ppermute | solution.py:47
  403.6 20.0 %collective-permute-start.54 = (bf16[256,1024]{1,0:T(8,128)(2,1)S(1)}, bf16[256,1024]{1,0:T(8,128)(2,1)S(1)}, u32[]{:S(2)}, u32[]{:S(2)}) collective-permute-start(bf16[256,1024]{1,0:T(8,128)(2,1)S(1)} %get-tuple-element.332), channel_id=1, source_target_pairs={{0,8},{4,12},{8,0},{12,4},{16,24},{20,28},{24,16},{28,20},{1,9},{5... | collective-permute-start | bytes 1572872 | tf_op jit(solution)/shard_map/ppermute | solution.py:47
  404.5 19.1 %collective-permute-start.55 = (bf16[256,1024]{1,0:T(8,128)(2,1)S(1)}, bf16[256,1024]{1,0:T(8,128)(2,1)S(1)}, u32[]{:S(2)}, u32[]{:S(2)}) collective-permute-start(bf16[256,1024]{1,0:T(8,128)(2,1)S(1)} %get-tuple-element.333), channel_id=1, source_target_pairs={{0,16},{4,20},{8,24},{12,28},{16,0},{20,4},{24,8},{28,12},{1,17},{... | collective-permute-start | bytes 1572872 | tf_op jit(solution)/shard_map/ppermute | solution.py:47
  405.0 18.0 %collective-permute-start.52 = (bf16[128,1024]{1,0:T(8,128)(2,1)S(1)}, bf16[128,1024]{1,0:T(8,128)(2,1)S(1)}, u32[]{:S(2)}, u32[]{:S(2)}) collective-permute-start(bf16[128,1024]{1,0:T(8,128)(2,1)S(1)} %add_convert_fusion.12), channel_id=1, source_target_pairs={{0,8},{4,12},{8,0},{12,4},{16,24},{20,28},{24,16},{28,20},{1,9},{5... | collective-permute-start | bytes 786440 | tf_op jit(solution)/shard_map/ppermute | solution.py:47
  406.0 17.6 %collective-permute-start.53 = (bf16[128,1024]{1,0:T(8,128)(2,1)S(1)}, bf16[128,1024]{1,0:T(8,128)(2,1)S(1)}, u32[]{:S(2)}, u32[]{:S(2)}) collective-permute-start(bf16[128,1024]{1,0:T(8,128)(2,1)S(1)} %add_convert_fusion.11), channel_id=1, source_target_pairs={{0,16},{4,20},{8,24},{12,28},{16,0},{20,4},{24,8},{28,12},{1,17},{... | collective-permute-start | bytes 786440 | tf_op jit(solution)/shard_map/ppermute | solution.py:47
  434.8 35.6 %all-to-all-start = ((bf16[4,144,1024]{2,1,0:T(8,128)(2,1)}), bf16[4,144,1024]{2,1,0:T(8,128)(2,1)}, u32[]{:S(2)}, u32[]{:S(2)}) async-start(bf16[4,144,1024]{2,1,0:T(8,128)(2,1)} %pad_maximum_fusion), calls=%async_computation.3 | async-start | bytes 2359296 | tf_op jit(solution)/shard_map/all_to_all | solution.py:761
  440.5 56.3 %reduce-scatter.11.cloned.1.call-start = ((), (), s32[]{:S(2)}) async-start(), calls=%async_computation.10 | async-start | bytes 1310720 | tf_op jit(solution)/shard_map/reduce_scatter | solution.py:685
  (88 other events, 792.5 us)
Sparse Core Ops, SparseCore 0:
  10.1 64.9 all-gather.2
  77.3 46.0 all-gather.4
  324.9 45.1 reduce-scatter.4
  372.9 44.4 reduce-scatter.8
  420.0 27.9 reduce-scatter.6
  470.6 26.1 reduce-scatter.10

commit v6 on v5

--- a/solution.py
+++ b/solution.py
@@ -586,24 +586,23 @@
     wq, wk, wv, wo = [w_attn[n] for n in range(4)]
     wkv = w_attn[1:3].reshape(2 * width, width)
 
+    wq, wkv, ff_own, up_own, down_own = fence(wq, wkv, ff_own, up_own, down_own)
+    f_one, f_far = along(ff_own, PAIR), along(ff_own, MIDDLE)
     q = mm(tokens, wq, NT, BF)
-    tokens_peer = swap(tokens, 1)
     upper_kv = mm(gathered[0], wkv, NT, BF)
-    upper_kv, q, tokens_peer, ff_own, up_own, down_own, *gathered = fence(
-        upper_kv, q, tokens_peer, ff_own, up_own, down_own, *gathered
-    )
-    f_one, f_far = along(ff_own, PAIR), along(ff_own, MIDDLE)
-    f_one, f_far, *kvs = fence(f_one, f_far, upper_kv, mm(gathered[1], wkv, NT, BF))
-    bias_row = bias[None]
+    f_one, f_far, q, upper_kv = fence(f_one, f_far, q, upper_kv)
     f_two, f_two_end = along(f_one, MIDDLE), along(f_far, OUTWARD)
     one_x, one_y = swap(f_one, 2), swap(f_one, 4)
-    held = attention_forward(q, kvs, bias_row, 0, 2)
-    f_two, f_two_end, one_x, one_y, *held = fence(f_two, f_two_end, one_x, one_y, *held)
+    tokens_peer = swap(tokens, 1)
+    f_two, f_two_end, one_x, one_y, tokens_peer, *kvs = fence(
+        f_two, f_two_end, one_x, one_y, tokens_peer, upper_kv, mm(gathered[1], wkv, NT, BF)
+    )
     f_three_end = along(f_two, OUTWARD)
     f_two = jnp.where(middle, f_two, f_two_end)
     two_x, two_y = swap(f_two, 2), swap(f_two, 4)
     one_d1, one_d2 = swap(one_y[:fp], 2), swap(one_x[fp:], 4)
-    held = attention_forward(q, kvs, bias_row, 2, 2, held)
+    bias_row = bias[None]
+    held = attention_forward(q, kvs, bias_row, 0, 3)
     f_three_end, one_d1, one_d2, two_x, two_y, *held = fence(
         f_three_end, one_d1, one_d2, two_x, two_y, *held
     )
@@ -613,8 +612,7 @@
 
     def moves(j, block):
         own, by_x, by_y, d1, d2 = block
-        last = (d1, d2, fp if d1 is d2 else 0)
-        sources = [(own, own, fp), (by_x, by_x, fp), (by_y, by_y, fp), last]
+        sources = [(own, own, fp), (by_x, by_x, fp), (by_y, by_y, fp), (d1, d2, 0)]
         for i, (a, b, at) in enumerate(sources):
             yield (a, 0, fp, 0, (4 * i + j) * fp)
             yield (b, at, fp, 1, (4 * i + j) * fp)
@@ -627,7 +625,7 @@
     w_ff = put_rows([*own, *one], (ff * 2, width), 2)
     w_ff = fence(*w_ff, *held)
     w_ff, held = w_ff[:2], w_ff[2:]
-    held = attention_forward(q, kvs, bias_row, 4, 2, held)
+    held = attention_forward(q, kvs, bias_row, 3, 3, held)
     two_d1, two_d2, three_x, three_y, *held = fence(two_d1, two_d2, three_x, three_y, *held)
     three_d1, three_d2 = swap(three_y[:fp], 2), swap(three_x[fp:], 4)
     held = attention_forward(q, kvs, bias_row, 6, 2, held)

time: 515 us -> 506 us (0.983)
  waiting for transfers between devices: 126 us -> 118 us
  local copies, waits for them, and re-layouts: 40.7 us -> 34.7 us
  starting transfers between devices: 69.1 us -> 74.9 us
    ppermute x8, waiting for transfers between devices: 26.4 us -> 35.5 us  [along(): return lax.ppermute(array, 'tp', pairs)]
    all_gather x2, waiting for transfers between devices: 8.75 us -> 0.04 us  [per_device(): lax.all_gather(tokens[n * upper:(n + 1) * upper], 'tp', axis=0, tiled=True)]
    ppermute x66, waiting for transfers between devices: 78.3 us -> 70.1 us  [swap(): return lax.ppermute(array, 'seq', [(i, i ^ bit) for i in range(self.size)])]
    ppermute x8, starting transfers between devices: 15 us -> 22.5 us  [along(): return lax.ppermute(array, 'tp', pairs)]
    unnamed x118 -> x124, local copies, waits for them, and re-layouts: 19.8 us -> 15.8 us
    pallas_call x4 -> x3, Pallas kernels: 31.3 us -> 31.5 us  [attention_forward(): pl.pallas_call(functools.partial(forward_kernel, len(kvs)), grid=(count,)...]
  transfers between devices with their start and end apart: 81 -> 81, of which waited for: 33 -> 31; matrix products, arithmetic and copies ran while one was open for 20% -> 20% of each run, Pallas kernels for 30% -> 31%
where the time goes in v6:
time: 506 us; the launch traced here: 497 us
  Pallas kernels  153 us (30%)
  waiting for transfers between devices  118 us (23%)
  starting transfers between devices  74.9 us (15%)
  matrix products  61 us (12%)
  local copies, waits for them, and re-layouts  34.7 us (7%)
  other arithmetic  34 us (7%)
  between operations  21.5 us (4%)
    pallas_call x2, Pallas kernels, attention_backward(): pl.pallas_call(backward_kernel, grid=(pairs,), in_specs=[by_pair, pl.Bloc...  72.1 us
    ppermute x66, waiting for transfers between devices, swap(): return lax.ppermute(array, 'seq', [(i, i ^ bit) for i in range(self.size)])  70.1 us
    dot_general x14, matrix products, mm(): return lax.dot_general(a, b, dims, preferred_element_type=F32).astype(out)  61 us
    ppermute x66, starting transfers between devices, swap(): return lax.ppermute(array, 'seq', [(i, i ^ bit) for i in range(self.size)])  47.7 us
    ppermute x8, waiting for transfers between devices, along(): return lax.ppermute(array, 'tp', pairs)  35.5 us
    pallas_call x3, Pallas kernels, attention_forward(): pl.pallas_call(functools.partial(forward_kernel, len(kvs)), grid=(count,)...  31.5 us
    ppermute x8, starting transfers between devices, along(): return lax.ppermute(array, 'tp', pairs)  22.5 us
    pallas_call x2, Pallas kernels, head_grads(): pl.pallas_call(functools.partial(head_grads_kernel, many), grid=(2,), in_...  21.3 us
  transfers between devices with their start and end apart: 81, of which 31 were waited for; matrix products, arithmetic and copies ran while one was open for 20% of the time, Pallas kernels for 31%

profile of v6, /device:TPU:0, one launch (start us, length us, event | category | flops | bytes accessed | tf_op | source)
XLA Modules:
  0.0 496.7 jit_solution(12663104087679223148)
XLA Ops:
  12.5 3.0 collective-permute-start
  15.6 2.6 collective-permute-start.1
  24.7 6.7 %collective-permute-done = bf16[128,1024]{1,0:T(8,128)(2,1)S(1)} collective-permute-done((bf16[128,1024]{1,0:T(8,128)(2,1)S(1)}, bf16[128,1024]{1,0:T(8,128)(2,1)S(1)}, u32[]{:S(2)}, u32[]{:S(2)}) %collective-permute-start) | collective-permute-done | bytes 262176 | tf_op jit(solution)/shard_map/ppermute | solution.py:35
  31.4 9.2 %collective-permute-done.1 = bf16[128,1024]{1,0:T(8,128)(2,1)S(1)} collective-permute-done((bf16[128,1024]{1,0:T(8,128)(2,1)S(1)}, bf16[128,1024]{1,0:T(8,128)(2,1)S(1)}, u32[]{:S(2)}, u32[]{:S(2)}) %collective-permute-start.1) | collective-permute-done | bytes 262176 | tf_op jit(solution)/shard_map/ppermute | solution.py:35
  40.6 5.9 %collective-permute-done.2 = bf16[128,1024]{1,0:T(8,128)(2,1)S(1)} collective-permute-done((bf16[128,1024]{1,0:T(8,128)(2,1)S(1)}, bf16[128,1024]{1,0:T(8,128)(2,1)S(1)}, u32[]{:S(2)}, u32[]{:S(2)}) %collective-permute-start.2) | collective-permute-done | bytes 262176 | tf_op jit(solution)/shard_map/ppermute | solution.py:35
  51.9 13.2 %collective-permute-done.3 = bf16[384,1024]{1,0:T(8,128)(2,1)} collective-permute-done((bf16[384,1024]{1,0:T(8,128)(2,1)}, bf16[384,1024]{1,0:T(8,128)(2,1)}, u32[]{:S(2)}, u32[]{:S(2)}) %collective-permute-start.3) | collective-permute-done | bytes 786464 | tf_op jit(solution)/shard_map/ppermute | solution.py:47
  81.4 5.5 %collective-permute-done.5 = bf16[192,1024]{1,0:T(8,128)(2,1)} collective-permute-done((bf16[192,1024]{1,0:T(8,128)(2,1)}, bf16[192,1024]{1,0:T(8,128)(2,1)}, u32[]{:S(2)}, u32[]{:S(2)}) %collective-permute-start.5) | collective-permute-done | bytes 393248 | tf_op jit(solution)/shard_map/ppermute | solution.py:47
  98.9 2.5 copy.49
  101.4 11.9 %collective-permute-start.12 = (bf16[256,1024]{1,0:T(8,128)(2,1)S(1)}, bf16[256,1024]{1,0:T(8,128)(2,1)}, u32[]{:S(2)}, u32[]{:S(2)}) collective-permute-start(bf16[256,1024]{1,0:T(8,128)(2,1)S(1)} %copy-done.44), channel_id=1, source_target_pairs={{0,1},{1,0},{2,3},{3,2},{4,5},{5,4},{6,7},{7,6},{8,9},{9,8},{10,11... | collective-permute-start | bytes 1572872 | tf_op jit(solution)/shard_map/ppermute | solution.py:35
  114.0 2.5 fusion.7.q_ref
  116.6 9.8 %convert_bitcast_fusion.1.refs_0_.refs_2_.k_ref.v_ref = bf16[1024,2048]{1,0:T(8,128)(2,1)} fusion(bf16[2048,1024]{1,0:T(8,128)(2,1)} %bitcast.134, bf16[1024,1024]{1,0:T(8,128)(2,1)} %all-gather.3.cloned.1.call-done.refs_4_), kind=kOutput, calls=%fused_computation.21 | convolution fusion | flops 4297064448 | bytes 10485760 | tf_op jit(solution)/shard_map/dot_general | solution.py:31
  126.3 6.6 %collective-permute-done.12.refs_2_ = bf16[256,1024]{1,0:T(8,128)(2,1)} collective-permute-done((bf16[256,1024]{1,0:T(8,128)(2,1)S(1)}, bf16[256,1024]{1,0:T(8,128)(2,1)}, u32[]{:S(2)}, u32[]{:S(2)}) %collective-permute-start.12) | collective-permute-done | bytes 524320 | tf_op jit(solution)/shard_map/ppermute | solution.py:35
  138.9 7.5 %convert_bitcast_fusion.refs_1_.refs_3_.k_ref.v_ref = bf16[1024,2048]{1,0:T(8,128)(2,1)S(1)} fusion(bf16[2048,1024]{1,0:T(8,128)(2,1)} %bitcast.135, bf16[1024,1024]{1,0:T(8,128)(2,1)} %all-gather.5.cloned.1.call-done.refs_5_), kind=kOutput, calls=%fused_computation.20 | convolution fusion | flops 4297064448 | bytes 10485760 | tf_op jit(solution)/shard_map/dot_general | solution.py:31
  146.5 7.1 %collective-permute-done.15 = bf16[256,1024]{1,0:T(8,128)(2,1)} collective-permute-done((bf16[256,1024]{1,0:T(8,128)(2,1)}, bf16[256,1024]{1,0:T(8,128)(2,1)}, u32[]{:S(2)}, u32[]{:S(2)}) %collective-permute-start.15) | collective-permute-done | bytes 524320 | tf_op jit(solution)/shard_map/ppermute | solution.py:35
  161.7 11.6 %attention_forward.3 = (bf16[512,1024]{1,0:T(8,128)(2,1)S(1)}, f32[8,2,512]{2,1,0:T(2,128)S(1)}) custom-call(bf16[512,1024]{1,0:T(8,128)(2,1)S(1)} %fusion.7.q_ref, bf16[1024,2048]{1,0:T(8,128)(2,1)S(1)} %copy-done.1, bf16[1024,2048]{1,0:T(8,128)(2,1)S(1)} %convert_bitcast_fusion.refs_1_.refs_3_.k_ref.v_ref, bf16[1024,2048]{1,0:T(8,128)(2,1)S(1)} %copy-done.1, ...), custom_call_target="tpu_custom_call" | custom-call | flops 1000000000 | bytes 1000000 | tf_op jit(solution)/shard_map/attention_forward/pallas_call | solution.py:105
  180.2 11.6 %attention_forward.4 = (bf16[512,1024]{1,0:T(8,128)(2,1)S(1)}, f32[8,2,512]{2,1,0:T(2,128)S(1)}) custom-call(bf16[512,1024]{1,0:T(8,128)(2,1)S(1)} %fusion.7.q_ref, bf16[1024,2048]{1,0:T(8,128)(2,1)S(1)} %copy-done.1, bf16[1024,2048]{1,0:T(8,128)(2,1)S(1)} %convert_bitcast_fusion.refs_1_.refs_3_.k_ref.v_ref, ...), custom_call_target="tpu_custom_call", output_to_operand_aliasing={{0}: (6, {}), {1}: (7, {})} | custom-call | flops 1000000000 | bytes 1000000 | tf_op jit(solution)/shard_map/attention_forward/pallas_call | solution.py:105
  194.1 8.2 %attention_forward.5 = (bf16[512,1024]{1,0:T(8,128)(2,1)S(1)}, f32[8,2,512]{2,1,0:T(2,128)S(1)}) custom-call(bf16[512,1024]{1,0:T(8,128)(2,1)S(1)} %fusion.7.q_ref, bf16[1024,2048]{1,0:T(8,128)(2,1)S(1)} %copy-done.1, bf16[1024,2048]{1,0:T(8,128)(2,1)S(1)} %convert_bitcast_fusion.refs_1_.refs_3_.k_ref.v_ref, ...), custom_call_target="tpu_custom_call", output_to_operand_aliasing={{0}: (6, {}), {1}: (7, {})} | custom-call | flops 1000000000 | bytes 1000000 | tf_op jit(solution)/shard_map/attention_forward/pallas_call | solution.py:105
  202.4 2.9 fusion.41
  209.0 6.5 %multiply_convert_fusion.2 = (bf16[512,2048]{1,0:T(8,128)(2,1)S(1)}, f32[512,2048]{1,0:T(8,128)}) fusion(bf16[512,1024]{1,0:T(8,128)(2,1)S(1)} %collective-permute-done.30.right_two_ref, bf16[2048,1024]{1,0:T(8,128)(2,1)S(1)} %get-tuple-element.245), kind=kOutput, calls=%fused_computation.14 | convolution fusion | flops 2169503744 | bytes 11534336 | tf_op jit(solution)/shard_map/dot_general | solution.py:31
  215.5 2.3 convolution_convert_fusion.3
  218.0 6.6 %multiply_convert_fusion.3 = (bf16[512,2048]{1,0:T(8,128)(2,1)S(1)}, f32[512,2048]{1,0:T(8,128)}) fusion(bf16[512,1024]{1,0:T(8,128)(2,1)S(1)} %multiply_convert_fusion.5.right_ref, bf16[2048,1024]{1,0:T(8,128)(2,1)S(1)} %get-tuple-element.245), kind=kOutput, calls=%fused_computation.17 | convolution fusion | flops 2169503744 | bytes 11534336 | tf_op jit(solution)/shard_map/dot_general | solution.py:31
  224.7 2.6 fusion.42
  233.1 5.3 %multiply_convert_fusion.left_two_ref = bf16[512,2048]{1,0:T(8,128)(2,1)S(1)} fusion(bf16[512,1024]{1,0:T(8,128)(2,1)S(1)} %collective-permute-done.32.right_two_ref, bf16[2048,1024]{1,0:T(8,128)(2,1)S(1)} %get-tuple-element.246, f32[512,2048]{1,0:T(8,128)S(1)} %copy-done.56), kind=kOutput, calls=%fused_computation.10 | convolution fusion | flops 2174746624 | bytes 11534336 | tf_op jit(solution)/shard_map/dot_general | solution.py:31
  238.4 2.3 convolution_convert_fusion.2
  241.2 5.5 %multiply_convert_fusion.1.left_ref = bf16[512,2048]{1,0:T(8,128)(2,1)S(1)} fusion(bf16[512,1024]{1,0:T(8,128)(2,1)S(1)} %fusion.33.right_ref, bf16[2048,1024]{1,0:T(8,128)(2,1)S(1)} %get-tuple-element.246, f32[512,2048]{1,0:T(8,128)S(1)} %copy-done.57), kind=kOutput, calls=%fused_computation.12 | convolution fusion | flops 2174746624 | bytes 11534336 | tf_op jit(solution)/shard_map/dot_general | solution.py:31
  246.8 2.3 fusion.43
  249.1 5.9 %outer_four.2 = (bf16[512,1024]{1,0:T(8,128)(2,1)S(1)}, bf16[512,1024]{1,0:T(8,128)(2,1)S(1)}, bf16[512,1024]{1,0:T(8,128)(2,1)S(1)}, bf16[512,1024]{1,0:T(8,128)(2,1)S(1)}) custom-call(bf16[512,2048]{1,0:T(8,128)(2,1)S(1)} %get-tuple-element.418.left_ref, bf16[512,1024]{1,0:T(8,128)(2,1)S(1)} %fusion.33.right_ref, ...), custom_call_target="tpu_custom_call" | custom-call | flops 1000000000 | bytes 1000000 | tf_op jit(solution)/shard_map/outer_four/pallas_call | solution.py:417
  255.0 2.9 multiply_reduce_fusion
  260.0 5.9 %outer_four.3 = (bf16[512,1024]{1,0:T(8,128)(2,1)S(1)}, bf16[512,1024]{1,0:T(8,128)(2,1)S(1)}, bf16[512,1024]{1,0:T(8,128)(2,1)S(1)}, bf16[512,1024]{1,0:T(8,128)(2,1)S(1)}) custom-call(bf16[512,2048]{1,0:T(8,128)(2,1)S(1)} %multiply_convert_fusion.1.left_ref, bf16[512,1024]{1,0:T(8,128)(2,1)S(1)} %multiply_convert_fusion.5.right_ref, ...), custom_call_target="tpu_custom_call" | custom-call | flops 1000000000 | bytes 1000000 | tf_op jit(solution)/shard_map/outer_four/pallas_call | solution.py:417
  273.6 36.6 %attention_backward.2 = (f32[512,1024]{1,0:T(8,128)S(1)}, bf16[2048,512]{1,0:T(8,128)(2,1)S(1)}, bf16[2048,512]{1,0:T(8,128)(2,1)}, bf16[2,1024,512]{2,1,0:T(8,128)(2,1)}, bf16[1024,1024]{1,0:T(8,128)(2,1)}) custom-call(bf16[512,1024]{1,0:T(8,128)(2,1)} %copy-done.3, bf16[1024,2048]{1,0:T(8,128)(2,1)} %convert_bitcast_fusion.1.refs_0_.refs_2_.k_ref.v_ref, ...), custom_call_target="tpu_custom_call" | custom-call | flops 1000000000 | bytes 1000000 | tf_op jit(solution)/shard_map/attention_backward/pallas_call | solution.py:213
  322.1 35.5 %attention_backward.3 = (bf16[512,1024]{1,0:T(8,128)(2,1)S(1)}, bf16[2048,512]{1,0:T(8,128)(2,1)}, bf16[2048,512]{1,0:T(8,128)(2,1)}, bf16[2,1024,512]{2,1,0:T(8,128)(2,1)S(1)}, bf16[1024,1024]{1,0:T(8,128)(2,1)S(1)}) custom-call(bf16[512,1024]{1,0:T(8,128)(2,1)} %copy-done.3, ...), custom_call_target="tpu_custom_call", output_to_operand_aliasing={{1}: (9, {}), {2}: (10, {})} | custom-call | flops 1000000000 | bytes 1000000 | tf_op jit(solution)/shard_map/attention_backward/pallas_call | solution.py:213
  358.9 5.2 %totals.1 = bf16[1024,1024]{1,0:T(8,128)(2,1)} custom-call(s32[1]{0:T(128)} %bitcast.48.at_ref, bf16[512,1024]{1,0:T(8,128)(2,1)} %copy-done.15, bf16[512,1024]{1,0:T(8,128)(2,1)} %copy-done.30, bf16[512,1024]{1,0:T(8,128)(2,1)} %collective-permute-done.44.refs_2_, bf16[512,1024]{1,0:T(8,128)(2,1)} %copy-done.14, ...), custom_call_target="tpu_custom_call" | custom-call | flops 1000000000 | bytes 1000000 | tf_op jit(solution)/shard_map/totals/pallas_call | solution.py:381
  365.3 2.8 collective-permute-done.48
  368.2 6.9 %head_grads.2 = (bf16[256,1024]{1,0:T(8,128)(2,1)}, bf16[256,1024]{1,0:T(8,128)(2,1)}, bf16[128,1024]{1,0:T(8,128)(2,1)S(1)}, bf16[128,1024]{1,0:T(8,128)(2,1)S(1)}, bf16[256,1024]{1,0:T(8,128)(2,1)S(1)}) custom-call(bf16[512,1024]{1,0:T(8,128)(2,1)} %copy-done.6, bf16[512,512]{1,0:T(8,128)(2,1)} %collective-permute-done.47.refs_1_, ...), custom_call_target="tpu_custom_call" | custom-call | flops 1000000000 | bytes 1000000 | tf_op jit(solution)/shard_map/head_grads/pallas_call | solution.py:318
  378.5 14.5 %head_grads.3 = (bf16[256,1024]{1,0:T(8,128)(2,1)S(1)}, bf16[256,1024]{1,0:T(8,128)(2,1)S(1)}, bf16[128,1024]{1,0:T(8,128)(2,1)S(1)}, bf16[128,1024]{1,0:T(8,128)(2,1)S(1)}, bf16[256,1024]{1,0:T(8,128)(2,1)S(1)}) custom-call(bf16[2048,512]{1,0:T(8,128)(2,1)} %get-tuple-element.303.refs_0_, bf16[2048,512]{1,0:T(8,128)(2,1)} %get-tuple-element.304.refs_1_, ...), custom_call_target="tpu_custom_call" | custom-call | flops 1000000000 | bytes 1000000 | tf_op jit(solution)/shard_map/head_grads/pallas_call | solution.py:318
  399.3 2.6 convolution_add_fusion
  401.8 12.7 %collective-permute-done.52 = bf16[128,1024]{1,0:T(8,128)(2,1)S(1)} collective-permute-done((bf16[128,1024]{1,0:T(8,128)(2,1)S(1)}, bf16[128,1024]{1,0:T(8,128)(2,1)S(1)}, u32[]{:S(2)}, u32[]{:S(2)}) %collective-permute-start.52) | collective-permute-done | bytes 262176 | tf_op jit(solution)/shard_map/ppermute | solution.py:47
  420.7 3.1 collective-permute-done.56
  426.4 4.5 all-to-all-start
  433.1 9.3 %collective-permute-done.60.refs_2_ = bf16[256,1024]{1,0:T(8,128)(2,1)S(1)} collective-permute-done((bf16[256,1024]{1,0:T(8,128)(2,1)S(1)}, bf16[256,1024]{1,0:T(8,128)(2,1)S(1)}, u32[]{:S(2)}, u32[]{:S(2)}) %collective-permute-start.60) | collective-permute-done | bytes 524320 | tf_op jit(solution)/shard_map/ppermute | solution.py:47
  445.9 6.5 %collective-permute-done.59.refs_6_ = bf16[128,1024]{1,0:T(8,128)(2,1)} collective-permute-done((bf16[128,1024]{1,0:T(8,128)(2,1)S(1)}, bf16[128,1024]{1,0:T(8,128)(2,1)}, u32[]{:S(2)}, u32[]{:S(2)}) %collective-permute-start.59) | collective-permute-done | bytes 262176 | tf_op jit(solution)/shard_map/ppermute | solution.py:47
  452.8 8.2 %all-to-all-done = bf16[4,144,1024]{2,1,0:T(8,128)(2,1)} async-done(((bf16[4,144,1024]{2,1,0:T(8,128)(2,1)}), bf16[4,144,1024]{2,1,0:T(8,128)(2,1)}, u32[]{:S(2)}, u32[]{:S(2)}) %all-to-all-start) | async-done | bytes 1179680 | tf_op jit(solution)/shard_map/all_to_all | solution.py:759
  467.5 3.5 placed.2
  471.0 2.4 placed.3
  473.4 4.8 collective-permute-done.68.refs_4_
  480.4 3.0 heads_placed.1
  483.5 3.9 reduce-scatter.11.cloned.1.call-done
  487.3 2.4 add_convert_fusion.2
  (360 shorter events, 130.4 us)
Async XLA Ops:
  7.2 109.4 %all-gather.3.cloned.1.call-start = ((), (), s32[]{:S(2)}) async-start(), calls=%async_computation.5 | async-start | bytes 2621440 | tf_op jit(solution)/shard_map/all_gather | solution.py:554
  9.5 129.4 %all-gather.5.cloned.1.call-start = ((), (), s32[]{:S(2)}) async-start(), calls=%async_computation.6 | async-start | bytes 2621440 | tf_op jit(solution)/shard_map/all_gather | solution.py:554
  12.5 18.9 %collective-permute-start = (bf16[128,1024]{1,0:T(8,128)(2,1)S(1)}, bf16[128,1024]{1,0:T(8,128)(2,1)S(1)}, u32[]{:S(2)}, u32[]{:S(2)}) collective-permute-start(bf16[128,1024]{1,0:T(8,128)(2,1)S(1)} %bitcast.160), channel_id=1, source_target_pairs={{0,1},{1,0},{2,3},{3,2},{4,5},{5,4},{6,7},{7,6},{8,9},{9,8},{10,11... | collective-permute-start | bytes 786440 | tf_op jit(solution)/shard_map/ppermute | solution.py:35
  15.6 25.1 %collective-permute-start.1 = (bf16[128,1024]{1,0:T(8,128)(2,1)S(1)}, bf16[128,1024]{1,0:T(8,128)(2,1)S(1)}, u32[]{:S(2)}, u32[]{:S(2)}) collective-permute-start(bf16[128,1024]{1,0:T(8,128)(2,1)S(1)} %bitcast.161), channel_id=1, source_target_pairs={{0,2},{1,3},{2,0},{3,1},{4,6},{5,7},{6,4},{7,5},{8,10},{9,11},{10,... | collective-permute-start | bytes 786440 | tf_op jit(solution)/shard_map/ppermute | solution.py:35
  18.2 28.4 %collective-permute-start.2 = (bf16[128,1024]{1,0:T(8,128)(2,1)S(1)}, bf16[128,1024]{1,0:T(8,128)(2,1)S(1)}, u32[]{:S(2)}, u32[]{:S(2)}) collective-permute-start(bf16[128,1024]{1,0:T(8,128)(2,1)S(1)} %bitcast.162), channel_id=1, source_target_pairs={{0,3},{1,2},{2,1},{3,0},{4,7},{5,6},{6,5},{7,4},{8,11},{9,10},{10,... | collective-permute-start | bytes 786440 | tf_op jit(solution)/shard_map/ppermute | solution.py:35
  48.7 16.4 %collective-permute-start.3 = (bf16[384,1024]{1,0:T(8,128)(2,1)}, bf16[384,1024]{1,0:T(8,128)(2,1)}, u32[]{:S(2)}, u32[]{:S(2)}) collective-permute-start(bf16[384,1024]{1,0:T(8,128)(2,1)} %constant_dynamic-update-slice_fusion), channel_id=1, source_target_pairs={{0,8},{4,12},{8,0},{12,4},{16,24},{20,28},{24,16},{28,20},{1,9},{5... | collective-permute-start | bytes 2359304 | tf_op jit(solution)/shard_map/ppermute | solution.py:47
  50.2 16.2 %collective-permute-start.4 = (bf16[384,1024]{1,0:T(8,128)(2,1)}, bf16[384,1024]{1,0:T(8,128)(2,1)}, u32[]{:S(2)}, u32[]{:S(2)}) collective-permute-start(bf16[384,1024]{1,0:T(8,128)(2,1)} %constant_dynamic-update-slice_fusion), channel_id=1, source_target_pairs={{0,16},{4,20},{8,24},{12,28},{16,0},{20,4},{24,8},{28,12},{1,17},{... | collective-permute-start | bytes 2359304 | tf_op jit(solution)/shard_map/ppermute | solution.py:47
  51.8 312.3 %reduce-scatter.5.cloned.1.call-start = ((), (), s32[]{:S(2)}) async-start(), calls=%async_computation.7 | async-start | bytes 2621440 | tf_op jit(solution)/shard_map/reduce_scatter | solution.py:683
  66.4 20.7 %collective-permute-start.7 = (bf16[384,1024]{1,0:T(8,128)(2,1)}, bf16[384,1024]{1,0:T(8,128)(2,1)}, u32[]{:S(2)}, u32[]{:S(2)}) collective-permute-start(bf16[384,1024]{1,0:T(8,128)(2,1)} %constant_dynamic-update-slice_fusion), channel_id=1, source_target_pairs={{0,4},{4,0},{8,12},{12,8},{16,20},{20,16},{24,28},{28,24},{1,5},{5... | collective-permute-start | bytes 2359304 | tf_op jit(solution)/shard_map/ppermute | solution.py:47
  66.4 20.7 %collective-permute-start.8 = (bf16[384,1024]{1,0:T(8,128)(2,1)}, bf16[384,1024]{1,0:T(8,128)(2,1)}, u32[]{:S(2)}, u32[]{:S(2)}) collective-permute-start(bf16[384,1024]{1,0:T(8,128)(2,1)} %collective-permute-done.3), channel_id=1, source_target_pairs={{0,4},{4,0},{8,12},{12,8},{16,20},{20,16},{24,28},{28,24},{1,5},{5... | collective-permute-start | bytes 2359304 | tf_op jit(solution)/shard_map/ppermute | solution.py:47
  66.9 20.2 %collective-permute-start.9 = (bf16[384,1024]{1,0:T(8,128)(2,1)}, bf16[384,1024]{1,0:T(8,128)(2,1)}, u32[]{:S(2)}, u32[]{:S(2)}) collective-permute-start(bf16[384,1024]{1,0:T(8,128)(2,1)} %collective-permute-done.4), channel_id=1, source_target_pairs={{0,4},{4,0},{8,12},{12,8},{16,20},{20,16},{24,28},{28,24},{1,5},{5... | collective-permute-start | bytes 2359304 | tf_op jit(solution)/shard_map/ppermute | solution.py:47
  86.9 59.6 %collective-permute-start.18 = (bf16[512,1024]{1,0:T(8,128)(2,1)}, bf16[512,1024]{1,0:T(8,128)(2,1)}, u32[]{:S(2)}, u32[]{:S(2)}) collective-permute-start(bf16[512,1024]{1,0:T(8,128)(2,1)} %refs_2_.1), channel_id=1, source_target_pairs={{0,4},{4,0},{8,12},{12,8},{16,20},{20,16},{24,28},{28,24},{1,5},{5... | collective-permute-start | bytes 3145736 | tf_op jit(solution)/shard_map/ppermute | solution.py:47
  101.4 31.6 %collective-permute-start.12 = (bf16[256,1024]{1,0:T(8,128)(2,1)S(1)}, bf16[256,1024]{1,0:T(8,128)(2,1)}, u32[]{:S(2)}, u32[]{:S(2)}) collective-permute-start(bf16[256,1024]{1,0:T(8,128)(2,1)S(1)} %copy-done.44), channel_id=1, source_target_pairs={{0,1},{1,0},{2,3},{3,2},{4,5},{5,4},{6,7},{7,6},{8,9},{9,8},{10,11... | collective-permute-start | bytes 1572872 | tf_op jit(solution)/shard_map/ppermute | solution.py:35
  113.3 19.6 %collective-permute-start.13 = (bf16[256,1024]{1,0:T(8,128)(2,1)S(1)}, bf16[256,1024]{1,0:T(8,128)(2,1)S(1)}, u32[]{:S(2)}, u32[]{:S(2)}) collective-permute-start(bf16[256,1024]{1,0:T(8,128)(2,1)S(1)} %copy-done.44), channel_id=1, source_target_pairs={{1,2},{2,1},{5,6},{6,5},{9,10},{10,9},{13,14},{14,13},{17,18},{18,... | collective-permute-start | bytes 1572872 | tf_op jit(solution)/shard_map/ppermute | solution.py:35
  134.5 19.1 %collective-permute-start.16 = (bf16[256,1024]{1,0:T(8,128)(2,1)}, bf16[256,1024]{1,0:T(8,128)(2,1)S(1)}, u32[]{:S(2)}, u32[]{:S(2)}) collective-permute-start(bf16[256,1024]{1,0:T(8,128)(2,1)} %collective-permute-done.12.refs_2_), channel_id=1, source_target_pairs={{0,8},{4,12},{8,0},{12,4},{16,24},{20,28},{24,16},{28,20},{1,9},{5... | collective-permute-start | bytes 1572872 | tf_op jit(solution)/shard_map/ppermute | solution.py:47
  135.9 17.6 %collective-permute-start.17 = (bf16[256,1024]{1,0:T(8,128)(2,1)}, bf16[256,1024]{1,0:T(8,128)(2,1)S(1)}, u32[]{:S(2)}, u32[]{:S(2)}) collective-permute-start(bf16[256,1024]{1,0:T(8,128)(2,1)} %collective-permute-done.12.refs_2_), channel_id=1, source_target_pairs={{0,16},{4,20},{8,24},{12,28},{16,0},{20,4},{24,8},{28,12},{1,17},{... | collective-permute-start | bytes 1572872 | tf_op jit(solution)/shard_map/ppermute | solution.py:47
  137.4 16.2 %collective-permute-start.15 = (bf16[256,1024]{1,0:T(8,128)(2,1)}, bf16[256,1024]{1,0:T(8,128)(2,1)}, u32[]{:S(2)}, u32[]{:S(2)}) collective-permute-start(bf16[256,1024]{1,0:T(8,128)(2,1)} %copy-done.45), channel_id=1, source_target_pairs={{1,0},{2,3},{5,4},{6,7},{9,8},{10,11},{13,12},{14,15},{17,16},{18,... | collective-permute-start | bytes 1572872 | tf_op jit(solution)/shard_map/ppermute | solution.py:35
  153.6 20.7 %collective-permute-start.19 = (bf16[256,1024]{1,0:T(8,128)(2,1)}, bf16[256,1024]{1,0:T(8,128)(2,1)S(1)}, u32[]{:S(2)}, u32[]{:S(2)}) collective-permute-start(bf16[256,1024]{1,0:T(8,128)(2,1)} %collective-permute-done.14), channel_id=1, source_target_pairs={{1,0},{2,3},{5,4},{6,7},{9,8},{10,11},{13,12},{14,15},{17,16},{18,... | collective-permute-start | bytes 1572872 | tf_op jit(solution)/shard_map/ppermute | solution.py:35
  156.0 18.3 %collective-permute-start.22 = (bf16[256,1024]{1,0:T(8,128)(2,1)S(1)}, bf16[256,1024]{1,0:T(8,128)(2,1)S(1)}, u32[]{:S(2)}, u32[]{:S(2)}) collective-permute-start(bf16[256,1024]{1,0:T(8,128)(2,1)S(1)} %broadcast_select_fusion.1.refs_0_), channel_id=1, source_target_pairs={{0,8},{4,12},{8,0},{12,4},{16,24},{20,28},{24,16},{28,20},{1,9},{5... | collective-permute-start | bytes 1572872 | tf_op jit(solution)/shard_map/ppermute | solution.py:47
  156.7 17.6 %collective-permute-start.23 = (bf16[256,1024]{1,0:T(8,128)(2,1)S(1)}, bf16[256,1024]{1,0:T(8,128)(2,1)S(1)}, u32[]{:S(2)}, u32[]{:S(2)}) collective-permute-start(bf16[256,1024]{1,0:T(8,128)(2,1)S(1)} %broadcast_select_fusion.1.refs_0_), channel_id=1, source_target_pairs={{0,16},{4,20},{8,24},{12,28},{16,0},{20,4},{24,8},{28,12},{1,17},{... | collective-permute-start | bytes 1572872 | tf_op jit(solution)/shard_map/ppermute | solution.py:47
  158.0 15.8 %collective-permute-start.20 = (bf16[128,1024]{1,0:T(8,128)(2,1)S(1)}, bf16[128,1024]{1,0:T(8,128)(2,1)S(1)}, u32[]{:S(2)}, u32[]{:S(2)}) collective-permute-start(bf16[128,1024]{1,0:T(8,128)(2,1)S(1)} %slice.149), channel_id=1, source_target_pairs={{0,8},{4,12},{8,0},{12,4},{16,24},{20,28},{24,16},{28,20},{1,9},{5... | collective-permute-start | bytes 786440 | tf_op jit(solution)/shard_map/ppermute | solution.py:47
  174.3 18.0 %collective-permute-start.26 = (bf16[256,1024]{1,0:T(8,128)(2,1)S(1)}, bf16[256,1024]{1,0:T(8,128)(2,1)S(1)}, u32[]{:S(2)}, u32[]{:S(2)}) collective-permute-start(bf16[256,1024]{1,0:T(8,128)(2,1)S(1)} %broadcast_select_fusion.refs_5_), channel_id=1, source_target_pairs={{0,8},{4,12},{8,0},{12,4},{16,24},{20,28},{24,16},{28,20},{1,9},{5... | collective-permute-start | bytes 1572872 | tf_op jit(solution)/shard_map/ppermute | solution.py:47
  175.7 16.6 %collective-permute-start.27 = (bf16[256,1024]{1,0:T(8,128)(2,1)S(1)}, bf16[256,1024]{1,0:T(8,128)(2,1)S(1)}, u32[]{:S(2)}, u32[]{:S(2)}) collective-permute-start(bf16[256,1024]{1,0:T(8,128)(2,1)S(1)} %broadcast_select_fusion.refs_5_), channel_id=1, source_target_pairs={{0,16},{4,20},{8,24},{12,28},{16,0},{20,4},{24,8},{28,12},{1,17},{... | collective-permute-start | bytes 1572872 | tf_op jit(solution)/shard_map/ppermute | solution.py:47
  176.3 15.5 %collective-permute-start.24 = (bf16[128,1024]{1,0:T(8,128)(2,1)S(1)}, bf16[128,1024]{1,0:T(8,128)(2,1)S(1)}, u32[]{:S(2)}, u32[]{:S(2)}) collective-permute-start(bf16[128,1024]{1,0:T(8,128)(2,1)S(1)} %slice.151), channel_id=1, source_target_pairs={{0,8},{4,12},{8,0},{12,4},{16,24},{20,28},{24,16},{28,20},{1,9},{5... | collective-permute-start | bytes 786440 | tf_op jit(solution)/shard_map/ppermute | solution.py:47
  177.0 15.3 %collective-permute-start.25 = (bf16[128,1024]{1,0:T(8,128)(2,1)S(1)}, bf16[128,1024]{1,0:T(8,128)(2,1)S(1)}, u32[]{:S(2)}, u32[]{:S(2)}) collective-permute-start(bf16[128,1024]{1,0:T(8,128)(2,1)S(1)} %slice.152), channel_id=1, source_target_pairs={{0,16},{4,20},{8,24},{12,28},{16,0},{20,4},{24,8},{28,12},{1,17},{... | collective-permute-start | bytes 786440 | tf_op jit(solution)/shard_map/ppermute | solution.py:47
  230.5 36.7 %collective-permute-start.40 = (bf16[1024,1024]{1,0:T(8,128)(2,1)}, bf16[1024,1024]{1,0:T(8,128)(2,1)}, u32[]{:S(2)}, u32[]{:S(2)}) collective-permute-start(bf16[1024,1024]{1,0:T(8,128)(2,1)} %all-gather.3.cloned.1.call-done.refs_4_), channel_id=1, source_target_pairs={{0,4},{4,0},{8,12},{12,8},{16,20},{20,16},{24,28},{28,24},{1,5},{5... | collective-permute-start | bytes 6291464 | tf_op jit(solution)/shard_map/ppermute | solution.py:47
  230.6 38.1 %collective-permute-start.41 = (bf16[1024,1024]{1,0:T(8,128)(2,1)}, bf16[1024,1024]{1,0:T(8,128)(2,1)}, u32[]{:S(2)}, u32[]{:S(2)}) collective-permute-start(bf16[1024,1024]{1,0:T(8,128)(2,1)} %all-gather.5.cloned.1.call-done.refs_5_), channel_id=1, source_target_pairs={{0,4},{4,0},{8,12},{12,8},{16,20},{20,16},{24,28},{28,24},{1,5},{5... | collective-permute-start | bytes 6291464 | tf_op jit(solution)/shard_map/ppermute | solution.py:47
  231.8 37.7 %collective-permute-start.39 = (bf16[512,512]{1,0:T(8,128)(2,1)}, bf16[512,512]{1,0:T(8,128)(2,1)S(1)}, u32[]{:S(2)}, u32[]{:S(2)}) collective-permute-start(bf16[512,512]{1,0:T(8,128)(2,1)} %slice.156), channel_id=1, source_target_pairs={{0,4},{4,0},{8,12},{12,8},{16,20},{20,16},{24,28},{28,24},{1,5},{5... | collective-permute-start | bytes 1572872 | tf_op jit(solution)/shard_map/ppermute | solution.py:47
  240.8 14.3 %collective-permute-start.33 = (bf16[512,1024]{1,0:T(8,128)(2,1)S(1)}, bf16[512,1024]{1,0:T(8,128)(2,1)S(1)}, u32[]{:S(2)}, u32[]{:S(2)}) collective-permute-start(bf16[512,1024]{1,0:T(8,128)(2,1)S(1)} %convolution_convert_fusion.2), channel_id=1, source_target_pairs={{0,4},{4,0},{8,12},{12,8},{16,20},{20,16},{24,28},{28,24},{1,5},{5... | collective-permute-start | bytes 3145736 | tf_op jit(solution)/shard_map/ppermute | solution.py:47
  266.0 46.9 %collective-permute-start.34 = (bf16[512,1024]{1,0:T(8,128)(2,1)S(1)}, bf16[512,1024]{1,0:T(8,128)(2,1)S(1)}, u32[]{:S(2)}, u32[]{:S(2)}) collective-permute-start(bf16[512,1024]{1,0:T(8,128)(2,1)S(1)} %get-tuple-element.257), channel_id=1, source_target_pairs={{0,8},{4,12},{8,0},{12,4},{16,24},{20,28},{24,16},{28,20},{1,9},{5... | collective-permute-start | bytes 3145736 | tf_op jit(solution)/shard_map/ppermute | solution.py:47
  267.2 45.6 %collective-permute-start.35 = (bf16[512,1024]{1,0:T(8,128)(2,1)S(1)}, bf16[512,1024]{1,0:T(8,128)(2,1)S(1)}, u32[]{:S(2)}, u32[]{:S(2)}) collective-permute-start(bf16[512,1024]{1,0:T(8,128)(2,1)S(1)} %get-tuple-element.258), channel_id=1, source_target_pairs={{0,16},{4,20},{8,24},{12,28},{16,0},{20,4},{24,8},{28,12},{1,17},{... | collective-permute-start | bytes 3145736 | tf_op jit(solution)/shard_map/ppermute | solution.py:47
  268.7 45.2 %collective-permute-start.36 = (bf16[512,1024]{1,0:T(8,128)(2,1)S(1)}, bf16[512,1024]{1,0:T(8,128)(2,1)S(1)}, u32[]{:S(2)}, u32[]{:S(2)}) collective-permute-start(bf16[512,1024]{1,0:T(8,128)(2,1)S(1)} %get-tuple-element.259), channel_id=1, source_target_pairs={{0,8},{4,12},{8,0},{12,4},{16,24},{20,28},{24,16},{28,20},{1,9},{5... | collective-permute-start | bytes 3145736 | tf_op jit(solution)/shard_map/ppermute | solution.py:47
  269.6 45.3 %collective-permute-start.37 = (bf16[512,1024]{1,0:T(8,128)(2,1)S(1)}, bf16[512,1024]{1,0:T(8,128)(2,1)S(1)}, u32[]{:S(2)}, u32[]{:S(2)}) collective-permute-start(bf16[512,1024]{1,0:T(8,128)(2,1)S(1)} %get-tuple-element.260), channel_id=1, source_target_pairs={{0,16},{4,20},{8,24},{12,28},{16,0},{20,4},{24,8},{28,12},{1,17},{... | collective-permute-start | bytes 3145736 | tf_op jit(solution)/shard_map/ppermute | solution.py:47
  272.4 40.4 %collective-permute-start.42 = (f32[2,1024]{1,0:T(2,128)S(1)}, f32[2,1024]{1,0:T(2,128)S(1)}, u32[]{:S(2)}, u32[]{:S(2)}) collective-permute-start(f32[2,1024]{1,0:T(2,128)S(1)} %pad_maximum_fusion.9), channel_id=1, source_target_pairs={{0,4},{4,0},{8,12},{12,8},{16,20},{20,16},{24,28},{28,24},{1,5},{5... | collective-permute-start | bytes 24584 | tf_op jit(solution)/shard_map/ppermute | solution.py:47
  316.0 100.5 %reduce-scatter.9.cloned.1.call-start = ((), (), s32[]{:S(2)}) async-start(), calls=%async_computation.9 | async-start | bytes 2621440 | tf_op jit(solution)/shard_map/reduce_scatter | solution.py:683
  316.0 42.9 %collective-permute-start.45 = (bf16[2,1024,512]{2,1,0:T(8,128)(2,1)}, bf16[2,1024,512]{2,1,0:T(8,128)(2,1)}, u32[]{:S(2)}, u32[]{:S(2)}) collective-permute-start(bf16[2,1024,512]{2,1,0:T(8,128)(2,1)} %get-tuple-element.277), channel_id=1, source_target_pairs={{0,4},{4,0},{8,12},{12,8},{16,20},{20,16},{24,28},{28,24},{1,5},{5... | collective-permute-start | bytes 6291464 | tf_op jit(solution)/shard_map/ppermute | solution.py:47
  318.2 40.7 %collective-permute-start.43 = (bf16[512,1024]{1,0:T(8,128)(2,1)S(1)}, bf16[512,1024]{1,0:T(8,128)(2,1)}, u32[]{:S(2)}, u32[]{:S(2)}) collective-permute-start(bf16[512,1024]{1,0:T(8,128)(2,1)S(1)} %add_convert_fusion.4), channel_id=1, source_target_pairs={{0,8},{4,12},{8,0},{12,4},{16,24},{20,28},{24,16},{28,20},{1,9},{5... | collective-permute-start | bytes 3145736 | tf_op jit(solution)/shard_map/ppermute | solution.py:47
  319.5 39.4 %collective-permute-start.44 = (bf16[512,1024]{1,0:T(8,128)(2,1)S(1)}, bf16[512,1024]{1,0:T(8,128)(2,1)}, u32[]{:S(2)}, u32[]{:S(2)}) collective-permute-start(bf16[512,1024]{1,0:T(8,128)(2,1)S(1)} %add_convert_fusion.3), channel_id=1, source_target_pairs={{0,16},{4,20},{8,24},{12,28},{16,0},{20,4},{24,8},{28,12},{1,17},{... | collective-permute-start | bytes 3145736 | tf_op jit(solution)/shard_map/ppermute | solution.py:47
  321.0 37.9 %collective-permute-start.46 = (f32[2,1024]{1,0:T(2,128)S(1)}, f32[2,1024]{1,0:T(2,128)S(1)}, u32[]{:S(2)}, u32[]{:S(2)}) collective-permute-start(f32[2,1024]{1,0:T(2,128)S(1)} %fusion.32), channel_id=1, source_target_pairs={{0,8},{4,12},{8,0},{12,4},{16,24},{20,28},{24,16},{28,20},{1,9},{5... | collective-permute-start | bytes 24584 | tf_op jit(solution)/shard_map/ppermute | solution.py:47
  364.2 119.3 %reduce-scatter.7.cloned.1.call-start = ((), (), s32[]{:S(2)}) async-start(), calls=%async_computation.8 | async-start | bytes 1310720 | tf_op jit(solution)/shard_map/reduce_scatter | solution.py:683
  375.0 17.9 %collective-permute-start.50 = (bf16[256,1024]{1,0:T(8,128)(2,1)}, bf16[256,1024]{1,0:T(8,128)(2,1)}, u32[]{:S(2)}, u32[]{:S(2)}) collective-permute-start(bf16[256,1024]{1,0:T(8,128)(2,1)} %get-tuple-element.301), channel_id=1, source_target_pairs={{0,8},{4,12},{8,0},{12,4},{16,24},{20,28},{24,16},{28,20},{1,9},{5... | collective-permute-start | bytes 1572872 | tf_op jit(solution)/shard_map/ppermute | solution.py:47
  376.5 16.5 %collective-permute-start.51 = (bf16[256,1024]{1,0:T(8,128)(2,1)}, bf16[256,1024]{1,0:T(8,128)(2,1)}, u32[]{:S(2)}, u32[]{:S(2)}) collective-permute-start(bf16[256,1024]{1,0:T(8,128)(2,1)} %get-tuple-element.302), channel_id=1, source_target_pairs={{0,16},{4,20},{8,24},{12,28},{16,0},{20,4},{24,8},{28,12},{1,17},{... | collective-permute-start | bytes 1572872 | tf_op jit(solution)/shard_map/ppermute | solution.py:47
  395.0 20.3 %collective-permute-start.54 = (bf16[256,1024]{1,0:T(8,128)(2,1)S(1)}, bf16[256,1024]{1,0:T(8,128)(2,1)S(1)}, u32[]{:S(2)}, u32[]{:S(2)}) collective-permute-start(bf16[256,1024]{1,0:T(8,128)(2,1)S(1)} %get-tuple-element.324), channel_id=1, source_target_pairs={{0,8},{4,12},{8,0},{12,4},{16,24},{20,28},{24,16},{28,20},{1,9},{5... | collective-permute-start | bytes 1572872 | tf_op jit(solution)/shard_map/ppermute | solution.py:47
  396.0 19.3 %collective-permute-start.55 = (bf16[256,1024]{1,0:T(8,128)(2,1)S(1)}, bf16[256,1024]{1,0:T(8,128)(2,1)S(1)}, u32[]{:S(2)}, u32[]{:S(2)}) collective-permute-start(bf16[256,1024]{1,0:T(8,128)(2,1)S(1)} %get-tuple-element.325), channel_id=1, source_target_pairs={{0,16},{4,20},{8,24},{12,28},{16,0},{20,4},{24,8},{28,12},{1,17},{... | collective-permute-start | bytes 1572872 | tf_op jit(solution)/shard_map/ppermute | solution.py:47
  397.6 16.9 %collective-permute-start.52 = (bf16[128,1024]{1,0:T(8,128)(2,1)S(1)}, bf16[128,1024]{1,0:T(8,128)(2,1)S(1)}, u32[]{:S(2)}, u32[]{:S(2)}) collective-permute-start(bf16[128,1024]{1,0:T(8,128)(2,1)S(1)} %add_convert_fusion.12), channel_id=1, source_target_pairs={{0,8},{4,12},{8,0},{12,4},{16,24},{20,28},{24,16},{28,20},{1,9},{5... | collective-permute-start | bytes 786440 | tf_op jit(solution)/shard_map/ppermute | solution.py:47
  399.0 16.3 %collective-permute-start.53 = (bf16[128,1024]{1,0:T(8,128)(2,1)S(1)}, bf16[128,1024]{1,0:T(8,128)(2,1)S(1)}, u32[]{:S(2)}, u32[]{:S(2)}) collective-permute-start(bf16[128,1024]{1,0:T(8,128)(2,1)S(1)} %add_convert_fusion.11), channel_id=1, source_target_pairs={{0,16},{4,20},{8,24},{12,28},{16,0},{20,4},{24,8},{28,12},{1,17},{... | collective-permute-start | bytes 786440 | tf_op jit(solution)/shard_map/ppermute | solution.py:47
  426.4 34.6 %all-to-all-start = ((bf16[4,144,1024]{2,1,0:T(8,128)(2,1)}), bf16[4,144,1024]{2,1,0:T(8,128)(2,1)}, u32[]{:S(2)}, u32[]{:S(2)}) async-start(bf16[4,144,1024]{2,1,0:T(8,128)(2,1)} %pad_maximum_fusion), calls=%async_computation.3 | async-start | bytes 2359296 | tf_op jit(solution)/shard_map/all_to_all | solution.py:759
  430.9 56.4 %reduce-scatter.11.cloned.1.call-start = ((), (), s32[]{:S(2)}) async-start(), calls=%async_computation.10 | async-start | bytes 1310720 | tf_op jit(solution)/shard_map/reduce_scatter | solution.py:683
  (91 other events, 823.2 us)
Sparse Core Ops, SparseCore 0:
  10.1 65.0 all-gather.2
  77.4 48.6 all-gather.4
  316.1 44.1 reduce-scatter.4
  364.3 43.4 reduce-scatter.8
  410.5 28.1 reduce-scatter.6
  461.1 26.1 reduce-scatter.10

commit v7 on v6

--- a/solution.py
+++ b/solution.py
@@ -147,7 +147,7 @@
     ]
     total_q = [0.0, 0.0]
     gks, gvs = [], []
-    sub = 512
+    sub = 1024
     for at in range(keys // sub):
         span = pl.ds(at * sub, sub)
         bias = bias_ref[span, 0:1]

time: 506 us -> 505 us (level)
  transfers between devices with their start and end apart: 81 -> 81, of which waited for: 31 -> 31; matrix products, arithmetic and copies ran while one was open for 20% -> 20% of each run, Pallas kernels for 31% -> 30%
where the time goes in v7:
time: 505 us; the launch traced here: 495 us
  Pallas kernels  150 us (30%)
  waiting for transfers between devices  119 us (24%)
  starting transfers between devices  74.6 us (15%)
  matrix products  61 us (12%)
  local copies, waits for them, and re-layouts  34.7 us (7%)
  other arithmetic  34 us (7%)
  between operations  21.5 us (4%)
    ppermute x66, waiting for transfers between devices, swap(): return lax.ppermute(array, 'seq', [(i, i ^ bit) for i in range(self.size)])  71.8 us
    pallas_call x2, Pallas kernels, attention_backward(): pl.pallas_call(backward_kernel, grid=(pairs,), in_specs=[by_pair, pl.Bloc...  69.5 us
    dot_general x14, matrix products, mm(): return lax.dot_general(a, b, dims, preferred_element_type=F32).astype(out)  61 us
    ppermute x66, starting transfers between devices, swap(): return lax.ppermute(array, 'seq', [(i, i ^ bit) for i in range(self.size)])  47.5 us
    ppermute x8, waiting for transfers between devices, along(): return lax.ppermute(array, 'tp', pairs)  35.5 us
    pallas_call x3, Pallas kernels, attention_forward(): pl.pallas_call(functools.partial(forward_kernel, len(kvs)), grid=(count,)...  31.5 us
    ppermute x8, starting transfers between devices, along(): return lax.ppermute(array, 'tp', pairs)  22.5 us
    pallas_call x2, Pallas kernels, head_grads(): pl.pallas_call(functools.partial(head_grads_kernel, many), grid=(2,), in_...  21.3 us
  transfers between devices with their start and end apart: 81, of which 31 were waited for; matrix products, arithmetic and copies ran while one was open for 20% of the time, Pallas kernels for 30%

profile of v7, /device:TPU:0, one launch (start us, length us, event | category | flops | bytes accessed | tf_op | source)
XLA Modules:
  0.0 495.4 jit_solution(15774289787676557952)
XLA Ops:
  12.5 3.0 collective-permute-start
  15.6 2.6 collective-permute-start.1
  24.7 6.7 %collective-permute-done = bf16[128,1024]{1,0:T(8,128)(2,1)S(1)} collective-permute-done((bf16[128,1024]{1,0:T(8,128)(2,1)S(1)}, bf16[128,1024]{1,0:T(8,128)(2,1)S(1)}, u32[]{:S(2)}, u32[]{:S(2)}) %collective-permute-start) | collective-permute-done | bytes 262176 | tf_op jit(solution)/shard_map/ppermute | solution.py:35
  31.4 9.2 %collective-permute-done.1 = bf16[128,1024]{1,0:T(8,128)(2,1)S(1)} collective-permute-done((bf16[128,1024]{1,0:T(8,128)(2,1)S(1)}, bf16[128,1024]{1,0:T(8,128)(2,1)S(1)}, u32[]{:S(2)}, u32[]{:S(2)}) %collective-permute-start.1) | collective-permute-done | bytes 262176 | tf_op jit(solution)/shard_map/ppermute | solution.py:35
  40.6 5.9 %collective-permute-done.2 = bf16[128,1024]{1,0:T(8,128)(2,1)S(1)} collective-permute-done((bf16[128,1024]{1,0:T(8,128)(2,1)S(1)}, bf16[128,1024]{1,0:T(8,128)(2,1)S(1)}, u32[]{:S(2)}, u32[]{:S(2)}) %collective-permute-start.2) | collective-permute-done | bytes 262176 | tf_op jit(solution)/shard_map/ppermute | solution.py:35
  51.9 13.2 %collective-permute-done.3 = bf16[384,1024]{1,0:T(8,128)(2,1)} collective-permute-done((bf16[384,1024]{1,0:T(8,128)(2,1)}, bf16[384,1024]{1,0:T(8,128)(2,1)}, u32[]{:S(2)}, u32[]{:S(2)}) %collective-permute-start.3) | collective-permute-done | bytes 786464 | tf_op jit(solution)/shard_map/ppermute | solution.py:47
  81.4 5.5 %collective-permute-done.5 = bf16[192,1024]{1,0:T(8,128)(2,1)} collective-permute-done((bf16[192,1024]{1,0:T(8,128)(2,1)}, bf16[192,1024]{1,0:T(8,128)(2,1)}, u32[]{:S(2)}, u32[]{:S(2)}) %collective-permute-start.5) | collective-permute-done | bytes 393248 | tf_op jit(solution)/shard_map/ppermute | solution.py:47
  98.9 2.5 copy.49
  101.4 11.9 %collective-permute-start.12 = (bf16[256,1024]{1,0:T(8,128)(2,1)S(1)}, bf16[256,1024]{1,0:T(8,128)(2,1)}, u32[]{:S(2)}, u32[]{:S(2)}) collective-permute-start(bf16[256,1024]{1,0:T(8,128)(2,1)S(1)} %copy-done.44), channel_id=1, source_target_pairs={{0,1},{1,0},{2,3},{3,2},{4,5},{5,4},{6,7},{7,6},{8,9},{9,8},{10,11... | collective-permute-start | bytes 1572872 | tf_op jit(solution)/shard_map/ppermute | solution.py:35
  114.0 2.5 fusion.7.q_ref
  116.6 9.8 %convert_bitcast_fusion.1.refs_0_.refs_2_.k_ref.v_ref = bf16[1024,2048]{1,0:T(8,128)(2,1)} fusion(bf16[2048,1024]{1,0:T(8,128)(2,1)} %bitcast.134, bf16[1024,1024]{1,0:T(8,128)(2,1)} %all-gather.3.cloned.1.call-done.refs_4_), kind=kOutput, calls=%fused_computation.21 | convolution fusion | flops 4297064448 | bytes 10485760 | tf_op jit(solution)/shard_map/dot_general | solution.py:31
  126.3 6.6 %collective-permute-done.12.refs_2_ = bf16[256,1024]{1,0:T(8,128)(2,1)} collective-permute-done((bf16[256,1024]{1,0:T(8,128)(2,1)S(1)}, bf16[256,1024]{1,0:T(8,128)(2,1)}, u32[]{:S(2)}, u32[]{:S(2)}) %collective-permute-start.12) | collective-permute-done | bytes 524320 | tf_op jit(solution)/shard_map/ppermute | solution.py:35
  138.9 7.5 %convert_bitcast_fusion.refs_1_.refs_3_.k_ref.v_ref = bf16[1024,2048]{1,0:T(8,128)(2,1)S(1)} fusion(bf16[2048,1024]{1,0:T(8,128)(2,1)} %bitcast.135, bf16[1024,1024]{1,0:T(8,128)(2,1)} %all-gather.5.cloned.1.call-done.refs_5_), kind=kOutput, calls=%fused_computation.20 | convolution fusion | flops 4297064448 | bytes 10485760 | tf_op jit(solution)/shard_map/dot_general | solution.py:31
  146.5 7.1 %collective-permute-done.15 = bf16[256,1024]{1,0:T(8,128)(2,1)} collective-permute-done((bf16[256,1024]{1,0:T(8,128)(2,1)}, bf16[256,1024]{1,0:T(8,128)(2,1)}, u32[]{:S(2)}, u32[]{:S(2)}) %collective-permute-start.15) | collective-permute-done | bytes 524320 | tf_op jit(solution)/shard_map/ppermute | solution.py:35
  161.7 11.6 %attention_forward.3 = (bf16[512,1024]{1,0:T(8,128)(2,1)S(1)}, f32[8,2,512]{2,1,0:T(2,128)S(1)}) custom-call(bf16[512,1024]{1,0:T(8,128)(2,1)S(1)} %fusion.7.q_ref, bf16[1024,2048]{1,0:T(8,128)(2,1)S(1)} %copy-done.1, bf16[1024,2048]{1,0:T(8,128)(2,1)S(1)} %convert_bitcast_fusion.refs_1_.refs_3_.k_ref.v_ref, bf16[1024,2048]{1,0:T(8,128)(2,1)S(1)} %copy-done.1, ...), custom_call_target="tpu_custom_call" | custom-call | flops 1000000000 | bytes 1000000 | tf_op jit(solution)/shard_map/attention_forward/pallas_call | solution.py:105
  180.2 11.6 %attention_forward.4 = (bf16[512,1024]{1,0:T(8,128)(2,1)S(1)}, f32[8,2,512]{2,1,0:T(2,128)S(1)}) custom-call(bf16[512,1024]{1,0:T(8,128)(2,1)S(1)} %fusion.7.q_ref, bf16[1024,2048]{1,0:T(8,128)(2,1)S(1)} %copy-done.1, bf16[1024,2048]{1,0:T(8,128)(2,1)S(1)} %convert_bitcast_fusion.refs_1_.refs_3_.k_ref.v_ref, ...), custom_call_target="tpu_custom_call", output_to_operand_aliasing={{0}: (6, {}), {1}: (7, {})} | custom-call | flops 1000000000 | bytes 1000000 | tf_op jit(solution)/shard_map/attention_forward/pallas_call | solution.py:105
  194.1 8.2 %attention_forward.5 = (bf16[512,1024]{1,0:T(8,128)(2,1)S(1)}, f32[8,2,512]{2,1,0:T(2,128)S(1)}) custom-call(bf16[512,1024]{1,0:T(8,128)(2,1)S(1)} %fusion.7.q_ref, bf16[1024,2048]{1,0:T(8,128)(2,1)S(1)} %copy-done.1, bf16[1024,2048]{1,0:T(8,128)(2,1)S(1)} %convert_bitcast_fusion.refs_1_.refs_3_.k_ref.v_ref, ...), custom_call_target="tpu_custom_call", output_to_operand_aliasing={{0}: (6, {}), {1}: (7, {})} | custom-call | flops 1000000000 | bytes 1000000 | tf_op jit(solution)/shard_map/attention_forward/pallas_call | solution.py:105
  202.4 2.9 fusion.41
  209.0 6.5 %multiply_convert_fusion.2 = (bf16[512,2048]{1,0:T(8,128)(2,1)S(1)}, f32[512,2048]{1,0:T(8,128)}) fusion(bf16[512,1024]{1,0:T(8,128)(2,1)S(1)} %collective-permute-done.30.right_two_ref, bf16[2048,1024]{1,0:T(8,128)(2,1)S(1)} %get-tuple-element.245), kind=kOutput, calls=%fused_computation.14 | convolution fusion | flops 2169503744 | bytes 11534336 | tf_op jit(solution)/shard_map/dot_general | solution.py:31
  218.0 6.6 %multiply_convert_fusion.3 = (bf16[512,2048]{1,0:T(8,128)(2,1)S(1)}, f32[512,2048]{1,0:T(8,128)}) fusion(bf16[512,1024]{1,0:T(8,128)(2,1)S(1)} %multiply_convert_fusion.5.right_ref, bf16[2048,1024]{1,0:T(8,128)(2,1)S(1)} %get-tuple-element.245), kind=kOutput, calls=%fused_computation.17 | convolution fusion | flops 2169503744 | bytes 11534336 | tf_op jit(solution)/shard_map/dot_general | solution.py:31
  224.7 2.6 fusion.42
  233.1 5.3 %multiply_convert_fusion.left_two_ref = bf16[512,2048]{1,0:T(8,128)(2,1)S(1)} fusion(bf16[512,1024]{1,0:T(8,128)(2,1)S(1)} %collective-permute-done.32.right_two_ref, bf16[2048,1024]{1,0:T(8,128)(2,1)S(1)} %get-tuple-element.246, f32[512,2048]{1,0:T(8,128)S(1)} %copy-done.56), kind=kOutput, calls=%fused_computation.10 | convolution fusion | flops 2174746624 | bytes 11534336 | tf_op jit(solution)/shard_map/dot_general | solution.py:31
  238.4 2.3 convolution_convert_fusion.2
  241.2 5.5 %multiply_convert_fusion.1.left_ref = bf16[512,2048]{1,0:T(8,128)(2,1)S(1)} fusion(bf16[512,1024]{1,0:T(8,128)(2,1)S(1)} %fusion.33.right_ref, bf16[2048,1024]{1,0:T(8,128)(2,1)S(1)} %get-tuple-element.246, f32[512,2048]{1,0:T(8,128)S(1)} %copy-done.57), kind=kOutput, calls=%fused_computation.12 | convolution fusion | flops 2174746624 | bytes 11534336 | tf_op jit(solution)/shard_map/dot_general | solution.py:31
  246.8 2.3 fusion.43
  249.1 5.9 %outer_four.2 = (bf16[512,1024]{1,0:T(8,128)(2,1)S(1)}, bf16[512,1024]{1,0:T(8,128)(2,1)S(1)}, bf16[512,1024]{1,0:T(8,128)(2,1)S(1)}, bf16[512,1024]{1,0:T(8,128)(2,1)S(1)}) custom-call(bf16[512,2048]{1,0:T(8,128)(2,1)S(1)} %get-tuple-element.418.left_ref, bf16[512,1024]{1,0:T(8,128)(2,1)S(1)} %fusion.33.right_ref, ...), custom_call_target="tpu_custom_call" | custom-call | flops 1000000000 | bytes 1000000 | tf_op jit(solution)/shard_map/outer_four/pallas_call | solution.py:417
  255.0 2.9 multiply_reduce_fusion
  260.0 5.9 %outer_four.3 = (bf16[512,1024]{1,0:T(8,128)(2,1)S(1)}, bf16[512,1024]{1,0:T(8,128)(2,1)S(1)}, bf16[512,1024]{1,0:T(8,128)(2,1)S(1)}, bf16[512,1024]{1,0:T(8,128)(2,1)S(1)}) custom-call(bf16[512,2048]{1,0:T(8,128)(2,1)S(1)} %multiply_convert_fusion.1.left_ref, bf16[512,1024]{1,0:T(8,128)(2,1)S(1)} %multiply_convert_fusion.5.right_ref, ...), custom_call_target="tpu_custom_call" | custom-call | flops 1000000000 | bytes 1000000 | tf_op jit(solution)/shard_map/outer_four/pallas_call | solution.py:417
  273.6 35.2 %attention_backward.2 = (f32[512,1024]{1,0:T(8,128)S(1)}, bf16[2048,512]{1,0:T(8,128)(2,1)S(1)}, bf16[2048,512]{1,0:T(8,128)(2,1)}, bf16[2,1024,512]{2,1,0:T(8,128)(2,1)}, bf16[1024,1024]{1,0:T(8,128)(2,1)}) custom-call(bf16[512,1024]{1,0:T(8,128)(2,1)} %copy-done.3, bf16[1024,2048]{1,0:T(8,128)(2,1)} %convert_bitcast_fusion.1.refs_0_.refs_2_.k_ref.v_ref, ...), custom_call_target="tpu_custom_call" | custom-call | flops 1000000000 | bytes 1000000 | tf_op jit(solution)/shard_map/attention_backward/pallas_call | solution.py:213
  311.6 2.4 collective-permute-done.36.refs_1_
  322.1 34.3 %attention_backward.3 = (bf16[512,1024]{1,0:T(8,128)(2,1)S(1)}, bf16[2048,512]{1,0:T(8,128)(2,1)}, bf16[2048,512]{1,0:T(8,128)(2,1)}, bf16[2,1024,512]{2,1,0:T(8,128)(2,1)S(1)}, bf16[1024,1024]{1,0:T(8,128)(2,1)S(1)}) custom-call(bf16[512,1024]{1,0:T(8,128)(2,1)} %copy-done.3, ...), custom_call_target="tpu_custom_call", output_to_operand_aliasing={{1}: (9, {}), {2}: (10, {})} | custom-call | flops 1000000000 | bytes 1000000 | tf_op jit(solution)/shard_map/attention_backward/pallas_call | solution.py:213
  357.7 5.2 %totals.1 = bf16[1024,1024]{1,0:T(8,128)(2,1)} custom-call(s32[1]{0:T(128)} %bitcast.48.at_ref, bf16[512,1024]{1,0:T(8,128)(2,1)} %copy-done.15, bf16[512,1024]{1,0:T(8,128)(2,1)} %copy-done.30, bf16[512,1024]{1,0:T(8,128)(2,1)} %collective-permute-done.44.refs_2_, bf16[512,1024]{1,0:T(8,128)(2,1)} %copy-done.14, ...), custom_call_target="tpu_custom_call" | custom-call | flops 1000000000 | bytes 1000000 | tf_op jit(solution)/shard_map/totals/pallas_call | solution.py:381
  364.1 2.8 collective-permute-done.48
  366.9 6.9 %head_grads.2 = (bf16[256,1024]{1,0:T(8,128)(2,1)}, bf16[256,1024]{1,0:T(8,128)(2,1)}, bf16[128,1024]{1,0:T(8,128)(2,1)S(1)}, bf16[128,1024]{1,0:T(8,128)(2,1)S(1)}, bf16[256,1024]{1,0:T(8,128)(2,1)S(1)}) custom-call(bf16[512,1024]{1,0:T(8,128)(2,1)} %copy-done.6, bf16[512,512]{1,0:T(8,128)(2,1)} %collective-permute-done.47.refs_1_, ...), custom_call_target="tpu_custom_call" | custom-call | flops 1000000000 | bytes 1000000 | tf_op jit(solution)/shard_map/head_grads/pallas_call | solution.py:318
  377.3 14.5 %head_grads.3 = (bf16[256,1024]{1,0:T(8,128)(2,1)S(1)}, bf16[256,1024]{1,0:T(8,128)(2,1)S(1)}, bf16[128,1024]{1,0:T(8,128)(2,1)S(1)}, bf16[128,1024]{1,0:T(8,128)(2,1)S(1)}, bf16[256,1024]{1,0:T(8,128)(2,1)S(1)}) custom-call(bf16[2048,512]{1,0:T(8,128)(2,1)} %get-tuple-element.303.refs_0_, bf16[2048,512]{1,0:T(8,128)(2,1)} %get-tuple-element.304.refs_1_, ...), custom_call_target="tpu_custom_call" | custom-call | flops 1000000000 | bytes 1000000 | tf_op jit(solution)/shard_map/head_grads/pallas_call | solution.py:318
  398.1 2.6 convolution_add_fusion
  400.7 12.8 %collective-permute-done.52 = bf16[128,1024]{1,0:T(8,128)(2,1)S(1)} collective-permute-done((bf16[128,1024]{1,0:T(8,128)(2,1)S(1)}, bf16[128,1024]{1,0:T(8,128)(2,1)S(1)}, u32[]{:S(2)}, u32[]{:S(2)}) %collective-permute-start.52) | collective-permute-done | bytes 262176 | tf_op jit(solution)/shard_map/ppermute | solution.py:47
  419.5 3.2 collective-permute-done.56
  425.3 4.4 all-to-all-start
  431.9 9.4 %collective-permute-done.60.refs_2_ = bf16[256,1024]{1,0:T(8,128)(2,1)S(1)} collective-permute-done((bf16[256,1024]{1,0:T(8,128)(2,1)S(1)}, bf16[256,1024]{1,0:T(8,128)(2,1)S(1)}, u32[]{:S(2)}, u32[]{:S(2)}) %collective-permute-start.60) | collective-permute-done | bytes 524320 | tf_op jit(solution)/shard_map/ppermute | solution.py:47
  444.6 6.7 %collective-permute-done.59.refs_6_ = bf16[128,1024]{1,0:T(8,128)(2,1)} collective-permute-done((bf16[128,1024]{1,0:T(8,128)(2,1)S(1)}, bf16[128,1024]{1,0:T(8,128)(2,1)}, u32[]{:S(2)}, u32[]{:S(2)}) %collective-permute-start.59) | collective-permute-done | bytes 262176 | tf_op jit(solution)/shard_map/ppermute | solution.py:47
  451.7 8.1 %all-to-all-done = bf16[4,144,1024]{2,1,0:T(8,128)(2,1)} async-done(((bf16[4,144,1024]{2,1,0:T(8,128)(2,1)}), bf16[4,144,1024]{2,1,0:T(8,128)(2,1)}, u32[]{:S(2)}, u32[]{:S(2)}) %all-to-all-start) | async-done | bytes 1179680 | tf_op jit(solution)/shard_map/all_to_all | solution.py:759
  466.2 3.5 placed.2
  469.7 2.4 placed.3
  472.1 4.8 collective-permute-done.68.refs_4_
  479.2 3.0 heads_placed.1
  482.2 3.9 reduce-scatter.11.cloned.1.call-done
  486.1 2.4 add_convert_fusion.2
  (360 shorter events, 131.4 us)
Async XLA Ops:
  7.2 109.4 %all-gather.3.cloned.1.call-start = ((), (), s32[]{:S(2)}) async-start(), calls=%async_computation.5 | async-start | bytes 2621440 | tf_op jit(solution)/shard_map/all_gather | solution.py:554
  9.5 129.4 %all-gather.5.cloned.1.call-start = ((), (), s32[]{:S(2)}) async-start(), calls=%async_computation.6 | async-start | bytes 2621440 | tf_op jit(solution)/shard_map/all_gather | solution.py:554
  12.5 18.9 %collective-permute-start = (bf16[128,1024]{1,0:T(8,128)(2,1)S(1)}, bf16[128,1024]{1,0:T(8,128)(2,1)S(1)}, u32[]{:S(2)}, u32[]{:S(2)}) collective-permute-start(bf16[128,1024]{1,0:T(8,128)(2,1)S(1)} %bitcast.160), channel_id=1, source_target_pairs={{0,1},{1,0},{2,3},{3,2},{4,5},{5,4},{6,7},{7,6},{8,9},{9,8},{10,11... | collective-permute-start | bytes 786440 | tf_op jit(solution)/shard_map/ppermute | solution.py:35
  15.6 25.1 %collective-permute-start.1 = (bf16[128,1024]{1,0:T(8,128)(2,1)S(1)}, bf16[128,1024]{1,0:T(8,128)(2,1)S(1)}, u32[]{:S(2)}, u32[]{:S(2)}) collective-permute-start(bf16[128,1024]{1,0:T(8,128)(2,1)S(1)} %bitcast.161), channel_id=1, source_target_pairs={{0,2},{1,3},{2,0},{3,1},{4,6},{5,7},{6,4},{7,5},{8,10},{9,11},{10,... | collective-permute-start | bytes 786440 | tf_op jit(solution)/shard_map/ppermute | solution.py:35
  18.2 28.4 %collective-permute-start.2 = (bf16[128,1024]{1,0:T(8,128)(2,1)S(1)}, bf16[128,1024]{1,0:T(8,128)(2,1)S(1)}, u32[]{:S(2)}, u32[]{:S(2)}) collective-permute-start(bf16[128,1024]{1,0:T(8,128)(2,1)S(1)} %bitcast.162), channel_id=1, source_target_pairs={{0,3},{1,2},{2,1},{3,0},{4,7},{5,6},{6,5},{7,4},{8,11},{9,10},{10,... | collective-permute-start | bytes 786440 | tf_op jit(solution)/shard_map/ppermute | solution.py:35
  48.7 16.4 %collective-permute-start.3 = (bf16[384,1024]{1,0:T(8,128)(2,1)}, bf16[384,1024]{1,0:T(8,128)(2,1)}, u32[]{:S(2)}, u32[]{:S(2)}) collective-permute-start(bf16[384,1024]{1,0:T(8,128)(2,1)} %constant_dynamic-update-slice_fusion), channel_id=1, source_target_pairs={{0,8},{4,12},{8,0},{12,4},{16,24},{20,28},{24,16},{28,20},{1,9},{5... | collective-permute-start | bytes 2359304 | tf_op jit(solution)/shard_map/ppermute | solution.py:47
  50.2 16.2 %collective-permute-start.4 = (bf16[384,1024]{1,0:T(8,128)(2,1)}, bf16[384,1024]{1,0:T(8,128)(2,1)}, u32[]{:S(2)}, u32[]{:S(2)}) collective-permute-start(bf16[384,1024]{1,0:T(8,128)(2,1)} %constant_dynamic-update-slice_fusion), channel_id=1, source_target_pairs={{0,16},{4,20},{8,24},{12,28},{16,0},{20,4},{24,8},{28,12},{1,17},{... | collective-permute-start | bytes 2359304 | tf_op jit(solution)/shard_map/ppermute | solution.py:47
  51.8 311.1 %reduce-scatter.5.cloned.1.call-start = ((), (), s32[]{:S(2)}) async-start(), calls=%async_computation.7 | async-start | bytes 2621440 | tf_op jit(solution)/shard_map/reduce_scatter | solution.py:683
  66.4 20.7 %collective-permute-start.7 = (bf16[384,1024]{1,0:T(8,128)(2,1)}, bf16[384,1024]{1,0:T(8,128)(2,1)}, u32[]{:S(2)}, u32[]{:S(2)}) collective-permute-start(bf16[384,1024]{1,0:T(8,128)(2,1)} %constant_dynamic-update-slice_fusion), channel_id=1, source_target_pairs={{0,4},{4,0},{8,12},{12,8},{16,20},{20,16},{24,28},{28,24},{1,5},{5... | collective-permute-start | bytes 2359304 | tf_op jit(solution)/shard_map/ppermute | solution.py:47
  66.4 20.7 %collective-permute-start.8 = (bf16[384,1024]{1,0:T(8,128)(2,1)}, bf16[384,1024]{1,0:T(8,128)(2,1)}, u32[]{:S(2)}, u32[]{:S(2)}) collective-permute-start(bf16[384,1024]{1,0:T(8,128)(2,1)} %collective-permute-done.3), channel_id=1, source_target_pairs={{0,4},{4,0},{8,12},{12,8},{16,20},{20,16},{24,28},{28,24},{1,5},{5... | collective-permute-start | bytes 2359304 | tf_op jit(solution)/shard_map/ppermute | solution.py:47
  66.9 20.2 %collective-permute-start.9 = (bf16[384,1024]{1,0:T(8,128)(2,1)}, bf16[384,1024]{1,0:T(8,128)(2,1)}, u32[]{:S(2)}, u32[]{:S(2)}) collective-permute-start(bf16[384,1024]{1,0:T(8,128)(2,1)} %collective-permute-done.4), channel_id=1, source_target_pairs={{0,4},{4,0},{8,12},{12,8},{16,20},{20,16},{24,28},{28,24},{1,5},{5... | collective-permute-start | bytes 2359304 | tf_op jit(solution)/shard_map/ppermute | solution.py:47
  86.9 59.6 %collective-permute-start.18 = (bf16[512,1024]{1,0:T(8,128)(2,1)}, bf16[512,1024]{1,0:T(8,128)(2,1)}, u32[]{:S(2)}, u32[]{:S(2)}) collective-permute-start(bf16[512,1024]{1,0:T(8,128)(2,1)} %refs_2_.1), channel_id=1, source_target_pairs={{0,4},{4,0},{8,12},{12,8},{16,20},{20,16},{24,28},{28,24},{1,5},{5... | collective-permute-start | bytes 3145736 | tf_op jit(solution)/shard_map/ppermute | solution.py:47
  101.4 31.6 %collective-permute-start.12 = (bf16[256,1024]{1,0:T(8,128)(2,1)S(1)}, bf16[256,1024]{1,0:T(8,128)(2,1)}, u32[]{:S(2)}, u32[]{:S(2)}) collective-permute-start(bf16[256,1024]{1,0:T(8,128)(2,1)S(1)} %copy-done.44), channel_id=1, source_target_pairs={{0,1},{1,0},{2,3},{3,2},{4,5},{5,4},{6,7},{7,6},{8,9},{9,8},{10,11... | collective-permute-start | bytes 1572872 | tf_op jit(solution)/shard_map/ppermute | solution.py:35
  113.3 19.6 %collective-permute-start.13 = (bf16[256,1024]{1,0:T(8,128)(2,1)S(1)}, bf16[256,1024]{1,0:T(8,128)(2,1)S(1)}, u32[]{:S(2)}, u32[]{:S(2)}) collective-permute-start(bf16[256,1024]{1,0:T(8,128)(2,1)S(1)} %copy-done.44), channel_id=1, source_target_pairs={{1,2},{2,1},{5,6},{6,5},{9,10},{10,9},{13,14},{14,13},{17,18},{18,... | collective-permute-start | bytes 1572872 | tf_op jit(solution)/shard_map/ppermute | solution.py:35
  134.5 19.1 %collective-permute-start.16 = (bf16[256,1024]{1,0:T(8,128)(2,1)}, bf16[256,1024]{1,0:T(8,128)(2,1)S(1)}, u32[]{:S(2)}, u32[]{:S(2)}) collective-permute-start(bf16[256,1024]{1,0:T(8,128)(2,1)} %collective-permute-done.12.refs_2_), channel_id=1, source_target_pairs={{0,8},{4,12},{8,0},{12,4},{16,24},{20,28},{24,16},{28,20},{1,9},{5... | collective-permute-start | bytes 1572872 | tf_op jit(solution)/shard_map/ppermute | solution.py:47
  135.9 17.6 %collective-permute-start.17 = (bf16[256,1024]{1,0:T(8,128)(2,1)}, bf16[256,1024]{1,0:T(8,128)(2,1)S(1)}, u32[]{:S(2)}, u32[]{:S(2)}) collective-permute-start(bf16[256,1024]{1,0:T(8,128)(2,1)} %collective-permute-done.12.refs_2_), channel_id=1, source_target_pairs={{0,16},{4,20},{8,24},{12,28},{16,0},{20,4},{24,8},{28,12},{1,17},{... | collective-permute-start | bytes 1572872 | tf_op jit(solution)/shard_map/ppermute | solution.py:47
  137.4 16.2 %collective-permute-start.15 = (bf16[256,1024]{1,0:T(8,128)(2,1)}, bf16[256,1024]{1,0:T(8,128)(2,1)}, u32[]{:S(2)}, u32[]{:S(2)}) collective-permute-start(bf16[256,1024]{1,0:T(8,128)(2,1)} %copy-done.45), channel_id=1, source_target_pairs={{1,0},{2,3},{5,4},{6,7},{9,8},{10,11},{13,12},{14,15},{17,16},{18,... | collective-permute-start | bytes 1572872 | tf_op jit(solution)/shard_map/ppermute | solution.py:35
  153.6 20.7 %collective-permute-start.19 = (bf16[256,1024]{1,0:T(8,128)(2,1)}, bf16[256,1024]{1,0:T(8,128)(2,1)S(1)}, u32[]{:S(2)}, u32[]{:S(2)}) collective-permute-start(bf16[256,1024]{1,0:T(8,128)(2,1)} %collective-permute-done.14), channel_id=1, source_target_pairs={{1,0},{2,3},{5,4},{6,7},{9,8},{10,11},{13,12},{14,15},{17,16},{18,... | collective-permute-start | bytes 1572872 | tf_op jit(solution)/shard_map/ppermute | solution.py:35
  156.0 18.3 %collective-permute-start.22 = (bf16[256,1024]{1,0:T(8,128)(2,1)S(1)}, bf16[256,1024]{1,0:T(8,128)(2,1)S(1)}, u32[]{:S(2)}, u32[]{:S(2)}) collective-permute-start(bf16[256,1024]{1,0:T(8,128)(2,1)S(1)} %broadcast_select_fusion.1.refs_0_), channel_id=1, source_target_pairs={{0,8},{4,12},{8,0},{12,4},{16,24},{20,28},{24,16},{28,20},{1,9},{5... | collective-permute-start | bytes 1572872 | tf_op jit(solution)/shard_map/ppermute | solution.py:47
  156.7 17.6 %collective-permute-start.23 = (bf16[256,1024]{1,0:T(8,128)(2,1)S(1)}, bf16[256,1024]{1,0:T(8,128)(2,1)S(1)}, u32[]{:S(2)}, u32[]{:S(2)}) collective-permute-start(bf16[256,1024]{1,0:T(8,128)(2,1)S(1)} %broadcast_select_fusion.1.refs_0_), channel_id=1, source_target_pairs={{0,16},{4,20},{8,24},{12,28},{16,0},{20,4},{24,8},{28,12},{1,17},{... | collective-permute-start | bytes 1572872 | tf_op jit(solution)/shard_map/ppermute | solution.py:47
  158.0 15.8 %collective-permute-start.20 = (bf16[128,1024]{1,0:T(8,128)(2,1)S(1)}, bf16[128,1024]{1,0:T(8,128)(2,1)S(1)}, u32[]{:S(2)}, u32[]{:S(2)}) collective-permute-start(bf16[128,1024]{1,0:T(8,128)(2,1)S(1)} %slice.149), channel_id=1, source_target_pairs={{0,8},{4,12},{8,0},{12,4},{16,24},{20,28},{24,16},{28,20},{1,9},{5... | collective-permute-start | bytes 786440 | tf_op jit(solution)/shard_map/ppermute | solution.py:47
  174.3 18.0 %collective-permute-start.26 = (bf16[256,1024]{1,0:T(8,128)(2,1)S(1)}, bf16[256,1024]{1,0:T(8,128)(2,1)S(1)}, u32[]{:S(2)}, u32[]{:S(2)}) collective-permute-start(bf16[256,1024]{1,0:T(8,128)(2,1)S(1)} %broadcast_select_fusion.refs_5_), channel_id=1, source_target_pairs={{0,8},{4,12},{8,0},{12,4},{16,24},{20,28},{24,16},{28,20},{1,9},{5... | collective-permute-start | bytes 1572872 | tf_op jit(solution)/shard_map/ppermute | solution.py:47
  175.7 16.6 %collective-permute-start.27 = (bf16[256,1024]{1,0:T(8,128)(2,1)S(1)}, bf16[256,1024]{1,0:T(8,128)(2,1)S(1)}, u32[]{:S(2)}, u32[]{:S(2)}) collective-permute-start(bf16[256,1024]{1,0:T(8,128)(2,1)S(1)} %broadcast_select_fusion.refs_5_), channel_id=1, source_target_pairs={{0,16},{4,20},{8,24},{12,28},{16,0},{20,4},{24,8},{28,12},{1,17},{... | collective-permute-start | bytes 1572872 | tf_op jit(solution)/shard_map/ppermute | solution.py:47
  176.3 15.5 %collective-permute-start.24 = (bf16[128,1024]{1,0:T(8,128)(2,1)S(1)}, bf16[128,1024]{1,0:T(8,128)(2,1)S(1)}, u32[]{:S(2)}, u32[]{:S(2)}) collective-permute-start(bf16[128,1024]{1,0:T(8,128)(2,1)S(1)} %slice.151), channel_id=1, source_target_pairs={{0,8},{4,12},{8,0},{12,4},{16,24},{20,28},{24,16},{28,20},{1,9},{5... | collective-permute-start | bytes 786440 | tf_op jit(solution)/shard_map/ppermute | solution.py:47
  177.0 15.3 %collective-permute-start.25 = (bf16[128,1024]{1,0:T(8,128)(2,1)S(1)}, bf16[128,1024]{1,0:T(8,128)(2,1)S(1)}, u32[]{:S(2)}, u32[]{:S(2)}) collective-permute-start(bf16[128,1024]{1,0:T(8,128)(2,1)S(1)} %slice.152), channel_id=1, source_target_pairs={{0,16},{4,20},{8,24},{12,28},{16,0},{20,4},{24,8},{28,12},{1,17},{... | collective-permute-start | bytes 786440 | tf_op jit(solution)/shard_map/ppermute | solution.py:47
  230.5 36.7 %collective-permute-start.40 = (bf16[1024,1024]{1,0:T(8,128)(2,1)}, bf16[1024,1024]{1,0:T(8,128)(2,1)}, u32[]{:S(2)}, u32[]{:S(2)}) collective-permute-start(bf16[1024,1024]{1,0:T(8,128)(2,1)} %all-gather.3.cloned.1.call-done.refs_4_), channel_id=1, source_target_pairs={{0,4},{4,0},{8,12},{12,8},{16,20},{20,16},{24,28},{28,24},{1,5},{5... | collective-permute-start | bytes 6291464 | tf_op jit(solution)/shard_map/ppermute | solution.py:47
  230.6 38.1 %collective-permute-start.41 = (bf16[1024,1024]{1,0:T(8,128)(2,1)}, bf16[1024,1024]{1,0:T(8,128)(2,1)}, u32[]{:S(2)}, u32[]{:S(2)}) collective-permute-start(bf16[1024,1024]{1,0:T(8,128)(2,1)} %all-gather.5.cloned.1.call-done.refs_5_), channel_id=1, source_target_pairs={{0,4},{4,0},{8,12},{12,8},{16,20},{20,16},{24,28},{28,24},{1,5},{5... | collective-permute-start | bytes 6291464 | tf_op jit(solution)/shard_map/ppermute | solution.py:47
  231.8 37.7 %collective-permute-start.39 = (bf16[512,512]{1,0:T(8,128)(2,1)}, bf16[512,512]{1,0:T(8,128)(2,1)S(1)}, u32[]{:S(2)}, u32[]{:S(2)}) collective-permute-start(bf16[512,512]{1,0:T(8,128)(2,1)} %slice.156), channel_id=1, source_target_pairs={{0,4},{4,0},{8,12},{12,8},{16,20},{20,16},{24,28},{28,24},{1,5},{5... | collective-permute-start | bytes 1572872 | tf_op jit(solution)/shard_map/ppermute | solution.py:47
  240.8 14.3 %collective-permute-start.33 = (bf16[512,1024]{1,0:T(8,128)(2,1)S(1)}, bf16[512,1024]{1,0:T(8,128)(2,1)S(1)}, u32[]{:S(2)}, u32[]{:S(2)}) collective-permute-start(bf16[512,1024]{1,0:T(8,128)(2,1)S(1)} %convolution_convert_fusion.2), channel_id=1, source_target_pairs={{0,4},{4,0},{8,12},{12,8},{16,20},{20,16},{24,28},{28,24},{1,5},{5... | collective-permute-start | bytes 3145736 | tf_op jit(solution)/shard_map/ppermute | solution.py:47
  266.0 45.6 %collective-permute-start.34 = (bf16[512,1024]{1,0:T(8,128)(2,1)S(1)}, bf16[512,1024]{1,0:T(8,128)(2,1)S(1)}, u32[]{:S(2)}, u32[]{:S(2)}) collective-permute-start(bf16[512,1024]{1,0:T(8,128)(2,1)S(1)} %get-tuple-element.257), channel_id=1, source_target_pairs={{0,8},{4,12},{8,0},{12,4},{16,24},{20,28},{24,16},{28,20},{1,9},{5... | collective-permute-start | bytes 3145736 | tf_op jit(solution)/shard_map/ppermute | solution.py:47
  267.2 44.3 %collective-permute-start.35 = (bf16[512,1024]{1,0:T(8,128)(2,1)S(1)}, bf16[512,1024]{1,0:T(8,128)(2,1)S(1)}, u32[]{:S(2)}, u32[]{:S(2)}) collective-permute-start(bf16[512,1024]{1,0:T(8,128)(2,1)S(1)} %get-tuple-element.258), channel_id=1, source_target_pairs={{0,16},{4,20},{8,24},{12,28},{16,0},{20,4},{24,8},{28,12},{1,17},{... | collective-permute-start | bytes 3145736 | tf_op jit(solution)/shard_map/ppermute | solution.py:47
  268.7 45.2 %collective-permute-start.36 = (bf16[512,1024]{1,0:T(8,128)(2,1)S(1)}, bf16[512,1024]{1,0:T(8,128)(2,1)S(1)}, u32[]{:S(2)}, u32[]{:S(2)}) collective-permute-start(bf16[512,1024]{1,0:T(8,128)(2,1)S(1)} %get-tuple-element.259), channel_id=1, source_target_pairs={{0,8},{4,12},{8,0},{12,4},{16,24},{20,28},{24,16},{28,20},{1,9},{5... | collective-permute-start | bytes 3145736 | tf_op jit(solution)/shard_map/ppermute | solution.py:47
  269.6 45.3 %collective-permute-start.37 = (bf16[512,1024]{1,0:T(8,128)(2,1)S(1)}, bf16[512,1024]{1,0:T(8,128)(2,1)S(1)}, u32[]{:S(2)}, u32[]{:S(2)}) collective-permute-start(bf16[512,1024]{1,0:T(8,128)(2,1)S(1)} %get-tuple-element.260), channel_id=1, source_target_pairs={{0,16},{4,20},{8,24},{12,28},{16,0},{20,4},{24,8},{28,12},{1,17},{... | collective-permute-start | bytes 3145736 | tf_op jit(solution)/shard_map/ppermute | solution.py:47
  272.4 39.1 %collective-permute-start.42 = (f32[2,1024]{1,0:T(2,128)S(1)}, f32[2,1024]{1,0:T(2,128)S(1)}, u32[]{:S(2)}, u32[]{:S(2)}) collective-permute-start(f32[2,1024]{1,0:T(2,128)S(1)} %pad_maximum_fusion.9), channel_id=1, source_target_pairs={{0,4},{4,0},{8,12},{12,8},{16,20},{20,16},{24,28},{28,24},{1,5},{5... | collective-permute-start | bytes 24584 | tf_op jit(solution)/shard_map/ppermute | solution.py:47
  316.0 99.4 %reduce-scatter.9.cloned.1.call-start = ((), (), s32[]{:S(2)}) async-start(), calls=%async_computation.9 | async-start | bytes 2621440 | tf_op jit(solution)/shard_map/reduce_scatter | solution.py:683
  316.0 41.6 %collective-permute-start.45 = (bf16[2,1024,512]{2,1,0:T(8,128)(2,1)}, bf16[2,1024,512]{2,1,0:T(8,128)(2,1)}, u32[]{:S(2)}, u32[]{:S(2)}) collective-permute-start(bf16[2,1024,512]{2,1,0:T(8,128)(2,1)} %get-tuple-element.277), channel_id=1, source_target_pairs={{0,4},{4,0},{8,12},{12,8},{16,20},{20,16},{24,28},{28,24},{1,5},{5... | collective-permute-start | bytes 6291464 | tf_op jit(solution)/shard_map/ppermute | solution.py:47
  318.2 39.4 %collective-permute-start.43 = (bf16[512,1024]{1,0:T(8,128)(2,1)S(1)}, bf16[512,1024]{1,0:T(8,128)(2,1)}, u32[]{:S(2)}, u32[]{:S(2)}) collective-permute-start(bf16[512,1024]{1,0:T(8,128)(2,1)S(1)} %add_convert_fusion.4), channel_id=1, source_target_pairs={{0,8},{4,12},{8,0},{12,4},{16,24},{20,28},{24,16},{28,20},{1,9},{5... | collective-permute-start | bytes 3145736 | tf_op jit(solution)/shard_map/ppermute | solution.py:47
  319.5 38.2 %collective-permute-start.44 = (bf16[512,1024]{1,0:T(8,128)(2,1)S(1)}, bf16[512,1024]{1,0:T(8,128)(2,1)}, u32[]{:S(2)}, u32[]{:S(2)}) collective-permute-start(bf16[512,1024]{1,0:T(8,128)(2,1)S(1)} %add_convert_fusion.3), channel_id=1, source_target_pairs={{0,16},{4,20},{8,24},{12,28},{16,0},{20,4},{24,8},{28,12},{1,17},{... | collective-permute-start | bytes 3145736 | tf_op jit(solution)/shard_map/ppermute | solution.py:47
  321.0 36.7 %collective-permute-start.46 = (f32[2,1024]{1,0:T(2,128)S(1)}, f32[2,1024]{1,0:T(2,128)S(1)}, u32[]{:S(2)}, u32[]{:S(2)}) collective-permute-start(f32[2,1024]{1,0:T(2,128)S(1)} %fusion.32), channel_id=1, source_target_pairs={{0,8},{4,12},{8,0},{12,4},{16,24},{20,28},{24,16},{28,20},{1,9},{5... | collective-permute-start | bytes 24584 | tf_op jit(solution)/shard_map/ppermute | solution.py:47
  362.9 119.3 %reduce-scatter.7.cloned.1.call-start = ((), (), s32[]{:S(2)}) async-start(), calls=%async_computation.8 | async-start | bytes 1310720 | tf_op jit(solution)/shard_map/reduce_scatter | solution.py:683
  373.8 18.0 %collective-permute-start.50 = (bf16[256,1024]{1,0:T(8,128)(2,1)}, bf16[256,1024]{1,0:T(8,128)(2,1)}, u32[]{:S(2)}, u32[]{:S(2)}) collective-permute-start(bf16[256,1024]{1,0:T(8,128)(2,1)} %get-tuple-element.301), channel_id=1, source_target_pairs={{0,8},{4,12},{8,0},{12,4},{16,24},{20,28},{24,16},{28,20},{1,9},{5... | collective-permute-start | bytes 1572872 | tf_op jit(solution)/shard_map/ppermute | solution.py:47
  375.3 16.5 %collective-permute-start.51 = (bf16[256,1024]{1,0:T(8,128)(2,1)}, bf16[256,1024]{1,0:T(8,128)(2,1)}, u32[]{:S(2)}, u32[]{:S(2)}) collective-permute-start(bf16[256,1024]{1,0:T(8,128)(2,1)} %get-tuple-element.302), channel_id=1, source_target_pairs={{0,16},{4,20},{8,24},{12,28},{16,0},{20,4},{24,8},{28,12},{1,17},{... | collective-permute-start | bytes 1572872 | tf_op jit(solution)/shard_map/ppermute | solution.py:47
  393.9 20.4 %collective-permute-start.54 = (bf16[256,1024]{1,0:T(8,128)(2,1)S(1)}, bf16[256,1024]{1,0:T(8,128)(2,1)S(1)}, u32[]{:S(2)}, u32[]{:S(2)}) collective-permute-start(bf16[256,1024]{1,0:T(8,128)(2,1)S(1)} %get-tuple-element.324), channel_id=1, source_target_pairs={{0,8},{4,12},{8,0},{12,4},{16,24},{20,28},{24,16},{28,20},{1,9},{5... | collective-permute-start | bytes 1572872 | tf_op jit(solution)/shard_map/ppermute | solution.py:47
  394.9 19.3 %collective-permute-start.55 = (bf16[256,1024]{1,0:T(8,128)(2,1)S(1)}, bf16[256,1024]{1,0:T(8,128)(2,1)S(1)}, u32[]{:S(2)}, u32[]{:S(2)}) collective-permute-start(bf16[256,1024]{1,0:T(8,128)(2,1)S(1)} %get-tuple-element.325), channel_id=1, source_target_pairs={{0,16},{4,20},{8,24},{12,28},{16,0},{20,4},{24,8},{28,12},{1,17},{... | collective-permute-start | bytes 1572872 | tf_op jit(solution)/shard_map/ppermute | solution.py:47
  396.4 17.0 %collective-permute-start.52 = (bf16[128,1024]{1,0:T(8,128)(2,1)S(1)}, bf16[128,1024]{1,0:T(8,128)(2,1)S(1)}, u32[]{:S(2)}, u32[]{:S(2)}) collective-permute-start(bf16[128,1024]{1,0:T(8,128)(2,1)S(1)} %add_convert_fusion.12), channel_id=1, source_target_pairs={{0,8},{4,12},{8,0},{12,4},{16,24},{20,28},{24,16},{28,20},{1,9},{5... | collective-permute-start | bytes 786440 | tf_op jit(solution)/shard_map/ppermute | solution.py:47
  397.8 16.4 %collective-permute-start.53 = (bf16[128,1024]{1,0:T(8,128)(2,1)S(1)}, bf16[128,1024]{1,0:T(8,128)(2,1)S(1)}, u32[]{:S(2)}, u32[]{:S(2)}) collective-permute-start(bf16[128,1024]{1,0:T(8,128)(2,1)S(1)} %add_convert_fusion.11), channel_id=1, source_target_pairs={{0,16},{4,20},{8,24},{12,28},{16,0},{20,4},{24,8},{28,12},{1,17},{... | collective-permute-start | bytes 786440 | tf_op jit(solution)/shard_map/ppermute | solution.py:47
  425.3 34.4 %all-to-all-start = ((bf16[4,144,1024]{2,1,0:T(8,128)(2,1)}), bf16[4,144,1024]{2,1,0:T(8,128)(2,1)}, u32[]{:S(2)}, u32[]{:S(2)}) async-start(bf16[4,144,1024]{2,1,0:T(8,128)(2,1)} %pad_maximum_fusion), calls=%async_computation.3 | async-start | bytes 2359296 | tf_op jit(solution)/shard_map/all_to_all | solution.py:759
  429.7 56.4 %reduce-scatter.11.cloned.1.call-start = ((), (), s32[]{:S(2)}) async-start(), calls=%async_computation.10 | async-start | bytes 1310720 | tf_op jit(solution)/shard_map/reduce_scatter | solution.py:683
  (91 other events, 825.9 us)
Sparse Core Ops, SparseCore 0:
  10.1 65.0 all-gather.2
  77.4 48.6 all-gather.4
  316.1 44.1 reduce-scatter.4
  363.1 43.3 reduce-scatter.8
  409.2 28.0 reduce-scatter.6
  459.9 26.1 reduce-scatter.10
